TPU v7x, 32 devices: a whole 2x2x4 slice. The times are simulated.
32 devices in a mesh: dp: 8 (over y, x, core), cache: 4 (over z).
Axes of the slice: x: 2, y: 2, z: 4, core: 2. Of those that a mesh axis runs over, the one named last changes fastest.
Arguments:
- queries: bfloat16 [2048, 64, 128], P('dp'), may hold values from -20 to 20
- out_grad: bfloat16 [2048, 64, 128], P('dp'), may hold values from -288 to 288
- self_lse: float32 [2048, 64], P('dp'), may hold values from 5 to 11
- self_dot: float32 [2048, 64], P('dp'), may hold values from -600 to 600
- cache: float32 [512, 2, 8, 128], P(('dp', 'cache')), may hold values from -20 to 20
- first_moment: float32 [512, 2, 8, 128], P(('dp', 'cache')), may hold values from -3 to 3
- second_moment: float32 [512, 2, 8, 128], P(('dp', 'cache')), may hold values from 0.3 to 6
Outputs:
- new_cache: float32 [512, 2, 8, 128], P(('dp', 'cache'))
- new_first: float32 [512, 2, 8, 128], P(('dp', 'cache'))
- new_second: float32 [512, 2, 8, 128], P(('dp', 'cache'))
All inputs are finite; a program needn't handle non-finite values.
Results may differ from a plain program's by a relative error of at most 0.0086.
Values may be sent and summed in bfloat16 or wider, within the bound.
No kernel may reach another device: no remote copies, remote signals or barrier semaphores. Data moves between devices by JAX's collectives and lax.ppermute only.
A program may use at most 128 MiB of HBM per device.

v0:
```python
import math

import jax
import jax.numpy as jnp
from jax import lax
from jax.sharding import PartitionSpec as P

QBLOCK = 128
STEP = 200


learn_rate = 0.02
beta_first = 0.9
beta_second = 0.999
epsilon = 1e-08


def combined_all(value, axis, join):
    pieces = jax.tree.map(lambda part: lax.all_gather(part, axis), value)
    head = jax.tree.map(lambda part: part[0], pieces)
    tail = jax.tree.map(lambda part: part[1:], pieces)
    running, _ = lax.scan(lambda running, piece: (join(running, piece), None), head, tail)
    return running


def combine_pair(earlier, later):
    top_score = jnp.maximum(earlier[0], later[0])
    row_sum = earlier[1] * jnp.exp(earlier[0] - top_score) + later[1] * jnp.exp(
        later[0] - top_score
    )
    return (top_score, row_sum)


def block_gradient(kept_block):
    dscore, weights, queries_block, grads_block = kept_block
    key_grad = jnp.einsum(
        "tgrj,tgre->jge", dscore, queries_block, preferred_element_type=jnp.float32
    )
    value_grad = jnp.einsum(
        "tgrj,tgre->jge", weights, grads_block, preferred_element_type=jnp.float32
    )
    return jnp.stack([key_grad, value_grad], axis=1)


def per_device(queries, out_grad, self_lse, self_dot, cache, first_moment, second_moment):
    groups = cache.shape[2]
    head_width = cache.shape[3]
    group_size = queries.shape[1] // groups
    score_scale = 1.0 / math.sqrt(head_width)
    rounded = cache.astype(jnp.bfloat16)
    gathered = lax.all_gather(rounded, "dp", axis=0, tiled=True)
    key_rows = gathered[:, 0]
    value_rows = gathered[:, 1]
    blocks = queries.shape[0] // QBLOCK
    saved_blocks = []
    for block_index in range(blocks):
        lowest = block_index * QBLOCK
        queries_block = queries[lowest : lowest + QBLOCK].reshape(
            QBLOCK, groups, group_size, head_width
        )
        grads_block = out_grad[lowest : lowest + QBLOCK].reshape(
            QBLOCK, groups, group_size, head_width
        )
        side_lse = self_lse[lowest : lowest + QBLOCK].reshape(QBLOCK, groups, group_size)
        side_dot = self_dot[lowest : lowest + QBLOCK].reshape(QBLOCK, groups, group_size)
        scores = (
            jnp.einsum(
                "tgre,jge->tgrj", queries_block, key_rows, preferred_element_type=jnp.float32
            )
            * score_scale
        )
        slopes = jnp.einsum(
            "tgre,jge->tgrj", grads_block, value_rows, preferred_element_type=jnp.float32
        )
        local_top = jnp.max(scores, axis=-1)
        shifted = jnp.exp(scores - local_top[..., None])
        local_sum = jnp.sum(shifted, axis=-1)
        top_score, row_sum = combined_all((local_top, local_sum), "cache", combine_pair)
        row_peak = jnp.maximum(top_score, side_lse)
        row_total = row_sum * jnp.exp(top_score - row_peak) + jnp.exp(side_lse - row_peak)
        log_total = row_peak + jnp.log(row_total)
        probability = jnp.exp(scores - log_total[..., None])
        partial_delta = jnp.sum(probability * slopes, axis=-1)
        row_delta = lax.psum(partial_delta, "cache") + jnp.exp(side_lse - log_total) * side_dot
        weights = probability.astype(jnp.bfloat16)
        dscore = (score_scale * probability * (slopes - row_delta[..., None])).astype(jnp.bfloat16)
        kept_block = (dscore, weights, queries_block, grads_block)
        saved_blocks.append(kept_block)
    total_grad = block_gradient(saved_blocks[0])
    for kept_block in saved_blocks[1:]:
        total_grad = total_grad + block_gradient(kept_block)
    gradient = lax.psum_scatter(total_grad, "dp", scatter_dimension=0, tiled=True)
    new_first = beta_first * first_moment + (1.0 - beta_first) * gradient
    new_second = beta_second * second_moment + (1.0 - beta_second) * gradient * gradient
    first_hat = new_first / (1.0 - beta_first**STEP)
    second_hat = new_second / (1.0 - beta_second**STEP)
    new_cache = cache - learn_rate * first_hat / (jnp.sqrt(second_hat) + epsilon)
    return (new_cache, new_first, new_second)


def solution(mesh):
    in_specs = (
        P("dp", None, None),
        P("dp", None, None),
        P("dp", None),
        P("dp", None),
        P(("dp", "cache"), None, None, None),
        P(("dp", "cache"), None, None, None),
        P(("dp", "cache"), None, None, None),
    )
    out_specs = (
        P(("dp", "cache"), None, None, None),
        P(("dp", "cache"), None, None, None),
        P(("dp", "cache"), None, None, None),
    )
    return jax.shard_map(
        per_device, mesh=mesh, in_specs=in_specs, out_specs=out_specs, check_vma=False
    )
```

profile of v0, /device:TPU:0, one launch (start us, length us, event | category | flops | bytes accessed | tf_op | source)
XLA Modules:
  0.0 195.8 jit_solution(16946711132619002930)
XLA Ops:
  7.2 0.0 all-reduce.3.cloned.1.call-start
  7.2 4.6 %fusion.68 = (bf16[128,64,128]{2,1,0:T(8,128)(2,1)S(1)}, bf16[128,64,128]{2,1,0:T(8,128)(2,1)}) fusion(bf16[256,64,128]{2,1,0:T(8,128)(2,1)} %param.11), kind=kLoop, calls=%fused_computation.86 | loop fusion | bytes 8388608 | tf_op jit(solution)/shard_map/slice | solution.py:58
  11.9 12.4 %all_gather.27 = bf16[128,2,8,128]{3,0,2,1:T(8,128)(2,1)S(1)} all-gather(bf16[16,2,8,128]{3,0,2,1:T(8,128)(2,1)S(1)} %copy.54), channel_id=1, replica_groups=mesh['dp'=8,'cache'=4] {'dp'}, dimensions={0}, use_global_device_ids=true | all-gather | bytes 589824 | tf_op jit(solution)/shard_map/all_gather | solution.py:51
  24.2 1.4 copy.27
  25.6 0.7 bitcast_reduce_fusion
  26.3 0.0 copy-start
  26.3 13.6 %all-gather.2 = f32[512,8,8]{0,2,1:T(8,128)S(1)} all-gather(f32[128,8,8]{0,2,1:T(8,128)S(1)} %get-tuple-element.120), channel_id=4, replica_groups=mesh['dp'=8,'cache'=4] {'cache'}, dimensions={0}, use_global_device_ids=true | all-gather | bytes 163840 | tf_op jit(solution)/shard_map/all_gather | solution.py:19
  39.9 1.0 fusion.4
  41.0 13.5 %all-gather.3 = f32[512,8,8]{0,2,1:T(8,128)S(1)} all-gather(f32[128,8,8]{0,2,1:T(8,128)S(1)} %fusion.4), channel_id=5, replica_groups=mesh['dp'=8,'cache'=4] {'cache'}, dimensions={0}, use_global_device_ids=true | all-gather | bytes 163840 | tf_op jit(solution)/shard_map/all_gather | solution.py:19
  54.4 3.0 %copy.23 = bf16[128,64,128]{2,0,1:T(8,128)(2,1)S(1)} copy(bf16[128,64,128]{2,1,0:T(8,128)(2,1)} %get-tuple-element.113) | data formatting | bytes 4194304 | tf_op jit(solution)/shard_map/slice | solution.py:58
  57.5 0.7 bitcast_reduce_fusion.1
  58.2 0.0 copy-start.10
  58.2 13.5 %all-gather = f32[512,8,8]{0,2,1:T(8,128)S(1)} all-gather(f32[128,8,8]{0,2,1:T(8,128)S(1)} %get-tuple-element.122), channel_id=2, replica_groups=mesh['dp'=8,'cache'=4] {'cache'}, dimensions={0}, use_global_device_ids=true | all-gather | bytes 163840 | tf_op jit(solution)/shard_map/all_gather | solution.py:19
  71.7 0.0 copy-done.4
  71.7 1.0 fusion.10
  72.8 0.0 copy-done.6
  72.8 13.5 %all-gather.1 = f32[512,8,8]{0,2,1:T(8,128)S(1)} all-gather(f32[128,8,8]{0,2,1:T(8,128)S(1)} %fusion.10), channel_id=3, replica_groups=mesh['dp'=8,'cache'=4] {'cache'}, dimensions={0}, use_global_device_ids=true | all-gather | bytes 163840 | tf_op jit(solution)/shard_map/all_gather | solution.py:19
  86.3 0.0 copy-done.10
  86.3 2.3 %fusion.69 = (bf16[128,64,128]{2,1,0:T(8,128)(2,1)}, bf16[128,64,128]{2,1,0:T(8,128)(2,1)S(1)}) fusion(bf16[256,64,128]{2,1,0:T(8,128)(2,1)S(1)} %copy-done.10), kind=kLoop, calls=%fused_computation.87 | loop fusion | bytes 8388608 | tf_op jit(solution)/shard_map/slice | solution.py:61
  88.7 0.0 copy-done.12
  88.7 0.0 slice-start.4
  88.7 0.0 slice-start.6
  88.7 0.0 slice-start.1
  88.7 0.0 slice-start.3
  88.7 0.0 slice-start
  88.7 0.0 slice-start.2
  88.8 2.7 %copy.26 = bf16[128,64,128]{2,0,1:T(8,128)(2,1)} copy(bf16[128,64,128]{2,1,0:T(8,128)(2,1)S(1)} %get-tuple-element.115) | data formatting | bytes 4194304 | tf_op jit(solution)/shard_map/slice | solution.py:61
  91.6 0.0 copy-start.16
  91.6 0.4 while.25
  91.6 0.1 constant_dynamic-slice_fusion.7
  91.7 0.1 constant_dynamic-slice_fusion.7
  91.8 0.1 constant_dynamic-slice_fusion.7
  92.0 0.0 slice-done.1
  92.1 0.4 while.24
  92.1 0.1 constant_dynamic-slice_fusion.6
  92.3 0.1 constant_dynamic-slice_fusion.6
  92.4 0.1 constant_dynamic-slice_fusion.6
  92.5 3.1 %copy.30 = bf16[128,64,128]{2,0,1:T(8,128)(2,1)S(1)} copy(bf16[128,64,128]{2,1,0:T(8,128)(2,1)} %get-tuple-element.114) | data formatting | bytes 4194304 | tf_op jit(solution)/shard_map/slice | solution.py:61
  95.7 0.0 copy-done.5
  95.7 0.0 copy-start.1
  95.7 5.9 %fusion.6 = (f32[128,8,8]{0,2,1:T(8,128)}, f32[8,128,128,8]{2,1,3,0:T(8,128)}) fusion(f32[8,128,128,8]{2,1,3,0:T(8,128)S(1)} %copy-done.5, f32[128,8,8]{0,2,1:T(8,128)S(1)} %get-tuple-element.119, bf16[128,8,8,128]{3,0,2,1:T(8,128)(2,1)} %bitcast.222, bf16[128,2,8,128]{3,0,2,1:T(8,128)(2,1)S(1)} %all_gather.27), kind=kOutput, calls=%fused_computation.19 | convolution fusion | flops 272621568 | bytes 10813440 | tf_op jit(solution)/shard_map/tgre,jge->tgrj/dot_general | solution.py:72
  101.6 3.6 %fusion = (f32[128,8,8]{0,2,1:T(8,128)}, f32[8,128,128,8]{2,1,3,0:T(8,128)}) fusion(f32[8,128,128,8]{2,1,3,0:T(8,128)S(1)} %copy-done.1, f32[128,8,8]{0,2,1:T(8,128)S(1)} %get-tuple-element.118, bf16[128,8,8,128]{3,0,2,1:T(8,128)(2,1)S(1)} %bitcast.224, bf16[128,2,8,128]{3,0,2,1:T(8,128)(2,1)S(1)} %all_gather.27), kind=kOutput, calls=%fused_computation.8 | convolution fusion | flops 272621568 | bytes 10813440 | tf_op jit(solution)/shard_map/tgre,jge->tgrj/dot_general | solution.py:72
  105.2 0.0 all-reduce.3.cloned.1.call-update
  105.2 0.0 reduce-scatter.2.cloned.1.call-start
  105.3 3.9 %fusion.32 = f32[128,1,8,128]{3,0,2,1:T(8,128)S(1)} fusion(bf16[128,8,8,128]{3,0,2,1:T(8,128)(2,1)} %bitcast.223, f32[8,128,128,8]{2,1,3,0:T(8,128)} %copy-done.4, f32[128,8,8]{0,2,1:T(8,128)S(1)} %get-tuple-element.119), kind=kOutput, calls=%fused_computation.40 | convolution fusion | flops 271581184 | bytes 6848512 | tf_op jit(solution)/shard_map/tgrj,tgre->jge/dot_general | solution.py:39
  109.2 0.2 copy-done.2
  109.3 0.7 copy-done.8
  110.0 0.9 fusion.35
  110.9 29.0 %all-reduce.3.cloned.1.call-done = (f32[128,8,8]{0,2,1:T(8,128)}, f32[128,8,8]{0,2,1:T(8,128)}) async-done(((f32[128,8,8]{0,2,1:T(8,128)}, f32[128,8,8]{0,2,1:T(8,128)}), (f32[128,8,8]{0,2,1:T(8,128)}, f32[128,8,8]{0,2,1:T(8,128)})) %all-reduce.3.cloned.1.call-update) | async-done | bytes 65552 | tf_op jit(solution)/shard_map/psum | solution.py:84
  139.9 0.0 copy-done.17
  139.9 0.8 fusion.44
  140.7 0.0 copy-start.3
  140.8 5.5 %fusion.29 = f32[128,1,8,128]{3,0,2,1:T(8,128)S(1)} fusion(bf16[128,8,8,128]{3,0,2,1:T(8,128)(2,1)} %bitcast.221, f32[8,128,128,8]{2,1,3,0:T(8,128)} %get-tuple-element.125, f32[8,128,128,8]{2,1,3,0:T(8,128)} %copy-done.4, f32[128,8,8]{0,2,1:T(8,128)S(1)} %get-tuple-element.117, f32[128,8,8]{0,2,1:T(8,128)S(1)} %get-tuple-element.119), kind=kOutput, calls=%fused_computation.39 | convolution fusion | flops 274726912 | bytes 11075584 | tf_op jit(solution)/shard_map/tgrj,tgre->jge/dot_general | solution.py:36
  146.3 1.0 copy-done.9
  147.3 1.4 fusion.26
  148.7 0.0 copy-start.18
  148.7 0.0 copy-start.19
  148.7 1.1 maximum_add_fusion
  149.8 0.0 reduce-scatter.2.cloned.1.call-update
  149.9 35.9 %reduce-scatter.2.cloned.1.call-done = f32[16,2,8,128]{3,0,2,1:T(8,128)} async-done(((f32[128,2,8,128]{3,0,2,1:T(8,128)}), f32[16,2,8,128]{3,0,2,1:T(8,128)}) %reduce-scatter.2.cloned.1.call-update) | async-done | bytes 131088 | tf_op jit(solution)/shard_map/reduce_scatter | solution.py:92
  185.8 1.1 divide_subtract_fusion
  186.8 0.7 copy.33
  187.5 0.7 copy.34
  188.2 0.7 copy.35
  (47 shorter events, 0.6 us)
Async XLA Ops:
  7.2 4.7 %copy-start.15 = (f32[16,2,8,128]{3,2,1,0:T(8,128)S(1)}, f32[16,2,8,128]{3,2,1,0:T(8,128)}, u32[]{:S(2)}) copy-start(f32[16,2,8,128]{3,2,1,0:T(8,128)} %param.15) | copy-start | bytes 393220
  7.2 132.8 %all-reduce.3.cloned.1.call-start = ((), (), s32[]{:S(2)}) async-start(), calls=%async_computation.2 | async-start | bytes 131072 | tf_op jit(solution)/shard_map/psum | solution.py:84
  26.3 13.6 %copy-start = (f32[8,128,128,8]{2,1,3,0:T(8,128)}, f32[8,128,128,8]{2,1,3,0:T(8,128)S(1)}, u32[]{:S(2)}) copy-start(f32[8,128,128,8]{2,1,3,0:T(8,128)S(1)} %get-tuple-element.121) | copy-start | bytes 12582916
  39.9 17.5 %copy-start.13 = (f32[512,8,8]{0,2,1:T(8,128)}, f32[512,8,8]{0,2,1:T(8,128)S(1)}, u32[]{:S(2)}) copy-start(f32[512,8,8]{0,2,1:T(8,128)S(1)} %all-gather.2) | copy-start | bytes 393220
  54.4 3.8 %copy-start.14 = (f32[512,8,8]{0,2,1:T(8,128)}, f32[512,8,8]{0,2,1:T(8,128)S(1)}, u32[]{:S(2)}) copy-start(f32[512,8,8]{0,2,1:T(8,128)S(1)} %all-gather.3) | copy-start | bytes 393220
  57.5 15.3 %copy-start.6 = (bf16[128,64,128]{2,0,1:T(8,128)(2,1)}, bf16[128,64,128]{2,0,1:T(8,128)(2,1)S(1)}, u32[]{:S(2)}) copy-start(bf16[128,64,128]{2,0,1:T(8,128)(2,1)S(1)} %copy.23) | copy-start | bytes 6291460
  58.2 13.5 %copy-start.4 = (f32[8,128,128,8]{2,1,3,0:T(8,128)}, f32[8,128,128,8]{2,1,3,0:T(8,128)S(1)}, u32[]{:S(2)}) copy-start(f32[8,128,128,8]{2,1,3,0:T(8,128)S(1)} %get-tuple-element.123) | copy-start | bytes 12582916
  58.2 28.1 %copy-start.10 = (bf16[256,64,128]{2,1,0:T(8,128)(2,1)S(1)}, bf16[256,64,128]{2,1,0:T(8,128)(2,1)}, u32[]{:S(2)}) copy-start(bf16[256,64,128]{2,1,0:T(8,128)(2,1)} %param.12) | copy-start | bytes 12582916
  71.7 16.9 %copy-start.11 = (f32[512,8,8]{0,2,1:T(8,128)}, f32[512,8,8]{0,2,1:T(8,128)S(1)}, u32[]{:S(2)}) copy-start(f32[512,8,8]{0,2,1:T(8,128)S(1)} %all-gather) | copy-start | bytes 393220
  86.3 2.4 %copy-start.12 = (f32[512,8,8]{0,2,1:T(8,128)}, f32[512,8,8]{0,2,1:T(8,128)S(1)}, u32[]{:S(2)}) copy-start(f32[512,8,8]{0,2,1:T(8,128)S(1)} %all-gather.1) | copy-start | bytes 393220
  88.7 2.8 %slice-start.5 = ((f32[512,8,8]{0,2,1:T(8,128)}), f32[384,8,8]{0,2,1:T(8,128)S(1)}, s32[]{:S(2)}) async-start(f32[512,8,8]{0,2,1:T(8,128)} %copy-done.13), calls=%async_computation.8 | async-start | bytes 196608 | tf_op jit(solution)/shard_map/slice | solution.py:21
  88.7 2.8 %slice-start.7 = ((f32[512,8,8]{0,2,1:T(8,128)}), f32[384,8,8]{0,2,1:T(8,128)S(1)}, s32[]{:S(2)}) async-start(f32[512,8,8]{0,2,1:T(8,128)} %copy-done.14), calls=%async_computation.10 | async-start | bytes 196608 | tf_op jit(solution)/shard_map/slice | solution.py:21
  88.7 2.9 %slice-start.4 = ((f32[512,8,8]{0,2,1:T(8,128)}), f32[128,8,8]{0,2,1:T(8,128)S(1)}, s32[]{:S(2)}) async-start(f32[512,8,8]{0,2,1:T(8,128)} %copy-done.13), calls=%async_computation.7 | async-start | bytes 65536 | tf_op jit(solution)/shard_map/slice | solution.py:20
  88.7 2.9 %slice-start.6 = ((f32[512,8,8]{0,2,1:T(8,128)}), f32[128,8,8]{0,2,1:T(8,128)S(1)}, s32[]{:S(2)}) async-start(f32[512,8,8]{0,2,1:T(8,128)} %copy-done.14), calls=%async_computation.9 | async-start | bytes 65536 | tf_op jit(solution)/shard_map/slice | solution.py:20
  88.7 3.3 %slice-start.1 = ((f32[512,8,8]{0,2,1:T(8,128)}), f32[384,8,8]{0,2,1:T(8,128)S(1)}, s32[]{:S(2)}) async-start(f32[512,8,8]{0,2,1:T(8,128)} %copy-done.11), calls=%async_computation.4 | async-start | bytes 196608 | tf_op jit(solution)/shard_map/slice | solution.py:21
  88.7 3.3 %slice-start.3 = ((f32[512,8,8]{0,2,1:T(8,128)}), f32[384,8,8]{0,2,1:T(8,128)S(1)}, s32[]{:S(2)}) async-start(f32[512,8,8]{0,2,1:T(8,128)} %copy-done.12), calls=%async_computation.6 | async-start | bytes 196608 | tf_op jit(solution)/shard_map/slice | solution.py:21
  88.7 3.4 %slice-start = ((f32[512,8,8]{0,2,1:T(8,128)}), f32[128,8,8]{0,2,1:T(8,128)S(1)}, s32[]{:S(2)}) async-start(f32[512,8,8]{0,2,1:T(8,128)} %copy-done.11), calls=%async_computation.3 | async-start | bytes 65536 | tf_op jit(solution)/shard_map/slice | solution.py:20
  88.7 3.4 %slice-start.2 = ((f32[512,8,8]{0,2,1:T(8,128)}), f32[128,8,8]{0,2,1:T(8,128)S(1)}, s32[]{:S(2)}) async-start(f32[512,8,8]{0,2,1:T(8,128)} %copy-done.12), calls=%async_computation.5 | async-start | bytes 65536 | tf_op jit(solution)/shard_map/slice | solution.py:20
  91.6 4.1 %copy-start.16 = (f32[256,64]{0,1:T(8,128)S(1)}, f32[256,64]{0,1:T(8,128)}, u32[]{:S(2)}) copy-start(f32[256,64]{0,1:T(8,128)} %param.13) | copy-start | bytes 196612
  92.5 3.2 %copy-start.5 = (f32[8,128,128,8]{2,1,3,0:T(8,128)S(1)}, f32[8,128,128,8]{2,1,3,0:T(8,128)}, u32[]{:S(2)}) copy-start(f32[8,128,128,8]{2,1,3,0:T(8,128)} %copy-done.4) | copy-start | bytes 12582916
  95.6 6.0 %copy-start.7 = (bf16[128,64,128]{2,0,1:T(8,128)(2,1)}, bf16[128,64,128]{2,0,1:T(8,128)(2,1)S(1)}, u32[]{:S(2)}) copy-start(bf16[128,64,128]{2,0,1:T(8,128)(2,1)S(1)} %copy.30) | copy-start | bytes 6291460
  95.7 5.9 %copy-start.1 = (f32[8,128,128,8]{2,1,3,0:T(8,128)S(1)}, f32[8,128,128,8]{2,1,3,0:T(8,128)}, u32[]{:S(2)}) copy-start(f32[8,128,128,8]{2,1,3,0:T(8,128)} %copy-done) | copy-start | bytes 12582916
  105.2 80.5 %reduce-scatter.2.cloned.1.call-start = ((), (), s32[]{:S(2)}) async-start(), calls=%async_computation.1 | async-start | bytes 1179648 | tf_op jit(solution)/shard_map/reduce_scatter | solution.py:92
  105.3 4.1 %copy-start.2 = (f32[8,128,128,8]{2,1,3,0:T(8,128)S(1)}, f32[8,128,128,8]{2,1,3,0:T(8,128)}, u32[]{:S(2)}) copy-start(f32[8,128,128,8]{2,1,3,0:T(8,128)} %copy-done) | copy-start | bytes 12582916
  105.3 4.7 %copy-start.8 = (bf16[128,64,128]{2,0,1:T(8,128)(2,1)S(1)}, bf16[128,64,128]{2,0,1:T(8,128)(2,1)}, u32[]{:S(2)}) copy-start(bf16[128,64,128]{2,0,1:T(8,128)(2,1)} %copy-done.7) | copy-start | bytes 6291460
  110.0 29.9 %copy-start.17 = (f32[256,64]{0,1:T(8,128)S(1)}, f32[256,64]{0,1:T(8,128)}, u32[]{:S(2)}) copy-start(f32[256,64]{0,1:T(8,128)} %param.13) | copy-start | bytes 196612
  110.0 29.9 %copy-start.20 = (f32[256,64]{0,1:T(8,128)S(1)}, f32[256,64]{0,1:T(8,128)}, u32[]{:S(2)}) copy-start(f32[256,64]{0,1:T(8,128)} %param.14) | copy-start | bytes 196612
  140.7 5.5 %copy-start.3 = (f32[8,128,128,8]{2,1,3,0:T(8,128)S(1)}, f32[8,128,128,8]{2,1,3,0:T(8,128)}, u32[]{:S(2)}) copy-start(f32[8,128,128,8]{2,1,3,0:T(8,128)} %copy-done) | copy-start | bytes 12582916
  140.7 6.5 %copy-start.9 = (f32[8,128,128,8]{2,1,3,0:T(8,128)S(1)}, f32[8,128,128,8]{2,1,3,0:T(8,128)}, u32[]{:S(2)}) copy-start(f32[8,128,128,8]{2,1,3,0:T(8,128)} %get-tuple-element.127) | copy-start | bytes 12582916
  148.7 37.1 %copy-start.18 = (f32[16,2,8,128]{3,2,1,0:T(8,128)S(1)}, f32[16,2,8,128]{3,2,1,0:T(8,128)}, u32[]{:S(2)}) copy-start(f32[16,2,8,128]{3,2,1,0:T(8,128)} %param.16) | copy-start | bytes 393220
  148.7 37.0 %copy-start.19 = (f32[16,2,8,128]{3,2,1,0:T(8,128)S(1)}, f32[16,2,8,128]{3,2,1,0:T(8,128)}, u32[]{:S(2)}) copy-start(f32[16,2,8,128]{3,2,1,0:T(8,128)} %param.17) | copy-start | bytes 393220
Sparse Core Ops, SparseCore 0:
  105.3 34.5 all-reduce.2
  150.0 35.7 reduce-scatter.1
where the time goes:
time: 196 us
  blocking collectives  66.5 us (34%)
  waiting for transfers between devices  64.9 us (33%)
  matrix products  22.6 us (12%)
  local copies, waits for them, and re-layouts  21.7 us (11%)
  between operations  14.4 us (7%)
  other arithmetic  5.35 us (3%)
    all_gather x4, blocking collectives, combined_all(): pieces = jax.tree.map(lambda part: lax.all_gather(part, axis), value)  54.1 us
    reduce_scatter x1, waiting for transfers between devices, per_device(): lax.psum_scatter(total_grad, 'dp', scatter_dimension=0, tiled=True)  35.9 us
    psum x1, waiting for transfers between devices, per_device(): lax.psum(partial_delta, 'cache') + jnp.exp(side_lse - log_total) * side_dot  29 us
    all_gather x1, blocking collectives, per_device(): gathered = lax.all_gather(rounded, 'dp', axis=0, tiled=True)  12.4 us
    dot_general x2, matrix products, per_device(): jnp.einsum('tgre,jge->tgrj', grads_block, value_rows, preferred_element_t...  9.48 us
    slice x3, local copies, waits for them, and re-layouts, per_device(): queries[lowest:lowest + QBLOCK]  8.94 us
    slice x3, local copies, waits for them, and re-layouts, per_device(): out_grad[lowest:lowest + QBLOCK]  8.12 us
    dot_general x2, matrix products, block_gradient(): jnp.einsum('tgrj,tgre->jge', dscore, queries_block, preferred_element_typ...  6.93 us
  transfers between devices with their start and end apart: 2, of which 2 were waited for; matrix products, arithmetic and copies ran while one was open for 2% of the time, Pallas kernels for 0%

commit v1 on v0

v1 whole, which is shorter than its diff:
```python
import functools
import math

import jax
import jax.numpy as jnp
from jax import lax
from jax.experimental import pallas as pl
from jax.experimental.pallas import tpu as pltpu
from jax.sharding import PartitionSpec as P

STEP = 200

learn_rate = 0.02
beta_first = 0.9
beta_second = 0.999
epsilon = 1e-08

ROW_TILE = 256


def attend_kernel(
    score_scale,
    row_tile,
    place_ref,
    kv_ref,
    queries_ref,
    grads_ref,
    lse_ref,
    dot_ref,
    out_ref,
    key_total,
    value_total,
):
    block = pl.program_id(1)

    @pl.when(block == 0)
    def _():
        key_total[...] = jnp.zeros_like(key_total)
        value_total[...] = jnp.zeros_like(value_total)

    senders, _, _, share, width = kv_ref.shape
    keys = kv_ref[:, 0, 0].reshape(senders * share, width)
    values = kv_ref[:, 1, 0].reshape(senders * share, width)
    tokens, _, heads, _ = queries_ref.shape
    tile_tokens = row_tile // heads
    across = (((1,), (1,)), ((), ()))
    along = (((1,), (0,)), ((), ()))
    for tile in range(tokens // tile_tokens):
        rows = pl.ds(tile * tile_tokens, tile_tokens)
        lanes = pl.ds(tile * row_tile, row_tile)
        queries = queries_ref[rows, 0].reshape(row_tile, width)
        grads = grads_ref[rows, 0].reshape(row_tile, width)
        side_lse = lse_ref[0, :, lanes]
        side_dot = dot_ref[0, :, lanes]
        scores = (
            lax.dot_general(keys, queries, across, preferred_element_type=jnp.float32)
            * score_scale
        )
        slopes = lax.dot_general(values, grads, across, preferred_element_type=jnp.float32)
        peak = jnp.maximum(jnp.max(scores, axis=0, keepdims=True), side_lse)
        shifted = jnp.exp(scores - peak)
        side = jnp.exp(side_lse - peak)
        inverse = 1.0 / (jnp.sum(shifted, axis=0, keepdims=True) + side)
        delta = (
            jnp.sum(shifted * slopes, axis=0, keepdims=True) + side * side_dot
        ) * inverse
        probability = shifted * inverse
        weights = probability.astype(jnp.bfloat16)
        dscore = (probability * ((slopes - delta) * score_scale)).astype(jnp.bfloat16)
        key_total[...] += lax.dot_general(
            dscore, queries, along, preferred_element_type=jnp.float32
        )
        value_total[...] += lax.dot_general(
            weights, grads, along, preferred_element_type=jnp.float32
        )

    @pl.when(block == pl.num_programs(1) - 1)
    def _():
        shape = (senders, share, width)
        out_ref[:, 0, 0] = key_total[...].astype(out_ref.dtype).reshape(shape)
        out_ref[:, 1, 0] = value_total[...].astype(out_ref.dtype).reshape(shape)


def attend(place, pairs, queries, out_grad, lse_rows, dot_rows, tokens, score_scale):
    senders, _, own, share, width = pairs.shape
    heads = queries.shape[2]
    rows = tokens * heads
    positions = senders * share
    block_tokens = min(tokens, 64)
    blocks = tokens // block_tokens
    pair_spec = pl.BlockSpec(
        (senders, 2, 1, share, width), lambda g, b, place: (0, 0, g, 0, 0)
    )
    token_spec = pl.BlockSpec(
        (block_tokens, 1, heads, width),
        lambda g, b, place: (place[1] * blocks + b, place[0] + g, 0, 0),
    )
    row_spec = pl.BlockSpec((1, 1, block_tokens * heads), lambda g, b, place: (g, 0, b))
    return pl.pallas_call(
        functools.partial(attend_kernel, score_scale, ROW_TILE),
        out_shape=jax.ShapeDtypeStruct(pairs.shape, jnp.bfloat16),
        grid_spec=pltpu.PrefetchScalarGridSpec(
            num_scalar_prefetch=1,
            grid=(own, blocks),
            in_specs=[pair_spec, token_spec, token_spec, row_spec, row_spec],
            out_specs=pair_spec,
            scratch_shapes=[
                pltpu.VMEM((positions, width), jnp.float32),
                pltpu.VMEM((positions, width), jnp.float32),
            ],
        ),
        compiler_params=pltpu.CompilerParams(vmem_limit_bytes=48 * 1024 * 1024),
        cost_estimate=pl.CostEstimate(
            flops=8 * own * rows * positions * width,
            bytes_accessed=4 * own * rows * width + 8 * own * positions * width,
            transcendentals=own * rows * positions,
        ),
    )(place, pairs, queries, out_grad, lse_rows, dot_rows)


def adam_kernel(parts_ref, cache_ref, first_ref, second_ref, new_cache, new_first, new_second):
    _, owners, _, own, _, _ = parts_ref.shape
    groups = cache_ref.shape[2]
    repeat = owners * own // groups
    for side in range(2):
        for group in range(groups):
            owner, slot = (group // own, group % own)
            gradient = jnp.sum(
                parts_ref[:, owner * repeat : (owner + 1) * repeat, side, slot].astype(
                    jnp.float32
                ),
                axis=(0, 1),
            )
            first = beta_first * first_ref[:, side, group] + (1.0 - beta_first) * gradient
            second = (
                beta_second * second_ref[:, side, group]
                + (1.0 - beta_second) * gradient * gradient
            )
            first_hat = first / (1.0 - beta_first**STEP)
            second_hat = second / (1.0 - beta_second**STEP)
            new_cache[:, side, group] = cache_ref[
                :, side, group
            ] - learn_rate * first_hat / (jnp.sqrt(second_hat) + epsilon)
            new_first[:, side, group] = first
            new_second[:, side, group] = second


def adam(parts, cache, first_moment, second_moment):
    shape = jax.ShapeDtypeStruct(cache.shape, jnp.float32)
    return pl.pallas_call(
        adam_kernel,
        out_shape=(shape, shape, shape),
        compiler_params=pltpu.CompilerParams(vmem_limit_bytes=32 * 1024 * 1024),
    )(parts, cache, first_moment, second_moment)


def per_device(
    dp_size, cache_size, queries, out_grad, self_lse, self_dot, cache, first_moment, second_moment
):
    share, _, groups, width = cache.shape
    tokens, heads, _ = queries.shape
    group_size = heads // groups
    score_scale = 1.0 / math.sqrt(width)
    own = max(1, groups // cache_size)
    repeat = own * cache_size // groups
    own_tokens = tokens // repeat
    column = lax.axis_index("cache")
    first_group = column // repeat * own
    token_part = column % repeat

    rounded = cache.astype(jnp.bfloat16).reshape(share, 2, groups // own, own, width)
    slices = jnp.repeat(rounded.transpose(2, 1, 3, 0, 4), repeat, axis=0)
    outgoing = jnp.broadcast_to(slices, (dp_size,) + slices.shape).reshape(
        (dp_size * cache_size,) + slices.shape[1:]
    )
    pairs = lax.all_to_all(outgoing, ("dp", "cache"), 0, 0, tiled=True)

    def rows_of(stat):
        part = lax.dynamic_slice(
            stat,
            (token_part * own_tokens, first_group * group_size),
            (own_tokens, own * group_size),
        )
        return (
            part.reshape(own_tokens, own, group_size)
            .transpose(1, 0, 2)
            .reshape(own, 1, own_tokens * group_size)
        )

    place = jnp.stack([first_group, token_part]).astype(jnp.int32)
    partial = attend(
        place,
        pairs,
        queries.reshape(tokens, groups, group_size, width),
        out_grad.reshape(tokens, groups, group_size, width),
        rows_of(self_lse),
        rows_of(self_dot),
        own_tokens,
        score_scale,
    )
    arrived = lax.all_to_all(partial, ("dp", "cache"), 0, 0, tiled=True)
    arrived = arrived.reshape((dp_size, cache_size) + arrived.shape[1:])
    return adam(arrived, cache, first_moment, second_moment)


def solution(mesh):
    in_specs = (
        P("dp", None, None),
        P("dp", None, None),
        P("dp", None),
        P("dp", None),
        P(("dp", "cache"), None, None, None),
        P(("dp", "cache"), None, None, None),
        P(("dp", "cache"), None, None, None),
    )
    out_specs = (
        P(("dp", "cache"), None, None, None),
        P(("dp", "cache"), None, None, None),
        P(("dp", "cache"), None, None, None),
    )
    return jax.shard_map(
        functools.partial(per_device, mesh.shape["dp"], mesh.shape["cache"]),
        mesh=mesh,
        in_specs=in_specs,
        out_specs=out_specs,
        check_vma=False,
    )
```

time: 196 us -> 60.8 us (0.31)
  waiting for transfers between devices: 64.9 us -> 12.9 us
  blocking collectives: 66.5 us -> 18.3 us
  matrix products: 22.6 us -> 0 us
  local copies, waits for them, and re-layouts: 21.7 us -> 4.46 us
  Pallas kernels: 0 us -> 15 us
  between operations: 14.4 us -> 0.7 us
  starting transfers between devices: 0.08 us -> 7.3 us
  other arithmetic: 5.35 us -> 1 us
    all_gather x5 -> x0, blocking collectives: 66.5 us -> none  [the longest x4 54.1 us: combined_all(): pieces = jax.tree.map(lambda part: lax.all_gather(part, axis), value)]
    reduce_scatter x1 -> x0, waiting for transfers between devices: 35.9 us -> none  [per_device(): lax.psum_scatter(total_grad, 'dp', scatter_dimension=0, tiled=True)]
    psum x1 -> x0, waiting for transfers between devices: 29 us -> none  [per_device(): lax.psum(partial_delta, 'cache') + jnp.exp(side_lse - log_total) * side_dot]
    dot_general x8 -> x0, matrix products: 22.6 us -> none  [the longest x2 9.48 us: per_device(): jnp.einsum('tgre,jge->tgrj', grads_block, value_rows, preferred_element_t...]
    all_to_all x0 -> x1, blocking collectives: none -> 18.3 us  [per_device(): arrived = lax.all_to_all(partial, ('dp', 'cache'), 0, 0, tiled=True)]
    slice x26 -> x0, local copies, waits for them, and re-layouts: 17.3 us -> none  [the longest x3 8.94 us: per_device(): queries[lowest:lowest + QBLOCK]]
    pallas_call x0 -> x2, Pallas kernels: none -> 15 us  [the longest x1 13.7 us: attend(): pl.pallas_call(functools.partial(attend_kernel, score_scale, ROW_TILE), o...]
    all_to_all x0 -> x1, waiting for transfers between devices: none -> 12.9 us  [per_device(): pairs = lax.all_to_all(outgoing, ('dp', 'cache'), 0, 0, tiled=True)]
  transfers between devices with their start and end apart: 2 -> 1, of which waited for: 2 -> 1; matrix products, arithmetic and copies ran while one was open for 2% -> 2% of each run, Pallas kernels for 0% -> 0%
where the time goes in v1:
time: 60.8 us; the launch traced here: 59.7 us
  blocking collectives  18.3 us (30%)
  Pallas kernels  15 us (25%)
  waiting for transfers between devices  12.9 us (21%)
  starting transfers between devices  7.3 us (12%)
  local copies, waits for them, and re-layouts  4.46 us (7%)
  other arithmetic  1 us (2%)
  between operations  0.7 us (1%)
    all_to_all x1, blocking collectives, per_device(): arrived = lax.all_to_all(partial, ('dp', 'cache'), 0, 0, tiled=True)  18.3 us
    pallas_call x1, Pallas kernels, attend(): pl.pallas_call(functools.partial(attend_kernel, score_scale, ROW_TILE), o...  13.7 us
    all_to_all x1, waiting for transfers between devices, per_device(): pairs = lax.all_to_all(outgoing, ('dp', 'cache'), 0, 0, tiled=True)  12.9 us
    all_to_all x1, starting transfers between devices, per_device(): pairs = lax.all_to_all(outgoing, ('dp', 'cache'), 0, 0, tiled=True)  7.3 us
    unnamed x8, local copies, waits for them, and re-layouts  2.2 us
    pallas_call x1, Pallas kernels, adam(): pl.pallas_call(adam_kernel, out_shape=(shape, shape, shape), compiler_par...  1.32 us
  transfers between devices with their start and end apart: 1, of which 1 were waited for; matrix products, arithmetic and copies ran while one was open for 2% of the time, Pallas kernels for 0%

profile of v1, /device:TPU:0, one launch (start us, length us, event | category | flops | bytes accessed | tf_op | source)
XLA Modules:
  0.0 59.7 jit_solution(2057780978533722789)
XLA Ops:
  0.6 0.9 %convert_element_type.3 = bf16[16,2,8,128]{3,2,1,0:T(8,128)(2,1)S(1)} convert(f32[16,2,8,128]{3,2,1,0:T(8,128)} %cache_ref.1) | non-fusion elementwise | flops 32768 | bytes 196608 | tf_op jit(solution)/shard_map/convert_element_type | solution.py:171
  1.6 0.9 %broadcast_in_dim.3 = bf16[8,4,2,2,16,128]{5,4,3,2,1,0:T(8,128)(2,1)} broadcast(bf16[4,2,2,16,128]{4,3,2,1,0:T(8,128)(2,1)S(1)} %copy.11), dimensions={1,2,3,4,5} | broadcast | bytes 589824 | tf_op jit(solution)/shard_map/broadcast_in_dim | solution.py:173
  2.5 7.3 %all-to-all-start = ((bf16[32,2,2,16,128]{4,3,2,1,0:T(8,128)(2,1)}), bf16[32,2,2,16,128]{4,3,2,1,0:T(8,128)(2,1)S(1)}, u32[]{:S(2)}, u32[]{:S(2)}) async-start(bf16[32,2,2,16,128]{4,3,2,1,0:T(8,128)(2,1)} %bitcast.3), calls=%async_computation | async-start | bytes 1048576 | tf_op jit(solution)/shard_map/all_to_all | solution.py:176
  9.8 0.7 %dynamic-slice_bitcast_fusion = (f32[2,256,8]{1,2,0:T(8,128)S(1)}, f32[2,256,8]{1,2,0:T(8,128)S(1)}) fusion(f32[256,64]{0,1:T(8,128)} %param.10, s32[]{:T(128)S(6)} %select_n.13, f32[256,64]{0,1:T(8,128)} %param.9), kind=kLoop, calls=%fused_computation | loop fusion | bytes 65540 | tf_op jit(solution)/shard_map/transpose | solution.py:186
  10.5 0.1 copy.12
  10.7 0.2 reshape.42.lse_ref
  10.9 0.1 copy.13
  11.0 0.2 reshape.43.dot_ref
  11.2 0.1 pad_add_fusion.place_ref
  11.2 12.9 %all-to-all-done.kv_ref = bf16[32,2,2,16,128]{4,3,2,1,0:T(8,128)(2,1)S(1)} async-done(((bf16[32,2,2,16,128]{4,3,2,1,0:T(8,128)(2,1)}), bf16[32,2,2,16,128]{4,3,2,1,0:T(8,128)(2,1)S(1)}, u32[]{:S(2)}, u32[]{:S(2)}) %all-to-all-start) | async-done | bytes 524320 | tf_op jit(solution)/shard_map/all_to_all | solution.py:176
  24.2 0.0 copy-start
  24.2 2.2 %copy-done = bf16[256,64,128]{2,1,0:T(8,128)(2,1)S(1)} copy-done((bf16[256,64,128]{2,1,0:T(8,128)(2,1)S(1)}, bf16[256,64,128]{2,1,0:T(8,128)(2,1)}, u32[]{:S(2)}) %copy-start) | copy-done | bytes 4194328
  26.4 0.0 copy-start.1
  26.4 0.0 copy-start.2
  26.4 0.0 copy-start.3
  26.4 13.7 %shard_map.94 = bf16[32,2,2,16,128]{4,3,2,1,0:T(8,128)(2,1)S(1)} custom-call(s32[2]{0:T(128)S(1)} %pad_add_fusion.place_ref, bf16[32,2,2,16,128]{4,3,2,1,0:T(8,128)(2,1)S(1)} %all-to-all-done.kv_ref, bf16[256,8,8,128]{3,2,1,0:T(8,128)(2,1)S(1)} %bitcast.16, bf16[256,8,8,128]{3,2,1,0:T(8,128)(2,1)} %bitcast.18, f32[2,1,2048]{2,1,0:T(1,128)S(1)} %reshape.42.lse_ref, ...), custom_call_target="tpu_custom_call" | custom-call | flops 2147483648 | bytes 3145728 | tf_op jit(solution)/shard_map/pallas_call | solution.py:99
  40.1 18.3 %all_to_all.10 = bf16[32,2,2,16,128]{4,3,2,1,0:T(8,128)(2,1)S(1)} all-to-all(bf16[32,2,2,16,128]{4,3,2,1,0:T(8,128)(2,1)S(1)} %shard_map.94), channel_id=1, replica_groups=mesh['dp'=8,'cache'=4] {'dp','cache'}, dimensions={0} | all-to-all | bytes 1048576 | tf_op jit(solution)/shard_map/all_to_all | solution.py:201
  58.3 0.0 copy-done.1
  58.3 0.0 copy-done.2
  58.3 0.0 copy-done.3
  58.3 1.3 %shard_map.95 = (f32[16,2,8,128]{3,2,1,0:T(8,128)}, f32[16,2,8,128]{3,2,1,0:T(8,128)}, f32[16,2,8,128]{3,2,1,0:T(8,128)}) custom-call(bf16[8,4,2,2,16,128]{5,4,3,2,1,0:T(8,128)(2,1)S(1)} %bitcast.17, f32[16,2,8,128]{3,2,1,0:T(8,128)S(1)} %copy-done.1, f32[16,2,8,128]{3,2,1,0:T(8,128)S(1)} %copy-done.2, f32[16,2,8,128]{3,2,1,0:T(8,128)S(1)} %copy-done.3), custom_call_target="tpu_custom_call" | custom-call | tf_op jit(solution)/shard_map/pallas_call | solution.py:150
  (1 shorter events, 0.0 us)
Async XLA Ops:
  2.5 21.7 %all-to-all-start = ((bf16[32,2,2,16,128]{4,3,2,1,0:T(8,128)(2,1)}), bf16[32,2,2,16,128]{4,3,2,1,0:T(8,128)(2,1)S(1)}, u32[]{:S(2)}, u32[]{:S(2)}) async-start(bf16[32,2,2,16,128]{4,3,2,1,0:T(8,128)(2,1)} %bitcast.3), calls=%async_computation | async-start | bytes 1048576 | tf_op jit(solution)/shard_map/all_to_all | solution.py:176
  24.2 2.2 %copy-start = (bf16[256,64,128]{2,1,0:T(8,128)(2,1)S(1)}, bf16[256,64,128]{2,1,0:T(8,128)(2,1)}, u32[]{:S(2)}) copy-start(bf16[256,64,128]{2,1,0:T(8,128)(2,1)} %param.7) | copy-start | bytes 12582916
  26.4 32.0 %copy-start.1 = (f32[16,2,8,128]{3,2,1,0:T(8,128)S(1)}, f32[16,2,8,128]{3,2,1,0:T(8,128)}, u32[]{:S(2)}) copy-start(f32[16,2,8,128]{3,2,1,0:T(8,128)} %cache_ref.1) | copy-start | bytes 393220
  26.4 32.0 %copy-start.2 = (f32[16,2,8,128]{3,2,1,0:T(8,128)S(1)}, f32[16,2,8,128]{3,2,1,0:T(8,128)}, u32[]{:S(2)}) copy-start(f32[16,2,8,128]{3,2,1,0:T(8,128)} %first_ref.1) | copy-start | bytes 393220
  26.4 32.0 %copy-start.3 = (f32[16,2,8,128]{3,2,1,0:T(8,128)S(1)}, f32[16,2,8,128]{3,2,1,0:T(8,128)}, u32[]{:S(2)}) copy-start(f32[16,2,8,128]{3,2,1,0:T(8,128)} %second_ref.1) | copy-start | bytes 393220

commit v2 on v0

v2 whole, which is shorter than its diff:
```python
import functools
import math

import jax
import jax.numpy as jnp
from jax import lax
from jax.experimental import pallas as pl
from jax.experimental.pallas import tpu as pltpu
from jax.sharding import PartitionSpec as P

STEP = 200

learn_rate = 0.02
beta_first = 0.9
beta_second = 0.999
epsilon = 1e-08

ROW_TILE = 256
CHUNK = 32
MIB = 1024 * 1024


def pack_kernel(columns, cache_ref, *refs):
    *outs, by_group = refs
    groups = cache_ref.shape[2]
    own = outs[0].shape[1]
    repeat = own * columns // groups
    for side in range(2):
        for group in range(groups):
            by_group[group, side] = cache_ref[:, side, group].astype(jnp.bfloat16)
    column = lax.axis_index("cache")
    for offset in range(columns):
        first = (column ^ offset) // repeat * own
        for slot in range(own):
            for side in range(2):
                outs[offset][side, slot] = by_group[first + slot, side]


def pack(cache, columns, own):
    share, _, groups, width = cache.shape
    slice_shape = jax.ShapeDtypeStruct((2, own, share, width), jnp.bfloat16)
    return pl.pallas_call(
        functools.partial(pack_kernel, columns),
        out_shape=[slice_shape] * columns,
        scratch_shapes=[pltpu.VMEM((groups, 2, share, width), jnp.bfloat16)],
        compiler_params=pltpu.CompilerParams(vmem_limit_bytes=16 * MIB),
        name="pack",
    )(cache)


def attend_kernel(score_scale, per_group, pieces, *refs):
    pair_refs, refs = refs[:pieces], refs[pieces:]
    queries_ref, grads_ref, lse_ref, dot_ref, mine_ref, mate_ref = refs[:6]
    keys, values, key_total, value_total = refs[6:10]
    even, odd = refs[10:14], refs[14:18]
    columns, _, own, share, width = pair_refs[0].shape
    length = columns * share
    positions = pieces * length
    tiles = queries_ref.shape[0]
    log2e = math.log2(math.e)
    factor = score_scale * log2e
    across = (((1,), (1,)), ((), ()))
    along = (((1,), (0,)), ((), ()))

    for piece, pair_ref in enumerate(pair_refs):
        at = pl.ds(piece * length, length)
        for slot in range(own):
            keys[slot, at] = pair_ref[:, 0, slot].reshape(length, width)
            values[slot, at] = pair_ref[:, 1, slot].reshape(length, width)
    key_total[...] = jnp.zeros_like(key_total)
    value_total[...] = jnp.zeros_like(value_total)

    def multiply(tile, buffers):
        scores, slopes, _, _ = buffers
        slot = tile // per_group
        scores[...] = lax.dot_general(
            keys[slot], queries_ref[tile], across, preferred_element_type=jnp.float32
        )
        slopes[...] = lax.dot_general(
            values[slot], grads_ref[tile], across, preferred_element_type=jnp.float32
        )

    def normalize(tile, buffers):
        scores, slopes, weights, dscores = buffers
        cuts = [pl.ds(start, CHUNK) for start in range(0, positions, CHUNK)]
        top = scores[cuts[0]]
        for cut in cuts[1:]:
            top = jnp.maximum(top, scores[cut])
        side_lse = lse_ref[tile] * log2e
        peak = jnp.maximum(jnp.max(top, axis=0, keepdims=True) * factor, side_lse)
        total = None
        dotted = None
        for cut in cuts:
            shifted = jnp.exp2(scores[cut] * factor - peak)
            product = shifted * slopes[cut]
            scores[cut] = shifted
            total = shifted if total is None else total + shifted
            dotted = product if dotted is None else dotted + product
        side = jnp.exp2(side_lse - peak)
        inverse = 1.0 / (jnp.sum(total, axis=0, keepdims=True) + side)
        delta = (jnp.sum(dotted, axis=0, keepdims=True) + side * dot_ref[tile]) * inverse
        for cut in cuts:
            probability = scores[cut] * inverse
            weights[cut] = probability.astype(jnp.bfloat16)
            dscores[cut] = (probability * (slopes[cut] - delta)).astype(jnp.bfloat16)

    def accumulate(tile, buffers):
        _, _, weights, dscores = buffers
        slot = tile // per_group
        key_total[slot] += lax.dot_general(
            dscores[...], queries_ref[tile], along, preferred_element_type=jnp.float32
        )
        value_total[slot] += lax.dot_general(
            weights[...], grads_ref[tile], along, preferred_element_type=jnp.float32
        )

    multiply(0, even)
    multiply(1, odd)
    normalize(0, even)

    def two_tiles(step, carry):
        tile = step * 2
        multiply(tile + 2, even)
        normalize(tile + 1, odd)
        accumulate(tile, even)
        multiply(tile + 3, odd)
        normalize(tile + 2, even)
        accumulate(tile + 1, odd)
        return carry

    lax.fori_loop(0, tiles // 2 - 1, two_tiles, 0)
    normalize(tiles - 1, odd)
    accumulate(tiles - 2, even)
    accumulate(tiles - 1, odd)

    half = positions // 2
    shape = mine_ref.shape[:2] + (share, width)
    for slot in range(own):
        key_sum = key_total[slot] * score_scale
        value_sum = value_total[slot]
        mine_ref[:, :, 0, slot] = key_sum[:half].reshape(shape)
        mine_ref[:, :, 1, slot] = value_sum[:half].reshape(shape)
        mate_ref[:, :, 0, slot] = key_sum[half:].astype(jnp.bfloat16).reshape(shape)
        mate_ref[:, :, 1, slot] = value_sum[half:].astype(jnp.bfloat16).reshape(shape)


def attend(pairs, queries, grads, lse_rows, dot_rows, score_scale):
    columns, _, own, share, width = pairs[0].shape
    pieces = len(pairs)
    positions = pieces * columns * share
    tiles, row_tile, _ = queries.shape
    rows = tiles * row_tile
    half = (pieces // 2, columns, 2, own, share, width)
    buffers = [
        pltpu.VMEM((positions, row_tile), jnp.float32),
        pltpu.VMEM((positions, row_tile), jnp.float32),
        pltpu.VMEM((positions, row_tile), jnp.bfloat16),
        pltpu.VMEM((positions, row_tile), jnp.bfloat16),
    ]
    return pl.pallas_call(
        functools.partial(attend_kernel, score_scale, tiles // own, pieces),
        out_shape=(
            jax.ShapeDtypeStruct(half, jnp.float32),
            jax.ShapeDtypeStruct(half, jnp.bfloat16),
        ),
        scratch_shapes=[
            pltpu.VMEM((own, positions, width), jnp.bfloat16),
            pltpu.VMEM((own, positions, width), jnp.bfloat16),
            pltpu.VMEM((own, positions, width), jnp.float32),
            pltpu.VMEM((own, positions, width), jnp.float32),
        ]
        + buffers
        + buffers,
        compiler_params=pltpu.CompilerParams(vmem_limit_bytes=44 * MIB),
        cost_estimate=pl.CostEstimate(
            flops=8 * rows * positions * width,
            bytes_accessed=4 * rows * width + 8 * own * positions * width,
            transcendentals=rows * positions,
        ),
        name="attend",
    )(*pairs, queries, grads, lse_rows, dot_rows)


def chip_sum_kernel(mine_ref, mate_ref, *outs):
    for offset, out in enumerate(outs):
        out[...] = (mine_ref[offset] + mate_ref[offset].astype(jnp.float32)).astype(out.dtype)


def chip_sum(mine, mate):
    chips = mine.shape[0]
    shape = mine.shape[1:]
    return pl.pallas_call(
        chip_sum_kernel,
        out_shape=[
            jax.ShapeDtypeStruct(shape, jnp.float32 if offset == 0 else jnp.bfloat16)
            for offset in range(chips)
        ],
        compiler_params=pltpu.CompilerParams(vmem_limit_bytes=16 * MIB),
        name="chip_sum",
    )(mine, mate)


def column_sum_kernel(away, mine_ref, *refs):
    others, outs = refs[:away], refs[away:]
    for offset, out in enumerate(outs):
        total = mine_ref[offset]
        for other in others:
            total = total + other[offset].astype(jnp.float32)
        out[...] = total.astype(out.dtype)


def column_sum(mine, others):
    columns = mine.shape[0]
    shape = mine.shape[1:]
    return pl.pallas_call(
        functools.partial(column_sum_kernel, len(others)),
        out_shape=[
            jax.ShapeDtypeStruct(shape, jnp.float32 if offset == 0 else jnp.bfloat16)
            for offset in range(columns)
        ],
        compiler_params=pltpu.CompilerParams(vmem_limit_bytes=16 * MIB),
        name="column_sum",
    )(mine, *others)


def adam_kernel(columns, *refs):
    parts, refs = refs[:columns], refs[columns:]
    cache_ref, first_ref, second_ref, new_cache, new_first, new_second, by_offset = refs
    groups = cache_ref.shape[2]
    own = parts[0].shape[1]
    repeat = own * columns // groups
    for offset, part in enumerate(parts):
        by_offset[offset] = part[...].astype(jnp.float32)
    column = lax.axis_index("cache")
    for side in range(2):
        for group in range(groups):
            first_owner = group // own * repeat
            slot = group % own
            gradient = by_offset[column ^ first_owner, side, slot]
            for owner in range(first_owner + 1, first_owner + repeat):
                gradient = gradient + by_offset[column ^ owner, side, slot]
            first = beta_first * first_ref[:, side, group] + (1.0 - beta_first) * gradient
            second = (
                beta_second * second_ref[:, side, group]
                + (1.0 - beta_second) * gradient * gradient
            )
            first_hat = first / (1.0 - beta_first**STEP)
            second_hat = second / (1.0 - beta_second**STEP)
            new_cache[:, side, group] = cache_ref[
                :, side, group
            ] - learn_rate * first_hat / (jnp.sqrt(second_hat) + epsilon)
            new_first[:, side, group] = first
            new_second[:, side, group] = second


def adam(parts, cache, first_moment, second_moment):
    shape = jax.ShapeDtypeStruct(cache.shape, jnp.float32)
    return pl.pallas_call(
        functools.partial(adam_kernel, len(parts)),
        out_shape=(shape, shape, shape),
        scratch_shapes=[pltpu.VMEM((len(parts),) + parts[0].shape, jnp.float32)],
        compiler_params=pltpu.CompilerParams(vmem_limit_bytes=16 * MIB),
        name="adam",
    )(*parts, cache, first_moment, second_moment)


def swap(value, axis, size, flip):
    return lax.ppermute(value, axis, [(place, place ^ flip) for place in range(size)])


def per_device(
    dp_size, columns, queries, out_grad, self_lse, self_dot, cache, first_moment, second_moment
):
    _, _, groups, width = cache.shape
    tokens, heads, _ = queries.shape
    chips = dp_size // 2
    group_size = heads // groups
    score_scale = 1.0 / math.sqrt(width)
    own = max(1, groups // columns)
    repeat = own * columns // groups
    own_tokens = tokens // repeat
    column = lax.axis_index("cache")
    first_group = column // repeat * own
    first_token = column % repeat * own_tokens

    slices = pack(cache, columns, own)
    gathered = jnp.stack(
        [slices[0]] + [swap(slices[k], "cache", columns, k) for k in range(1, columns)]
    )
    pairs = [gathered] + [swap(gathered, "dp", dp_size, 2 * k) for k in range(1, chips)]
    pairs = pairs + [swap(pair, "dp", dp_size, 1) for pair in pairs]

    def tiles_of(array):
        parts = array.reshape((tokens, groups, group_size) + array.shape[2:])
        part = lax.dynamic_slice_in_dim(parts, first_token, own_tokens, 0)
        part = lax.dynamic_slice_in_dim(part, first_group, own, 1)
        return jnp.moveaxis(part, 1, 0).reshape((-1, ROW_TILE) + array.shape[2:])

    mine, mate = attend(
        pairs,
        tiles_of(queries),
        tiles_of(out_grad),
        tiles_of(self_lse)[:, None],
        tiles_of(self_dot)[:, None],
        score_scale,
    )
    by_chip = chip_sum(mine, swap(mate, "dp", dp_size, 1))
    by_column = column_sum(
        by_chip[0], [swap(by_chip[k], "dp", dp_size, 2 * k) for k in range(1, chips)]
    )
    parts = [by_column[0]] + [
        swap(by_column[k], "cache", columns, k) for k in range(1, columns)
    ]
    return adam(parts, cache, first_moment, second_moment)


def solution(mesh):
    in_specs = (
        P("dp", None, None),
        P("dp", None, None),
        P("dp", None),
        P("dp", None),
        P(("dp", "cache"), None, None, None),
        P(("dp", "cache"), None, None, None),
        P(("dp", "cache"), None, None, None),
    )
    out_specs = (
        P(("dp", "cache"), None, None, None),
        P(("dp", "cache"), None, None, None),
        P(("dp", "cache"), None, None, None),
    )
    return jax.shard_map(
        functools.partial(per_device, mesh.shape["dp"], mesh.shape["cache"]),
        mesh=mesh,
        in_specs=in_specs,
        out_specs=out_specs,
        check_vma=False,
    )
```

time: 196 us -> 48.3 us (0.25)
  blocking collectives: 66.5 us -> 0 us
  waiting for transfers between devices: 64.9 us -> 13.7 us
  matrix products: 22.6 us -> 0 us
  starting transfers between devices: 0.08 us -> 18.5 us
  local copies, waits for them, and re-layouts: 21.7 us -> 4.33 us
  between operations: 14.4 us -> 0.8 us
  Pallas kernels: 0 us -> 10.7 us
  other arithmetic: 5.35 us -> 0.01 us
    all_gather x5 -> x0, blocking collectives: 66.5 us -> none  [the longest x4 54.1 us: combined_all(): pieces = jax.tree.map(lambda part: lax.all_gather(part, axis), value)]
    reduce_scatter x1 -> x0, waiting for transfers between devices: 35.9 us -> none  [per_device(): lax.psum_scatter(total_grad, 'dp', scatter_dimension=0, tiled=True)]
    psum x1 -> x0, waiting for transfers between devices: 29 us -> none  [per_device(): lax.psum(partial_delta, 'cache') + jnp.exp(side_lse - log_total) * side_dot]
    dot_general x8 -> x0, matrix products: 22.6 us -> none  [the longest x2 9.48 us: per_device(): jnp.einsum('tgre,jge->tgrj', grads_block, value_rows, preferred_element_t...]
    ppermute x0 -> x17, starting transfers between devices: none -> 18.5 us  [swap(): lax.ppermute(value, axis, [(place, place ^ flip) for place in range(size)])]
    slice x26 -> x0, local copies, waits for them, and re-layouts: 17.3 us -> none  [the longest x3 8.94 us: per_device(): queries[lowest:lowest + QBLOCK]]
    ppermute x0 -> x17, waiting for transfers between devices: none -> 13.7 us  [swap(): lax.ppermute(value, axis, [(place, place ^ flip) for place in range(size)])]
    pallas_call x0 -> x5, Pallas kernels: none -> 10.7 us  [the longest x1 9.16 us: attend(): pl.pallas_call(functools.partial(attend_kernel, score_scale, tiles // own...]
  transfers between devices with their start and end apart: 2 -> 17, of which waited for: 2 -> 9; matrix products, arithmetic and copies ran while one was open for 2% -> 7% of each run, Pallas kernels for 0% -> 0%
where the time goes in v2:
time: 48.3 us; the launch traced here: 47.9 us
  starting transfers between devices  18.5 us (38%)
  waiting for transfers between devices  13.7 us (28%)
  Pallas kernels  10.7 us (22%)
  local copies, waits for them, and re-layouts  4.33 us (9%)
  between operations  0.8 us (2%)
    ppermute x17, starting transfers between devices, swap(): lax.ppermute(value, axis, [(place, place ^ flip) for place in range(size)])  18.5 us
    ppermute x17, waiting for transfers between devices, swap(): lax.ppermute(value, axis, [(place, place ^ flip) for place in range(size)])  13.7 us
    pallas_call x1, Pallas kernels, attend(): pl.pallas_call(functools.partial(attend_kernel, score_scale, tiles // own...  9.16 us
    dynamic_slice x2, local copies, waits for them, and re-layouts, tiles_of(): part = lax.dynamic_slice_in_dim(part, first_group, own, 1)  2.69 us
    unnamed x12, local copies, waits for them, and re-layouts  1.3 us
    pallas_call x1, Pallas kernels, adam(): pl.pallas_call(functools.partial(adam_kernel, len(parts)), out_shape=(sha...  1.27 us
  transfers between devices with their start and end apart: 17, of which 9 were waited for; matrix products, arithmetic and copies ran while one was open for 7% of the time, Pallas kernels for 0%

profile of v2, /device:TPU:0, one launch (start us, length us, event | category | flops | bytes accessed | tf_op | source)
XLA Modules:
  0.0 47.9 jit_solution(8233864864021137381)
XLA Ops:
  0.6 0.0 copy-start
  0.6 0.9 %copy-done = f32[16,2,8,128]{3,2,1,0:T(8,128)S(1)} copy-done((f32[16,2,8,128]{3,2,1,0:T(8,128)S(1)}, f32[16,2,8,128]{3,2,1,0:T(8,128)}, u32[]{:S(2)}) %copy-start) | copy-done | bytes 131096
  1.5 0.1 pack.1
  1.7 3.1 %collective-permute-start = (bf16[2,2,16,128]{3,2,1,0:T(8,128)(2,1)S(1)}, bf16[2,2,16,128]{3,2,1,0:T(8,128)(2,1)S(1)}, u32[]{:S(2)}, u32[]{:S(2)}) collective-permute-start(bf16[2,2,16,128]{3,2,1,0:T(8,128)(2,1)S(1)} %get-tuple-element.18), channel_id=1, source_target_pairs={{0,1},{1,0},{2,3},{3,2},{4,5},{5,4},{6,7},{7,6},{8,9},{9,8},{10,11... | collective-permute-start | bytes 49160 | tf_op jit(solution)/shard_map/ppermute | solution.py:268
  4.8 2.6 %collective-permute-start.1 = (bf16[2,2,16,128]{3,2,1,0:T(8,128)(2,1)S(1)}, bf16[2,2,16,128]{3,2,1,0:T(8,128)(2,1)S(1)}, u32[]{:S(2)}, u32[]{:S(2)}) collective-permute-start(bf16[2,2,16,128]{3,2,1,0:T(8,128)(2,1)S(1)} %get-tuple-element.19), channel_id=1, source_target_pairs={{0,2},{1,3},{2,0},{3,1},{4,6},{5,7},{6,4},{7,5},{8,10},{9,11},{10,... | collective-permute-start | bytes 49160 | tf_op jit(solution)/shard_map/ppermute | solution.py:268
  7.4 0.0 collective-permute-start.2
  7.4 0.0 collective-permute-done
  7.4 2.1 %collective-permute-done.1 = bf16[2,2,16,128]{3,2,1,0:T(8,128)(2,1)S(1)} collective-permute-done((bf16[2,2,16,128]{3,2,1,0:T(8,128)(2,1)S(1)}, bf16[2,2,16,128]{3,2,1,0:T(8,128)(2,1)S(1)}, u32[]{:S(2)}, u32[]{:S(2)}) %collective-permute-start.1) | collective-permute-done | bytes 16416 | tf_op jit(solution)/shard_map/ppermute | solution.py:268
  9.5 3.4 %collective-permute-done.2 = bf16[2,2,16,128]{3,2,1,0:T(8,128)(2,1)S(1)} collective-permute-done((bf16[2,2,16,128]{3,2,1,0:T(8,128)(2,1)S(1)}, bf16[2,2,16,128]{3,2,1,0:T(8,128)(2,1)S(1)}, u32[]{:S(2)}, u32[]{:S(2)}) %collective-permute-start.2) | collective-permute-done | bytes 16416 | tf_op jit(solution)/shard_map/ppermute | solution.py:268
  12.9 1.6 %collective-permute-start.3 = (bf16[4,2,2,16,128]{4,3,2,1,0:T(8,128)(2,1)S(1)}, bf16[4,2,2,16,128]{4,3,2,1,0:T(8,128)(2,1)S(1)}, u32[]{:S(2)}, u32[]{:S(2)}) collective-permute-start(bf16[4,2,2,16,128]{4,3,2,1,0:T(8,128)(2,1)S(1)} %pad_maximum_fusion.refs_0_), channel_id=1, source_target_pairs={{0,8},{4,12},{8,0},{12,4},{16,24},{20,28},{24,16},{28,20},{1,9},{5... | collective-permute-start | bytes 196616 | tf_op jit(solution)/shard_map/ppermute | solution.py:268
  14.5 1.5 %collective-permute-start.4 = (bf16[4,2,2,16,128]{4,3,2,1,0:T(8,128)(2,1)S(1)}, bf16[4,2,2,16,128]{4,3,2,1,0:T(8,128)(2,1)S(1)}, u32[]{:S(2)}, u32[]{:S(2)}) collective-permute-start(bf16[4,2,2,16,128]{4,3,2,1,0:T(8,128)(2,1)S(1)} %pad_maximum_fusion.refs_0_), channel_id=1, source_target_pairs={{0,16},{4,20},{8,24},{12,28},{16,0},{20,4},{24,8},{28,12},{1,17},{... | collective-permute-start | bytes 196616 | tf_op jit(solution)/shard_map/ppermute | solution.py:268
  16.0 0.5 collective-permute-start.5
  16.5 2.0 %constant_dynamic-slice_fusion.2 = (bf16[256,2,8,128]{3,2,1,0:T(8,128)(2,1)S(1)}, bf16[256,2,8,128]{3,2,1,0:T(8,128)(2,1)S(1)}) fusion(bf16[256,8,8,128]{3,2,1,0:T(8,128)(2,1)} %bitcast.21, s32[]{:T(128)S(6)} %select_n.9, bf16[256,8,8,128]{3,2,1,0:T(8,128)(2,1)} %bitcast.22), kind=kLoop, calls=%fused_computation.3 | loop fusion | bytes 4194308 | tf_op jit(solution)/shard_map/dynamic_slice | solution.py:296
  18.4 0.1 copy.20
  18.5 0.1 copy.21
  18.6 0.1 collective-permute-start.6
  18.7 0.0 collective-permute-done.3.refs_1_
  18.7 0.5 %collective-permute-start.7 = (bf16[4,2,2,16,128]{4,3,2,1,0:T(8,128)(2,1)S(1)}, bf16[4,2,2,16,128]{4,3,2,1,0:T(8,128)(2,1)S(1)}, u32[]{:S(2)}, u32[]{:S(2)}) collective-permute-start(bf16[4,2,2,16,128]{4,3,2,1,0:T(8,128)(2,1)S(1)} %collective-permute-done.3.refs_1_), channel_id=1, source_target_pairs={{0,4},{4,0},{8,12},{12,8},{16,20},{20,16},{24,28},{28,24},{1,5},{5... | collective-permute-start | bytes 196616 | tf_op jit(solution)/shard_map/ppermute | solution.py:268
  19.2 0.0 collective-permute-done.4.refs_2_
  19.2 0.1 collective-permute-start.8
  19.2 1.9 %collective-permute-done.5.refs_3_ = bf16[4,2,2,16,128]{4,3,2,1,0:T(8,128)(2,1)S(1)} collective-permute-done((bf16[4,2,2,16,128]{4,3,2,1,0:T(8,128)(2,1)S(1)}, bf16[4,2,2,16,128]{4,3,2,1,0:T(8,128)(2,1)S(1)}, u32[]{:S(2)}, u32[]{:S(2)}) %collective-permute-start.5) | collective-permute-done | bytes 65568 | tf_op jit(solution)/shard_map/ppermute | solution.py:268
  21.2 0.0 collective-permute-start.9
  21.2 0.7 %constant_dynamic-slice_fusion = (f32[256,2,8]{0,2,1:T(8,128)S(1)}, f32[256,2,8]{0,2,1:T(8,128)S(1)}) fusion(f32[256,8,8]{0,2,1:T(8,128)} %bitcast.26, s32[]{:T(128)S(6)} %select_n.9, f32[256,8,8]{0,2,1:T(8,128)} %bitcast.27), kind=kLoop, calls=%fused_computation.1 | loop fusion | bytes 65540 | tf_op jit(solution)/shard_map/dynamic_slice | solution.py:296
  21.9 0.1 copy.22
  22.0 0.2 broadcast_in_dim_reshape.8.refs_10_
  22.2 0.1 copy.23
  22.3 0.2 broadcast_in_dim_reshape.9.refs_11_
  22.5 0.0 collective-permute-done.6.refs_4_
  22.5 0.0 collective-permute-done.7.refs_5_
  22.5 0.0 collective-permute-done.8.refs_6_
  22.5 0.0 collective-permute-done.9.refs_7_
  22.6 0.0 copy-start.1
  22.6 0.0 copy-start.2
  22.6 0.0 copy-start.3
  22.6 9.2 %attend.1 = (f32[4,4,2,2,16,128]{5,4,3,2,1,0:T(8,128)S(1)}, bf16[4,4,2,2,16,128]{5,4,3,2,1,0:T(8,128)(2,1)S(1)}) custom-call(bf16[4,2,2,16,128]{4,3,2,1,0:T(8,128)(2,1)S(1)} %pad_maximum_fusion.refs_0_, bf16[4,2,2,16,128]{4,3,2,1,0:T(8,128)(2,1)S(1)} %collective-permute-done.3.refs_1_, bf16[4,2,2,16,128]{4,3,2,1,0:T(8,128)(2,1)S(1)} %collective-permute-done.4.refs_2_, ...), custom_call_target="tpu_custom_call" | custom-call | flops 2147483648 | bytes 3145728 | tf_op jit(solution)/shard_map/attend/pallas_call | solution.py:160
  31.8 0.6 %collective-permute-start.10 = (bf16[4,4,2,2,16,128]{5,4,3,2,1,0:T(8,128)(2,1)S(1)}, bf16[4,4,2,2,16,128]{5,4,3,2,1,0:T(8,128)(2,1)S(1)}, u32[]{:S(2)}, u32[]{:S(2)}) collective-permute-start(bf16[4,4,2,2,16,128]{5,4,3,2,1,0:T(8,128)(2,1)S(1)} %get-tuple-element.22), channel_id=1, source_target_pairs={{0,4},{4,0},{8,12},{12,8},{16,20},{20,16},{24,28},{28,24},{1,5},{5... | collective-permute-start | bytes 786440 | tf_op jit(solution)/shard_map/ppermute | solution.py:268
  32.3 1.2 %collective-permute-done.10.mate_ref = bf16[4,4,2,2,16,128]{5,4,3,2,1,0:T(8,128)(2,1)S(1)} collective-permute-done((bf16[4,4,2,2,16,128]{5,4,3,2,1,0:T(8,128)(2,1)S(1)}, bf16[4,4,2,2,16,128]{5,4,3,2,1,0:T(8,128)(2,1)S(1)}, u32[]{:S(2)}, u32[]{:S(2)}) %collective-permute-start.10) | collective-permute-done | bytes 262176 | tf_op jit(solution)/shard_map/ppermute | solution.py:268
  33.6 0.6 %collective-permute-start.11 = (bf16[4,2,2,16,128]{4,3,2,1,0:T(8,128)(2,1)S(1)}, bf16[4,2,2,16,128]{4,3,2,1,0:T(8,128)(2,1)S(1)}, u32[]{:S(2)}, u32[]{:S(2)}) collective-permute-start(bf16[4,2,2,16,128]{4,3,2,1,0:T(8,128)(2,1)S(1)} %get-tuple-element.24), channel_id=1, source_target_pairs={{0,8},{4,12},{8,0},{12,4},{16,24},{20,28},{24,16},{28,20},{1,9},{5... | collective-permute-start | bytes 196616 | tf_op jit(solution)/shard_map/ppermute | solution.py:268
  34.2 0.8 %collective-permute-start.12 = (bf16[4,2,2,16,128]{4,3,2,1,0:T(8,128)(2,1)S(1)}, bf16[4,2,2,16,128]{4,3,2,1,0:T(8,128)(2,1)S(1)}, u32[]{:S(2)}, u32[]{:S(2)}) collective-permute-start(bf16[4,2,2,16,128]{4,3,2,1,0:T(8,128)(2,1)S(1)} %get-tuple-element.25), channel_id=1, source_target_pairs={{0,16},{4,20},{8,24},{12,28},{16,0},{20,4},{24,8},{28,12},{1,17},{... | collective-permute-start | bytes 196616 | tf_op jit(solution)/shard_map/ppermute | solution.py:268
  35.0 2.1 %collective-permute-start.13 = (bf16[4,2,2,16,128]{4,3,2,1,0:T(8,128)(2,1)S(1)}, bf16[4,2,2,16,128]{4,3,2,1,0:T(8,128)(2,1)S(1)}, u32[]{:S(2)}, u32[]{:S(2)}) collective-permute-start(bf16[4,2,2,16,128]{4,3,2,1,0:T(8,128)(2,1)S(1)} %get-tuple-element.26), channel_id=1, source_target_pairs={{0,24},{4,28},{8,16},{12,20},{16,8},{20,12},{24,0},{28,4},{1,25},{... | collective-permute-start | bytes 196616 | tf_op jit(solution)/shard_map/ppermute | solution.py:268
  37.1 0.9 %collective-permute-done.11.refs_0_ = bf16[4,2,2,16,128]{4,3,2,1,0:T(8,128)(2,1)S(1)} collective-permute-done((bf16[4,2,2,16,128]{4,3,2,1,0:T(8,128)(2,1)S(1)}, bf16[4,2,2,16,128]{4,3,2,1,0:T(8,128)(2,1)S(1)}, u32[]{:S(2)}, u32[]{:S(2)}) %collective-permute-start.11) | collective-permute-done | bytes 65568 | tf_op jit(solution)/shard_map/ppermute | solution.py:268
  38.0 1.1 %collective-permute-done.12.refs_1_ = bf16[4,2,2,16,128]{4,3,2,1,0:T(8,128)(2,1)S(1)} collective-permute-done((bf16[4,2,2,16,128]{4,3,2,1,0:T(8,128)(2,1)S(1)}, bf16[4,2,2,16,128]{4,3,2,1,0:T(8,128)(2,1)S(1)}, u32[]{:S(2)}, u32[]{:S(2)}) %collective-permute-start.12) | collective-permute-done | bytes 65568 | tf_op jit(solution)/shard_map/ppermute | solution.py:268
  39.1 1.0 %collective-permute-done.13.refs_2_ = bf16[4,2,2,16,128]{4,3,2,1,0:T(8,128)(2,1)S(1)} collective-permute-done((bf16[4,2,2,16,128]{4,3,2,1,0:T(8,128)(2,1)S(1)}, bf16[4,2,2,16,128]{4,3,2,1,0:T(8,128)(2,1)S(1)}, u32[]{:S(2)}, u32[]{:S(2)}) %collective-permute-start.13) | collective-permute-done | bytes 65568 | tf_op jit(solution)/shard_map/ppermute | solution.py:268
  40.2 0.1 collective-permute-start.14
  40.3 0.8 %collective-permute-start.15 = (bf16[2,2,16,128]{3,2,1,0:T(8,128)(2,1)S(1)}, bf16[2,2,16,128]{3,2,1,0:T(8,128)(2,1)S(1)}, u32[]{:S(2)}, u32[]{:S(2)}) collective-permute-start(bf16[2,2,16,128]{3,2,1,0:T(8,128)(2,1)S(1)} %get-tuple-element.29), channel_id=1, source_target_pairs={{0,2},{1,3},{2,0},{3,1},{4,6},{5,7},{6,4},{7,5},{8,10},{9,11},{10,... | collective-permute-start | bytes 49160 | tf_op jit(solution)/shard_map/ppermute | solution.py:268
  41.1 3.6 %collective-permute-start.16 = (bf16[2,2,16,128]{3,2,1,0:T(8,128)(2,1)S(1)}, bf16[2,2,16,128]{3,2,1,0:T(8,128)(2,1)S(1)}, u32[]{:S(2)}, u32[]{:S(2)}) collective-permute-start(bf16[2,2,16,128]{3,2,1,0:T(8,128)(2,1)S(1)} %get-tuple-element.30), channel_id=1, source_target_pairs={{0,3},{1,2},{2,1},{3,0},{4,7},{5,6},{6,5},{7,4},{8,11},{9,10},{10,... | collective-permute-start | bytes 49160 | tf_op jit(solution)/shard_map/ppermute | solution.py:268
  44.7 0.0 collective-permute-done.14.refs_1_
  44.7 0.3 collective-permute-done.15.refs_2_
  45.0 1.6 %collective-permute-done.16.refs_3_ = bf16[2,2,16,128]{3,2,1,0:T(8,128)(2,1)S(1)} collective-permute-done((bf16[2,2,16,128]{3,2,1,0:T(8,128)(2,1)S(1)}, bf16[2,2,16,128]{3,2,1,0:T(8,128)(2,1)S(1)}, u32[]{:S(2)}, u32[]{:S(2)}) %collective-permute-start.16) | collective-permute-done | bytes 16416 | tf_op jit(solution)/shard_map/ppermute | solution.py:268
  46.6 0.0 copy-done.1
  46.6 0.0 copy-done.2
  46.6 0.0 copy-done.3
  46.7 1.3 %adam.1 = (f32[16,2,8,128]{3,2,1,0:T(8,128)}, f32[16,2,8,128]{3,2,1,0:T(8,128)}, f32[16,2,8,128]{3,2,1,0:T(8,128)}) custom-call(f32[2,2,16,128]{3,2,1,0:T(8,128)S(1)} %get-tuple-element.27.refs_0_, bf16[2,2,16,128]{3,2,1,0:T(8,128)(2,1)S(1)} %collective-permute-done.14.refs_1_, bf16[2,2,16,128]{3,2,1,0:T(8,128)(2,1)S(1)} %collective-permute-done.15.refs_2_, ...), custom_call_target="tpu_custom_call" | custom-call | tf_op jit(solution)/shard_map/adam/pallas_call | solution.py:258
  (3 shorter events, 0.1 us)
Async XLA Ops:
  0.6 0.9 %copy-start = (f32[16,2,8,128]{3,2,1,0:T(8,128)S(1)}, f32[16,2,8,128]{3,2,1,0:T(8,128)}, u32[]{:S(2)}) copy-start(f32[16,2,8,128]{3,2,1,0:T(8,128)} %refs_4_.1) | copy-start | bytes 393220
  1.7 5.7 %collective-permute-start = (bf16[2,2,16,128]{3,2,1,0:T(8,128)(2,1)S(1)}, bf16[2,2,16,128]{3,2,1,0:T(8,128)(2,1)S(1)}, u32[]{:S(2)}, u32[]{:S(2)}) collective-permute-start(bf16[2,2,16,128]{3,2,1,0:T(8,128)(2,1)S(1)} %get-tuple-element.18), channel_id=1, source_target_pairs={{0,1},{1,0},{2,3},{3,2},{4,5},{5,4},{6,7},{7,6},{8,9},{9,8},{10,11... | collective-permute-start | bytes 49160 | tf_op jit(solution)/shard_map/ppermute | solution.py:268
  4.8 4.7 %collective-permute-start.1 = (bf16[2,2,16,128]{3,2,1,0:T(8,128)(2,1)S(1)}, bf16[2,2,16,128]{3,2,1,0:T(8,128)(2,1)S(1)}, u32[]{:S(2)}, u32[]{:S(2)}) collective-permute-start(bf16[2,2,16,128]{3,2,1,0:T(8,128)(2,1)S(1)} %get-tuple-element.19), channel_id=1, source_target_pairs={{0,2},{1,3},{2,0},{3,1},{4,6},{5,7},{6,4},{7,5},{8,10},{9,11},{10,... | collective-permute-start | bytes 49160 | tf_op jit(solution)/shard_map/ppermute | solution.py:268
  7.4 5.5 %collective-permute-start.2 = (bf16[2,2,16,128]{3,2,1,0:T(8,128)(2,1)S(1)}, bf16[2,2,16,128]{3,2,1,0:T(8,128)(2,1)S(1)}, u32[]{:S(2)}, u32[]{:S(2)}) collective-permute-start(bf16[2,2,16,128]{3,2,1,0:T(8,128)(2,1)S(1)} %get-tuple-element.20), channel_id=1, source_target_pairs={{0,3},{1,2},{2,1},{3,0},{4,7},{5,6},{6,5},{7,4},{8,11},{9,10},{10,... | collective-permute-start | bytes 49160 | tf_op jit(solution)/shard_map/ppermute | solution.py:268
  12.9 5.7 %collective-permute-start.3 = (bf16[4,2,2,16,128]{4,3,2,1,0:T(8,128)(2,1)S(1)}, bf16[4,2,2,16,128]{4,3,2,1,0:T(8,128)(2,1)S(1)}, u32[]{:S(2)}, u32[]{:S(2)}) collective-permute-start(bf16[4,2,2,16,128]{4,3,2,1,0:T(8,128)(2,1)S(1)} %pad_maximum_fusion.refs_0_), channel_id=1, source_target_pairs={{0,8},{4,12},{8,0},{12,4},{16,24},{20,28},{24,16},{28,20},{1,9},{5... | collective-permute-start | bytes 196616 | tf_op jit(solution)/shard_map/ppermute | solution.py:268
  14.5 4.7 %collective-permute-start.4 = (bf16[4,2,2,16,128]{4,3,2,1,0:T(8,128)(2,1)S(1)}, bf16[4,2,2,16,128]{4,3,2,1,0:T(8,128)(2,1)S(1)}, u32[]{:S(2)}, u32[]{:S(2)}) collective-permute-start(bf16[4,2,2,16,128]{4,3,2,1,0:T(8,128)(2,1)S(1)} %pad_maximum_fusion.refs_0_), channel_id=1, source_target_pairs={{0,16},{4,20},{8,24},{12,28},{16,0},{20,4},{24,8},{28,12},{1,17},{... | collective-permute-start | bytes 196616 | tf_op jit(solution)/shard_map/ppermute | solution.py:268
  16.0 5.2 %collective-permute-start.5 = (bf16[4,2,2,16,128]{4,3,2,1,0:T(8,128)(2,1)S(1)}, bf16[4,2,2,16,128]{4,3,2,1,0:T(8,128)(2,1)S(1)}, u32[]{:S(2)}, u32[]{:S(2)}) collective-permute-start(bf16[4,2,2,16,128]{4,3,2,1,0:T(8,128)(2,1)S(1)} %pad_maximum_fusion.refs_0_), channel_id=1, source_target_pairs={{0,24},{4,28},{8,16},{12,20},{16,8},{20,12},{24,0},{28,4},{1,25},{... | collective-permute-start | bytes 196616 | tf_op jit(solution)/shard_map/ppermute | solution.py:268
  18.6 3.9 %collective-permute-start.6 = (bf16[4,2,2,16,128]{4,3,2,1,0:T(8,128)(2,1)S(1)}, bf16[4,2,2,16,128]{4,3,2,1,0:T(8,128)(2,1)S(1)}, u32[]{:S(2)}, u32[]{:S(2)}) collective-permute-start(bf16[4,2,2,16,128]{4,3,2,1,0:T(8,128)(2,1)S(1)} %pad_maximum_fusion.refs_0_), channel_id=1, source_target_pairs={{0,4},{4,0},{8,12},{12,8},{16,20},{20,16},{24,28},{28,24},{1,5},{5... | collective-permute-start | bytes 196616 | tf_op jit(solution)/shard_map/ppermute | solution.py:268
  18.7 3.9 %collective-permute-start.7 = (bf16[4,2,2,16,128]{4,3,2,1,0:T(8,128)(2,1)S(1)}, bf16[4,2,2,16,128]{4,3,2,1,0:T(8,128)(2,1)S(1)}, u32[]{:S(2)}, u32[]{:S(2)}) collective-permute-start(bf16[4,2,2,16,128]{4,3,2,1,0:T(8,128)(2,1)S(1)} %collective-permute-done.3.refs_1_), channel_id=1, source_target_pairs={{0,4},{4,0},{8,12},{12,8},{16,20},{20,16},{24,28},{28,24},{1,5},{5... | collective-permute-start | bytes 196616 | tf_op jit(solution)/shard_map/ppermute | solution.py:268
  19.2 3.4 %collective-permute-start.8 = (bf16[4,2,2,16,128]{4,3,2,1,0:T(8,128)(2,1)S(1)}, bf16[4,2,2,16,128]{4,3,2,1,0:T(8,128)(2,1)S(1)}, u32[]{:S(2)}, u32[]{:S(2)}) collective-permute-start(bf16[4,2,2,16,128]{4,3,2,1,0:T(8,128)(2,1)S(1)} %collective-permute-done.4.refs_2_), channel_id=1, source_target_pairs={{0,4},{4,0},{8,12},{12,8},{16,20},{20,16},{24,28},{28,24},{1,5},{5... | collective-permute-start | bytes 196616 | tf_op jit(solution)/shard_map/ppermute | solution.py:268
  21.2 1.4 %collective-permute-start.9 = (bf16[4,2,2,16,128]{4,3,2,1,0:T(8,128)(2,1)S(1)}, bf16[4,2,2,16,128]{4,3,2,1,0:T(8,128)(2,1)S(1)}, u32[]{:S(2)}, u32[]{:S(2)}) collective-permute-start(bf16[4,2,2,16,128]{4,3,2,1,0:T(8,128)(2,1)S(1)} %collective-permute-done.5.refs_3_), channel_id=1, source_target_pairs={{0,4},{4,0},{8,12},{12,8},{16,20},{20,16},{24,28},{28,24},{1,5},{5... | collective-permute-start | bytes 196616 | tf_op jit(solution)/shard_map/ppermute | solution.py:268
  22.6 24.1 %copy-start.1 = (f32[16,2,8,128]{3,2,1,0:T(8,128)S(1)}, f32[16,2,8,128]{3,2,1,0:T(8,128)}, u32[]{:S(2)}) copy-start(f32[16,2,8,128]{3,2,1,0:T(8,128)} %refs_4_.1) | copy-start | bytes 393220
  22.6 24.1 %copy-start.2 = (f32[16,2,8,128]{3,2,1,0:T(8,128)S(1)}, f32[16,2,8,128]{3,2,1,0:T(8,128)}, u32[]{:S(2)}) copy-start(f32[16,2,8,128]{3,2,1,0:T(8,128)} %refs_5_.1) | copy-start | bytes 393220
  22.6 24.1 %copy-start.3 = (f32[16,2,8,128]{3,2,1,0:T(8,128)S(1)}, f32[16,2,8,128]{3,2,1,0:T(8,128)}, u32[]{:S(2)}) copy-start(f32[16,2,8,128]{3,2,1,0:T(8,128)} %refs_6_.1) | copy-start | bytes 393220
  31.8 1.7 %collective-permute-start.10 = (bf16[4,4,2,2,16,128]{5,4,3,2,1,0:T(8,128)(2,1)S(1)}, bf16[4,4,2,2,16,128]{5,4,3,2,1,0:T(8,128)(2,1)S(1)}, u32[]{:S(2)}, u32[]{:S(2)}) collective-permute-start(bf16[4,4,2,2,16,128]{5,4,3,2,1,0:T(8,128)(2,1)S(1)} %get-tuple-element.22), channel_id=1, source_target_pairs={{0,4},{4,0},{8,12},{12,8},{16,20},{20,16},{24,28},{28,24},{1,5},{5... | collective-permute-start | bytes 786440 | tf_op jit(solution)/shard_map/ppermute | solution.py:268
  33.6 4.4 %collective-permute-start.11 = (bf16[4,2,2,16,128]{4,3,2,1,0:T(8,128)(2,1)S(1)}, bf16[4,2,2,16,128]{4,3,2,1,0:T(8,128)(2,1)S(1)}, u32[]{:S(2)}, u32[]{:S(2)}) collective-permute-start(bf16[4,2,2,16,128]{4,3,2,1,0:T(8,128)(2,1)S(1)} %get-tuple-element.24), channel_id=1, source_target_pairs={{0,8},{4,12},{8,0},{12,4},{16,24},{20,28},{24,16},{28,20},{1,9},{5... | collective-permute-start | bytes 196616 | tf_op jit(solution)/shard_map/ppermute | solution.py:268
  34.2 5.0 %collective-permute-start.12 = (bf16[4,2,2,16,128]{4,3,2,1,0:T(8,128)(2,1)S(1)}, bf16[4,2,2,16,128]{4,3,2,1,0:T(8,128)(2,1)S(1)}, u32[]{:S(2)}, u32[]{:S(2)}) collective-permute-start(bf16[4,2,2,16,128]{4,3,2,1,0:T(8,128)(2,1)S(1)} %get-tuple-element.25), channel_id=1, source_target_pairs={{0,16},{4,20},{8,24},{12,28},{16,0},{20,4},{24,8},{28,12},{1,17},{... | collective-permute-start | bytes 196616 | tf_op jit(solution)/shard_map/ppermute | solution.py:268
  35.0 5.2 %collective-permute-start.13 = (bf16[4,2,2,16,128]{4,3,2,1,0:T(8,128)(2,1)S(1)}, bf16[4,2,2,16,128]{4,3,2,1,0:T(8,128)(2,1)S(1)}, u32[]{:S(2)}, u32[]{:S(2)}) collective-permute-start(bf16[4,2,2,16,128]{4,3,2,1,0:T(8,128)(2,1)S(1)} %get-tuple-element.26), channel_id=1, source_target_pairs={{0,24},{4,28},{8,16},{12,20},{16,8},{20,12},{24,0},{28,4},{1,25},{... | collective-permute-start | bytes 196616 | tf_op jit(solution)/shard_map/ppermute | solution.py:268
  40.2 4.5 %collective-permute-start.14 = (bf16[2,2,16,128]{3,2,1,0:T(8,128)(2,1)S(1)}, bf16[2,2,16,128]{3,2,1,0:T(8,128)(2,1)S(1)}, u32[]{:S(2)}, u32[]{:S(2)}) collective-permute-start(bf16[2,2,16,128]{3,2,1,0:T(8,128)(2,1)S(1)} %get-tuple-element.28), channel_id=1, source_target_pairs={{0,1},{1,0},{2,3},{3,2},{4,5},{5,4},{6,7},{7,6},{8,9},{9,8},{10,11... | collective-permute-start | bytes 49160 | tf_op jit(solution)/shard_map/ppermute | solution.py:268
  40.3 4.7 %collective-permute-start.15 = (bf16[2,2,16,128]{3,2,1,0:T(8,128)(2,1)S(1)}, bf16[2,2,16,128]{3,2,1,0:T(8,128)(2,1)S(1)}, u32[]{:S(2)}, u32[]{:S(2)}) collective-permute-start(bf16[2,2,16,128]{3,2,1,0:T(8,128)(2,1)S(1)} %get-tuple-element.29), channel_id=1, source_target_pairs={{0,2},{1,3},{2,0},{3,1},{4,6},{5,7},{6,4},{7,5},{8,10},{9,11},{10,... | collective-permute-start | bytes 49160 | tf_op jit(solution)/shard_map/ppermute | solution.py:268
  41.1 5.5 %collective-permute-start.16 = (bf16[2,2,16,128]{3,2,1,0:T(8,128)(2,1)S(1)}, bf16[2,2,16,128]{3,2,1,0:T(8,128)(2,1)S(1)}, u32[]{:S(2)}, u32[]{:S(2)}) collective-permute-start(bf16[2,2,16,128]{3,2,1,0:T(8,128)(2,1)S(1)} %get-tuple-element.30), channel_id=1, source_target_pairs={{0,3},{1,2},{2,1},{3,0},{4,7},{5,6},{6,5},{7,4},{8,11},{9,10},{10,... | collective-permute-start | bytes 49160 | tf_op jit(solution)/shard_map/ppermute | solution.py:268

commit v3 on v2

--- a/solution.py
+++ b/solution.py
@@ -20,42 +20,33 @@
 MIB = 1024 * 1024
 
 
-def pack_kernel(columns, cache_ref, *refs):
-    *outs, by_group = refs
-    groups = cache_ref.shape[2]
-    own = outs[0].shape[1]
-    repeat = own * columns // groups
-    for side in range(2):
-        for group in range(groups):
-            by_group[group, side] = cache_ref[:, side, group].astype(jnp.bfloat16)
-    column = lax.axis_index("cache")
-    for offset in range(columns):
-        first = (column ^ offset) // repeat * own
-        for slot in range(own):
-            for side in range(2):
-                outs[offset][side, slot] = by_group[first + slot, side]
+def pack_kernel(repeat, cache_ref, out_ref):
+    columns, _, own, _, _ = out_ref.shape
+    for column in range(columns):
+        for side in range(2):
+            for slot in range(own):
+                group = column // repeat * own + slot
+                out_ref[column, side, slot] = cache_ref[:, side, group].astype(jnp.bfloat16)
 
 
 def pack(cache, columns, own):
     share, _, groups, width = cache.shape
-    slice_shape = jax.ShapeDtypeStruct((2, own, share, width), jnp.bfloat16)
-    return pl.pallas_call(
-        functools.partial(pack_kernel, columns),
-        out_shape=[slice_shape] * columns,
-        scratch_shapes=[pltpu.VMEM((groups, 2, share, width), jnp.bfloat16)],
+    return pl.pallas_call(
+        functools.partial(pack_kernel, own * columns // groups),
+        out_shape=jax.ShapeDtypeStruct((columns, 2, own, share, width), jnp.bfloat16),
         compiler_params=pltpu.CompilerParams(vmem_limit_bytes=16 * MIB),
         name="pack",
     )(cache)
 
 
-def attend_kernel(score_scale, per_group, pieces, *refs):
-    pair_refs, refs = refs[:pieces], refs[pieces:]
+def attend_kernel(score_scale, per_group, *refs):
+    pair_refs, refs = refs[:2], refs[2:]
     queries_ref, grads_ref, lse_ref, dot_ref, mine_ref, mate_ref = refs[:6]
     keys, values, key_total, value_total = refs[6:10]
     even, odd = refs[10:14], refs[14:18]
-    columns, _, own, share, width = pair_refs[0].shape
-    length = columns * share
-    positions = pieces * length
+    chips, columns, _, own, share, width = pair_refs[0].shape
+    half = chips * columns * share
+    positions = 2 * half
     tiles = queries_ref.shape[0]
     log2e = math.log2(math.e)
     factor = score_scale * log2e
@@ -63,10 +54,10 @@
     along = (((1,), (0,)), ((), ()))
 
     for piece, pair_ref in enumerate(pair_refs):
-        at = pl.ds(piece * length, length)
+        at = pl.ds(piece * half, half)
         for slot in range(own):
-            keys[slot, at] = pair_ref[:, 0, slot].reshape(length, width)
-            values[slot, at] = pair_ref[:, 1, slot].reshape(length, width)
+            keys[slot, at] = pair_ref[:, :, 0, slot].reshape(half, width)
+            values[slot, at] = pair_ref[:, :, 1, slot].reshape(half, width)
     key_total[...] = jnp.zeros_like(key_total)
     value_total[...] = jnp.zeros_like(value_total)
 
@@ -133,7 +124,6 @@
     accumulate(tiles - 2, even)
     accumulate(tiles - 1, odd)
 
-    half = positions // 2
     shape = mine_ref.shape[:2] + (share, width)
     for slot in range(own):
         key_sum = key_total[slot] * score_scale
@@ -145,12 +135,11 @@
 
 
 def attend(pairs, queries, grads, lse_rows, dot_rows, score_scale):
-    columns, _, own, share, width = pairs[0].shape
-    pieces = len(pairs)
-    positions = pieces * columns * share
+    half = pairs[0].shape
+    chips, columns, _, own, share, width = half
+    positions = 2 * chips * columns * share
     tiles, row_tile, _ = queries.shape
     rows = tiles * row_tile
-    half = (pieces // 2, columns, 2, own, share, width)
     buffers = [
         pltpu.VMEM((positions, row_tile), jnp.float32),
         pltpu.VMEM((positions, row_tile), jnp.float32),
@@ -158,7 +147,7 @@
         pltpu.VMEM((positions, row_tile), jnp.bfloat16),
     ]
     return pl.pallas_call(
-        functools.partial(attend_kernel, score_scale, tiles // own, pieces),
+        functools.partial(attend_kernel, score_scale, tiles // own),
         out_shape=(
             jax.ShapeDtypeStruct(half, jnp.float32),
             jax.ShapeDtypeStruct(half, jnp.bfloat16),
@@ -181,64 +170,45 @@
     )(*pairs, queries, grads, lse_rows, dot_rows)
 
 
-def chip_sum_kernel(mine_ref, mate_ref, *outs):
-    for offset, out in enumerate(outs):
-        out[...] = (mine_ref[offset] + mate_ref[offset].astype(jnp.float32)).astype(out.dtype)
-
-
-def chip_sum(mine, mate):
-    chips = mine.shape[0]
-    shape = mine.shape[1:]
+def core_sum_kernel(mine_ref, mate_ref, out_ref):
+    out_ref[...] = (mine_ref[...] + mate_ref[...].astype(jnp.float32)).astype(out_ref.dtype)
+
+
+def core_sum(mine, mate):
+    return pl.pallas_call(
+        core_sum_kernel,
+        out_shape=jax.ShapeDtypeStruct(mate.shape, mate.dtype),
+        compiler_params=pltpu.CompilerParams(vmem_limit_bytes=16 * MIB),
+        name="core_sum",
+    )(mine, mate)
+
+
+def chip_sum_kernel(parts_ref, out_ref):
+    total = parts_ref[0].astype(jnp.float32)
+    for chip in range(1, parts_ref.shape[0]):
+        total = total + parts_ref[chip].astype(jnp.float32)
+    out_ref[...] = total.astype(out_ref.dtype)
+
+
+def chip_sum(parts):
     return pl.pallas_call(
         chip_sum_kernel,
-        out_shape=[
-            jax.ShapeDtypeStruct(shape, jnp.float32 if offset == 0 else jnp.bfloat16)
-            for offset in range(chips)
-        ],
+        out_shape=jax.ShapeDtypeStruct(parts.shape[1:], parts.dtype),
         compiler_params=pltpu.CompilerParams(vmem_limit_bytes=16 * MIB),
         name="chip_sum",
-    )(mine, mate)
-
-
-def column_sum_kernel(away, mine_ref, *refs):
-    others, outs = refs[:away], refs[away:]
-    for offset, out in enumerate(outs):
-        total = mine_ref[offset]
-        for other in others:
-            total = total + other[offset].astype(jnp.float32)
-        out[...] = total.astype(out.dtype)
-
-
-def column_sum(mine, others):
-    columns = mine.shape[0]
-    shape = mine.shape[1:]
-    return pl.pallas_call(
-        functools.partial(column_sum_kernel, len(others)),
-        out_shape=[
-            jax.ShapeDtypeStruct(shape, jnp.float32 if offset == 0 else jnp.bfloat16)
-            for offset in range(columns)
-        ],
-        compiler_params=pltpu.CompilerParams(vmem_limit_bytes=16 * MIB),
-        name="column_sum",
-    )(mine, *others)
-
-
-def adam_kernel(columns, *refs):
-    parts, refs = refs[:columns], refs[columns:]
-    cache_ref, first_ref, second_ref, new_cache, new_first, new_second, by_offset = refs
+    )(parts)
+
+
+def adam_kernel(parts_ref, cache_ref, first_ref, second_ref, new_cache, new_first, new_second):
+    columns, _, own, _, _ = parts_ref.shape
     groups = cache_ref.shape[2]
-    own = parts[0].shape[1]
     repeat = own * columns // groups
-    for offset, part in enumerate(parts):
-        by_offset[offset] = part[...].astype(jnp.float32)
-    column = lax.axis_index("cache")
     for side in range(2):
         for group in range(groups):
-            first_owner = group // own * repeat
-            slot = group % own
-            gradient = by_offset[column ^ first_owner, side, slot]
-            for owner in range(first_owner + 1, first_owner + repeat):
-                gradient = gradient + by_offset[column ^ owner, side, slot]
+            owner, slot = group // own * repeat, group % own
+            gradient = parts_ref[owner, side, slot].astype(jnp.float32)
+            for other in range(owner + 1, owner + repeat):
+                gradient = gradient + parts_ref[other, side, slot].astype(jnp.float32)
             first = beta_first * first_ref[:, side, group] + (1.0 - beta_first) * gradient
             second = (
                 beta_second * second_ref[:, side, group]
@@ -256,16 +226,20 @@
 def adam(parts, cache, first_moment, second_moment):
     shape = jax.ShapeDtypeStruct(cache.shape, jnp.float32)
     return pl.pallas_call(
-        functools.partial(adam_kernel, len(parts)),
+        adam_kernel,
         out_shape=(shape, shape, shape),
-        scratch_shapes=[pltpu.VMEM((len(parts),) + parts[0].shape, jnp.float32)],
         compiler_params=pltpu.CompilerParams(vmem_limit_bytes=16 * MIB),
         name="adam",
-    )(*parts, cache, first_moment, second_moment)
-
-
-def swap(value, axis, size, flip):
-    return lax.ppermute(value, axis, [(place, place ^ flip) for place in range(size)])
+    )(parts, cache, first_moment, second_moment)
+
+
+def core_swap(value, dp_size):
+    return lax.ppermute(value, "dp", [(place, place ^ 1) for place in range(dp_size)])
+
+
+def chips_exchange(value, dp_size):
+    same_core = [list(range(core, dp_size, 2)) for core in range(2)]
+    return lax.all_to_all(value, "dp", 0, 0, axis_index_groups=same_core, tiled=True)
 
 
 def per_device(
@@ -283,12 +257,10 @@
     first_group = column // repeat * own
     first_token = column % repeat * own_tokens
 
-    slices = pack(cache, columns, own)
-    gathered = jnp.stack(
-        [slices[0]] + [swap(slices[k], "cache", columns, k) for k in range(1, columns)]
-    )
-    pairs = [gathered] + [swap(gathered, "dp", dp_size, 2 * k) for k in range(1, chips)]
-    pairs = pairs + [swap(pair, "dp", dp_size, 1) for pair in pairs]
+    column_pairs = lax.all_to_all(pack(cache, columns, own), "cache", 0, 0, tiled=True)
+    copies = jnp.broadcast_to(column_pairs, (chips,) + column_pairs.shape)
+    core_pairs = chips_exchange(copies, dp_size)
+    pairs = (core_pairs, core_swap(core_pairs, dp_size))
 
     def tiles_of(array):
         parts = array.reshape((tokens, groups, group_size) + array.shape[2:])
@@ -304,14 +276,9 @@
         tiles_of(self_dot)[:, None],
         score_scale,
     )
-    by_chip = chip_sum(mine, swap(mate, "dp", dp_size, 1))
-    by_column = column_sum(
-        by_chip[0], [swap(by_chip[k], "dp", dp_size, 2 * k) for k in range(1, chips)]
-    )
-    parts = [by_column[0]] + [
-        swap(by_column[k], "cache", columns, k) for k in range(1, columns)
-    ]
-    return adam(parts, cache, first_moment, second_moment)
+    by_chip = chips_exchange(core_sum(mine, core_swap(mate, dp_size)), dp_size)
+    by_column = lax.all_to_all(chip_sum(by_chip), "cache", 0, 0, tiled=True)
+    return adam(by_column, cache, first_moment, second_moment)
 
 
 def solution(mesh):

time: 48.3 us -> 56.7 us (1.17)
  blocking collectives: 0 us -> 28.9 us
  starting transfers between devices: 18.5 us -> 4.29 us
  waiting for transfers between devices: 13.7 us -> 6.54 us
  local copies, waits for them, and re-layouts: 4.33 us -> 5.11 us
    all_to_all x0 -> x3, blocking collectives: none -> 28.9 us  [the longest x1 11.9 us: per_device(): lax.all_to_all(pack(cache, columns, own), 'cache', 0, 0, tiled=True)]
    ppermute x17 -> x2, starting transfers between devices: 18.5 us -> 0.57 us  [core_swap(): lax.ppermute(value, 'dp', [(place, place ^ 1) for place in range(dp_size)])]
    ppermute x17 -> x2, waiting for transfers between devices: 13.7 us -> 1.16 us  [core_swap(): lax.ppermute(value, 'dp', [(place, place ^ 1) for place in range(dp_size)])]
    all_to_all x0 -> x1, waiting for transfers between devices: none -> 5.37 us  [chips_exchange(): lax.all_to_all(value, 'dp', 0, 0, axis_index_groups=same_core, tiled=True)]
    all_to_all x0 -> x1, starting transfers between devices: none -> 3.72 us  [chips_exchange(): lax.all_to_all(value, 'dp', 0, 0, axis_index_groups=same_core, tiled=True)]
    broadcast_in_dim x0 -> x1, local copies, waits for them, and re-layouts: none -> 0.76 us  [per_device(): copies = jnp.broadcast_to(column_pairs, (chips,) + column_pairs.shape)]
  transfers between devices with their start and end apart: 17 -> 3, of which waited for: 9 -> 2; matrix products, arithmetic and copies ran while one was open for 7% -> 6% of each run, Pallas kernels for 0% -> 0%
where the time goes in v3:
time: 56.7 us; the launch traced here: 56.2 us
  blocking collectives  28.9 us (51%)
  Pallas kernels  10.7 us (19%)
  waiting for transfers between devices  6.54 us (12%)
  local copies, waits for them, and re-layouts  5.11 us (9%)
  starting transfers between devices  4.29 us (8%)
  between operations  0.75 us (1%)
    all_to_all x1, blocking collectives, per_device(): lax.all_to_all(pack(cache, columns, own), 'cache', 0, 0, tiled=True)  11.9 us
    pallas_call x1, Pallas kernels, attend(): pl.pallas_call(functools.partial(attend_kernel, score_scale, tiles // own...  9.18 us
    all_to_all x1, blocking collectives, chips_exchange(): lax.all_to_all(value, 'dp', 0, 0, axis_index_groups=same_core, tiled=True)  8.92 us
    all_to_all x1, blocking collectives, per_device(): by_column = lax.all_to_all(chip_sum(by_chip), 'cache', 0, 0, tiled=True)  8.11 us
    all_to_all x1, waiting for transfers between devices, chips_exchange(): lax.all_to_all(value, 'dp', 0, 0, axis_index_groups=same_core, tiled=True)  5.37 us
    all_to_all x1, starting transfers between devices, chips_exchange(): lax.all_to_all(value, 'dp', 0, 0, axis_index_groups=same_core, tiled=True)  3.72 us
    dynamic_slice x2, local copies, waits for them, and re-layouts, tiles_of(): part = lax.dynamic_slice_in_dim(part, first_group, own, 1)  2.7 us
    unnamed x12, local copies, waits for them, and re-layouts  1.3 us
  transfers between devices with their start and end apart: 3, of which 2 were waited for; matrix products, arithmetic and copies ran while one was open for 6% of the time, Pallas kernels for 0%

profile of v3, /device:TPU:0, one launch (start us, length us, event | category | flops | bytes accessed | tf_op | source)
XLA Modules:
  0.0 56.2 jit_solution(3012244894687226341)
XLA Ops:
  0.6 0.0 copy-start
  0.6 0.9 %copy-done = f32[16,2,8,128]{3,2,1,0:T(8,128)S(1)} copy-done((f32[16,2,8,128]{3,2,1,0:T(8,128)S(1)}, f32[16,2,8,128]{3,2,1,0:T(8,128)}, u32[]{:S(2)}) %copy-start) | copy-done | bytes 131096
  1.5 0.1 pack.1
  1.7 11.9 %all_to_all.20 = bf16[4,2,2,16,128]{4,3,2,1,0:T(8,128)(2,1)S(1)} all-to-all(bf16[4,2,2,16,128]{4,3,2,1,0:T(8,128)(2,1)S(1)} %pack.1), channel_id=1, replica_groups=mesh['dp'=8,'cache'=4] {'cache'}, dimensions={0} | all-to-all | bytes 131072 | tf_op jit(solution)/shard_map/all_to_all | solution.py:260
  13.5 0.8 %broadcast_in_dim.3 = bf16[4,4,2,2,16,128]{5,4,3,2,1,0:T(8,128)(2,1)} broadcast(bf16[4,2,2,16,128]{4,3,2,1,0:T(8,128)(2,1)S(1)} %all_to_all.20), dimensions={1,2,3,4,5} | broadcast | bytes 327680 | tf_op jit(solution)/shard_map/broadcast_in_dim | solution.py:261
  14.3 3.7 %all-to-all-start.1 = ((bf16[4,4,2,2,16,128]{5,4,3,2,1,0:T(8,128)(2,1)}), bf16[4,4,2,2,16,128]{5,4,3,2,1,0:T(8,128)(2,1)S(1)}, u32[]{:S(2)}, u32[]{:S(2)}) async-start(bf16[4,4,2,2,16,128]{5,4,3,2,1,0:T(8,128)(2,1)} %broadcast_in_dim.3), calls=%async_computation.1 | async-start | bytes 524288 | tf_op jit(solution)/shard_map/all_to_all | solution.py:242
  18.0 5.4 %all-to-all-done.1.refs_0_ = bf16[4,4,2,2,16,128]{5,4,3,2,1,0:T(8,128)(2,1)S(1)} async-done(((bf16[4,4,2,2,16,128]{5,4,3,2,1,0:T(8,128)(2,1)}), bf16[4,4,2,2,16,128]{5,4,3,2,1,0:T(8,128)(2,1)S(1)}, u32[]{:S(2)}, u32[]{:S(2)}) %all-to-all-start.1) | async-done | bytes 262176 | tf_op jit(solution)/shard_map/all_to_all | solution.py:242
  23.4 0.0 collective-permute-start
  23.4 2.0 %constant_dynamic-slice_fusion.2 = (bf16[256,2,8,128]{3,2,1,0:T(8,128)(2,1)S(1)}, bf16[256,2,8,128]{3,2,1,0:T(8,128)(2,1)S(1)}) fusion(bf16[256,8,8,128]{3,2,1,0:T(8,128)(2,1)} %bitcast.16, s32[]{:T(128)S(6)} %select_n.9, bf16[256,8,8,128]{3,2,1,0:T(8,128)(2,1)} %bitcast.17), kind=kLoop, calls=%fused_computation.2 | loop fusion | bytes 4194308 | tf_op jit(solution)/shard_map/dynamic_slice | solution.py:268
  25.4 0.1 copy.20
  25.4 0.1 copy.21
  25.5 0.7 %constant_dynamic-slice_fusion = (f32[256,2,8]{0,2,1:T(8,128)S(1)}, f32[256,2,8]{0,2,1:T(8,128)S(1)}) fusion(f32[256,8,8]{0,2,1:T(8,128)} %bitcast.18, s32[]{:T(128)S(6)} %select_n.9, f32[256,8,8]{0,2,1:T(8,128)} %bitcast.19), kind=kLoop, calls=%fused_computation | loop fusion | bytes 65540 | tf_op jit(solution)/shard_map/dynamic_slice | solution.py:268
  26.3 0.1 copy.22
  26.4 0.2 broadcast_in_dim_reshape.8.refs_4_
  26.6 0.1 copy.23
  26.7 0.2 broadcast_in_dim_reshape.9.refs_5_
  26.9 0.0 collective-permute-done.refs_1_
  26.9 0.0 copy-start.1
  26.9 0.0 copy-start.2
  26.9 0.0 copy-start.3
  26.9 9.2 %attend.1 = (f32[4,4,2,2,16,128]{5,4,3,2,1,0:T(8,128)S(1)}, bf16[4,4,2,2,16,128]{5,4,3,2,1,0:T(8,128)(2,1)S(1)}) custom-call(bf16[4,4,2,2,16,128]{5,4,3,2,1,0:T(8,128)(2,1)S(1)} %all-to-all-done.1.refs_0_, bf16[4,4,2,2,16,128]{5,4,3,2,1,0:T(8,128)(2,1)S(1)} %collective-permute-done.refs_1_, bf16[16,256,128]{2,1,0:T(8,128)(2,1)S(1)} %bitcast.12, ...), custom_call_target="tpu_custom_call" | custom-call | flops 2147483648 | bytes 3145728 | tf_op jit(solution)/shard_map/attend/pallas_call | solution.py:149
  36.1 0.6 %collective-permute-start.1 = (bf16[4,4,2,2,16,128]{5,4,3,2,1,0:T(8,128)(2,1)S(1)}, bf16[4,4,2,2,16,128]{5,4,3,2,1,0:T(8,128)(2,1)S(1)}, u32[]{:S(2)}, u32[]{:S(2)}) collective-permute-start(bf16[4,4,2,2,16,128]{5,4,3,2,1,0:T(8,128)(2,1)S(1)} %get-tuple-element.6), channel_id=1, source_target_pairs={{0,4},{4,0},{8,12},{12,8},{16,20},{20,16},{24,28},{28,24},{1,5},{5... | collective-permute-start | bytes 786440 | tf_op jit(solution)/shard_map/ppermute | solution.py:237
  36.7 1.2 %collective-permute-done.1.mate_ref = bf16[4,4,2,2,16,128]{5,4,3,2,1,0:T(8,128)(2,1)S(1)} collective-permute-done((bf16[4,4,2,2,16,128]{5,4,3,2,1,0:T(8,128)(2,1)S(1)}, bf16[4,4,2,2,16,128]{5,4,3,2,1,0:T(8,128)(2,1)S(1)}, u32[]{:S(2)}, u32[]{:S(2)}) %collective-permute-start.1) | collective-permute-done | bytes 262176 | tf_op jit(solution)/shard_map/ppermute | solution.py:237
  37.9 8.9 %all_to_all.21.parts_ref = bf16[4,4,2,2,16,128]{5,4,3,2,1,0:T(8,128)(2,1)S(1)} all-to-all(bf16[4,4,2,2,16,128]{5,4,3,2,1,0:T(8,128)(2,1)S(1)} %core_sum.1), channel_id=1, replica_groups={{0,8,16,24},{4,12,20,28},{1,9,17,25},{5,13,21,29},{2,10,18,26},{6,14,22..., dimensions={0} | all-to-all | bytes 524288 | tf_op jit(solution)/shard_map/all_to_all | solution.py:242
  46.8 8.1 %all_to_all.22.parts_ref = bf16[4,2,2,16,128]{4,3,2,1,0:T(8,128)(2,1)S(1)} all-to-all(bf16[4,2,2,16,128]{4,3,2,1,0:T(8,128)(2,1)S(1)} %chip_sum.1), channel_id=1, replica_groups=mesh['dp'=8,'cache'=4] {'cache'}, dimensions={0} | all-to-all | bytes 131072 | tf_op jit(solution)/shard_map/all_to_all | solution.py:280
  54.9 0.0 copy-done.1
  55.0 0.0 copy-done.2
  55.0 0.0 copy-done.3
  55.0 1.3 %adam.1 = (f32[16,2,8,128]{3,2,1,0:T(8,128)}, f32[16,2,8,128]{3,2,1,0:T(8,128)}, f32[16,2,8,128]{3,2,1,0:T(8,128)}) custom-call(bf16[4,2,2,16,128]{4,3,2,1,0:T(8,128)(2,1)S(1)} %all_to_all.22.parts_ref, f32[16,2,8,128]{3,2,1,0:T(8,128)S(1)} %copy-done.1, f32[16,2,8,128]{3,2,1,0:T(8,128)S(1)} %copy-done.2, f32[16,2,8,128]{3,2,1,0:T(8,128)S(1)} %copy-done.3), custom_call_target="tpu_custom_call" | custom-call | tf_op jit(solution)/shard_map/adam/pallas_call | solution.py:228
  (2 shorter events, 0.1 us)
Async XLA Ops:
  0.6 0.9 %copy-start = (f32[16,2,8,128]{3,2,1,0:T(8,128)S(1)}, f32[16,2,8,128]{3,2,1,0:T(8,128)}, u32[]{:S(2)}) copy-start(f32[16,2,8,128]{3,2,1,0:T(8,128)} %cache_ref.3) | copy-start | bytes 393220
  14.3 9.1 %all-to-all-start.1 = ((bf16[4,4,2,2,16,128]{5,4,3,2,1,0:T(8,128)(2,1)}), bf16[4,4,2,2,16,128]{5,4,3,2,1,0:T(8,128)(2,1)S(1)}, u32[]{:S(2)}, u32[]{:S(2)}) async-start(bf16[4,4,2,2,16,128]{5,4,3,2,1,0:T(8,128)(2,1)} %broadcast_in_dim.3), calls=%async_computation.1 | async-start | bytes 524288 | tf_op jit(solution)/shard_map/all_to_all | solution.py:242
  23.4 3.5 %collective-permute-start = (bf16[4,4,2,2,16,128]{5,4,3,2,1,0:T(8,128)(2,1)S(1)}, bf16[4,4,2,2,16,128]{5,4,3,2,1,0:T(8,128)(2,1)S(1)}, u32[]{:S(2)}, u32[]{:S(2)}) collective-permute-start(bf16[4,4,2,2,16,128]{5,4,3,2,1,0:T(8,128)(2,1)S(1)} %all-to-all-done.1.refs_0_), channel_id=1, source_target_pairs={{0,4},{4,0},{8,12},{12,8},{16,20},{20,16},{24,28},{28,24},{1,5},{5... | collective-permute-start | bytes 786440 | tf_op jit(solution)/shard_map/ppermute | solution.py:237
  26.9 28.1 %copy-start.1 = (f32[16,2,8,128]{3,2,1,0:T(8,128)S(1)}, f32[16,2,8,128]{3,2,1,0:T(8,128)}, u32[]{:S(2)}) copy-start(f32[16,2,8,128]{3,2,1,0:T(8,128)} %cache_ref.3) | copy-start | bytes 393220
  26.9 28.1 %copy-start.2 = (f32[16,2,8,128]{3,2,1,0:T(8,128)S(1)}, f32[16,2,8,128]{3,2,1,0:T(8,128)}, u32[]{:S(2)}) copy-start(f32[16,2,8,128]{3,2,1,0:T(8,128)} %first_ref.1) | copy-start | bytes 393220
  26.9 28.1 %copy-start.3 = (f32[16,2,8,128]{3,2,1,0:T(8,128)S(1)}, f32[16,2,8,128]{3,2,1,0:T(8,128)}, u32[]{:S(2)}) copy-start(f32[16,2,8,128]{3,2,1,0:T(8,128)} %second_ref.1) | copy-start | bytes 393220
  36.1 1.7 %collective-permute-start.1 = (bf16[4,4,2,2,16,128]{5,4,3,2,1,0:T(8,128)(2,1)S(1)}, bf16[4,4,2,2,16,128]{5,4,3,2,1,0:T(8,128)(2,1)S(1)}, u32[]{:S(2)}, u32[]{:S(2)}) collective-permute-start(bf16[4,4,2,2,16,128]{5,4,3,2,1,0:T(8,128)(2,1)S(1)} %get-tuple-element.6), channel_id=1, source_target_pairs={{0,4},{4,0},{8,12},{12,8},{16,20},{20,16},{24,28},{28,24},{1,5},{5... | collective-permute-start | bytes 786440 | tf_op jit(solution)/shard_map/ppermute | solution.py:237

commit v4 on v2

--- a/solution.py
+++ b/solution.py
@@ -15,9 +15,13 @@
 beta_second = 0.999
 epsilon = 1e-08
 
-ROW_TILE = 256
-CHUNK = 32
+ROW_TILE = 512
+CHUNK = 16
 MIB = 1024 * 1024
+
+
+def flips(size):
+    return list(range(size - 1, -1, -1))
 
 
 def pack_kernel(columns, cache_ref, *refs):
@@ -29,11 +33,11 @@
         for group in range(groups):
             by_group[group, side] = cache_ref[:, side, group].astype(jnp.bfloat16)
     column = lax.axis_index("cache")
-    for offset in range(columns):
-        first = (column ^ offset) // repeat * own
+    for out, flip in zip(outs, flips(columns)):
+        first = (column ^ flip) // repeat * own
         for slot in range(own):
             for side in range(2):
-                outs[offset][side, slot] = by_group[first + slot, side]
+                out[side, slot] = by_group[first + slot, side]
 
 
 def pack(cache, columns, own):
@@ -192,8 +196,8 @@
     return pl.pallas_call(
         chip_sum_kernel,
         out_shape=[
-            jax.ShapeDtypeStruct(shape, jnp.float32 if offset == 0 else jnp.bfloat16)
-            for offset in range(chips)
+            jax.ShapeDtypeStruct(shape, jnp.bfloat16 if flip else jnp.float32)
+            for flip in flips(chips)
         ],
         compiler_params=pltpu.CompilerParams(vmem_limit_bytes=16 * MIB),
         name="chip_sum",
@@ -215,8 +219,8 @@
     return pl.pallas_call(
         functools.partial(column_sum_kernel, len(others)),
         out_shape=[
-            jax.ShapeDtypeStruct(shape, jnp.float32 if offset == 0 else jnp.bfloat16)
-            for offset in range(columns)
+            jax.ShapeDtypeStruct(shape, jnp.bfloat16 if flip else jnp.float32)
+            for flip in flips(columns)
         ],
         compiler_params=pltpu.CompilerParams(vmem_limit_bytes=16 * MIB),
         name="column_sum",
@@ -225,20 +229,20 @@
 
 def adam_kernel(columns, *refs):
     parts, refs = refs[:columns], refs[columns:]
-    cache_ref, first_ref, second_ref, new_cache, new_first, new_second, by_offset = refs
+    cache_ref, first_ref, second_ref, new_cache, new_first, new_second, by_flip = refs
     groups = cache_ref.shape[2]
     own = parts[0].shape[1]
     repeat = own * columns // groups
-    for offset, part in enumerate(parts):
-        by_offset[offset] = part[...].astype(jnp.float32)
+    for part, flip in zip(parts, flips(columns)):
+        by_flip[flip] = part[...].astype(jnp.float32)
     column = lax.axis_index("cache")
     for side in range(2):
         for group in range(groups):
             first_owner = group // own * repeat
             slot = group % own
-            gradient = by_offset[column ^ first_owner, side, slot]
+            gradient = by_flip[column ^ first_owner, side, slot]
             for owner in range(first_owner + 1, first_owner + repeat):
-                gradient = gradient + by_offset[column ^ owner, side, slot]
+                gradient = gradient + by_flip[column ^ owner, side, slot]
             first = beta_first * first_ref[:, side, group] + (1.0 - beta_first) * gradient
             second = (
                 beta_second * second_ref[:, side, group]
@@ -266,6 +270,13 @@
 
 def swap(value, axis, size, flip):
     return lax.ppermute(value, axis, [(place, place ^ flip) for place in range(size)])
+
+
+def swap_all(values, axis, size, stride):
+    return [
+        swap(value, axis, size, flip * stride) if flip else value
+        for value, flip in zip(values, flips(len(values)))
+    ]
 
 
 def per_device(
@@ -284,10 +295,8 @@
     first_token = column % repeat * own_tokens
 
     slices = pack(cache, columns, own)
-    gathered = jnp.stack(
-        [slices[0]] + [swap(slices[k], "cache", columns, k) for k in range(1, columns)]
-    )
-    pairs = [gathered] + [swap(gathered, "dp", dp_size, 2 * k) for k in range(1, chips)]
+    gathered = jnp.stack(swap_all(slices, "cache", columns, 1))
+    pairs = swap_all([gathered] * chips, "dp", dp_size, 2)
     pairs = pairs + [swap(pair, "dp", dp_size, 1) for pair in pairs]
 
     def tiles_of(array):
@@ -305,12 +314,9 @@
         score_scale,
     )
     by_chip = chip_sum(mine, swap(mate, "dp", dp_size, 1))
-    by_column = column_sum(
-        by_chip[0], [swap(by_chip[k], "dp", dp_size, 2 * k) for k in range(1, chips)]
-    )
-    parts = [by_column[0]] + [
-        swap(by_column[k], "cache", columns, k) for k in range(1, columns)
-    ]
+    *away, home = swap_all(by_chip, "dp", dp_size, 2)
+    by_column = column_sum(home, away)
+    parts = swap_all(by_column, "cache", columns, 1)
     return adam(parts, cache, first_moment, second_moment)
 
 

time: 48.3 us -> 44.6 us (0.923)
  waiting for transfers between devices: 13.7 us -> 11.4 us
  Pallas kernels: 10.7 us -> 9.32 us
    ppermute x17, waiting for transfers between devices: 13.7 us -> 11.4 us  [swap(): lax.ppermute(value, axis, [(place, place ^ flip) for place in range(size)])]
    pallas_call x1, Pallas kernels: 9.16 us -> 7.83 us  [attend(): pl.pallas_call(functools.partial(attend_kernel, score_scale, tiles // own...]
  transfers between devices with their start and end apart: 17 -> 17, of which waited for: 9 -> 12; matrix products, arithmetic and copies ran while one was open for 7% -> 8% of each run, Pallas kernels for 0% -> 0%
where the time goes in v4:
time: 44.6 us; the launch traced here: 44.3 us
  starting transfers between devices  18.4 us (41%)
  waiting for transfers between devices  11.4 us (26%)
  Pallas kernels  9.32 us (21%)
  local copies, waits for them, and re-layouts  4.33 us (10%)
  between operations  0.79 us (2%)
    ppermute x17, starting transfers between devices, swap(): lax.ppermute(value, axis, [(place, place ^ flip) for place in range(size)])  18.4 us
    ppermute x17, waiting for transfers between devices, swap(): lax.ppermute(value, axis, [(place, place ^ flip) for place in range(size)])  11.4 us
    pallas_call x1, Pallas kernels, attend(): pl.pallas_call(functools.partial(attend_kernel, score_scale, tiles // own...  7.83 us
    dynamic_slice x2, local copies, waits for them, and re-layouts, tiles_of(): part = lax.dynamic_slice_in_dim(part, first_group, own, 1)  2.69 us
    unnamed x12, local copies, waits for them, and re-layouts  1.3 us
    pallas_call x1, Pallas kernels, adam(): pl.pallas_call(functools.partial(adam_kernel, len(parts)), out_shape=(sha...  1.27 us
  transfers between devices with their start and end apart: 17, of which 12 were waited for; matrix products, arithmetic and copies ran while one was open for 8% of the time, Pallas kernels for 0%

profile of v4, /device:TPU:0, one launch (start us, length us, event | category | flops | bytes accessed | tf_op | source)
XLA Modules:
  0.0 44.3 jit_solution(18304351295595252115)
XLA Ops:
  0.6 0.0 copy-start
  0.6 0.9 %copy-done = f32[16,2,8,128]{3,2,1,0:T(8,128)S(1)} copy-done((f32[16,2,8,128]{3,2,1,0:T(8,128)S(1)}, f32[16,2,8,128]{3,2,1,0:T(8,128)}, u32[]{:S(2)}) %copy-start) | copy-done | bytes 131096
  1.5 0.1 pack.1
  1.7 5.1 %collective-permute-start = (bf16[2,2,16,128]{3,2,1,0:T(8,128)(2,1)S(1)}, bf16[2,2,16,128]{3,2,1,0:T(8,128)(2,1)S(1)}, u32[]{:S(2)}, u32[]{:S(2)}) collective-permute-start(bf16[2,2,16,128]{3,2,1,0:T(8,128)(2,1)S(1)} %get-tuple-element.17), channel_id=1, source_target_pairs={{0,3},{1,2},{2,1},{3,0},{4,7},{5,6},{6,5},{7,4},{8,11},{9,10},{10,... | collective-permute-start | bytes 49160 | tf_op jit(solution)/shard_map/ppermute | solution.py:272
  6.8 0.0 collective-permute-start.1
  6.8 0.6 %collective-permute-start.2 = (bf16[2,2,16,128]{3,2,1,0:T(8,128)(2,1)S(1)}, bf16[2,2,16,128]{3,2,1,0:T(8,128)(2,1)S(1)}, u32[]{:S(2)}, u32[]{:S(2)}) collective-permute-start(bf16[2,2,16,128]{3,2,1,0:T(8,128)(2,1)S(1)} %get-tuple-element.19), channel_id=1, source_target_pairs={{0,1},{1,0},{2,3},{3,2},{4,5},{5,4},{6,7},{7,6},{8,9},{9,8},{10,11... | collective-permute-start | bytes 49160 | tf_op jit(solution)/shard_map/ppermute | solution.py:272
  7.4 1.1 %collective-permute-done = bf16[2,2,16,128]{3,2,1,0:T(8,128)(2,1)S(1)} collective-permute-done((bf16[2,2,16,128]{3,2,1,0:T(8,128)(2,1)S(1)}, bf16[2,2,16,128]{3,2,1,0:T(8,128)(2,1)S(1)}, u32[]{:S(2)}, u32[]{:S(2)}) %collective-permute-start) | collective-permute-done | bytes 16416 | tf_op jit(solution)/shard_map/ppermute | solution.py:272
  8.5 2.9 %collective-permute-done.1 = bf16[2,2,16,128]{3,2,1,0:T(8,128)(2,1)S(1)} collective-permute-done((bf16[2,2,16,128]{3,2,1,0:T(8,128)(2,1)S(1)}, bf16[2,2,16,128]{3,2,1,0:T(8,128)(2,1)S(1)}, u32[]{:S(2)}, u32[]{:S(2)}) %collective-permute-start.1) | collective-permute-done | bytes 16416 | tf_op jit(solution)/shard_map/ppermute | solution.py:272
  11.4 0.0 collective-permute-done.2
  11.5 2.5 %collective-permute-start.3 = (bf16[4,2,2,16,128]{4,3,2,1,0:T(8,128)(2,1)S(1)}, bf16[4,2,2,16,128]{4,3,2,1,0:T(8,128)(2,1)S(1)}, u32[]{:S(2)}, u32[]{:S(2)}) collective-permute-start(bf16[4,2,2,16,128]{4,3,2,1,0:T(8,128)(2,1)S(1)} %pad_maximum_fusion.refs_3_), channel_id=1, source_target_pairs={{0,24},{4,28},{8,16},{12,20},{16,8},{20,12},{24,0},{28,4},{1,25},{... | collective-permute-start | bytes 196616 | tf_op jit(solution)/shard_map/ppermute | solution.py:272
  14.0 0.5 %collective-permute-start.4 = (bf16[4,2,2,16,128]{4,3,2,1,0:T(8,128)(2,1)S(1)}, bf16[4,2,2,16,128]{4,3,2,1,0:T(8,128)(2,1)S(1)}, u32[]{:S(2)}, u32[]{:S(2)}) collective-permute-start(bf16[4,2,2,16,128]{4,3,2,1,0:T(8,128)(2,1)S(1)} %pad_maximum_fusion.refs_3_), channel_id=1, source_target_pairs={{0,16},{4,20},{8,24},{12,28},{16,0},{20,4},{24,8},{28,12},{1,17},{... | collective-permute-start | bytes 196616 | tf_op jit(solution)/shard_map/ppermute | solution.py:272
  14.5 0.5 %collective-permute-start.5 = (bf16[4,2,2,16,128]{4,3,2,1,0:T(8,128)(2,1)S(1)}, bf16[4,2,2,16,128]{4,3,2,1,0:T(8,128)(2,1)S(1)}, u32[]{:S(2)}, u32[]{:S(2)}) collective-permute-start(bf16[4,2,2,16,128]{4,3,2,1,0:T(8,128)(2,1)S(1)} %pad_maximum_fusion.refs_3_), channel_id=1, source_target_pairs={{0,8},{4,12},{8,0},{12,4},{16,24},{20,28},{24,16},{28,20},{1,9},{5... | collective-permute-start | bytes 196616 | tf_op jit(solution)/shard_map/ppermute | solution.py:272
  15.0 2.0 %constant_dynamic-slice_fusion.2 = (bf16[256,2,8,128]{3,2,1,0:T(8,128)(2,1)S(1)}, bf16[256,2,8,128]{3,2,1,0:T(8,128)(2,1)S(1)}) fusion(bf16[256,8,8,128]{3,2,1,0:T(8,128)(2,1)} %bitcast.21, s32[]{:T(128)S(6)} %select_n.9, bf16[256,8,8,128]{3,2,1,0:T(8,128)(2,1)} %bitcast.22), kind=kLoop, calls=%fused_computation.3 | loop fusion | bytes 4194308 | tf_op jit(solution)/shard_map/dynamic_slice | solution.py:305
  17.0 0.1 copy.20
  17.0 0.1 copy.21
  17.1 0.1 collective-permute-start.9
  17.2 0.1 collective-permute-done.3.refs_0_
  17.3 0.4 collective-permute-start.6
  17.7 0.5 %collective-permute-done.4.refs_1_ = bf16[4,2,2,16,128]{4,3,2,1,0:T(8,128)(2,1)S(1)} collective-permute-done((bf16[4,2,2,16,128]{4,3,2,1,0:T(8,128)(2,1)S(1)}, bf16[4,2,2,16,128]{4,3,2,1,0:T(8,128)(2,1)S(1)}, u32[]{:S(2)}, u32[]{:S(2)}) %collective-permute-start.4) | collective-permute-done | bytes 65568 | tf_op jit(solution)/shard_map/ppermute | solution.py:272
  18.2 0.0 collective-permute-start.7
  18.2 0.5 %collective-permute-done.5.refs_2_ = bf16[4,2,2,16,128]{4,3,2,1,0:T(8,128)(2,1)S(1)} collective-permute-done((bf16[4,2,2,16,128]{4,3,2,1,0:T(8,128)(2,1)S(1)}, bf16[4,2,2,16,128]{4,3,2,1,0:T(8,128)(2,1)S(1)}, u32[]{:S(2)}, u32[]{:S(2)}) %collective-permute-start.5) | collective-permute-done | bytes 65568 | tf_op jit(solution)/shard_map/ppermute | solution.py:272
  18.7 0.0 collective-permute-start.8
  18.7 0.7 %constant_dynamic-slice_fusion = (f32[256,2,8]{0,2,1:T(8,128)S(1)}, f32[256,2,8]{0,2,1:T(8,128)S(1)}) fusion(f32[256,8,8]{0,2,1:T(8,128)} %bitcast.26, s32[]{:T(128)S(6)} %select_n.9, f32[256,8,8]{0,2,1:T(8,128)} %bitcast.27), kind=kLoop, calls=%fused_computation.1 | loop fusion | bytes 65540 | tf_op jit(solution)/shard_map/dynamic_slice | solution.py:305
  19.5 0.1 copy.22
  19.6 0.2 broadcast_in_dim_reshape.8.refs_10_
  19.8 0.1 copy.23
  19.9 0.2 broadcast_in_dim_reshape.9.refs_11_
  20.1 0.0 collective-permute-done.9.refs_7_
  20.1 0.0 collective-permute-done.6.refs_4_
  20.1 0.0 collective-permute-done.7.refs_5_
  20.1 0.0 collective-permute-done.8.refs_6_
  20.1 0.0 copy-start.1
  20.2 0.0 copy-start.2
  20.2 0.0 copy-start.3
  20.2 7.8 %attend.1 = (f32[4,4,2,2,16,128]{5,4,3,2,1,0:T(8,128)S(1)}, bf16[4,4,2,2,16,128]{5,4,3,2,1,0:T(8,128)(2,1)S(1)}) custom-call(bf16[4,2,2,16,128]{4,3,2,1,0:T(8,128)(2,1)S(1)} %collective-permute-done.3.refs_0_, bf16[4,2,2,16,128]{4,3,2,1,0:T(8,128)(2,1)S(1)} %collective-permute-done.4.refs_1_, bf16[4,2,2,16,128]{4,3,2,1,0:T(8,128)(2,1)S(1)} %collective-permute-done.5.refs_2_, ...), custom_call_target="tpu_custom_call" | custom-call | flops 2147483648 | bytes 3145728 | tf_op jit(solution)/shard_map/attend/pallas_call | solution.py:164
  28.0 0.6 %collective-permute-start.10 = (bf16[4,4,2,2,16,128]{5,4,3,2,1,0:T(8,128)(2,1)S(1)}, bf16[4,4,2,2,16,128]{5,4,3,2,1,0:T(8,128)(2,1)S(1)}, u32[]{:S(2)}, u32[]{:S(2)}) collective-permute-start(bf16[4,4,2,2,16,128]{5,4,3,2,1,0:T(8,128)(2,1)S(1)} %get-tuple-element.22), channel_id=1, source_target_pairs={{0,4},{4,0},{8,12},{12,8},{16,20},{20,16},{24,28},{28,24},{1,5},{5... | collective-permute-start | bytes 786440 | tf_op jit(solution)/shard_map/ppermute | solution.py:272
  28.6 1.2 %collective-permute-done.10.mate_ref = bf16[4,4,2,2,16,128]{5,4,3,2,1,0:T(8,128)(2,1)S(1)} collective-permute-done((bf16[4,4,2,2,16,128]{5,4,3,2,1,0:T(8,128)(2,1)S(1)}, bf16[4,4,2,2,16,128]{5,4,3,2,1,0:T(8,128)(2,1)S(1)}, u32[]{:S(2)}, u32[]{:S(2)}) %collective-permute-start.10) | collective-permute-done | bytes 262176 | tf_op jit(solution)/shard_map/ppermute | solution.py:272
  29.8 1.9 %collective-permute-start.11 = (bf16[4,2,2,16,128]{4,3,2,1,0:T(8,128)(2,1)S(1)}, bf16[4,2,2,16,128]{4,3,2,1,0:T(8,128)(2,1)S(1)}, u32[]{:S(2)}, u32[]{:S(2)}) collective-permute-start(bf16[4,2,2,16,128]{4,3,2,1,0:T(8,128)(2,1)S(1)} %get-tuple-element.24), channel_id=1, source_target_pairs={{0,24},{4,28},{8,16},{12,20},{16,8},{20,12},{24,0},{28,4},{1,25},{... | collective-permute-start | bytes 196616 | tf_op jit(solution)/shard_map/ppermute | solution.py:272
  31.7 0.5 %collective-permute-start.12 = (bf16[4,2,2,16,128]{4,3,2,1,0:T(8,128)(2,1)S(1)}, bf16[4,2,2,16,128]{4,3,2,1,0:T(8,128)(2,1)S(1)}, u32[]{:S(2)}, u32[]{:S(2)}) collective-permute-start(bf16[4,2,2,16,128]{4,3,2,1,0:T(8,128)(2,1)S(1)} %get-tuple-element.25), channel_id=1, source_target_pairs={{0,16},{4,20},{8,24},{12,28},{16,0},{20,4},{24,8},{28,12},{1,17},{... | collective-permute-start | bytes 196616 | tf_op jit(solution)/shard_map/ppermute | solution.py:272
  32.2 1.2 %collective-permute-start.13 = (bf16[4,2,2,16,128]{4,3,2,1,0:T(8,128)(2,1)S(1)}, bf16[4,2,2,16,128]{4,3,2,1,0:T(8,128)(2,1)S(1)}, u32[]{:S(2)}, u32[]{:S(2)}) collective-permute-start(bf16[4,2,2,16,128]{4,3,2,1,0:T(8,128)(2,1)S(1)} %get-tuple-element.26), channel_id=1, source_target_pairs={{0,8},{4,12},{8,0},{12,4},{16,24},{20,28},{24,16},{28,20},{1,9},{5... | collective-permute-start | bytes 196616 | tf_op jit(solution)/shard_map/ppermute | solution.py:272
  33.4 1.9 %collective-permute-done.11.refs_0_ = bf16[4,2,2,16,128]{4,3,2,1,0:T(8,128)(2,1)S(1)} collective-permute-done((bf16[4,2,2,16,128]{4,3,2,1,0:T(8,128)(2,1)S(1)}, bf16[4,2,2,16,128]{4,3,2,1,0:T(8,128)(2,1)S(1)}, u32[]{:S(2)}, u32[]{:S(2)}) %collective-permute-start.11) | collective-permute-done | bytes 65568 | tf_op jit(solution)/shard_map/ppermute | solution.py:272
  35.2 1.3 %collective-permute-done.12.refs_1_ = bf16[4,2,2,16,128]{4,3,2,1,0:T(8,128)(2,1)S(1)} collective-permute-done((bf16[4,2,2,16,128]{4,3,2,1,0:T(8,128)(2,1)S(1)}, bf16[4,2,2,16,128]{4,3,2,1,0:T(8,128)(2,1)S(1)}, u32[]{:S(2)}, u32[]{:S(2)}) %collective-permute-start.12) | collective-permute-done | bytes 65568 | tf_op jit(solution)/shard_map/ppermute | solution.py:272
  36.5 0.1 collective-permute-done.13.refs_2_
  36.6 1.5 %collective-permute-start.14 = (bf16[2,2,16,128]{3,2,1,0:T(8,128)(2,1)S(1)}, bf16[2,2,16,128]{3,2,1,0:T(8,128)(2,1)S(1)}, u32[]{:S(2)}, u32[]{:S(2)}) collective-permute-start(bf16[2,2,16,128]{3,2,1,0:T(8,128)(2,1)S(1)} %get-tuple-element.27), channel_id=1, source_target_pairs={{0,3},{1,2},{2,1},{3,0},{4,7},{5,6},{6,5},{7,4},{8,11},{9,10},{10,... | collective-permute-start | bytes 49160 | tf_op jit(solution)/shard_map/ppermute | solution.py:272
  38.2 0.6 %collective-permute-start.15 = (bf16[2,2,16,128]{3,2,1,0:T(8,128)(2,1)S(1)}, bf16[2,2,16,128]{3,2,1,0:T(8,128)(2,1)S(1)}, u32[]{:S(2)}, u32[]{:S(2)}) collective-permute-start(bf16[2,2,16,128]{3,2,1,0:T(8,128)(2,1)S(1)} %get-tuple-element.28), channel_id=1, source_target_pairs={{0,2},{1,3},{2,0},{3,1},{4,6},{5,7},{6,4},{7,5},{8,10},{9,11},{10,... | collective-permute-start | bytes 49160 | tf_op jit(solution)/shard_map/ppermute | solution.py:272
  38.8 2.3 %collective-permute-start.16 = (bf16[2,2,16,128]{3,2,1,0:T(8,128)(2,1)S(1)}, bf16[2,2,16,128]{3,2,1,0:T(8,128)(2,1)S(1)}, u32[]{:S(2)}, u32[]{:S(2)}) collective-permute-start(bf16[2,2,16,128]{3,2,1,0:T(8,128)(2,1)S(1)} %get-tuple-element.29), channel_id=1, source_target_pairs={{0,1},{1,0},{2,3},{3,2},{4,5},{5,4},{6,7},{7,6},{8,9},{9,8},{10,11... | collective-permute-start | bytes 49160 | tf_op jit(solution)/shard_map/ppermute | solution.py:272
  41.1 1.2 %collective-permute-done.14.refs_0_ = bf16[2,2,16,128]{3,2,1,0:T(8,128)(2,1)S(1)} collective-permute-done((bf16[2,2,16,128]{3,2,1,0:T(8,128)(2,1)S(1)}, bf16[2,2,16,128]{3,2,1,0:T(8,128)(2,1)S(1)}, u32[]{:S(2)}, u32[]{:S(2)}) %collective-permute-start.14) | collective-permute-done | bytes 16416 | tf_op jit(solution)/shard_map/ppermute | solution.py:272
  42.2 0.6 %collective-permute-done.15.refs_1_ = bf16[2,2,16,128]{3,2,1,0:T(8,128)(2,1)S(1)} collective-permute-done((bf16[2,2,16,128]{3,2,1,0:T(8,128)(2,1)S(1)}, bf16[2,2,16,128]{3,2,1,0:T(8,128)(2,1)S(1)}, u32[]{:S(2)}, u32[]{:S(2)}) %collective-permute-start.15) | collective-permute-done | bytes 16416 | tf_op jit(solution)/shard_map/ppermute | solution.py:272
  42.8 0.2 collective-permute-done.16.refs_2_
  43.0 0.0 copy-done.1
  43.0 0.0 copy-done.2
  43.0 0.0 copy-done.3
  43.0 1.3 %adam.1 = (f32[16,2,8,128]{3,2,1,0:T(8,128)}, f32[16,2,8,128]{3,2,1,0:T(8,128)}, f32[16,2,8,128]{3,2,1,0:T(8,128)}) custom-call(bf16[2,2,16,128]{3,2,1,0:T(8,128)(2,1)S(1)} %collective-permute-done.14.refs_0_, bf16[2,2,16,128]{3,2,1,0:T(8,128)(2,1)S(1)} %collective-permute-done.15.refs_1_, bf16[2,2,16,128]{3,2,1,0:T(8,128)(2,1)S(1)} %collective-permute-done.16.refs_2_, ...), custom_call_target="tpu_custom_call" | custom-call | tf_op jit(solution)/shard_map/adam/pallas_call | solution.py:262
  (3 shorter events, 0.1 us)
Async XLA Ops:
  0.6 0.9 %copy-start = (f32[16,2,8,128]{3,2,1,0:T(8,128)S(1)}, f32[16,2,8,128]{3,2,1,0:T(8,128)}, u32[]{:S(2)}) copy-start(f32[16,2,8,128]{3,2,1,0:T(8,128)} %refs_4_.1) | copy-start | bytes 393220
  1.7 6.8 %collective-permute-start = (bf16[2,2,16,128]{3,2,1,0:T(8,128)(2,1)S(1)}, bf16[2,2,16,128]{3,2,1,0:T(8,128)(2,1)S(1)}, u32[]{:S(2)}, u32[]{:S(2)}) collective-permute-start(bf16[2,2,16,128]{3,2,1,0:T(8,128)(2,1)S(1)} %get-tuple-element.17), channel_id=1, source_target_pairs={{0,3},{1,2},{2,1},{3,0},{4,7},{5,6},{6,5},{7,4},{8,11},{9,10},{10,... | collective-permute-start | bytes 49160 | tf_op jit(solution)/shard_map/ppermute | solution.py:272
  6.8 4.6 %collective-permute-start.1 = (bf16[2,2,16,128]{3,2,1,0:T(8,128)(2,1)S(1)}, bf16[2,2,16,128]{3,2,1,0:T(8,128)(2,1)S(1)}, u32[]{:S(2)}, u32[]{:S(2)}) collective-permute-start(bf16[2,2,16,128]{3,2,1,0:T(8,128)(2,1)S(1)} %get-tuple-element.18), channel_id=1, source_target_pairs={{0,2},{1,3},{2,0},{3,1},{4,6},{5,7},{6,4},{7,5},{8,10},{9,11},{10,... | collective-permute-start | bytes 49160 | tf_op jit(solution)/shard_map/ppermute | solution.py:272
  6.8 4.6 %collective-permute-start.2 = (bf16[2,2,16,128]{3,2,1,0:T(8,128)(2,1)S(1)}, bf16[2,2,16,128]{3,2,1,0:T(8,128)(2,1)S(1)}, u32[]{:S(2)}, u32[]{:S(2)}) collective-permute-start(bf16[2,2,16,128]{3,2,1,0:T(8,128)(2,1)S(1)} %get-tuple-element.19), channel_id=1, source_target_pairs={{0,1},{1,0},{2,3},{3,2},{4,5},{5,4},{6,7},{7,6},{8,9},{9,8},{10,11... | collective-permute-start | bytes 49160 | tf_op jit(solution)/shard_map/ppermute | solution.py:272
  11.5 5.8 %collective-permute-start.3 = (bf16[4,2,2,16,128]{4,3,2,1,0:T(8,128)(2,1)S(1)}, bf16[4,2,2,16,128]{4,3,2,1,0:T(8,128)(2,1)S(1)}, u32[]{:S(2)}, u32[]{:S(2)}) collective-permute-start(bf16[4,2,2,16,128]{4,3,2,1,0:T(8,128)(2,1)S(1)} %pad_maximum_fusion.refs_3_), channel_id=1, source_target_pairs={{0,24},{4,28},{8,16},{12,20},{16,8},{20,12},{24,0},{28,4},{1,25},{... | collective-permute-start | bytes 196616 | tf_op jit(solution)/shard_map/ppermute | solution.py:272
  14.0 4.3 %collective-permute-start.4 = (bf16[4,2,2,16,128]{4,3,2,1,0:T(8,128)(2,1)S(1)}, bf16[4,2,2,16,128]{4,3,2,1,0:T(8,128)(2,1)S(1)}, u32[]{:S(2)}, u32[]{:S(2)}) collective-permute-start(bf16[4,2,2,16,128]{4,3,2,1,0:T(8,128)(2,1)S(1)} %pad_maximum_fusion.refs_3_), channel_id=1, source_target_pairs={{0,16},{4,20},{8,24},{12,28},{16,0},{20,4},{24,8},{28,12},{1,17},{... | collective-permute-start | bytes 196616 | tf_op jit(solution)/shard_map/ppermute | solution.py:272
  14.5 4.3 %collective-permute-start.5 = (bf16[4,2,2,16,128]{4,3,2,1,0:T(8,128)(2,1)S(1)}, bf16[4,2,2,16,128]{4,3,2,1,0:T(8,128)(2,1)S(1)}, u32[]{:S(2)}, u32[]{:S(2)}) collective-permute-start(bf16[4,2,2,16,128]{4,3,2,1,0:T(8,128)(2,1)S(1)} %pad_maximum_fusion.refs_3_), channel_id=1, source_target_pairs={{0,8},{4,12},{8,0},{12,4},{16,24},{20,28},{24,16},{28,20},{1,9},{5... | collective-permute-start | bytes 196616 | tf_op jit(solution)/shard_map/ppermute | solution.py:272
  17.1 3.0 %collective-permute-start.9 = (bf16[4,2,2,16,128]{4,3,2,1,0:T(8,128)(2,1)S(1)}, bf16[4,2,2,16,128]{4,3,2,1,0:T(8,128)(2,1)S(1)}, u32[]{:S(2)}, u32[]{:S(2)}) collective-permute-start(bf16[4,2,2,16,128]{4,3,2,1,0:T(8,128)(2,1)S(1)} %pad_maximum_fusion.refs_3_), channel_id=1, source_target_pairs={{0,4},{4,0},{8,12},{12,8},{16,20},{20,16},{24,28},{28,24},{1,5},{5... | collective-permute-start | bytes 196616 | tf_op jit(solution)/shard_map/ppermute | solution.py:272
  17.3 2.8 %collective-permute-start.6 = (bf16[4,2,2,16,128]{4,3,2,1,0:T(8,128)(2,1)S(1)}, bf16[4,2,2,16,128]{4,3,2,1,0:T(8,128)(2,1)S(1)}, u32[]{:S(2)}, u32[]{:S(2)}) collective-permute-start(bf16[4,2,2,16,128]{4,3,2,1,0:T(8,128)(2,1)S(1)} %collective-permute-done.3.refs_0_), channel_id=1, source_target_pairs={{0,4},{4,0},{8,12},{12,8},{16,20},{20,16},{24,28},{28,24},{1,5},{5... | collective-permute-start | bytes 196616 | tf_op jit(solution)/shard_map/ppermute | solution.py:272
  18.2 1.9 %collective-permute-start.7 = (bf16[4,2,2,16,128]{4,3,2,1,0:T(8,128)(2,1)S(1)}, bf16[4,2,2,16,128]{4,3,2,1,0:T(8,128)(2,1)S(1)}, u32[]{:S(2)}, u32[]{:S(2)}) collective-permute-start(bf16[4,2,2,16,128]{4,3,2,1,0:T(8,128)(2,1)S(1)} %collective-permute-done.4.refs_1_), channel_id=1, source_target_pairs={{0,4},{4,0},{8,12},{12,8},{16,20},{20,16},{24,28},{28,24},{1,5},{5... | collective-permute-start | bytes 196616 | tf_op jit(solution)/shard_map/ppermute | solution.py:272
  18.7 1.4 %collective-permute-start.8 = (bf16[4,2,2,16,128]{4,3,2,1,0:T(8,128)(2,1)S(1)}, bf16[4,2,2,16,128]{4,3,2,1,0:T(8,128)(2,1)S(1)}, u32[]{:S(2)}, u32[]{:S(2)}) collective-permute-start(bf16[4,2,2,16,128]{4,3,2,1,0:T(8,128)(2,1)S(1)} %collective-permute-done.5.refs_2_), channel_id=1, source_target_pairs={{0,4},{4,0},{8,12},{12,8},{16,20},{20,16},{24,28},{28,24},{1,5},{5... | collective-permute-start | bytes 196616 | tf_op jit(solution)/shard_map/ppermute | solution.py:272
  20.1 22.8 %copy-start.1 = (f32[16,2,8,128]{3,2,1,0:T(8,128)S(1)}, f32[16,2,8,128]{3,2,1,0:T(8,128)}, u32[]{:S(2)}) copy-start(f32[16,2,8,128]{3,2,1,0:T(8,128)} %refs_4_.1) | copy-start | bytes 393220
  20.2 22.8 %copy-start.2 = (f32[16,2,8,128]{3,2,1,0:T(8,128)S(1)}, f32[16,2,8,128]{3,2,1,0:T(8,128)}, u32[]{:S(2)}) copy-start(f32[16,2,8,128]{3,2,1,0:T(8,128)} %refs_5_.1) | copy-start | bytes 393220
  20.2 22.8 %copy-start.3 = (f32[16,2,8,128]{3,2,1,0:T(8,128)S(1)}, f32[16,2,8,128]{3,2,1,0:T(8,128)}, u32[]{:S(2)}) copy-start(f32[16,2,8,128]{3,2,1,0:T(8,128)} %refs_6_.1) | copy-start | bytes 393220
  28.0 1.7 %collective-permute-start.10 = (bf16[4,4,2,2,16,128]{5,4,3,2,1,0:T(8,128)(2,1)S(1)}, bf16[4,4,2,2,16,128]{5,4,3,2,1,0:T(8,128)(2,1)S(1)}, u32[]{:S(2)}, u32[]{:S(2)}) collective-permute-start(bf16[4,4,2,2,16,128]{5,4,3,2,1,0:T(8,128)(2,1)S(1)} %get-tuple-element.22), channel_id=1, source_target_pairs={{0,4},{4,0},{8,12},{12,8},{16,20},{20,16},{24,28},{28,24},{1,5},{5... | collective-permute-start | bytes 786440 | tf_op jit(solution)/shard_map/ppermute | solution.py:272
  29.8 5.4 %collective-permute-start.11 = (bf16[4,2,2,16,128]{4,3,2,1,0:T(8,128)(2,1)S(1)}, bf16[4,2,2,16,128]{4,3,2,1,0:T(8,128)(2,1)S(1)}, u32[]{:S(2)}, u32[]{:S(2)}) collective-permute-start(bf16[4,2,2,16,128]{4,3,2,1,0:T(8,128)(2,1)S(1)} %get-tuple-element.24), channel_id=1, source_target_pairs={{0,24},{4,28},{8,16},{12,20},{16,8},{20,12},{24,0},{28,4},{1,25},{... | collective-permute-start | bytes 196616 | tf_op jit(solution)/shard_map/ppermute | solution.py:272
  31.7 4.9 %collective-permute-start.12 = (bf16[4,2,2,16,128]{4,3,2,1,0:T(8,128)(2,1)S(1)}, bf16[4,2,2,16,128]{4,3,2,1,0:T(8,128)(2,1)S(1)}, u32[]{:S(2)}, u32[]{:S(2)}) collective-permute-start(bf16[4,2,2,16,128]{4,3,2,1,0:T(8,128)(2,1)S(1)} %get-tuple-element.25), channel_id=1, source_target_pairs={{0,16},{4,20},{8,24},{12,28},{16,0},{20,4},{24,8},{28,12},{1,17},{... | collective-permute-start | bytes 196616 | tf_op jit(solution)/shard_map/ppermute | solution.py:272
  32.2 4.4 %collective-permute-start.13 = (bf16[4,2,2,16,128]{4,3,2,1,0:T(8,128)(2,1)S(1)}, bf16[4,2,2,16,128]{4,3,2,1,0:T(8,128)(2,1)S(1)}, u32[]{:S(2)}, u32[]{:S(2)}) collective-permute-start(bf16[4,2,2,16,128]{4,3,2,1,0:T(8,128)(2,1)S(1)} %get-tuple-element.26), channel_id=1, source_target_pairs={{0,8},{4,12},{8,0},{12,4},{16,24},{20,28},{24,16},{28,20},{1,9},{5... | collective-permute-start | bytes 196616 | tf_op jit(solution)/shard_map/ppermute | solution.py:272
  36.6 5.6 %collective-permute-start.14 = (bf16[2,2,16,128]{3,2,1,0:T(8,128)(2,1)S(1)}, bf16[2,2,16,128]{3,2,1,0:T(8,128)(2,1)S(1)}, u32[]{:S(2)}, u32[]{:S(2)}) collective-permute-start(bf16[2,2,16,128]{3,2,1,0:T(8,128)(2,1)S(1)} %get-tuple-element.27), channel_id=1, source_target_pairs={{0,3},{1,2},{2,1},{3,0},{4,7},{5,6},{6,5},{7,4},{8,11},{9,10},{10,... | collective-permute-start | bytes 49160 | tf_op jit(solution)/shard_map/ppermute | solution.py:272
  38.2 4.7 %collective-permute-start.15 = (bf16[2,2,16,128]{3,2,1,0:T(8,128)(2,1)S(1)}, bf16[2,2,16,128]{3,2,1,0:T(8,128)(2,1)S(1)}, u32[]{:S(2)}, u32[]{:S(2)}) collective-permute-start(bf16[2,2,16,128]{3,2,1,0:T(8,128)(2,1)S(1)} %get-tuple-element.28), channel_id=1, source_target_pairs={{0,2},{1,3},{2,0},{3,1},{4,6},{5,7},{6,4},{7,5},{8,10},{9,11},{10,... | collective-permute-start | bytes 49160 | tf_op jit(solution)/shard_map/ppermute | solution.py:272
  38.8 4.2 %collective-permute-start.16 = (bf16[2,2,16,128]{3,2,1,0:T(8,128)(2,1)S(1)}, bf16[2,2,16,128]{3,2,1,0:T(8,128)(2,1)S(1)}, u32[]{:S(2)}, u32[]{:S(2)}) collective-permute-start(bf16[2,2,16,128]{3,2,1,0:T(8,128)(2,1)S(1)} %get-tuple-element.29), channel_id=1, source_target_pairs={{0,1},{1,0},{2,3},{3,2},{4,5},{5,4},{6,7},{7,6},{8,9},{9,8},{10,11... | collective-permute-start | bytes 49160 | tf_op jit(solution)/shard_map/ppermute | solution.py:272

commit v5 on v4

--- a/solution.py
+++ b/solution.py
@@ -24,28 +24,28 @@
     return list(range(size - 1, -1, -1))
 
 
-def pack_kernel(columns, cache_ref, *refs):
-    *outs, by_group = refs
+def pack_kernel(columns, cache_ref, keep_ref, send_ref, by_group):
     groups = cache_ref.shape[2]
-    own = outs[0].shape[1]
+    own = keep_ref.shape[3]
     repeat = own * columns // groups
     for side in range(2):
         for group in range(groups):
             by_group[group, side] = cache_ref[:, side, group].astype(jnp.bfloat16)
     column = lax.axis_index("cache")
-    for out, flip in zip(outs, flips(columns)):
+    for flip in range(columns):
         first = (column ^ flip) // repeat * own
+        out_ref = send_ref if flip % 2 else keep_ref
         for slot in range(own):
             for side in range(2):
-                out[side, slot] = by_group[first + slot, side]
+                out_ref[flip // 2, 0, side, slot] = by_group[first + slot, side]
 
 
 def pack(cache, columns, own):
     share, _, groups, width = cache.shape
-    slice_shape = jax.ShapeDtypeStruct((2, own, share, width), jnp.bfloat16)
+    half = jax.ShapeDtypeStruct((columns // 2, 1, 2, own, share, width), jnp.bfloat16)
     return pl.pallas_call(
         functools.partial(pack_kernel, columns),
-        out_shape=[slice_shape] * columns,
+        out_shape=(half, half),
         scratch_shapes=[pltpu.VMEM((groups, 2, share, width), jnp.bfloat16)],
         compiler_params=pltpu.CompilerParams(vmem_limit_bytes=16 * MIB),
         name="pack",
@@ -54,12 +54,13 @@
 
 def attend_kernel(score_scale, per_group, pieces, *refs):
     pair_refs, refs = refs[:pieces], refs[pieces:]
-    queries_ref, grads_ref, lse_ref, dot_ref, mine_ref, mate_ref = refs[:6]
-    keys, values, key_total, value_total = refs[6:10]
-    even, odd = refs[10:14], refs[14:18]
+    queries_ref, grads_ref, lse_ref, dot_ref, mate_ref, weights_ref, dscores_ref = refs[:7]
+    keys, values, key_total, value_total = refs[7:11]
+    even, odd = refs[11:15], refs[15:19]
     columns, _, own, share, width = pair_refs[0].shape
     length = columns * share
     positions = pieces * length
+    half = positions // 2
     tiles = queries_ref.shape[0]
     log2e = math.log2(math.e)
     factor = score_scale * log2e
@@ -103,10 +104,16 @@
         side = jnp.exp2(side_lse - peak)
         inverse = 1.0 / (jnp.sum(total, axis=0, keepdims=True) + side)
         delta = (jnp.sum(dotted, axis=0, keepdims=True) + side * dot_ref[tile]) * inverse
-        for cut in cuts:
+        for start, cut in zip(range(0, positions, CHUNK), cuts):
             probability = scores[cut] * inverse
-            weights[cut] = probability.astype(jnp.bfloat16)
-            dscores[cut] = (probability * (slopes[cut] - delta)).astype(jnp.bfloat16)
+            weight = probability.astype(jnp.bfloat16)
+            dscore = (probability * (slopes[cut] - delta)).astype(jnp.bfloat16)
+            if start < half:
+                weights_ref[tile, cut] = weight
+                dscores_ref[tile, cut] = dscore
+            else:
+                weights[pl.ds(start - half, CHUNK)] = weight
+                dscores[pl.ds(start - half, CHUNK)] = dscore
 
     def accumulate(tile, buffers):
         _, _, weights, dscores = buffers
@@ -137,52 +144,90 @@
     accumulate(tiles - 2, even)
     accumulate(tiles - 1, odd)
 
-    half = positions // 2
-    shape = mine_ref.shape[:2] + (share, width)
+    shape = mate_ref.shape[:2] + (share, width)
     for slot in range(own):
         key_sum = key_total[slot] * score_scale
-        value_sum = value_total[slot]
-        mine_ref[:, :, 0, slot] = key_sum[:half].reshape(shape)
-        mine_ref[:, :, 1, slot] = value_sum[:half].reshape(shape)
-        mate_ref[:, :, 0, slot] = key_sum[half:].astype(jnp.bfloat16).reshape(shape)
-        mate_ref[:, :, 1, slot] = value_sum[half:].astype(jnp.bfloat16).reshape(shape)
+        mate_ref[:, :, 0, slot] = key_sum.astype(jnp.bfloat16).reshape(shape)
+        mate_ref[:, :, 1, slot] = value_total[slot].astype(jnp.bfloat16).reshape(shape)
 
 
 def attend(pairs, queries, grads, lse_rows, dot_rows, score_scale):
     columns, _, own, share, width = pairs[0].shape
     pieces = len(pairs)
     positions = pieces * columns * share
+    half = positions // 2
     tiles, row_tile, _ = queries.shape
     rows = tiles * row_tile
-    half = (pieces // 2, columns, 2, own, share, width)
     buffers = [
         pltpu.VMEM((positions, row_tile), jnp.float32),
         pltpu.VMEM((positions, row_tile), jnp.float32),
-        pltpu.VMEM((positions, row_tile), jnp.bfloat16),
-        pltpu.VMEM((positions, row_tile), jnp.bfloat16),
+        pltpu.VMEM((half, row_tile), jnp.bfloat16),
+        pltpu.VMEM((half, row_tile), jnp.bfloat16),
     ]
+    kept = jax.ShapeDtypeStruct((tiles, half, row_tile), jnp.bfloat16)
     return pl.pallas_call(
         functools.partial(attend_kernel, score_scale, tiles // own, pieces),
         out_shape=(
-            jax.ShapeDtypeStruct(half, jnp.float32),
-            jax.ShapeDtypeStruct(half, jnp.bfloat16),
+            jax.ShapeDtypeStruct((pieces // 2,) + pairs[0].shape, jnp.bfloat16),
+            kept,
+            kept,
         ),
         scratch_shapes=[
             pltpu.VMEM((own, positions, width), jnp.bfloat16),
             pltpu.VMEM((own, positions, width), jnp.bfloat16),
-            pltpu.VMEM((own, positions, width), jnp.float32),
-            pltpu.VMEM((own, positions, width), jnp.float32),
+            pltpu.VMEM((own, half, width), jnp.float32),
+            pltpu.VMEM((own, half, width), jnp.float32),
         ]
         + buffers
         + buffers,
-        compiler_params=pltpu.CompilerParams(vmem_limit_bytes=44 * MIB),
+        compiler_params=pltpu.CompilerParams(vmem_limit_bytes=40 * MIB),
         cost_estimate=pl.CostEstimate(
-            flops=8 * rows * positions * width,
+            flops=6 * rows * positions * width,
             bytes_accessed=4 * rows * width + 8 * own * positions * width,
             transcendentals=rows * positions,
         ),
         name="attend",
     )(*pairs, queries, grads, lse_rows, dot_rows)
+
+
+def own_half_kernel(
+    score_scale, per_group, weights_ref, dscores_ref, queries_ref, grads_ref, out_ref
+):
+    tiles = queries_ref.shape[0]
+    chips, columns, _, own, share, width = out_ref.shape
+    along = (((1,), (0,)), ((), ()))
+    for slot in range(own):
+        key_sum = None
+        value_sum = None
+        for tile in range(slot * per_group, (slot + 1) * per_group):
+            key_part = lax.dot_general(
+                dscores_ref[tile], queries_ref[tile], along, preferred_element_type=jnp.float32
+            )
+            value_part = lax.dot_general(
+                weights_ref[tile], grads_ref[tile], along, preferred_element_type=jnp.float32
+            )
+            key_sum = key_part if key_sum is None else key_sum + key_part
+            value_sum = value_part if value_sum is None else value_sum + value_part
+        shape = (chips, columns, share, width)
+        out_ref[:, :, 0, slot] = (key_sum * score_scale).reshape(shape)
+        out_ref[:, :, 1, slot] = value_sum.reshape(shape)
+
+
+def own_half(weights, dscores, queries, grads, shape, score_scale):
+    tiles, half, row_tile = weights.shape
+    width = shape[-1]
+    own = shape[3]
+    return pl.pallas_call(
+        functools.partial(own_half_kernel, score_scale, tiles // own),
+        out_shape=jax.ShapeDtypeStruct(shape, jnp.float32),
+        compiler_params=pltpu.CompilerParams(vmem_limit_bytes=24 * MIB),
+        cost_estimate=pl.CostEstimate(
+            flops=4 * tiles * row_tile * half * width,
+            bytes_accessed=4 * tiles * row_tile * (half + width),
+            transcendentals=0,
+        ),
+        name="own_half",
+    )(weights, dscores, queries, grads)
 
 
 def chip_sum_kernel(mine_ref, mate_ref, *outs):
@@ -205,36 +250,37 @@
 
 
 def column_sum_kernel(away, mine_ref, *refs):
-    others, outs = refs[:away], refs[away:]
-    for offset, out in enumerate(outs):
-        total = mine_ref[offset]
+    others, (keep_ref, send_ref) = refs[:away], refs[away:]
+    for flip in range(mine_ref.shape[0]):
+        total = mine_ref[flip]
         for other in others:
-            total = total + other[offset].astype(jnp.float32)
-        out[...] = total.astype(out.dtype)
+            total = total + other[flip].astype(jnp.float32)
+        out_ref = send_ref if flip % 2 else keep_ref
+        out_ref[flip // 2, 0] = total.astype(jnp.bfloat16)
 
 
 def column_sum(mine, others):
     columns = mine.shape[0]
-    shape = mine.shape[1:]
+    half = jax.ShapeDtypeStruct((columns // 2, 1) + mine.shape[1:], jnp.bfloat16)
     return pl.pallas_call(
         functools.partial(column_sum_kernel, len(others)),
-        out_shape=[
-            jax.ShapeDtypeStruct(shape, jnp.bfloat16 if flip else jnp.float32)
-            for flip in flips(columns)
-        ],
+        out_shape=(half, half),
         compiler_params=pltpu.CompilerParams(vmem_limit_bytes=16 * MIB),
         name="column_sum",
     )(mine, *others)
 
 
-def adam_kernel(columns, *refs):
-    parts, refs = refs[:columns], refs[columns:]
+def adam_kernel(columns, pieces, *refs):
+    parts, refs = refs[:pieces], refs[pieces:]
     cache_ref, first_ref, second_ref, new_cache, new_first, new_second, by_flip = refs
     groups = cache_ref.shape[2]
-    own = parts[0].shape[1]
+    own = by_flip.shape[2]
     repeat = own * columns // groups
-    for part, flip in zip(parts, flips(columns)):
-        by_flip[flip] = part[...].astype(jnp.float32)
+    flip = 0
+    for part in parts:
+        sources = part.shape[1]
+        by_flip[flip : flip + sources] = part[0].astype(jnp.float32)
+        flip += sources
     column = lax.axis_index("cache")
     for side in range(2):
         for group in range(groups):
@@ -257,12 +303,12 @@
             new_second[:, side, group] = second
 
 
-def adam(parts, cache, first_moment, second_moment):
+def adam(parts, columns, cache, first_moment, second_moment):
     shape = jax.ShapeDtypeStruct(cache.shape, jnp.float32)
     return pl.pallas_call(
-        functools.partial(adam_kernel, len(parts)),
+        functools.partial(adam_kernel, columns, len(parts)),
         out_shape=(shape, shape, shape),
-        scratch_shapes=[pltpu.VMEM((len(parts),) + parts[0].shape, jnp.float32)],
+        scratch_shapes=[pltpu.VMEM((columns,) + parts[0].shape[2:], jnp.float32)],
         compiler_params=pltpu.CompilerParams(vmem_limit_bytes=16 * MIB),
         name="adam",
     )(*parts, cache, first_moment, second_moment)
@@ -277,6 +323,19 @@
         swap(value, axis, size, flip * stride) if flip else value
         for value, flip in zip(values, flips(len(values)))
     ]
+
+
+def column_exchange(keep, send, columns):
+    arrived = swap(send, "cache", columns, 1)
+    bit = 2
+    pieces = [keep, arrived]
+    while bit < columns:
+        evens = [piece[0::2] for piece in pieces]
+        odds = [piece[1::2] for piece in pieces]
+        arrived = swap(jnp.concatenate(odds, axis=1), "cache", columns, bit)
+        pieces = evens + [arrived]
+        bit *= 2
+    return pieces
 
 
 def per_device(
@@ -294,8 +353,8 @@
     first_group = column // repeat * own
     first_token = column % repeat * own_tokens
 
-    slices = pack(cache, columns, own)
-    gathered = jnp.stack(swap_all(slices, "cache", columns, 1))
+    pieces = column_exchange(*pack(cache, columns, own), columns)
+    gathered = jnp.concatenate([piece[0] for piece in pieces])
     pairs = swap_all([gathered] * chips, "dp", dp_size, 2)
     pairs = pairs + [swap(pair, "dp", dp_size, 1) for pair in pairs]
 
@@ -305,19 +364,20 @@
         part = lax.dynamic_slice_in_dim(part, first_group, own, 1)
         return jnp.moveaxis(part, 1, 0).reshape((-1, ROW_TILE) + array.shape[2:])
 
-    mine, mate = attend(
+    query_tiles, grad_tiles = tiles_of(queries), tiles_of(out_grad)
+    mate, weights, dscores = attend(
         pairs,
-        tiles_of(queries),
-        tiles_of(out_grad),
+        query_tiles,
+        grad_tiles,
         tiles_of(self_lse)[:, None],
         tiles_of(self_dot)[:, None],
         score_scale,
     )
-    by_chip = chip_sum(mine, swap(mate, "dp", dp_size, 1))
-    *away, home = swap_all(by_chip, "dp", dp_size, 2)
-    by_column = column_sum(home, away)
-    parts = swap_all(by_column, "cache", columns, 1)
-    return adam(parts, cache, first_moment, second_moment)
+    from_mate = swap(mate, "dp", dp_size, 1)
+    mine = own_half(weights, dscores, query_tiles, grad_tiles, mate.shape, score_scale)
+    *away, home = swap_all(chip_sum(mine, from_mate), "dp", dp_size, 2)
+    parts = column_exchange(*column_sum(home, away), columns)
+    return adam(parts, columns, cache, first_moment, second_moment)
 
 
 def solution(mesh):

time: 44.6 us -> 48.3 us (1.083)
  waiting for transfers between devices: 11.4 us -> 13.6 us
  Pallas kernels: 9.32 us -> 10.4 us
    ppermute x17 -> x15, waiting for transfers between devices: 11.4 us -> 13.6 us  [swap(): lax.ppermute(value, axis, [(place, place ^ flip) for place in range(size)])]
    pallas_call x2 -> x3, Pallas kernels: 1.41 us -> 2.65 us  [the longest x1 1.27 us: adam(): pl.pallas_call(functools.partial(adam_kernel, columns, len(parts)), out_s...]
    ppermute x17 -> x15, starting transfers between devices: 18.4 us -> 18.8 us  [swap(): lax.ppermute(value, axis, [(place, place ^ flip) for place in range(size)])]
  transfers between devices with their start and end apart: 17 -> 15, of which waited for: 12 -> 9; matrix products, arithmetic and copies ran while one was open for 8% -> 7% of each run, Pallas kernels for 0% -> 3%
where the time goes in v5:
time: 48.3 us; the launch traced here: 47.9 us
  starting transfers between devices  18.8 us (39%)
  waiting for transfers between devices  13.6 us (28%)
  Pallas kernels  10.4 us (22%)
  local copies, waits for them, and re-layouts  4.35 us (9%)
  between operations  0.82 us (2%)
    ppermute x15, starting transfers between devices, swap(): lax.ppermute(value, axis, [(place, place ^ flip) for place in range(size)])  18.8 us
    ppermute x15, waiting for transfers between devices, swap(): lax.ppermute(value, axis, [(place, place ^ flip) for place in range(size)])  13.6 us
    pallas_call x1, Pallas kernels, attend(): pl.pallas_call(functools.partial(attend_kernel, score_scale, tiles // own...  7.66 us
    dynamic_slice x2, local copies, waits for them, and re-layouts, tiles_of(): part = lax.dynamic_slice_in_dim(part, first_group, own, 1)  2.69 us
    unnamed x12, local copies, waits for them, and re-layouts  1.3 us
    pallas_call x1, Pallas kernels, adam(): pl.pallas_call(functools.partial(adam_kernel, columns, len(parts)), out_s...  1.27 us
    pallas_call x1, Pallas kernels, own_half(): pl.pallas_call(functools.partial(own_half_kernel, score_scale, tiles // o...  1.24 us
  transfers between devices with their start and end apart: 15, of which 9 were waited for; matrix products, arithmetic and copies ran while one was open for 7% of the time, Pallas kernels for 3%

profile of v5, /device:TPU:0, one launch (start us, length us, event | category | flops | bytes accessed | tf_op | source)
XLA Modules:
  0.0 47.9 jit_solution(5108727403342275212)
XLA Ops:
  0.6 0.0 copy-start
  0.6 0.9 %copy-done = f32[16,2,8,128]{3,2,1,0:T(8,128)S(1)} copy-done((f32[16,2,8,128]{3,2,1,0:T(8,128)S(1)}, f32[16,2,8,128]{3,2,1,0:T(8,128)}, u32[]{:S(2)}) %copy-start) | copy-done | bytes 131096
  1.5 0.1 pack.1
  1.7 3.1 %collective-permute-start = (bf16[2,1,2,2,16,128]{5,4,3,2,1,0:T(8,128)(2,1)S(1)}, bf16[2,1,2,2,16,128]{5,4,3,2,1,0:T(8,128)(2,1)S(1)}, u32[]{:S(2)}, u32[]{:S(2)}) collective-permute-start(bf16[2,1,2,2,16,128]{5,4,3,2,1,0:T(8,128)(2,1)S(1)} %get-tuple-element.15), channel_id=1, source_target_pairs={{0,1},{1,0},{2,3},{3,2},{4,5},{5,4},{6,7},{7,6},{8,9},{9,8},{10,11... | collective-permute-start | bytes 98312 | tf_op jit(solution)/shard_map/ppermute | solution.py:318
  4.8 1.9 %collective-permute-done = bf16[2,1,2,2,16,128]{5,4,3,2,1,0:T(8,128)(2,1)S(1)} collective-permute-done((bf16[2,1,2,2,16,128]{5,4,3,2,1,0:T(8,128)(2,1)S(1)}, bf16[2,1,2,2,16,128]{5,4,3,2,1,0:T(8,128)(2,1)S(1)}, u32[]{:S(2)}, u32[]{:S(2)}) %collective-permute-start) | collective-permute-done | bytes 32800 | tf_op jit(solution)/shard_map/ppermute | solution.py:318
  6.7 3.1 %collective-permute-start.1 = (bf16[1,2,2,2,16,128]{5,4,3,2,1,0:T(8,128)(2,1)S(1)}, bf16[1,2,2,2,16,128]{5,4,3,2,1,0:T(8,128)(2,1)S(1)}, u32[]{:S(2)}, u32[]{:S(2)}) collective-permute-start(bf16[1,2,2,2,16,128]{5,4,3,2,1,0:T(8,128)(2,1)S(1)} %pad_maximum_fusion.1), channel_id=1, source_target_pairs={{0,2},{1,3},{2,0},{3,1},{4,6},{5,7},{6,4},{7,5},{8,10},{9,11},{10,... | collective-permute-start | bytes 98312 | tf_op jit(solution)/shard_map/ppermute | solution.py:318
  9.8 1.9 %collective-permute-done.1 = bf16[1,2,2,2,16,128]{5,4,3,2,1,0:T(8,128)(2,1)S(1)} collective-permute-done((bf16[1,2,2,2,16,128]{5,4,3,2,1,0:T(8,128)(2,1)S(1)}, bf16[1,2,2,2,16,128]{5,4,3,2,1,0:T(8,128)(2,1)S(1)}, u32[]{:S(2)}, u32[]{:S(2)}) %collective-permute-start.1) | collective-permute-done | bytes 32800 | tf_op jit(solution)/shard_map/ppermute | solution.py:318
  11.7 1.9 %collective-permute-start.4 = (bf16[4,2,2,16,128]{4,3,2,1,0:T(8,128)(2,1)S(1)}, bf16[4,2,2,16,128]{4,3,2,1,0:T(8,128)(2,1)S(1)}, u32[]{:S(2)}, u32[]{:S(2)}) collective-permute-start(bf16[4,2,2,16,128]{4,3,2,1,0:T(8,128)(2,1)S(1)} %pad_maximum_fusion.refs_3_), channel_id=1, source_target_pairs={{0,8},{4,12},{8,0},{12,4},{16,24},{20,28},{24,16},{28,20},{1,9},{5... | collective-permute-start | bytes 196616 | tf_op jit(solution)/shard_map/ppermute | solution.py:318
  13.6 1.5 %collective-permute-start.3 = (bf16[4,2,2,16,128]{4,3,2,1,0:T(8,128)(2,1)S(1)}, bf16[4,2,2,16,128]{4,3,2,1,0:T(8,128)(2,1)S(1)}, u32[]{:S(2)}, u32[]{:S(2)}) collective-permute-start(bf16[4,2,2,16,128]{4,3,2,1,0:T(8,128)(2,1)S(1)} %pad_maximum_fusion.refs_3_), channel_id=1, source_target_pairs={{0,16},{4,20},{8,24},{12,28},{16,0},{20,4},{24,8},{28,12},{1,17},{... | collective-permute-start | bytes 196616 | tf_op jit(solution)/shard_map/ppermute | solution.py:318
  15.1 0.1 collective-permute-start.2
  15.2 2.0 %constant_dynamic-slice_fusion.2 = (bf16[256,2,8,128]{3,2,1,0:T(8,128)(2,1)S(1)}, bf16[256,2,8,128]{3,2,1,0:T(8,128)(2,1)S(1)}) fusion(bf16[256,8,8,128]{3,2,1,0:T(8,128)(2,1)} %bitcast.23, s32[]{:T(128)S(6)} %select_n.9, bf16[256,8,8,128]{3,2,1,0:T(8,128)(2,1)} %bitcast.24), kind=kLoop, calls=%fused_computation.7 | loop fusion | bytes 4194308 | tf_op jit(solution)/shard_map/dynamic_slice | solution.py:364
  17.2 0.1 collective-permute-start.8
  17.3 0.0 collective-permute-done.4.refs_2_
  17.3 0.5 %collective-permute-start.7 = (bf16[4,2,2,16,128]{4,3,2,1,0:T(8,128)(2,1)S(1)}, bf16[4,2,2,16,128]{4,3,2,1,0:T(8,128)(2,1)S(1)}, u32[]{:S(2)}, u32[]{:S(2)}) collective-permute-start(bf16[4,2,2,16,128]{4,3,2,1,0:T(8,128)(2,1)S(1)} %collective-permute-done.4.refs_2_), channel_id=1, source_target_pairs={{0,4},{4,0},{8,12},{12,8},{16,20},{20,16},{24,28},{28,24},{1,5},{5... | collective-permute-start | bytes 196616 | tf_op jit(solution)/shard_map/ppermute | solution.py:318
  17.8 0.1 collective-permute-done.3.refs_1_
  17.8 0.0 collective-permute-start.6
  17.9 2.4 %collective-permute-done.2.refs_0_ = bf16[4,2,2,16,128]{4,3,2,1,0:T(8,128)(2,1)S(1)} collective-permute-done((bf16[4,2,2,16,128]{4,3,2,1,0:T(8,128)(2,1)S(1)}, bf16[4,2,2,16,128]{4,3,2,1,0:T(8,128)(2,1)S(1)}, u32[]{:S(2)}, u32[]{:S(2)}) %collective-permute-start.2) | collective-permute-done | bytes 65568 | tf_op jit(solution)/shard_map/ppermute | solution.py:318
  20.3 0.0 collective-permute-start.5
  20.3 0.7 %constant_dynamic-slice_fusion = (f32[256,2,8]{0,2,1:T(8,128)S(1)}, f32[256,2,8]{0,2,1:T(8,128)S(1)}) fusion(f32[256,8,8]{0,2,1:T(8,128)} %bitcast.26, s32[]{:T(128)S(6)} %select_n.9, f32[256,8,8]{0,2,1:T(8,128)} %bitcast.27), kind=kLoop, calls=%fused_computation.5 | loop fusion | bytes 65540 | tf_op jit(solution)/shard_map/dynamic_slice | solution.py:364
  21.0 0.1 copy.23
  21.1 0.2 broadcast_in_dim_reshape.9.refs_11_
  21.3 0.1 copy.22
  21.4 0.2 broadcast_in_dim_reshape.8.refs_10_
  21.6 0.1 copy.21
  21.7 0.1 copy.20
  21.8 0.0 collective-permute-done.8.refs_7_
  21.8 0.0 collective-permute-done.7.refs_6_
  21.8 0.0 collective-permute-done.6.refs_5_
  21.8 0.0 collective-permute-done.5.refs_4_
  21.8 7.7 %attend.1 = (bf16[4,4,2,2,16,128]{5,4,3,2,1,0:T(8,128)(2,1)S(1)}, bf16[8,256,512]{2,1,0:T(8,128)(2,1)S(1)}, bf16[8,256,512]{2,1,0:T(8,128)(2,1)S(1)}) custom-call(bf16[4,2,2,16,128]{4,3,2,1,0:T(8,128)(2,1)S(1)} %collective-permute-done.2.refs_0_, bf16[4,2,2,16,128]{4,3,2,1,0:T(8,128)(2,1)S(1)} %collective-permute-done.3.refs_1_, ...), custom_call_target="tpu_custom_call" | custom-call | flops 1610612736 | bytes 3145728 | tf_op jit(solution)/shard_map/attend/pallas_call | solution.py:168
  29.5 0.0 copy-start.1
  29.5 0.0 copy-start.2
  29.5 0.0 copy-start.3
  29.5 0.6 %collective-permute-start.9 = (bf16[4,4,2,2,16,128]{5,4,3,2,1,0:T(8,128)(2,1)S(1)}, bf16[4,4,2,2,16,128]{5,4,3,2,1,0:T(8,128)(2,1)S(1)}, u32[]{:S(2)}, u32[]{:S(2)}) collective-permute-start(bf16[4,4,2,2,16,128]{5,4,3,2,1,0:T(8,128)(2,1)S(1)} %get-tuple-element.18), channel_id=1, source_target_pairs={{0,4},{4,0},{8,12},{12,8},{16,20},{20,16},{24,28},{28,24},{1,5},{5... | collective-permute-start | bytes 786440 | tf_op jit(solution)/shard_map/ppermute | solution.py:318
  30.1 1.2 %own_half.1.mine_ref = f32[4,4,2,2,16,128]{5,4,3,2,1,0:T(8,128)S(1)} custom-call(bf16[8,256,512]{2,1,0:T(8,128)(2,1)S(1)} %get-tuple-element.16.weights_ref, bf16[8,256,512]{2,1,0:T(8,128)(2,1)S(1)} %get-tuple-element.17.dscores_ref, bf16[8,512,128]{2,1,0:T(8,128)(2,1)S(1)} %bitcast.20, bf16[8,512,128]{2,1,0:T(8,128)(2,1)S(1)} %bitcast.18), custom_call_target="tpu_custom_call" | custom-call | flops 536870912 | bytes 6291456 | tf_op jit(solution)/shard_map/own_half/pallas_call | solution.py:220
  31.3 0.0 collective-permute-done.9.mate_ref
  31.4 0.6 %collective-permute-start.10 = (bf16[4,2,2,16,128]{4,3,2,1,0:T(8,128)(2,1)S(1)}, bf16[4,2,2,16,128]{4,3,2,1,0:T(8,128)(2,1)S(1)}, u32[]{:S(2)}, u32[]{:S(2)}) collective-permute-start(bf16[4,2,2,16,128]{4,3,2,1,0:T(8,128)(2,1)S(1)} %get-tuple-element.20), channel_id=1, source_target_pairs={{0,24},{4,28},{8,16},{12,20},{16,8},{20,12},{24,0},{28,4},{1,25},{... | collective-permute-start | bytes 196616 | tf_op jit(solution)/shard_map/ppermute | solution.py:318
  32.0 1.4 %collective-permute-start.11 = (bf16[4,2,2,16,128]{4,3,2,1,0:T(8,128)(2,1)S(1)}, bf16[4,2,2,16,128]{4,3,2,1,0:T(8,128)(2,1)S(1)}, u32[]{:S(2)}, u32[]{:S(2)}) collective-permute-start(bf16[4,2,2,16,128]{4,3,2,1,0:T(8,128)(2,1)S(1)} %get-tuple-element.21), channel_id=1, source_target_pairs={{0,16},{4,20},{8,24},{12,28},{16,0},{20,4},{24,8},{28,12},{1,17},{... | collective-permute-start | bytes 196616 | tf_op jit(solution)/shard_map/ppermute | solution.py:318
  33.5 1.5 %collective-permute-start.12 = (bf16[4,2,2,16,128]{4,3,2,1,0:T(8,128)(2,1)S(1)}, bf16[4,2,2,16,128]{4,3,2,1,0:T(8,128)(2,1)S(1)}, u32[]{:S(2)}, u32[]{:S(2)}) collective-permute-start(bf16[4,2,2,16,128]{4,3,2,1,0:T(8,128)(2,1)S(1)} %get-tuple-element.22), channel_id=1, source_target_pairs={{0,8},{4,12},{8,0},{12,4},{16,24},{20,28},{24,16},{28,20},{1,9},{5... | collective-permute-start | bytes 196616 | tf_op jit(solution)/shard_map/ppermute | solution.py:318
  35.0 2.3 %collective-permute-done.10.refs_0_ = bf16[4,2,2,16,128]{4,3,2,1,0:T(8,128)(2,1)S(1)} collective-permute-done((bf16[4,2,2,16,128]{4,3,2,1,0:T(8,128)(2,1)S(1)}, bf16[4,2,2,16,128]{4,3,2,1,0:T(8,128)(2,1)S(1)}, u32[]{:S(2)}, u32[]{:S(2)}) %collective-permute-start.10) | collective-permute-done | bytes 65568 | tf_op jit(solution)/shard_map/ppermute | solution.py:318
  37.3 0.1 collective-permute-done.11.refs_1_
  37.4 0.3 collective-permute-done.12.refs_2_
  37.8 1.6 %collective-permute-start.13 = (bf16[2,1,2,2,16,128]{5,4,3,2,1,0:T(8,128)(2,1)S(1)}, bf16[2,1,2,2,16,128]{5,4,3,2,1,0:T(8,128)(2,1)S(1)}, u32[]{:S(2)}, u32[]{:S(2)}) collective-permute-start(bf16[2,1,2,2,16,128]{5,4,3,2,1,0:T(8,128)(2,1)S(1)} %get-tuple-element.24), channel_id=1, source_target_pairs={{0,1},{1,0},{2,3},{3,2},{4,5},{5,4},{6,7},{7,6},{8,9},{9,8},{10,11... | collective-permute-start | bytes 98312 | tf_op jit(solution)/shard_map/ppermute | solution.py:318
  39.4 2.3 %collective-permute-done.13 = bf16[2,1,2,2,16,128]{5,4,3,2,1,0:T(8,128)(2,1)S(1)} collective-permute-done((bf16[2,1,2,2,16,128]{5,4,3,2,1,0:T(8,128)(2,1)S(1)}, bf16[2,1,2,2,16,128]{5,4,3,2,1,0:T(8,128)(2,1)S(1)}, u32[]{:S(2)}, u32[]{:S(2)}) %collective-permute-start.13) | collective-permute-done | bytes 32800 | tf_op jit(solution)/shard_map/ppermute | solution.py:318
  41.8 2.7 %collective-permute-start.14 = (bf16[1,2,2,2,16,128]{5,4,3,2,1,0:T(8,128)(2,1)S(1)}, bf16[1,2,2,2,16,128]{5,4,3,2,1,0:T(8,128)(2,1)S(1)}, u32[]{:S(2)}, u32[]{:S(2)}) collective-permute-start(bf16[1,2,2,2,16,128]{5,4,3,2,1,0:T(8,128)(2,1)S(1)} %pad_maximum_fusion.2), channel_id=1, source_target_pairs={{0,2},{1,3},{2,0},{3,1},{4,6},{5,7},{6,4},{7,5},{8,10},{9,11},{10,... | collective-permute-start | bytes 98312 | tf_op jit(solution)/shard_map/ppermute | solution.py:318
  44.4 2.2 %collective-permute-done.14.refs_2_ = bf16[1,2,2,2,16,128]{5,4,3,2,1,0:T(8,128)(2,1)S(1)} collective-permute-done((bf16[1,2,2,2,16,128]{5,4,3,2,1,0:T(8,128)(2,1)S(1)}, bf16[1,2,2,2,16,128]{5,4,3,2,1,0:T(8,128)(2,1)S(1)}, u32[]{:S(2)}, u32[]{:S(2)}) %collective-permute-start.14) | collective-permute-done | bytes 32800 | tf_op jit(solution)/shard_map/ppermute | solution.py:318
  46.6 0.0 copy-done.1
  46.6 0.0 copy-done.2
  46.6 0.0 copy-done.3
  46.6 1.3 %adam.1 = (f32[16,2,8,128]{3,2,1,0:T(8,128)}, f32[16,2,8,128]{3,2,1,0:T(8,128)}, f32[16,2,8,128]{3,2,1,0:T(8,128)}) custom-call(bf16[1,1,2,2,16,128]{5,4,3,2,1,0:T(8,128)(2,1)S(1)} %get-tuple-element.26.refs_0_, bf16[1,1,2,2,16,128]{5,4,3,2,1,0:T(8,128)(2,1)S(1)} %get-tuple-element.28.refs_1_, ...), custom_call_target="tpu_custom_call" | custom-call | tf_op jit(solution)/shard_map/adam/pallas_call | solution.py:308
  (9 shorter events, 0.1 us)
Async XLA Ops:
  0.6 0.9 %copy-start = (f32[16,2,8,128]{3,2,1,0:T(8,128)S(1)}, f32[16,2,8,128]{3,2,1,0:T(8,128)}, u32[]{:S(2)}) copy-start(f32[16,2,8,128]{3,2,1,0:T(8,128)} %refs_3_.1) | copy-start | bytes 393220
  1.7 5.0 %collective-permute-start = (bf16[2,1,2,2,16,128]{5,4,3,2,1,0:T(8,128)(2,1)S(1)}, bf16[2,1,2,2,16,128]{5,4,3,2,1,0:T(8,128)(2,1)S(1)}, u32[]{:S(2)}, u32[]{:S(2)}) collective-permute-start(bf16[2,1,2,2,16,128]{5,4,3,2,1,0:T(8,128)(2,1)S(1)} %get-tuple-element.15), channel_id=1, source_target_pairs={{0,1},{1,0},{2,3},{3,2},{4,5},{5,4},{6,7},{7,6},{8,9},{9,8},{10,11... | collective-permute-start | bytes 98312 | tf_op jit(solution)/shard_map/ppermute | solution.py:318
  6.7 5.0 %collective-permute-start.1 = (bf16[1,2,2,2,16,128]{5,4,3,2,1,0:T(8,128)(2,1)S(1)}, bf16[1,2,2,2,16,128]{5,4,3,2,1,0:T(8,128)(2,1)S(1)}, u32[]{:S(2)}, u32[]{:S(2)}) collective-permute-start(bf16[1,2,2,2,16,128]{5,4,3,2,1,0:T(8,128)(2,1)S(1)} %pad_maximum_fusion.1), channel_id=1, source_target_pairs={{0,2},{1,3},{2,0},{3,1},{4,6},{5,7},{6,4},{7,5},{8,10},{9,11},{10,... | collective-permute-start | bytes 98312 | tf_op jit(solution)/shard_map/ppermute | solution.py:318
  11.7 5.6 %collective-permute-start.4 = (bf16[4,2,2,16,128]{4,3,2,1,0:T(8,128)(2,1)S(1)}, bf16[4,2,2,16,128]{4,3,2,1,0:T(8,128)(2,1)S(1)}, u32[]{:S(2)}, u32[]{:S(2)}) collective-permute-start(bf16[4,2,2,16,128]{4,3,2,1,0:T(8,128)(2,1)S(1)} %pad_maximum_fusion.refs_3_), channel_id=1, source_target_pairs={{0,8},{4,12},{8,0},{12,4},{16,24},{20,28},{24,16},{28,20},{1,9},{5... | collective-permute-start | bytes 196616 | tf_op jit(solution)/shard_map/ppermute | solution.py:318
  13.6 4.3 %collective-permute-start.3 = (bf16[4,2,2,16,128]{4,3,2,1,0:T(8,128)(2,1)S(1)}, bf16[4,2,2,16,128]{4,3,2,1,0:T(8,128)(2,1)S(1)}, u32[]{:S(2)}, u32[]{:S(2)}) collective-permute-start(bf16[4,2,2,16,128]{4,3,2,1,0:T(8,128)(2,1)S(1)} %pad_maximum_fusion.refs_3_), channel_id=1, source_target_pairs={{0,16},{4,20},{8,24},{12,28},{16,0},{20,4},{24,8},{28,12},{1,17},{... | collective-permute-start | bytes 196616 | tf_op jit(solution)/shard_map/ppermute | solution.py:318
  15.1 5.2 %collective-permute-start.2 = (bf16[4,2,2,16,128]{4,3,2,1,0:T(8,128)(2,1)S(1)}, bf16[4,2,2,16,128]{4,3,2,1,0:T(8,128)(2,1)S(1)}, u32[]{:S(2)}, u32[]{:S(2)}) collective-permute-start(bf16[4,2,2,16,128]{4,3,2,1,0:T(8,128)(2,1)S(1)} %pad_maximum_fusion.refs_3_), channel_id=1, source_target_pairs={{0,24},{4,28},{8,16},{12,20},{16,8},{20,12},{24,0},{28,4},{1,25},{... | collective-permute-start | bytes 196616 | tf_op jit(solution)/shard_map/ppermute | solution.py:318
  17.2 4.6 %collective-permute-start.8 = (bf16[4,2,2,16,128]{4,3,2,1,0:T(8,128)(2,1)S(1)}, bf16[4,2,2,16,128]{4,3,2,1,0:T(8,128)(2,1)S(1)}, u32[]{:S(2)}, u32[]{:S(2)}) collective-permute-start(bf16[4,2,2,16,128]{4,3,2,1,0:T(8,128)(2,1)S(1)} %pad_maximum_fusion.refs_3_), channel_id=1, source_target_pairs={{0,4},{4,0},{8,12},{12,8},{16,20},{20,16},{24,28},{28,24},{1,5},{5... | collective-permute-start | bytes 196616 | tf_op jit(solution)/shard_map/ppermute | solution.py:318
  17.3 4.5 %collective-permute-start.7 = (bf16[4,2,2,16,128]{4,3,2,1,0:T(8,128)(2,1)S(1)}, bf16[4,2,2,16,128]{4,3,2,1,0:T(8,128)(2,1)S(1)}, u32[]{:S(2)}, u32[]{:S(2)}) collective-permute-start(bf16[4,2,2,16,128]{4,3,2,1,0:T(8,128)(2,1)S(1)} %collective-permute-done.4.refs_2_), channel_id=1, source_target_pairs={{0,4},{4,0},{8,12},{12,8},{16,20},{20,16},{24,28},{28,24},{1,5},{5... | collective-permute-start | bytes 196616 | tf_op jit(solution)/shard_map/ppermute | solution.py:318
  17.8 4.0 %collective-permute-start.6 = (bf16[4,2,2,16,128]{4,3,2,1,0:T(8,128)(2,1)S(1)}, bf16[4,2,2,16,128]{4,3,2,1,0:T(8,128)(2,1)S(1)}, u32[]{:S(2)}, u32[]{:S(2)}) collective-permute-start(bf16[4,2,2,16,128]{4,3,2,1,0:T(8,128)(2,1)S(1)} %collective-permute-done.3.refs_1_), channel_id=1, source_target_pairs={{0,4},{4,0},{8,12},{12,8},{16,20},{20,16},{24,28},{28,24},{1,5},{5... | collective-permute-start | bytes 196616 | tf_op jit(solution)/shard_map/ppermute | solution.py:318
  20.3 1.6 %collective-permute-start.5 = (bf16[4,2,2,16,128]{4,3,2,1,0:T(8,128)(2,1)S(1)}, bf16[4,2,2,16,128]{4,3,2,1,0:T(8,128)(2,1)S(1)}, u32[]{:S(2)}, u32[]{:S(2)}) collective-permute-start(bf16[4,2,2,16,128]{4,3,2,1,0:T(8,128)(2,1)S(1)} %collective-permute-done.2.refs_0_), channel_id=1, source_target_pairs={{0,4},{4,0},{8,12},{12,8},{16,20},{20,16},{24,28},{28,24},{1,5},{5... | collective-permute-start | bytes 196616 | tf_op jit(solution)/shard_map/ppermute | solution.py:318
  29.5 17.2 %copy-start.1 = (f32[16,2,8,128]{3,2,1,0:T(8,128)S(1)}, f32[16,2,8,128]{3,2,1,0:T(8,128)}, u32[]{:S(2)}) copy-start(f32[16,2,8,128]{3,2,1,0:T(8,128)} %refs_3_.1) | copy-start | bytes 393220
  29.5 17.1 %copy-start.2 = (f32[16,2,8,128]{3,2,1,0:T(8,128)S(1)}, f32[16,2,8,128]{3,2,1,0:T(8,128)}, u32[]{:S(2)}) copy-start(f32[16,2,8,128]{3,2,1,0:T(8,128)} %refs_4_.1) | copy-start | bytes 393220
  29.5 17.1 %copy-start.3 = (f32[16,2,8,128]{3,2,1,0:T(8,128)S(1)}, f32[16,2,8,128]{3,2,1,0:T(8,128)}, u32[]{:S(2)}) copy-start(f32[16,2,8,128]{3,2,1,0:T(8,128)} %refs_5_.1) | copy-start | bytes 393220
  29.5 1.8 %collective-permute-start.9 = (bf16[4,4,2,2,16,128]{5,4,3,2,1,0:T(8,128)(2,1)S(1)}, bf16[4,4,2,2,16,128]{5,4,3,2,1,0:T(8,128)(2,1)S(1)}, u32[]{:S(2)}, u32[]{:S(2)}) collective-permute-start(bf16[4,4,2,2,16,128]{5,4,3,2,1,0:T(8,128)(2,1)S(1)} %get-tuple-element.18), channel_id=1, source_target_pairs={{0,4},{4,0},{8,12},{12,8},{16,20},{20,16},{24,28},{28,24},{1,5},{5... | collective-permute-start | bytes 786440 | tf_op jit(solution)/shard_map/ppermute | solution.py:318
  31.4 5.9 %collective-permute-start.10 = (bf16[4,2,2,16,128]{4,3,2,1,0:T(8,128)(2,1)S(1)}, bf16[4,2,2,16,128]{4,3,2,1,0:T(8,128)(2,1)S(1)}, u32[]{:S(2)}, u32[]{:S(2)}) collective-permute-start(bf16[4,2,2,16,128]{4,3,2,1,0:T(8,128)(2,1)S(1)} %get-tuple-element.20), channel_id=1, source_target_pairs={{0,24},{4,28},{8,16},{12,20},{16,8},{20,12},{24,0},{28,4},{1,25},{... | collective-permute-start | bytes 196616 | tf_op jit(solution)/shard_map/ppermute | solution.py:318
  32.0 5.4 %collective-permute-start.11 = (bf16[4,2,2,16,128]{4,3,2,1,0:T(8,128)(2,1)S(1)}, bf16[4,2,2,16,128]{4,3,2,1,0:T(8,128)(2,1)S(1)}, u32[]{:S(2)}, u32[]{:S(2)}) collective-permute-start(bf16[4,2,2,16,128]{4,3,2,1,0:T(8,128)(2,1)S(1)} %get-tuple-element.21), channel_id=1, source_target_pairs={{0,16},{4,20},{8,24},{12,28},{16,0},{20,4},{24,8},{28,12},{1,17},{... | collective-permute-start | bytes 196616 | tf_op jit(solution)/shard_map/ppermute | solution.py:318
  33.5 4.3 %collective-permute-start.12 = (bf16[4,2,2,16,128]{4,3,2,1,0:T(8,128)(2,1)S(1)}, bf16[4,2,2,16,128]{4,3,2,1,0:T(8,128)(2,1)S(1)}, u32[]{:S(2)}, u32[]{:S(2)}) collective-permute-start(bf16[4,2,2,16,128]{4,3,2,1,0:T(8,128)(2,1)S(1)} %get-tuple-element.22), channel_id=1, source_target_pairs={{0,8},{4,12},{8,0},{12,4},{16,24},{20,28},{24,16},{28,20},{1,9},{5... | collective-permute-start | bytes 196616 | tf_op jit(solution)/shard_map/ppermute | solution.py:318
  37.8 4.0 %collective-permute-start.13 = (bf16[2,1,2,2,16,128]{5,4,3,2,1,0:T(8,128)(2,1)S(1)}, bf16[2,1,2,2,16,128]{5,4,3,2,1,0:T(8,128)(2,1)S(1)}, u32[]{:S(2)}, u32[]{:S(2)}) collective-permute-start(bf16[2,1,2,2,16,128]{5,4,3,2,1,0:T(8,128)(2,1)S(1)} %get-tuple-element.24), channel_id=1, source_target_pairs={{0,1},{1,0},{2,3},{3,2},{4,5},{5,4},{6,7},{7,6},{8,9},{9,8},{10,11... | collective-permute-start | bytes 98312 | tf_op jit(solution)/shard_map/ppermute | solution.py:318
  41.8 4.9 %collective-permute-start.14 = (bf16[1,2,2,2,16,128]{5,4,3,2,1,0:T(8,128)(2,1)S(1)}, bf16[1,2,2,2,16,128]{5,4,3,2,1,0:T(8,128)(2,1)S(1)}, u32[]{:S(2)}, u32[]{:S(2)}) collective-permute-start(bf16[1,2,2,2,16,128]{5,4,3,2,1,0:T(8,128)(2,1)S(1)} %pad_maximum_fusion.2), channel_id=1, source_target_pairs={{0,2},{1,3},{2,0},{3,1},{4,6},{5,7},{6,4},{7,5},{8,10},{9,11},{10,... | collective-permute-start | bytes 98312 | tf_op jit(solution)/shard_map/ppermute | solution.py:318

commit v6 on v4

--- a/solution.py
+++ b/solution.py
@@ -16,7 +16,8 @@
 epsilon = 1e-08
 
 ROW_TILE = 512
-CHUNK = 16
+LANES = 256
+CHUNK = 32
 MIB = 1024 * 1024
 
 
@@ -87,26 +88,40 @@
     def normalize(tile, buffers):
         scores, slopes, weights, dscores = buffers
         cuts = [pl.ds(start, CHUNK) for start in range(0, positions, CHUNK)]
-        top = scores[cuts[0]]
-        for cut in cuts[1:]:
-            top = jnp.maximum(top, scores[cut])
-        side_lse = lse_ref[tile] * log2e
-        peak = jnp.maximum(jnp.max(top, axis=0, keepdims=True) * factor, side_lse)
-        total = None
-        dotted = None
+        blocks = [pl.ds(start, LANES) for start in range(0, scores.shape[1], LANES)]
+
+        def largest(top, cut, lanes):
+            here = scores[cut, lanes]
+            return here if top is None else jnp.maximum(top, here)
+
+        top = None
         for cut in cuts:
-            shifted = jnp.exp2(scores[cut] * factor - peak)
-            product = shifted * slopes[cut]
-            scores[cut] = shifted
-            total = shifted if total is None else total + shifted
-            dotted = product if dotted is None else dotted + product
-        side = jnp.exp2(side_lse - peak)
-        inverse = 1.0 / (jnp.sum(total, axis=0, keepdims=True) + side)
-        delta = (jnp.sum(dotted, axis=0, keepdims=True) + side * dot_ref[tile]) * inverse
-        for cut in cuts:
-            probability = scores[cut] * inverse
-            weights[cut] = probability.astype(jnp.bfloat16)
-            dscores[cut] = (probability * (slopes[cut] - delta)).astype(jnp.bfloat16)
+            top = largest(top, cut, blocks[0])
+        for number, lanes in enumerate(blocks):
+            following = blocks[number + 1] if number + 1 < len(blocks) else None
+            side_lse = lse_ref[tile, :, lanes] * log2e
+            peak = jnp.maximum(jnp.max(top, axis=0, keepdims=True) * factor, side_lse)
+            total = None
+            dotted = None
+            for cut in cuts:
+                shifted = jnp.exp2(scores[cut, lanes] * factor - peak)
+                product = shifted * slopes[cut, lanes]
+                scores[cut, lanes] = shifted
+                total = shifted if total is None else total + shifted
+                dotted = product if dotted is None else dotted + product
+            side = jnp.exp2(side_lse - peak)
+            inverse = 1.0 / (jnp.sum(total, axis=0, keepdims=True) + side)
+            delta = jnp.sum(dotted, axis=0, keepdims=True) + side * dot_ref[tile, :, lanes]
+            delta = delta * inverse
+            top = None
+            for cut in cuts:
+                if following is not None:
+                    top = largest(top, cut, following)
+                probability = scores[cut, lanes] * inverse
+                weights[cut, lanes] = probability.astype(jnp.bfloat16)
+                dscores[cut, lanes] = (probability * (slopes[cut, lanes] - delta)).astype(
+                    jnp.bfloat16
+                )
 
     def accumulate(tile, buffers):
         _, _, weights, dscores = buffers

time: 44.6 us -> 44.7 us (level)
  transfers between devices with their start and end apart: 17 -> 17, of which waited for: 12 -> 11; matrix products, arithmetic and copies ran while one was open for 8% -> 8% of each run, Pallas kernels for 0% -> 0%
where the time goes in v6:
time: 44.7 us; the launch traced here: 44.4 us
  starting transfers between devices  18.4 us (41%)
  waiting for transfers between devices  11.4 us (26%)
  Pallas kernels  9.48 us (21%)
  local copies, waits for them, and re-layouts  4.33 us (10%)
  between operations  0.79 us (2%)
    ppermute x17, starting transfers between devices, swap(): lax.ppermute(value, axis, [(place, place ^ flip) for place in range(size)])  18.4 us
    ppermute x17, waiting for transfers between devices, swap(): lax.ppermute(value, axis, [(place, place ^ flip) for place in range(size)])  11.4 us
    pallas_call x1, Pallas kernels, attend(): pl.pallas_call(functools.partial(attend_kernel, score_scale, tiles // own...  7.99 us
    dynamic_slice x2, local copies, waits for them, and re-layouts, tiles_of(): part = lax.dynamic_slice_in_dim(part, first_group, own, 1)  2.69 us
    unnamed x12, local copies, waits for them, and re-layouts  1.3 us
    pallas_call x1, Pallas kernels, adam(): pl.pallas_call(functools.partial(adam_kernel, len(parts)), out_shape=(sha...  1.27 us
  transfers between devices with their start and end apart: 17, of which 11 were waited for; matrix products, arithmetic and copies ran while one was open for 8% of the time, Pallas kernels for 0%

profile of v6, /device:TPU:0, one launch (start us, length us, event | category | flops | bytes accessed | tf_op | source)
XLA Modules:
  0.0 44.4 jit_solution(12370373132768941473)
XLA Ops:
  0.6 0.0 copy-start
  0.6 0.9 %copy-done = f32[16,2,8,128]{3,2,1,0:T(8,128)S(1)} copy-done((f32[16,2,8,128]{3,2,1,0:T(8,128)S(1)}, f32[16,2,8,128]{3,2,1,0:T(8,128)}, u32[]{:S(2)}) %copy-start) | copy-done | bytes 131096
  1.5 0.1 pack.1
  1.7 5.1 %collective-permute-start = (bf16[2,2,16,128]{3,2,1,0:T(8,128)(2,1)S(1)}, bf16[2,2,16,128]{3,2,1,0:T(8,128)(2,1)S(1)}, u32[]{:S(2)}, u32[]{:S(2)}) collective-permute-start(bf16[2,2,16,128]{3,2,1,0:T(8,128)(2,1)S(1)} %get-tuple-element.17), channel_id=1, source_target_pairs={{0,3},{1,2},{2,1},{3,0},{4,7},{5,6},{6,5},{7,4},{8,11},{9,10},{10,... | collective-permute-start | bytes 49160 | tf_op jit(solution)/shard_map/ppermute | solution.py:287
  6.8 0.0 collective-permute-start.1
  6.8 0.6 %collective-permute-start.2 = (bf16[2,2,16,128]{3,2,1,0:T(8,128)(2,1)S(1)}, bf16[2,2,16,128]{3,2,1,0:T(8,128)(2,1)S(1)}, u32[]{:S(2)}, u32[]{:S(2)}) collective-permute-start(bf16[2,2,16,128]{3,2,1,0:T(8,128)(2,1)S(1)} %get-tuple-element.19), channel_id=1, source_target_pairs={{0,1},{1,0},{2,3},{3,2},{4,5},{5,4},{6,7},{7,6},{8,9},{9,8},{10,11... | collective-permute-start | bytes 49160 | tf_op jit(solution)/shard_map/ppermute | solution.py:287
  7.4 1.1 %collective-permute-done = bf16[2,2,16,128]{3,2,1,0:T(8,128)(2,1)S(1)} collective-permute-done((bf16[2,2,16,128]{3,2,1,0:T(8,128)(2,1)S(1)}, bf16[2,2,16,128]{3,2,1,0:T(8,128)(2,1)S(1)}, u32[]{:S(2)}, u32[]{:S(2)}) %collective-permute-start) | collective-permute-done | bytes 16416 | tf_op jit(solution)/shard_map/ppermute | solution.py:287
  8.5 2.9 %collective-permute-done.1 = bf16[2,2,16,128]{3,2,1,0:T(8,128)(2,1)S(1)} collective-permute-done((bf16[2,2,16,128]{3,2,1,0:T(8,128)(2,1)S(1)}, bf16[2,2,16,128]{3,2,1,0:T(8,128)(2,1)S(1)}, u32[]{:S(2)}, u32[]{:S(2)}) %collective-permute-start.1) | collective-permute-done | bytes 16416 | tf_op jit(solution)/shard_map/ppermute | solution.py:287
  11.4 0.0 collective-permute-done.2
  11.5 2.5 %collective-permute-start.3 = (bf16[4,2,2,16,128]{4,3,2,1,0:T(8,128)(2,1)S(1)}, bf16[4,2,2,16,128]{4,3,2,1,0:T(8,128)(2,1)S(1)}, u32[]{:S(2)}, u32[]{:S(2)}) collective-permute-start(bf16[4,2,2,16,128]{4,3,2,1,0:T(8,128)(2,1)S(1)} %pad_maximum_fusion.refs_3_), channel_id=1, source_target_pairs={{0,24},{4,28},{8,16},{12,20},{16,8},{20,12},{24,0},{28,4},{1,25},{... | collective-permute-start | bytes 196616 | tf_op jit(solution)/shard_map/ppermute | solution.py:287
  14.0 0.5 %collective-permute-start.4 = (bf16[4,2,2,16,128]{4,3,2,1,0:T(8,128)(2,1)S(1)}, bf16[4,2,2,16,128]{4,3,2,1,0:T(8,128)(2,1)S(1)}, u32[]{:S(2)}, u32[]{:S(2)}) collective-permute-start(bf16[4,2,2,16,128]{4,3,2,1,0:T(8,128)(2,1)S(1)} %pad_maximum_fusion.refs_3_), channel_id=1, source_target_pairs={{0,16},{4,20},{8,24},{12,28},{16,0},{20,4},{24,8},{28,12},{1,17},{... | collective-permute-start | bytes 196616 | tf_op jit(solution)/shard_map/ppermute | solution.py:287
  14.5 0.5 %collective-permute-start.5 = (bf16[4,2,2,16,128]{4,3,2,1,0:T(8,128)(2,1)S(1)}, bf16[4,2,2,16,128]{4,3,2,1,0:T(8,128)(2,1)S(1)}, u32[]{:S(2)}, u32[]{:S(2)}) collective-permute-start(bf16[4,2,2,16,128]{4,3,2,1,0:T(8,128)(2,1)S(1)} %pad_maximum_fusion.refs_3_), channel_id=1, source_target_pairs={{0,8},{4,12},{8,0},{12,4},{16,24},{20,28},{24,16},{28,20},{1,9},{5... | collective-permute-start | bytes 196616 | tf_op jit(solution)/shard_map/ppermute | solution.py:287
  15.0 2.0 %constant_dynamic-slice_fusion.2 = (bf16[256,2,8,128]{3,2,1,0:T(8,128)(2,1)S(1)}, bf16[256,2,8,128]{3,2,1,0:T(8,128)(2,1)S(1)}) fusion(bf16[256,8,8,128]{3,2,1,0:T(8,128)(2,1)} %bitcast.21, s32[]{:T(128)S(6)} %select_n.9, bf16[256,8,8,128]{3,2,1,0:T(8,128)(2,1)} %bitcast.22), kind=kLoop, calls=%fused_computation.3 | loop fusion | bytes 4194308 | tf_op jit(solution)/shard_map/dynamic_slice | solution.py:320
  17.0 0.1 copy.20
  17.0 0.1 copy.21
  17.1 0.1 collective-permute-start.9
  17.2 0.1 collective-permute-done.3.refs_0_
  17.3 0.4 collective-permute-start.6
  17.7 0.5 %collective-permute-done.4.refs_1_ = bf16[4,2,2,16,128]{4,3,2,1,0:T(8,128)(2,1)S(1)} collective-permute-done((bf16[4,2,2,16,128]{4,3,2,1,0:T(8,128)(2,1)S(1)}, bf16[4,2,2,16,128]{4,3,2,1,0:T(8,128)(2,1)S(1)}, u32[]{:S(2)}, u32[]{:S(2)}) %collective-permute-start.4) | collective-permute-done | bytes 65568 | tf_op jit(solution)/shard_map/ppermute | solution.py:287
  18.2 0.0 collective-permute-start.7
  18.2 0.5 %collective-permute-done.5.refs_2_ = bf16[4,2,2,16,128]{4,3,2,1,0:T(8,128)(2,1)S(1)} collective-permute-done((bf16[4,2,2,16,128]{4,3,2,1,0:T(8,128)(2,1)S(1)}, bf16[4,2,2,16,128]{4,3,2,1,0:T(8,128)(2,1)S(1)}, u32[]{:S(2)}, u32[]{:S(2)}) %collective-permute-start.5) | collective-permute-done | bytes 65568 | tf_op jit(solution)/shard_map/ppermute | solution.py:287
  18.7 0.0 collective-permute-start.8
  18.7 0.7 %constant_dynamic-slice_fusion = (f32[256,2,8]{0,2,1:T(8,128)S(1)}, f32[256,2,8]{0,2,1:T(8,128)S(1)}) fusion(f32[256,8,8]{0,2,1:T(8,128)} %bitcast.26, s32[]{:T(128)S(6)} %select_n.9, f32[256,8,8]{0,2,1:T(8,128)} %bitcast.27), kind=kLoop, calls=%fused_computation.1 | loop fusion | bytes 65540 | tf_op jit(solution)/shard_map/dynamic_slice | solution.py:320
  19.5 0.1 copy.22
  19.6 0.2 broadcast_in_dim_reshape.8.refs_10_
  19.8 0.1 copy.23
  19.9 0.2 broadcast_in_dim_reshape.9.refs_11_
  20.1 0.0 collective-permute-done.9.refs_7_
  20.1 0.0 collective-permute-done.6.refs_4_
  20.1 0.0 collective-permute-done.7.refs_5_
  20.1 0.0 collective-permute-done.8.refs_6_
  20.1 0.0 copy-start.1
  20.2 0.0 copy-start.2
  20.2 0.0 copy-start.3
  20.2 8.0 %attend.1 = (f32[4,4,2,2,16,128]{5,4,3,2,1,0:T(8,128)S(1)}, bf16[4,4,2,2,16,128]{5,4,3,2,1,0:T(8,128)(2,1)S(1)}) custom-call(bf16[4,2,2,16,128]{4,3,2,1,0:T(8,128)(2,1)S(1)} %collective-permute-done.3.refs_0_, bf16[4,2,2,16,128]{4,3,2,1,0:T(8,128)(2,1)S(1)} %collective-permute-done.4.refs_1_, bf16[4,2,2,16,128]{4,3,2,1,0:T(8,128)(2,1)S(1)} %collective-permute-done.5.refs_2_, ...), custom_call_target="tpu_custom_call" | custom-call | flops 2147483648 | bytes 3145728 | tf_op jit(solution)/shard_map/attend/pallas_call | solution.py:179
  28.2 0.6 %collective-permute-start.10 = (bf16[4,4,2,2,16,128]{5,4,3,2,1,0:T(8,128)(2,1)S(1)}, bf16[4,4,2,2,16,128]{5,4,3,2,1,0:T(8,128)(2,1)S(1)}, u32[]{:S(2)}, u32[]{:S(2)}) collective-permute-start(bf16[4,4,2,2,16,128]{5,4,3,2,1,0:T(8,128)(2,1)S(1)} %get-tuple-element.22), channel_id=1, source_target_pairs={{0,4},{4,0},{8,12},{12,8},{16,20},{20,16},{24,28},{28,24},{1,5},{5... | collective-permute-start | bytes 786440 | tf_op jit(solution)/shard_map/ppermute | solution.py:287
  28.8 1.2 %collective-permute-done.10.mate_ref = bf16[4,4,2,2,16,128]{5,4,3,2,1,0:T(8,128)(2,1)S(1)} collective-permute-done((bf16[4,4,2,2,16,128]{5,4,3,2,1,0:T(8,128)(2,1)S(1)}, bf16[4,4,2,2,16,128]{5,4,3,2,1,0:T(8,128)(2,1)S(1)}, u32[]{:S(2)}, u32[]{:S(2)}) %collective-permute-start.10) | collective-permute-done | bytes 262176 | tf_op jit(solution)/shard_map/ppermute | solution.py:287
  30.0 1.8 %collective-permute-start.11 = (bf16[4,2,2,16,128]{4,3,2,1,0:T(8,128)(2,1)S(1)}, bf16[4,2,2,16,128]{4,3,2,1,0:T(8,128)(2,1)S(1)}, u32[]{:S(2)}, u32[]{:S(2)}) collective-permute-start(bf16[4,2,2,16,128]{4,3,2,1,0:T(8,128)(2,1)S(1)} %get-tuple-element.24), channel_id=1, source_target_pairs={{0,24},{4,28},{8,16},{12,20},{16,8},{20,12},{24,0},{28,4},{1,25},{... | collective-permute-start | bytes 196616 | tf_op jit(solution)/shard_map/ppermute | solution.py:287
  31.8 0.5 %collective-permute-start.12 = (bf16[4,2,2,16,128]{4,3,2,1,0:T(8,128)(2,1)S(1)}, bf16[4,2,2,16,128]{4,3,2,1,0:T(8,128)(2,1)S(1)}, u32[]{:S(2)}, u32[]{:S(2)}) collective-permute-start(bf16[4,2,2,16,128]{4,3,2,1,0:T(8,128)(2,1)S(1)} %get-tuple-element.25), channel_id=1, source_target_pairs={{0,16},{4,20},{8,24},{12,28},{16,0},{20,4},{24,8},{28,12},{1,17},{... | collective-permute-start | bytes 196616 | tf_op jit(solution)/shard_map/ppermute | solution.py:287
  32.3 1.2 %collective-permute-start.13 = (bf16[4,2,2,16,128]{4,3,2,1,0:T(8,128)(2,1)S(1)}, bf16[4,2,2,16,128]{4,3,2,1,0:T(8,128)(2,1)S(1)}, u32[]{:S(2)}, u32[]{:S(2)}) collective-permute-start(bf16[4,2,2,16,128]{4,3,2,1,0:T(8,128)(2,1)S(1)} %get-tuple-element.26), channel_id=1, source_target_pairs={{0,8},{4,12},{8,0},{12,4},{16,24},{20,28},{24,16},{28,20},{1,9},{5... | collective-permute-start | bytes 196616 | tf_op jit(solution)/shard_map/ppermute | solution.py:287
  33.5 1.9 %collective-permute-done.11.refs_0_ = bf16[4,2,2,16,128]{4,3,2,1,0:T(8,128)(2,1)S(1)} collective-permute-done((bf16[4,2,2,16,128]{4,3,2,1,0:T(8,128)(2,1)S(1)}, bf16[4,2,2,16,128]{4,3,2,1,0:T(8,128)(2,1)S(1)}, u32[]{:S(2)}, u32[]{:S(2)}) %collective-permute-start.11) | collective-permute-done | bytes 65568 | tf_op jit(solution)/shard_map/ppermute | solution.py:287
  35.4 1.3 %collective-permute-done.12.refs_1_ = bf16[4,2,2,16,128]{4,3,2,1,0:T(8,128)(2,1)S(1)} collective-permute-done((bf16[4,2,2,16,128]{4,3,2,1,0:T(8,128)(2,1)S(1)}, bf16[4,2,2,16,128]{4,3,2,1,0:T(8,128)(2,1)S(1)}, u32[]{:S(2)}, u32[]{:S(2)}) %collective-permute-start.12) | collective-permute-done | bytes 65568 | tf_op jit(solution)/shard_map/ppermute | solution.py:287
  36.7 0.0 collective-permute-done.13.refs_2_
  36.8 1.5 %collective-permute-start.14 = (bf16[2,2,16,128]{3,2,1,0:T(8,128)(2,1)S(1)}, bf16[2,2,16,128]{3,2,1,0:T(8,128)(2,1)S(1)}, u32[]{:S(2)}, u32[]{:S(2)}) collective-permute-start(bf16[2,2,16,128]{3,2,1,0:T(8,128)(2,1)S(1)} %get-tuple-element.27), channel_id=1, source_target_pairs={{0,3},{1,2},{2,1},{3,0},{4,7},{5,6},{6,5},{7,4},{8,11},{9,10},{10,... | collective-permute-start | bytes 49160 | tf_op jit(solution)/shard_map/ppermute | solution.py:287
  38.3 0.6 %collective-permute-start.15 = (bf16[2,2,16,128]{3,2,1,0:T(8,128)(2,1)S(1)}, bf16[2,2,16,128]{3,2,1,0:T(8,128)(2,1)S(1)}, u32[]{:S(2)}, u32[]{:S(2)}) collective-permute-start(bf16[2,2,16,128]{3,2,1,0:T(8,128)(2,1)S(1)} %get-tuple-element.28), channel_id=1, source_target_pairs={{0,2},{1,3},{2,0},{3,1},{4,6},{5,7},{6,4},{7,5},{8,10},{9,11},{10,... | collective-permute-start | bytes 49160 | tf_op jit(solution)/shard_map/ppermute | solution.py:287
  38.9 2.3 %collective-permute-start.16 = (bf16[2,2,16,128]{3,2,1,0:T(8,128)(2,1)S(1)}, bf16[2,2,16,128]{3,2,1,0:T(8,128)(2,1)S(1)}, u32[]{:S(2)}, u32[]{:S(2)}) collective-permute-start(bf16[2,2,16,128]{3,2,1,0:T(8,128)(2,1)S(1)} %get-tuple-element.29), channel_id=1, source_target_pairs={{0,1},{1,0},{2,3},{3,2},{4,5},{5,4},{6,7},{7,6},{8,9},{9,8},{10,11... | collective-permute-start | bytes 49160 | tf_op jit(solution)/shard_map/ppermute | solution.py:287
  41.2 1.1 %collective-permute-done.14.refs_0_ = bf16[2,2,16,128]{3,2,1,0:T(8,128)(2,1)S(1)} collective-permute-done((bf16[2,2,16,128]{3,2,1,0:T(8,128)(2,1)S(1)}, bf16[2,2,16,128]{3,2,1,0:T(8,128)(2,1)S(1)}, u32[]{:S(2)}, u32[]{:S(2)}) %collective-permute-start.14) | collective-permute-done | bytes 16416 | tf_op jit(solution)/shard_map/ppermute | solution.py:287
  42.4 0.6 %collective-permute-done.15.refs_1_ = bf16[2,2,16,128]{3,2,1,0:T(8,128)(2,1)S(1)} collective-permute-done((bf16[2,2,16,128]{3,2,1,0:T(8,128)(2,1)S(1)}, bf16[2,2,16,128]{3,2,1,0:T(8,128)(2,1)S(1)}, u32[]{:S(2)}, u32[]{:S(2)}) %collective-permute-start.15) | collective-permute-done | bytes 16416 | tf_op jit(solution)/shard_map/ppermute | solution.py:287
  42.9 0.2 collective-permute-done.16.refs_2_
  43.1 0.0 copy-done.1
  43.1 0.0 copy-done.2
  43.1 0.0 copy-done.3
  43.1 1.3 %adam.1 = (f32[16,2,8,128]{3,2,1,0:T(8,128)}, f32[16,2,8,128]{3,2,1,0:T(8,128)}, f32[16,2,8,128]{3,2,1,0:T(8,128)}) custom-call(bf16[2,2,16,128]{3,2,1,0:T(8,128)(2,1)S(1)} %collective-permute-done.14.refs_0_, bf16[2,2,16,128]{3,2,1,0:T(8,128)(2,1)S(1)} %collective-permute-done.15.refs_1_, bf16[2,2,16,128]{3,2,1,0:T(8,128)(2,1)S(1)} %collective-permute-done.16.refs_2_, ...), custom_call_target="tpu_custom_call" | custom-call | tf_op jit(solution)/shard_map/adam/pallas_call | solution.py:277
  (3 shorter events, 0.1 us)
Async XLA Ops:
  0.6 0.9 %copy-start = (f32[16,2,8,128]{3,2,1,0:T(8,128)S(1)}, f32[16,2,8,128]{3,2,1,0:T(8,128)}, u32[]{:S(2)}) copy-start(f32[16,2,8,128]{3,2,1,0:T(8,128)} %refs_4_.1) | copy-start | bytes 393220
  1.7 6.8 %collective-permute-start = (bf16[2,2,16,128]{3,2,1,0:T(8,128)(2,1)S(1)}, bf16[2,2,16,128]{3,2,1,0:T(8,128)(2,1)S(1)}, u32[]{:S(2)}, u32[]{:S(2)}) collective-permute-start(bf16[2,2,16,128]{3,2,1,0:T(8,128)(2,1)S(1)} %get-tuple-element.17), channel_id=1, source_target_pairs={{0,3},{1,2},{2,1},{3,0},{4,7},{5,6},{6,5},{7,4},{8,11},{9,10},{10,... | collective-permute-start | bytes 49160 | tf_op jit(solution)/shard_map/ppermute | solution.py:287
  6.8 4.6 %collective-permute-start.1 = (bf16[2,2,16,128]{3,2,1,0:T(8,128)(2,1)S(1)}, bf16[2,2,16,128]{3,2,1,0:T(8,128)(2,1)S(1)}, u32[]{:S(2)}, u32[]{:S(2)}) collective-permute-start(bf16[2,2,16,128]{3,2,1,0:T(8,128)(2,1)S(1)} %get-tuple-element.18), channel_id=1, source_target_pairs={{0,2},{1,3},{2,0},{3,1},{4,6},{5,7},{6,4},{7,5},{8,10},{9,11},{10,... | collective-permute-start | bytes 49160 | tf_op jit(solution)/shard_map/ppermute | solution.py:287
  6.8 4.6 %collective-permute-start.2 = (bf16[2,2,16,128]{3,2,1,0:T(8,128)(2,1)S(1)}, bf16[2,2,16,128]{3,2,1,0:T(8,128)(2,1)S(1)}, u32[]{:S(2)}, u32[]{:S(2)}) collective-permute-start(bf16[2,2,16,128]{3,2,1,0:T(8,128)(2,1)S(1)} %get-tuple-element.19), channel_id=1, source_target_pairs={{0,1},{1,0},{2,3},{3,2},{4,5},{5,4},{6,7},{7,6},{8,9},{9,8},{10,11... | collective-permute-start | bytes 49160 | tf_op jit(solution)/shard_map/ppermute | solution.py:287
  11.5 5.8 %collective-permute-start.3 = (bf16[4,2,2,16,128]{4,3,2,1,0:T(8,128)(2,1)S(1)}, bf16[4,2,2,16,128]{4,3,2,1,0:T(8,128)(2,1)S(1)}, u32[]{:S(2)}, u32[]{:S(2)}) collective-permute-start(bf16[4,2,2,16,128]{4,3,2,1,0:T(8,128)(2,1)S(1)} %pad_maximum_fusion.refs_3_), channel_id=1, source_target_pairs={{0,24},{4,28},{8,16},{12,20},{16,8},{20,12},{24,0},{28,4},{1,25},{... | collective-permute-start | bytes 196616 | tf_op jit(solution)/shard_map/ppermute | solution.py:287
  14.0 4.3 %collective-permute-start.4 = (bf16[4,2,2,16,128]{4,3,2,1,0:T(8,128)(2,1)S(1)}, bf16[4,2,2,16,128]{4,3,2,1,0:T(8,128)(2,1)S(1)}, u32[]{:S(2)}, u32[]{:S(2)}) collective-permute-start(bf16[4,2,2,16,128]{4,3,2,1,0:T(8,128)(2,1)S(1)} %pad_maximum_fusion.refs_3_), channel_id=1, source_target_pairs={{0,16},{4,20},{8,24},{12,28},{16,0},{20,4},{24,8},{28,12},{1,17},{... | collective-permute-start | bytes 196616 | tf_op jit(solution)/shard_map/ppermute | solution.py:287
  14.5 4.3 %collective-permute-start.5 = (bf16[4,2,2,16,128]{4,3,2,1,0:T(8,128)(2,1)S(1)}, bf16[4,2,2,16,128]{4,3,2,1,0:T(8,128)(2,1)S(1)}, u32[]{:S(2)}, u32[]{:S(2)}) collective-permute-start(bf16[4,2,2,16,128]{4,3,2,1,0:T(8,128)(2,1)S(1)} %pad_maximum_fusion.refs_3_), channel_id=1, source_target_pairs={{0,8},{4,12},{8,0},{12,4},{16,24},{20,28},{24,16},{28,20},{1,9},{5... | collective-permute-start | bytes 196616 | tf_op jit(solution)/shard_map/ppermute | solution.py:287
  17.1 3.0 %collective-permute-start.9 = (bf16[4,2,2,16,128]{4,3,2,1,0:T(8,128)(2,1)S(1)}, bf16[4,2,2,16,128]{4,3,2,1,0:T(8,128)(2,1)S(1)}, u32[]{:S(2)}, u32[]{:S(2)}) collective-permute-start(bf16[4,2,2,16,128]{4,3,2,1,0:T(8,128)(2,1)S(1)} %pad_maximum_fusion.refs_3_), channel_id=1, source_target_pairs={{0,4},{4,0},{8,12},{12,8},{16,20},{20,16},{24,28},{28,24},{1,5},{5... | collective-permute-start | bytes 196616 | tf_op jit(solution)/shard_map/ppermute | solution.py:287
  17.3 2.8 %collective-permute-start.6 = (bf16[4,2,2,16,128]{4,3,2,1,0:T(8,128)(2,1)S(1)}, bf16[4,2,2,16,128]{4,3,2,1,0:T(8,128)(2,1)S(1)}, u32[]{:S(2)}, u32[]{:S(2)}) collective-permute-start(bf16[4,2,2,16,128]{4,3,2,1,0:T(8,128)(2,1)S(1)} %collective-permute-done.3.refs_0_), channel_id=1, source_target_pairs={{0,4},{4,0},{8,12},{12,8},{16,20},{20,16},{24,28},{28,24},{1,5},{5... | collective-permute-start | bytes 196616 | tf_op jit(solution)/shard_map/ppermute | solution.py:287
  18.2 1.9 %collective-permute-start.7 = (bf16[4,2,2,16,128]{4,3,2,1,0:T(8,128)(2,1)S(1)}, bf16[4,2,2,16,128]{4,3,2,1,0:T(8,128)(2,1)S(1)}, u32[]{:S(2)}, u32[]{:S(2)}) collective-permute-start(bf16[4,2,2,16,128]{4,3,2,1,0:T(8,128)(2,1)S(1)} %collective-permute-done.4.refs_1_), channel_id=1, source_target_pairs={{0,4},{4,0},{8,12},{12,8},{16,20},{20,16},{24,28},{28,24},{1,5},{5... | collective-permute-start | bytes 196616 | tf_op jit(solution)/shard_map/ppermute | solution.py:287
  18.7 1.4 %collective-permute-start.8 = (bf16[4,2,2,16,128]{4,3,2,1,0:T(8,128)(2,1)S(1)}, bf16[4,2,2,16,128]{4,3,2,1,0:T(8,128)(2,1)S(1)}, u32[]{:S(2)}, u32[]{:S(2)}) collective-permute-start(bf16[4,2,2,16,128]{4,3,2,1,0:T(8,128)(2,1)S(1)} %collective-permute-done.5.refs_2_), channel_id=1, source_target_pairs={{0,4},{4,0},{8,12},{12,8},{16,20},{20,16},{24,28},{28,24},{1,5},{5... | collective-permute-start | bytes 196616 | tf_op jit(solution)/shard_map/ppermute | solution.py:287
  20.1 23.0 %copy-start.1 = (f32[16,2,8,128]{3,2,1,0:T(8,128)S(1)}, f32[16,2,8,128]{3,2,1,0:T(8,128)}, u32[]{:S(2)}) copy-start(f32[16,2,8,128]{3,2,1,0:T(8,128)} %refs_4_.1) | copy-start | bytes 393220
  20.2 23.0 %copy-start.2 = (f32[16,2,8,128]{3,2,1,0:T(8,128)S(1)}, f32[16,2,8,128]{3,2,1,0:T(8,128)}, u32[]{:S(2)}) copy-start(f32[16,2,8,128]{3,2,1,0:T(8,128)} %refs_5_.1) | copy-start | bytes 393220
  20.2 22.9 %copy-start.3 = (f32[16,2,8,128]{3,2,1,0:T(8,128)S(1)}, f32[16,2,8,128]{3,2,1,0:T(8,128)}, u32[]{:S(2)}) copy-start(f32[16,2,8,128]{3,2,1,0:T(8,128)} %refs_6_.1) | copy-start | bytes 393220
  28.2 1.7 %collective-permute-start.10 = (bf16[4,4,2,2,16,128]{5,4,3,2,1,0:T(8,128)(2,1)S(1)}, bf16[4,4,2,2,16,128]{5,4,3,2,1,0:T(8,128)(2,1)S(1)}, u32[]{:S(2)}, u32[]{:S(2)}) collective-permute-start(bf16[4,4,2,2,16,128]{5,4,3,2,1,0:T(8,128)(2,1)S(1)} %get-tuple-element.22), channel_id=1, source_target_pairs={{0,4},{4,0},{8,12},{12,8},{16,20},{20,16},{24,28},{28,24},{1,5},{5... | collective-permute-start | bytes 786440 | tf_op jit(solution)/shard_map/ppermute | solution.py:287
  30.0 5.4 %collective-permute-start.11 = (bf16[4,2,2,16,128]{4,3,2,1,0:T(8,128)(2,1)S(1)}, bf16[4,2,2,16,128]{4,3,2,1,0:T(8,128)(2,1)S(1)}, u32[]{:S(2)}, u32[]{:S(2)}) collective-permute-start(bf16[4,2,2,16,128]{4,3,2,1,0:T(8,128)(2,1)S(1)} %get-tuple-element.24), channel_id=1, source_target_pairs={{0,24},{4,28},{8,16},{12,20},{16,8},{20,12},{24,0},{28,4},{1,25},{... | collective-permute-start | bytes 196616 | tf_op jit(solution)/shard_map/ppermute | solution.py:287
  31.8 4.9 %collective-permute-start.12 = (bf16[4,2,2,16,128]{4,3,2,1,0:T(8,128)(2,1)S(1)}, bf16[4,2,2,16,128]{4,3,2,1,0:T(8,128)(2,1)S(1)}, u32[]{:S(2)}, u32[]{:S(2)}) collective-permute-start(bf16[4,2,2,16,128]{4,3,2,1,0:T(8,128)(2,1)S(1)} %get-tuple-element.25), channel_id=1, source_target_pairs={{0,16},{4,20},{8,24},{12,28},{16,0},{20,4},{24,8},{28,12},{1,17},{... | collective-permute-start | bytes 196616 | tf_op jit(solution)/shard_map/ppermute | solution.py:287
  32.3 4.4 %collective-permute-start.13 = (bf16[4,2,2,16,128]{4,3,2,1,0:T(8,128)(2,1)S(1)}, bf16[4,2,2,16,128]{4,3,2,1,0:T(8,128)(2,1)S(1)}, u32[]{:S(2)}, u32[]{:S(2)}) collective-permute-start(bf16[4,2,2,16,128]{4,3,2,1,0:T(8,128)(2,1)S(1)} %get-tuple-element.26), channel_id=1, source_target_pairs={{0,8},{4,12},{8,0},{12,4},{16,24},{20,28},{24,16},{28,20},{1,9},{5... | collective-permute-start | bytes 196616 | tf_op jit(solution)/shard_map/ppermute | solution.py:287
  36.8 5.6 %collective-permute-start.14 = (bf16[2,2,16,128]{3,2,1,0:T(8,128)(2,1)S(1)}, bf16[2,2,16,128]{3,2,1,0:T(8,128)(2,1)S(1)}, u32[]{:S(2)}, u32[]{:S(2)}) collective-permute-start(bf16[2,2,16,128]{3,2,1,0:T(8,128)(2,1)S(1)} %get-tuple-element.27), channel_id=1, source_target_pairs={{0,3},{1,2},{2,1},{3,0},{4,7},{5,6},{6,5},{7,4},{8,11},{9,10},{10,... | collective-permute-start | bytes 49160 | tf_op jit(solution)/shard_map/ppermute | solution.py:287
  38.3 4.6 %collective-permute-start.15 = (bf16[2,2,16,128]{3,2,1,0:T(8,128)(2,1)S(1)}, bf16[2,2,16,128]{3,2,1,0:T(8,128)(2,1)S(1)}, u32[]{:S(2)}, u32[]{:S(2)}) collective-permute-start(bf16[2,2,16,128]{3,2,1,0:T(8,128)(2,1)S(1)} %get-tuple-element.28), channel_id=1, source_target_pairs={{0,2},{1,3},{2,0},{3,1},{4,6},{5,7},{6,4},{7,5},{8,10},{9,11},{10,... | collective-permute-start | bytes 49160 | tf_op jit(solution)/shard_map/ppermute | solution.py:287
  38.9 4.2 %collective-permute-start.16 = (bf16[2,2,16,128]{3,2,1,0:T(8,128)(2,1)S(1)}, bf16[2,2,16,128]{3,2,1,0:T(8,128)(2,1)S(1)}, u32[]{:S(2)}, u32[]{:S(2)}) collective-permute-start(bf16[2,2,16,128]{3,2,1,0:T(8,128)(2,1)S(1)} %get-tuple-element.29), channel_id=1, source_target_pairs={{0,1},{1,0},{2,3},{3,2},{4,5},{5,4},{6,7},{7,6},{8,9},{9,8},{10,11... | collective-permute-start | bytes 49160 | tf_op jit(solution)/shard_map/ppermute | solution.py:287

commit v7 on v4

--- a/solution.py
+++ b/solution.py
@@ -61,8 +61,7 @@
     length = columns * share
     positions = pieces * length
     tiles = queries_ref.shape[0]
-    log2e = math.log2(math.e)
-    factor = score_scale * log2e
+    factor = score_scale
     across = (((1,), (1,)), ((), ()))
     along = (((1,), (0,)), ((), ()))
 
@@ -90,17 +89,17 @@
         top = scores[cuts[0]]
         for cut in cuts[1:]:
             top = jnp.maximum(top, scores[cut])
-        side_lse = lse_ref[tile] * log2e
+        side_lse = lse_ref[tile]
         peak = jnp.maximum(jnp.max(top, axis=0, keepdims=True) * factor, side_lse)
         total = None
         dotted = None
         for cut in cuts:
-            shifted = jnp.exp2(scores[cut] * factor - peak)
+            shifted = jnp.exp(scores[cut] * factor - peak)
             product = shifted * slopes[cut]
             scores[cut] = shifted
             total = shifted if total is None else total + shifted
             dotted = product if dotted is None else dotted + product
-        side = jnp.exp2(side_lse - peak)
+        side = jnp.exp(side_lse - peak)
         inverse = 1.0 / (jnp.sum(total, axis=0, keepdims=True) + side)
         delta = (jnp.sum(dotted, axis=0, keepdims=True) + side * dot_ref[tile]) * inverse
         for cut in cuts:

time: 44.6 us -> 44.7 us (level)
  transfers between devices with their start and end apart: 17 -> 17, of which waited for: 12 -> 11; matrix products, arithmetic and copies ran while one was open for 8% -> 8% of each run, Pallas kernels for 0% -> 0%
where the time goes in v7:
time: 44.7 us; the launch traced here: 44.3 us
  starting transfers between devices  18.4 us (41%)
  waiting for transfers between devices  11.4 us (26%)
  Pallas kernels  9.42 us (21%)
  local copies, waits for them, and re-layouts  4.33 us (10%)
  between operations  0.79 us (2%)
    ppermute x17, starting transfers between devices, swap(): lax.ppermute(value, axis, [(place, place ^ flip) for place in range(size)])  18.4 us
    ppermute x17, waiting for transfers between devices, swap(): lax.ppermute(value, axis, [(place, place ^ flip) for place in range(size)])  11.4 us
    pallas_call x1, Pallas kernels, attend(): pl.pallas_call(functools.partial(attend_kernel, score_scale, tiles // own...  7.93 us
    dynamic_slice x2, local copies, waits for them, and re-layouts, tiles_of(): part = lax.dynamic_slice_in_dim(part, first_group, own, 1)  2.69 us
    unnamed x12, local copies, waits for them, and re-layouts  1.3 us
    pallas_call x1, Pallas kernels, adam(): pl.pallas_call(functools.partial(adam_kernel, len(parts)), out_shape=(sha...  1.27 us
  transfers between devices with their start and end apart: 17, of which 11 were waited for; matrix products, arithmetic and copies ran while one was open for 8% of the time, Pallas kernels for 0%

profile of v7, /device:TPU:0, one launch (start us, length us, event | category | flops | bytes accessed | tf_op | source)
XLA Modules:
  0.0 44.3 jit_solution(384492845849075465)
XLA Ops:
  0.6 0.0 copy-start
  0.6 0.9 %copy-done = f32[16,2,8,128]{3,2,1,0:T(8,128)S(1)} copy-done((f32[16,2,8,128]{3,2,1,0:T(8,128)S(1)}, f32[16,2,8,128]{3,2,1,0:T(8,128)}, u32[]{:S(2)}) %copy-start) | copy-done | bytes 131096
  1.5 0.1 pack.1
  1.7 5.1 %collective-permute-start = (bf16[2,2,16,128]{3,2,1,0:T(8,128)(2,1)S(1)}, bf16[2,2,16,128]{3,2,1,0:T(8,128)(2,1)S(1)}, u32[]{:S(2)}, u32[]{:S(2)}) collective-permute-start(bf16[2,2,16,128]{3,2,1,0:T(8,128)(2,1)S(1)} %get-tuple-element.17), channel_id=1, source_target_pairs={{0,3},{1,2},{2,1},{3,0},{4,7},{5,6},{6,5},{7,4},{8,11},{9,10},{10,... | collective-permute-start | bytes 49160 | tf_op jit(solution)/shard_map/ppermute | solution.py:271
  6.8 0.0 collective-permute-start.1
  6.8 0.6 %collective-permute-start.2 = (bf16[2,2,16,128]{3,2,1,0:T(8,128)(2,1)S(1)}, bf16[2,2,16,128]{3,2,1,0:T(8,128)(2,1)S(1)}, u32[]{:S(2)}, u32[]{:S(2)}) collective-permute-start(bf16[2,2,16,128]{3,2,1,0:T(8,128)(2,1)S(1)} %get-tuple-element.19), channel_id=1, source_target_pairs={{0,1},{1,0},{2,3},{3,2},{4,5},{5,4},{6,7},{7,6},{8,9},{9,8},{10,11... | collective-permute-start | bytes 49160 | tf_op jit(solution)/shard_map/ppermute | solution.py:271
  7.4 1.1 %collective-permute-done = bf16[2,2,16,128]{3,2,1,0:T(8,128)(2,1)S(1)} collective-permute-done((bf16[2,2,16,128]{3,2,1,0:T(8,128)(2,1)S(1)}, bf16[2,2,16,128]{3,2,1,0:T(8,128)(2,1)S(1)}, u32[]{:S(2)}, u32[]{:S(2)}) %collective-permute-start) | collective-permute-done | bytes 16416 | tf_op jit(solution)/shard_map/ppermute | solution.py:271
  8.5 2.9 %collective-permute-done.1 = bf16[2,2,16,128]{3,2,1,0:T(8,128)(2,1)S(1)} collective-permute-done((bf16[2,2,16,128]{3,2,1,0:T(8,128)(2,1)S(1)}, bf16[2,2,16,128]{3,2,1,0:T(8,128)(2,1)S(1)}, u32[]{:S(2)}, u32[]{:S(2)}) %collective-permute-start.1) | collective-permute-done | bytes 16416 | tf_op jit(solution)/shard_map/ppermute | solution.py:271
  11.4 0.0 collective-permute-done.2
  11.5 2.5 %collective-permute-start.3 = (bf16[4,2,2,16,128]{4,3,2,1,0:T(8,128)(2,1)S(1)}, bf16[4,2,2,16,128]{4,3,2,1,0:T(8,128)(2,1)S(1)}, u32[]{:S(2)}, u32[]{:S(2)}) collective-permute-start(bf16[4,2,2,16,128]{4,3,2,1,0:T(8,128)(2,1)S(1)} %pad_maximum_fusion.refs_3_), channel_id=1, source_target_pairs={{0,24},{4,28},{8,16},{12,20},{16,8},{20,12},{24,0},{28,4},{1,25},{... | collective-permute-start | bytes 196616 | tf_op jit(solution)/shard_map/ppermute | solution.py:271
  14.0 0.5 %collective-permute-start.4 = (bf16[4,2,2,16,128]{4,3,2,1,0:T(8,128)(2,1)S(1)}, bf16[4,2,2,16,128]{4,3,2,1,0:T(8,128)(2,1)S(1)}, u32[]{:S(2)}, u32[]{:S(2)}) collective-permute-start(bf16[4,2,2,16,128]{4,3,2,1,0:T(8,128)(2,1)S(1)} %pad_maximum_fusion.refs_3_), channel_id=1, source_target_pairs={{0,16},{4,20},{8,24},{12,28},{16,0},{20,4},{24,8},{28,12},{1,17},{... | collective-permute-start | bytes 196616 | tf_op jit(solution)/shard_map/ppermute | solution.py:271
  14.5 0.5 %collective-permute-start.5 = (bf16[4,2,2,16,128]{4,3,2,1,0:T(8,128)(2,1)S(1)}, bf16[4,2,2,16,128]{4,3,2,1,0:T(8,128)(2,1)S(1)}, u32[]{:S(2)}, u32[]{:S(2)}) collective-permute-start(bf16[4,2,2,16,128]{4,3,2,1,0:T(8,128)(2,1)S(1)} %pad_maximum_fusion.refs_3_), channel_id=1, source_target_pairs={{0,8},{4,12},{8,0},{12,4},{16,24},{20,28},{24,16},{28,20},{1,9},{5... | collective-permute-start | bytes 196616 | tf_op jit(solution)/shard_map/ppermute | solution.py:271
  15.0 2.0 %constant_dynamic-slice_fusion.2 = (bf16[256,2,8,128]{3,2,1,0:T(8,128)(2,1)S(1)}, bf16[256,2,8,128]{3,2,1,0:T(8,128)(2,1)S(1)}) fusion(bf16[256,8,8,128]{3,2,1,0:T(8,128)(2,1)} %bitcast.21, s32[]{:T(128)S(6)} %select_n.9, bf16[256,8,8,128]{3,2,1,0:T(8,128)(2,1)} %bitcast.22), kind=kLoop, calls=%fused_computation.3 | loop fusion | bytes 4194308 | tf_op jit(solution)/shard_map/dynamic_slice | solution.py:304
  17.0 0.1 copy.20
  17.0 0.1 copy.21
  17.1 0.1 collective-permute-start.9
  17.2 0.1 collective-permute-done.3.refs_0_
  17.3 0.4 collective-permute-start.6
  17.7 0.5 %collective-permute-done.4.refs_1_ = bf16[4,2,2,16,128]{4,3,2,1,0:T(8,128)(2,1)S(1)} collective-permute-done((bf16[4,2,2,16,128]{4,3,2,1,0:T(8,128)(2,1)S(1)}, bf16[4,2,2,16,128]{4,3,2,1,0:T(8,128)(2,1)S(1)}, u32[]{:S(2)}, u32[]{:S(2)}) %collective-permute-start.4) | collective-permute-done | bytes 65568 | tf_op jit(solution)/shard_map/ppermute | solution.py:271
  18.2 0.0 collective-permute-start.7
  18.2 0.5 %collective-permute-done.5.refs_2_ = bf16[4,2,2,16,128]{4,3,2,1,0:T(8,128)(2,1)S(1)} collective-permute-done((bf16[4,2,2,16,128]{4,3,2,1,0:T(8,128)(2,1)S(1)}, bf16[4,2,2,16,128]{4,3,2,1,0:T(8,128)(2,1)S(1)}, u32[]{:S(2)}, u32[]{:S(2)}) %collective-permute-start.5) | collective-permute-done | bytes 65568 | tf_op jit(solution)/shard_map/ppermute | solution.py:271
  18.7 0.0 collective-permute-start.8
  18.7 0.7 %constant_dynamic-slice_fusion = (f32[256,2,8]{0,2,1:T(8,128)S(1)}, f32[256,2,8]{0,2,1:T(8,128)S(1)}) fusion(f32[256,8,8]{0,2,1:T(8,128)} %bitcast.26, s32[]{:T(128)S(6)} %select_n.9, f32[256,8,8]{0,2,1:T(8,128)} %bitcast.27), kind=kLoop, calls=%fused_computation.1 | loop fusion | bytes 65540 | tf_op jit(solution)/shard_map/dynamic_slice | solution.py:304
  19.5 0.1 copy.22
  19.6 0.2 broadcast_in_dim_reshape.8.refs_10_
  19.8 0.1 copy.23
  19.9 0.2 broadcast_in_dim_reshape.9.refs_11_
  20.1 0.0 collective-permute-done.9.refs_7_
  20.1 0.0 collective-permute-done.6.refs_4_
  20.1 0.0 collective-permute-done.7.refs_5_
  20.1 0.0 collective-permute-done.8.refs_6_
  20.1 0.0 copy-start.1
  20.2 0.0 copy-start.2
  20.2 0.0 copy-start.3
  20.2 7.9 %attend.1 = (f32[4,4,2,2,16,128]{5,4,3,2,1,0:T(8,128)S(1)}, bf16[4,4,2,2,16,128]{5,4,3,2,1,0:T(8,128)(2,1)S(1)}) custom-call(bf16[4,2,2,16,128]{4,3,2,1,0:T(8,128)(2,1)S(1)} %collective-permute-done.3.refs_0_, bf16[4,2,2,16,128]{4,3,2,1,0:T(8,128)(2,1)S(1)} %collective-permute-done.4.refs_1_, bf16[4,2,2,16,128]{4,3,2,1,0:T(8,128)(2,1)S(1)} %collective-permute-done.5.refs_2_, ...), custom_call_target="tpu_custom_call" | custom-call | flops 2147483648 | bytes 3145728 | tf_op jit(solution)/shard_map/attend/pallas_call | solution.py:163
  28.1 0.6 %collective-permute-start.10 = (bf16[4,4,2,2,16,128]{5,4,3,2,1,0:T(8,128)(2,1)S(1)}, bf16[4,4,2,2,16,128]{5,4,3,2,1,0:T(8,128)(2,1)S(1)}, u32[]{:S(2)}, u32[]{:S(2)}) collective-permute-start(bf16[4,4,2,2,16,128]{5,4,3,2,1,0:T(8,128)(2,1)S(1)} %get-tuple-element.22), channel_id=1, source_target_pairs={{0,4},{4,0},{8,12},{12,8},{16,20},{20,16},{24,28},{28,24},{1,5},{5... | collective-permute-start | bytes 786440 | tf_op jit(solution)/shard_map/ppermute | solution.py:271
  28.7 1.2 %collective-permute-done.10.mate_ref = bf16[4,4,2,2,16,128]{5,4,3,2,1,0:T(8,128)(2,1)S(1)} collective-permute-done((bf16[4,4,2,2,16,128]{5,4,3,2,1,0:T(8,128)(2,1)S(1)}, bf16[4,4,2,2,16,128]{5,4,3,2,1,0:T(8,128)(2,1)S(1)}, u32[]{:S(2)}, u32[]{:S(2)}) %collective-permute-start.10) | collective-permute-done | bytes 262176 | tf_op jit(solution)/shard_map/ppermute | solution.py:271
  29.9 1.9 %collective-permute-start.11 = (bf16[4,2,2,16,128]{4,3,2,1,0:T(8,128)(2,1)S(1)}, bf16[4,2,2,16,128]{4,3,2,1,0:T(8,128)(2,1)S(1)}, u32[]{:S(2)}, u32[]{:S(2)}) collective-permute-start(bf16[4,2,2,16,128]{4,3,2,1,0:T(8,128)(2,1)S(1)} %get-tuple-element.24), channel_id=1, source_target_pairs={{0,24},{4,28},{8,16},{12,20},{16,8},{20,12},{24,0},{28,4},{1,25},{... | collective-permute-start | bytes 196616 | tf_op jit(solution)/shard_map/ppermute | solution.py:271
  31.8 0.5 %collective-permute-start.12 = (bf16[4,2,2,16,128]{4,3,2,1,0:T(8,128)(2,1)S(1)}, bf16[4,2,2,16,128]{4,3,2,1,0:T(8,128)(2,1)S(1)}, u32[]{:S(2)}, u32[]{:S(2)}) collective-permute-start(bf16[4,2,2,16,128]{4,3,2,1,0:T(8,128)(2,1)S(1)} %get-tuple-element.25), channel_id=1, source_target_pairs={{0,16},{4,20},{8,24},{12,28},{16,0},{20,4},{24,8},{28,12},{1,17},{... | collective-permute-start | bytes 196616 | tf_op jit(solution)/shard_map/ppermute | solution.py:271
  32.3 1.2 %collective-permute-start.13 = (bf16[4,2,2,16,128]{4,3,2,1,0:T(8,128)(2,1)S(1)}, bf16[4,2,2,16,128]{4,3,2,1,0:T(8,128)(2,1)S(1)}, u32[]{:S(2)}, u32[]{:S(2)}) collective-permute-start(bf16[4,2,2,16,128]{4,3,2,1,0:T(8,128)(2,1)S(1)} %get-tuple-element.26), channel_id=1, source_target_pairs={{0,8},{4,12},{8,0},{12,4},{16,24},{20,28},{24,16},{28,20},{1,9},{5... | collective-permute-start | bytes 196616 | tf_op jit(solution)/shard_map/ppermute | solution.py:271
  33.5 1.9 %collective-permute-done.11.refs_0_ = bf16[4,2,2,16,128]{4,3,2,1,0:T(8,128)(2,1)S(1)} collective-permute-done((bf16[4,2,2,16,128]{4,3,2,1,0:T(8,128)(2,1)S(1)}, bf16[4,2,2,16,128]{4,3,2,1,0:T(8,128)(2,1)S(1)}, u32[]{:S(2)}, u32[]{:S(2)}) %collective-permute-start.11) | collective-permute-done | bytes 65568 | tf_op jit(solution)/shard_map/ppermute | solution.py:271
  35.3 1.3 %collective-permute-done.12.refs_1_ = bf16[4,2,2,16,128]{4,3,2,1,0:T(8,128)(2,1)S(1)} collective-permute-done((bf16[4,2,2,16,128]{4,3,2,1,0:T(8,128)(2,1)S(1)}, bf16[4,2,2,16,128]{4,3,2,1,0:T(8,128)(2,1)S(1)}, u32[]{:S(2)}, u32[]{:S(2)}) %collective-permute-start.12) | collective-permute-done | bytes 65568 | tf_op jit(solution)/shard_map/ppermute | solution.py:271
  36.6 0.0 collective-permute-done.13.refs_2_
  36.7 1.5 %collective-permute-start.14 = (bf16[2,2,16,128]{3,2,1,0:T(8,128)(2,1)S(1)}, bf16[2,2,16,128]{3,2,1,0:T(8,128)(2,1)S(1)}, u32[]{:S(2)}, u32[]{:S(2)}) collective-permute-start(bf16[2,2,16,128]{3,2,1,0:T(8,128)(2,1)S(1)} %get-tuple-element.27), channel_id=1, source_target_pairs={{0,3},{1,2},{2,1},{3,0},{4,7},{5,6},{6,5},{7,4},{8,11},{9,10},{10,... | collective-permute-start | bytes 49160 | tf_op jit(solution)/shard_map/ppermute | solution.py:271
  38.2 0.6 %collective-permute-start.15 = (bf16[2,2,16,128]{3,2,1,0:T(8,128)(2,1)S(1)}, bf16[2,2,16,128]{3,2,1,0:T(8,128)(2,1)S(1)}, u32[]{:S(2)}, u32[]{:S(2)}) collective-permute-start(bf16[2,2,16,128]{3,2,1,0:T(8,128)(2,1)S(1)} %get-tuple-element.28), channel_id=1, source_target_pairs={{0,2},{1,3},{2,0},{3,1},{4,6},{5,7},{6,4},{7,5},{8,10},{9,11},{10,... | collective-permute-start | bytes 49160 | tf_op jit(solution)/shard_map/ppermute | solution.py:271
  38.9 2.3 %collective-permute-start.16 = (bf16[2,2,16,128]{3,2,1,0:T(8,128)(2,1)S(1)}, bf16[2,2,16,128]{3,2,1,0:T(8,128)(2,1)S(1)}, u32[]{:S(2)}, u32[]{:S(2)}) collective-permute-start(bf16[2,2,16,128]{3,2,1,0:T(8,128)(2,1)S(1)} %get-tuple-element.29), channel_id=1, source_target_pairs={{0,1},{1,0},{2,3},{3,2},{4,5},{5,4},{6,7},{7,6},{8,9},{9,8},{10,11... | collective-permute-start | bytes 49160 | tf_op jit(solution)/shard_map/ppermute | solution.py:271
  41.2 1.2 %collective-permute-done.14.refs_0_ = bf16[2,2,16,128]{3,2,1,0:T(8,128)(2,1)S(1)} collective-permute-done((bf16[2,2,16,128]{3,2,1,0:T(8,128)(2,1)S(1)}, bf16[2,2,16,128]{3,2,1,0:T(8,128)(2,1)S(1)}, u32[]{:S(2)}, u32[]{:S(2)}) %collective-permute-start.14) | collective-permute-done | bytes 16416 | tf_op jit(solution)/shard_map/ppermute | solution.py:271
  42.3 0.6 %collective-permute-done.15.refs_1_ = bf16[2,2,16,128]{3,2,1,0:T(8,128)(2,1)S(1)} collective-permute-done((bf16[2,2,16,128]{3,2,1,0:T(8,128)(2,1)S(1)}, bf16[2,2,16,128]{3,2,1,0:T(8,128)(2,1)S(1)}, u32[]{:S(2)}, u32[]{:S(2)}) %collective-permute-start.15) | collective-permute-done | bytes 16416 | tf_op jit(solution)/shard_map/ppermute | solution.py:271
  42.9 0.2 collective-permute-done.16.refs_2_
  43.1 0.0 copy-done.1
  43.1 0.0 copy-done.2
  43.1 0.0 copy-done.3
  43.1 1.3 %adam.1 = (f32[16,2,8,128]{3,2,1,0:T(8,128)}, f32[16,2,8,128]{3,2,1,0:T(8,128)}, f32[16,2,8,128]{3,2,1,0:T(8,128)}) custom-call(bf16[2,2,16,128]{3,2,1,0:T(8,128)(2,1)S(1)} %collective-permute-done.14.refs_0_, bf16[2,2,16,128]{3,2,1,0:T(8,128)(2,1)S(1)} %collective-permute-done.15.refs_1_, bf16[2,2,16,128]{3,2,1,0:T(8,128)(2,1)S(1)} %collective-permute-done.16.refs_2_, ...), custom_call_target="tpu_custom_call" | custom-call | tf_op jit(solution)/shard_map/adam/pallas_call | solution.py:261
  (3 shorter events, 0.1 us)
Async XLA Ops:
  0.6 0.9 %copy-start = (f32[16,2,8,128]{3,2,1,0:T(8,128)S(1)}, f32[16,2,8,128]{3,2,1,0:T(8,128)}, u32[]{:S(2)}) copy-start(f32[16,2,8,128]{3,2,1,0:T(8,128)} %refs_4_.1) | copy-start | bytes 393220
  1.7 6.8 %collective-permute-start = (bf16[2,2,16,128]{3,2,1,0:T(8,128)(2,1)S(1)}, bf16[2,2,16,128]{3,2,1,0:T(8,128)(2,1)S(1)}, u32[]{:S(2)}, u32[]{:S(2)}) collective-permute-start(bf16[2,2,16,128]{3,2,1,0:T(8,128)(2,1)S(1)} %get-tuple-element.17), channel_id=1, source_target_pairs={{0,3},{1,2},{2,1},{3,0},{4,7},{5,6},{6,5},{7,4},{8,11},{9,10},{10,... | collective-permute-start | bytes 49160 | tf_op jit(solution)/shard_map/ppermute | solution.py:271
  6.8 4.6 %collective-permute-start.1 = (bf16[2,2,16,128]{3,2,1,0:T(8,128)(2,1)S(1)}, bf16[2,2,16,128]{3,2,1,0:T(8,128)(2,1)S(1)}, u32[]{:S(2)}, u32[]{:S(2)}) collective-permute-start(bf16[2,2,16,128]{3,2,1,0:T(8,128)(2,1)S(1)} %get-tuple-element.18), channel_id=1, source_target_pairs={{0,2},{1,3},{2,0},{3,1},{4,6},{5,7},{6,4},{7,5},{8,10},{9,11},{10,... | collective-permute-start | bytes 49160 | tf_op jit(solution)/shard_map/ppermute | solution.py:271
  6.8 4.6 %collective-permute-start.2 = (bf16[2,2,16,128]{3,2,1,0:T(8,128)(2,1)S(1)}, bf16[2,2,16,128]{3,2,1,0:T(8,128)(2,1)S(1)}, u32[]{:S(2)}, u32[]{:S(2)}) collective-permute-start(bf16[2,2,16,128]{3,2,1,0:T(8,128)(2,1)S(1)} %get-tuple-element.19), channel_id=1, source_target_pairs={{0,1},{1,0},{2,3},{3,2},{4,5},{5,4},{6,7},{7,6},{8,9},{9,8},{10,11... | collective-permute-start | bytes 49160 | tf_op jit(solution)/shard_map/ppermute | solution.py:271
  11.5 5.8 %collective-permute-start.3 = (bf16[4,2,2,16,128]{4,3,2,1,0:T(8,128)(2,1)S(1)}, bf16[4,2,2,16,128]{4,3,2,1,0:T(8,128)(2,1)S(1)}, u32[]{:S(2)}, u32[]{:S(2)}) collective-permute-start(bf16[4,2,2,16,128]{4,3,2,1,0:T(8,128)(2,1)S(1)} %pad_maximum_fusion.refs_3_), channel_id=1, source_target_pairs={{0,24},{4,28},{8,16},{12,20},{16,8},{20,12},{24,0},{28,4},{1,25},{... | collective-permute-start | bytes 196616 | tf_op jit(solution)/shard_map/ppermute | solution.py:271
  14.0 4.3 %collective-permute-start.4 = (bf16[4,2,2,16,128]{4,3,2,1,0:T(8,128)(2,1)S(1)}, bf16[4,2,2,16,128]{4,3,2,1,0:T(8,128)(2,1)S(1)}, u32[]{:S(2)}, u32[]{:S(2)}) collective-permute-start(bf16[4,2,2,16,128]{4,3,2,1,0:T(8,128)(2,1)S(1)} %pad_maximum_fusion.refs_3_), channel_id=1, source_target_pairs={{0,16},{4,20},{8,24},{12,28},{16,0},{20,4},{24,8},{28,12},{1,17},{... | collective-permute-start | bytes 196616 | tf_op jit(solution)/shard_map/ppermute | solution.py:271
  14.5 4.3 %collective-permute-start.5 = (bf16[4,2,2,16,128]{4,3,2,1,0:T(8,128)(2,1)S(1)}, bf16[4,2,2,16,128]{4,3,2,1,0:T(8,128)(2,1)S(1)}, u32[]{:S(2)}, u32[]{:S(2)}) collective-permute-start(bf16[4,2,2,16,128]{4,3,2,1,0:T(8,128)(2,1)S(1)} %pad_maximum_fusion.refs_3_), channel_id=1, source_target_pairs={{0,8},{4,12},{8,0},{12,4},{16,24},{20,28},{24,16},{28,20},{1,9},{5... | collective-permute-start | bytes 196616 | tf_op jit(solution)/shard_map/ppermute | solution.py:271
  17.1 3.0 %collective-permute-start.9 = (bf16[4,2,2,16,128]{4,3,2,1,0:T(8,128)(2,1)S(1)}, bf16[4,2,2,16,128]{4,3,2,1,0:T(8,128)(2,1)S(1)}, u32[]{:S(2)}, u32[]{:S(2)}) collective-permute-start(bf16[4,2,2,16,128]{4,3,2,1,0:T(8,128)(2,1)S(1)} %pad_maximum_fusion.refs_3_), channel_id=1, source_target_pairs={{0,4},{4,0},{8,12},{12,8},{16,20},{20,16},{24,28},{28,24},{1,5},{5... | collective-permute-start | bytes 196616 | tf_op jit(solution)/shard_map/ppermute | solution.py:271
  17.3 2.8 %collective-permute-start.6 = (bf16[4,2,2,16,128]{4,3,2,1,0:T(8,128)(2,1)S(1)}, bf16[4,2,2,16,128]{4,3,2,1,0:T(8,128)(2,1)S(1)}, u32[]{:S(2)}, u32[]{:S(2)}) collective-permute-start(bf16[4,2,2,16,128]{4,3,2,1,0:T(8,128)(2,1)S(1)} %collective-permute-done.3.refs_0_), channel_id=1, source_target_pairs={{0,4},{4,0},{8,12},{12,8},{16,20},{20,16},{24,28},{28,24},{1,5},{5... | collective-permute-start | bytes 196616 | tf_op jit(solution)/shard_map/ppermute | solution.py:271
  18.2 1.9 %collective-permute-start.7 = (bf16[4,2,2,16,128]{4,3,2,1,0:T(8,128)(2,1)S(1)}, bf16[4,2,2,16,128]{4,3,2,1,0:T(8,128)(2,1)S(1)}, u32[]{:S(2)}, u32[]{:S(2)}) collective-permute-start(bf16[4,2,2,16,128]{4,3,2,1,0:T(8,128)(2,1)S(1)} %collective-permute-done.4.refs_1_), channel_id=1, source_target_pairs={{0,4},{4,0},{8,12},{12,8},{16,20},{20,16},{24,28},{28,24},{1,5},{5... | collective-permute-start | bytes 196616 | tf_op jit(solution)/shard_map/ppermute | solution.py:271
  18.7 1.4 %collective-permute-start.8 = (bf16[4,2,2,16,128]{4,3,2,1,0:T(8,128)(2,1)S(1)}, bf16[4,2,2,16,128]{4,3,2,1,0:T(8,128)(2,1)S(1)}, u32[]{:S(2)}, u32[]{:S(2)}) collective-permute-start(bf16[4,2,2,16,128]{4,3,2,1,0:T(8,128)(2,1)S(1)} %collective-permute-done.5.refs_2_), channel_id=1, source_target_pairs={{0,4},{4,0},{8,12},{12,8},{16,20},{20,16},{24,28},{28,24},{1,5},{5... | collective-permute-start | bytes 196616 | tf_op jit(solution)/shard_map/ppermute | solution.py:271
  20.1 22.9 %copy-start.1 = (f32[16,2,8,128]{3,2,1,0:T(8,128)S(1)}, f32[16,2,8,128]{3,2,1,0:T(8,128)}, u32[]{:S(2)}) copy-start(f32[16,2,8,128]{3,2,1,0:T(8,128)} %refs_4_.1) | copy-start | bytes 393220
  20.2 22.9 %copy-start.2 = (f32[16,2,8,128]{3,2,1,0:T(8,128)S(1)}, f32[16,2,8,128]{3,2,1,0:T(8,128)}, u32[]{:S(2)}) copy-start(f32[16,2,8,128]{3,2,1,0:T(8,128)} %refs_5_.1) | copy-start | bytes 393220
  20.2 22.9 %copy-start.3 = (f32[16,2,8,128]{3,2,1,0:T(8,128)S(1)}, f32[16,2,8,128]{3,2,1,0:T(8,128)}, u32[]{:S(2)}) copy-start(f32[16,2,8,128]{3,2,1,0:T(8,128)} %refs_6_.1) | copy-start | bytes 393220
  28.1 1.7 %collective-permute-start.10 = (bf16[4,4,2,2,16,128]{5,4,3,2,1,0:T(8,128)(2,1)S(1)}, bf16[4,4,2,2,16,128]{5,4,3,2,1,0:T(8,128)(2,1)S(1)}, u32[]{:S(2)}, u32[]{:S(2)}) collective-permute-start(bf16[4,4,2,2,16,128]{5,4,3,2,1,0:T(8,128)(2,1)S(1)} %get-tuple-element.22), channel_id=1, source_target_pairs={{0,4},{4,0},{8,12},{12,8},{16,20},{20,16},{24,28},{28,24},{1,5},{5... | collective-permute-start | bytes 786440 | tf_op jit(solution)/shard_map/ppermute | solution.py:271
  29.9 5.4 %collective-permute-start.11 = (bf16[4,2,2,16,128]{4,3,2,1,0:T(8,128)(2,1)S(1)}, bf16[4,2,2,16,128]{4,3,2,1,0:T(8,128)(2,1)S(1)}, u32[]{:S(2)}, u32[]{:S(2)}) collective-permute-start(bf16[4,2,2,16,128]{4,3,2,1,0:T(8,128)(2,1)S(1)} %get-tuple-element.24), channel_id=1, source_target_pairs={{0,24},{4,28},{8,16},{12,20},{16,8},{20,12},{24,0},{28,4},{1,25},{... | collective-permute-start | bytes 196616 | tf_op jit(solution)/shard_map/ppermute | solution.py:271
  31.8 4.9 %collective-permute-start.12 = (bf16[4,2,2,16,128]{4,3,2,1,0:T(8,128)(2,1)S(1)}, bf16[4,2,2,16,128]{4,3,2,1,0:T(8,128)(2,1)S(1)}, u32[]{:S(2)}, u32[]{:S(2)}) collective-permute-start(bf16[4,2,2,16,128]{4,3,2,1,0:T(8,128)(2,1)S(1)} %get-tuple-element.25), channel_id=1, source_target_pairs={{0,16},{4,20},{8,24},{12,28},{16,0},{20,4},{24,8},{28,12},{1,17},{... | collective-permute-start | bytes 196616 | tf_op jit(solution)/shard_map/ppermute | solution.py:271
  32.3 4.4 %collective-permute-start.13 = (bf16[4,2,2,16,128]{4,3,2,1,0:T(8,128)(2,1)S(1)}, bf16[4,2,2,16,128]{4,3,2,1,0:T(8,128)(2,1)S(1)}, u32[]{:S(2)}, u32[]{:S(2)}) collective-permute-start(bf16[4,2,2,16,128]{4,3,2,1,0:T(8,128)(2,1)S(1)} %get-tuple-element.26), channel_id=1, source_target_pairs={{0,8},{4,12},{8,0},{12,4},{16,24},{20,28},{24,16},{28,20},{1,9},{5... | collective-permute-start | bytes 196616 | tf_op jit(solution)/shard_map/ppermute | solution.py:271
  36.7 5.6 %collective-permute-start.14 = (bf16[2,2,16,128]{3,2,1,0:T(8,128)(2,1)S(1)}, bf16[2,2,16,128]{3,2,1,0:T(8,128)(2,1)S(1)}, u32[]{:S(2)}, u32[]{:S(2)}) collective-permute-start(bf16[2,2,16,128]{3,2,1,0:T(8,128)(2,1)S(1)} %get-tuple-element.27), channel_id=1, source_target_pairs={{0,3},{1,2},{2,1},{3,0},{4,7},{5,6},{6,5},{7,4},{8,11},{9,10},{10,... | collective-permute-start | bytes 49160 | tf_op jit(solution)/shard_map/ppermute | solution.py:271
  38.2 4.7 %collective-permute-start.15 = (bf16[2,2,16,128]{3,2,1,0:T(8,128)(2,1)S(1)}, bf16[2,2,16,128]{3,2,1,0:T(8,128)(2,1)S(1)}, u32[]{:S(2)}, u32[]{:S(2)}) collective-permute-start(bf16[2,2,16,128]{3,2,1,0:T(8,128)(2,1)S(1)} %get-tuple-element.28), channel_id=1, source_target_pairs={{0,2},{1,3},{2,0},{3,1},{4,6},{5,7},{6,4},{7,5},{8,10},{9,11},{10,... | collective-permute-start | bytes 49160 | tf_op jit(solution)/shard_map/ppermute | solution.py:271
  38.9 4.2 %collective-permute-start.16 = (bf16[2,2,16,128]{3,2,1,0:T(8,128)(2,1)S(1)}, bf16[2,2,16,128]{3,2,1,0:T(8,128)(2,1)S(1)}, u32[]{:S(2)}, u32[]{:S(2)}) collective-permute-start(bf16[2,2,16,128]{3,2,1,0:T(8,128)(2,1)S(1)} %get-tuple-element.29), channel_id=1, source_target_pairs={{0,1},{1,0},{2,3},{3,2},{4,5},{5,4},{6,7},{7,6},{8,9},{9,8},{10,11... | collective-permute-start | bytes 49160 | tf_op jit(solution)/shard_map/ppermute | solution.py:271

commit v8 on v7

--- a/solution.py
+++ b/solution.py
@@ -52,108 +52,202 @@
     )(cache)
 
 
-def attend_kernel(score_scale, per_group, pieces, *refs):
-    pair_refs, refs = refs[:pieces], refs[pieces:]
-    queries_ref, grads_ref, lse_ref, dot_ref, mine_ref, mate_ref = refs[:6]
-    keys, values, key_total, value_total = refs[6:10]
-    even, odd = refs[10:14], refs[14:18]
+LOG2E = math.log2(math.e)
+ACROSS = (((1,), (1,)), ((), ()))
+ALONG = (((1,), (0,)), ((), ()))
+
+
+def load_pairs(pair_refs, keys, values):
     columns, _, own, share, width = pair_refs[0].shape
     length = columns * share
-    positions = pieces * length
-    tiles = queries_ref.shape[0]
-    factor = score_scale
-    across = (((1,), (1,)), ((), ()))
-    along = (((1,), (0,)), ((), ()))
-
     for piece, pair_ref in enumerate(pair_refs):
         at = pl.ds(piece * length, length)
         for slot in range(own):
             keys[slot, at] = pair_ref[:, 0, slot].reshape(length, width)
             values[slot, at] = pair_ref[:, 1, slot].reshape(length, width)
+
+
+def multiply(keys, values, queries, grads, scores, slopes):
+    scores[...] = lax.dot_general(keys, queries, ACROSS, preferred_element_type=jnp.float32)
+    slopes[...] = lax.dot_general(values, grads, ACROSS, preferred_element_type=jnp.float32)
+
+
+def cuts_of(ref):
+    return [pl.ds(start, CHUNK) for start in range(0, ref.shape[0], CHUNK)]
+
+
+def largest(scores):
+    cuts = cuts_of(scores)
+    top = scores[cuts[0]]
+    for cut in cuts[1:]:
+        top = jnp.maximum(top, scores[cut])
+    return jnp.max(top, axis=0, keepdims=True)
+
+
+def exponentiate(scores, slopes, factor, peak):
+    total = None
+    dotted = None
+    for cut in cuts_of(scores):
+        shifted = jnp.exp2(scores[cut] * factor - peak)
+        product = shifted * slopes[cut]
+        scores[cut] = shifted
+        total = shifted if total is None else total + shifted
+        dotted = product if dotted is None else dotted + product
+    return jnp.sum(total, axis=0, keepdims=True), jnp.sum(dotted, axis=0, keepdims=True)
+
+
+def weigh(shifted, slopes, inverse, delta, weights, dscores):
+    for cut in cuts_of(weights):
+        probability = shifted[cut] * inverse
+        weights[cut] = probability.astype(jnp.bfloat16)
+        dscores[cut] = (probability * (slopes[cut] - delta)).astype(jnp.bfloat16)
+
+
+def accumulate(key_total, value_total, slot, weights, dscores, queries, grads):
+    key_total[slot] += lax.dot_general(
+        dscores[...], queries, ALONG, preferred_element_type=jnp.float32
+    )
+    value_total[slot] += lax.dot_general(
+        weights[...], grads, ALONG, preferred_element_type=jnp.float32
+    )
+
+
+def first_half_kernel(score_scale, per_group, pieces, *refs):
+    pair_refs, refs = refs[:pieces], refs[pieces:]
+    queries_ref, grads_ref, lse_ref, dot_ref = refs[:4]
+    kept, (peak_ref, total_ref, dotted_ref, keys, values) = refs[4:8], refs[8:]
+    tiles = queries_ref.shape[0]
+    factor = score_scale * LOG2E
+    load_pairs(pair_refs, keys, values)
+
+    def place(tile, parity, step):
+        return kept[2 * parity].at[step], kept[2 * parity + 1].at[step]
+
+    def products(tile, parity, step):
+        slot = tile // per_group
+        multiply(
+            keys[slot], values[slot], queries_ref[tile], grads_ref[tile], *place(tile, parity, step)
+        )
+
+    def normalize(tile, parity, step):
+        scores, slopes = place(tile, parity, step)
+        side_lse = lse_ref[pl.ds(tile, 1)] * LOG2E
+        peak = jnp.maximum(largest(scores) * factor, side_lse)
+        total, dotted = exponentiate(scores, slopes, factor, peak)
+        side = jnp.exp2(side_lse - peak)
+        peak_ref[tile] = peak
+        total_ref[tile] = total + side
+        dotted_ref[tile] = dotted + side * dot_ref[pl.ds(tile, 1)]
+
+    products(0, 0, 0)
+
+    def two_tiles(step, carry):
+        products(2 * step + 1, 1, step)
+        normalize(2 * step, 0, step)
+        products(2 * step + 2, 0, step + 1)
+        normalize(2 * step + 1, 1, step)
+        return carry
+
+    last = tiles // 2 - 1
+    lax.fori_loop(0, last, two_tiles, 0)
+    products(tiles - 1, 1, last)
+    normalize(tiles - 2, 0, last)
+    normalize(tiles - 1, 1, last)
+
+
+def first_half(pairs, queries, grads, lse_rows, dot_rows, score_scale):
+    columns, _, own, share, width = pairs[0].shape
+    positions = len(pairs) * columns * share
+    tiles, row_tile, _ = queries.shape
+    kept = jax.ShapeDtypeStruct((tiles // 2, positions, row_tile), jnp.float32)
+    stat = jax.ShapeDtypeStruct((tiles, 1, row_tile), jnp.float32)
+    return pl.pallas_call(
+        functools.partial(first_half_kernel, score_scale, tiles // own, len(pairs)),
+        out_shape=[kept] * 4 + [stat] * 3,
+        scratch_shapes=[
+            pltpu.VMEM((own, positions, width), jnp.bfloat16),
+            pltpu.VMEM((own, positions, width), jnp.bfloat16),
+        ],
+        compiler_params=pltpu.CompilerParams(vmem_limit_bytes=30 * MIB),
+        cost_estimate=pl.CostEstimate(
+            flops=4 * tiles * row_tile * positions * width,
+            bytes_accessed=8 * tiles * row_tile * positions,
+            transcendentals=tiles * row_tile * positions,
+        ),
+        name="first_half",
+    )(*pairs, queries, grads, lse_rows, dot_rows)
+
+
+def second_half_kernel(score_scale, per_group, pieces, *refs):
+    pair_refs, refs = refs[:pieces], refs[pieces:]
+    queries_ref, grads_ref, peak_ref, total_ref, dotted_ref = refs[:5]
+    out_ref, inverse_ref, delta_ref = refs[5:8]
+    keys, values, key_total, value_total = refs[8:12]
+    even, odd = refs[12:16], refs[16:20]
+    _, columns, _, own, share, width = out_ref.shape
+    tiles = queries_ref.shape[0]
+    factor = score_scale * LOG2E
+    load_pairs(pair_refs, keys, values)
     key_total[...] = jnp.zeros_like(key_total)
     value_total[...] = jnp.zeros_like(value_total)
 
-    def multiply(tile, buffers):
-        scores, slopes, _, _ = buffers
+    def products(tile, buffers):
         slot = tile // per_group
-        scores[...] = lax.dot_general(
-            keys[slot], queries_ref[tile], across, preferred_element_type=jnp.float32
-        )
-        slopes[...] = lax.dot_general(
-            values[slot], grads_ref[tile], across, preferred_element_type=jnp.float32
-        )
+        multiply(keys[slot], values[slot], queries_ref[tile], grads_ref[tile], *buffers[:2])
 
     def normalize(tile, buffers):
         scores, slopes, weights, dscores = buffers
-        cuts = [pl.ds(start, CHUNK) for start in range(0, positions, CHUNK)]
-        top = scores[cuts[0]]
-        for cut in cuts[1:]:
-            top = jnp.maximum(top, scores[cut])
-        side_lse = lse_ref[tile]
-        peak = jnp.maximum(jnp.max(top, axis=0, keepdims=True) * factor, side_lse)
-        total = None
-        dotted = None
-        for cut in cuts:
-            shifted = jnp.exp(scores[cut] * factor - peak)
-            product = shifted * slopes[cut]
-            scores[cut] = shifted
-            total = shifted if total is None else total + shifted
-            dotted = product if dotted is None else dotted + product
-        side = jnp.exp(side_lse - peak)
-        inverse = 1.0 / (jnp.sum(total, axis=0, keepdims=True) + side)
-        delta = (jnp.sum(dotted, axis=0, keepdims=True) + side * dot_ref[tile]) * inverse
-        for cut in cuts:
-            probability = scores[cut] * inverse
-            weights[cut] = probability.astype(jnp.bfloat16)
-            dscores[cut] = (probability * (slopes[cut] - delta)).astype(jnp.bfloat16)
-
-    def accumulate(tile, buffers):
-        _, _, weights, dscores = buffers
-        slot = tile // per_group
-        key_total[slot] += lax.dot_general(
-            dscores[...], queries_ref[tile], along, preferred_element_type=jnp.float32
+        first_peak = peak_ref[tile]
+        peak = jnp.maximum(largest(scores) * factor, first_peak)
+        total, dotted = exponentiate(scores, slopes, factor, peak)
+        rescale = jnp.exp2(first_peak - peak)
+        inverse = 1.0 / (total + total_ref[tile] * rescale)
+        delta = (dotted + dotted_ref[tile] * rescale) * inverse
+        inverse_ref[tile] = inverse * rescale
+        delta_ref[tile] = delta
+        weigh(scores, slopes, inverse, delta, weights, dscores)
+
+    def gather(tile, buffers):
+        accumulate(
+            key_total,
+            value_total,
+            tile // per_group,
+            buffers[2],
+            buffers[3],
+            queries_ref[tile],
+            grads_ref[tile],
         )
-        value_total[slot] += lax.dot_general(
-            weights[...], grads_ref[tile], along, preferred_element_type=jnp.float32
-        )
-
-    multiply(0, even)
-    multiply(1, odd)
+
+    products(0, even)
+    products(1, odd)
     normalize(0, even)
 
     def two_tiles(step, carry):
         tile = step * 2
-        multiply(tile + 2, even)
+        products(tile + 2, even)
         normalize(tile + 1, odd)
-        accumulate(tile, even)
-        multiply(tile + 3, odd)
+        gather(tile, even)
+        products(tile + 3, odd)
         normalize(tile + 2, even)
-        accumulate(tile + 1, odd)
+        gather(tile + 1, odd)
         return carry
 
     lax.fori_loop(0, tiles // 2 - 1, two_tiles, 0)
     normalize(tiles - 1, odd)
-    accumulate(tiles - 2, even)
-    accumulate(tiles - 1, odd)
-
-    half = positions // 2
-    shape = mine_ref.shape[:2] + (share, width)
+    gather(tiles - 2, even)
+    gather(tiles - 1, odd)
+    shape = out_ref.shape[:2] + (share, width)
     for slot in range(own):
         key_sum = key_total[slot] * score_scale
-        value_sum = value_total[slot]
-        mine_ref[:, :, 0, slot] = key_sum[:half].reshape(shape)
-        mine_ref[:, :, 1, slot] = value_sum[:half].reshape(shape)
-        mate_ref[:, :, 0, slot] = key_sum[half:].astype(jnp.bfloat16).reshape(shape)
-        mate_ref[:, :, 1, slot] = value_sum[half:].astype(jnp.bfloat16).reshape(shape)
-
-
-def attend(pairs, queries, grads, lse_rows, dot_rows, score_scale):
+        out_ref[:, :, 0, slot] = key_sum.astype(jnp.bfloat16).reshape(shape)
+        out_ref[:, :, 1, slot] = value_total[slot].astype(jnp.bfloat16).reshape(shape)
+
+
+def second_half(pairs, queries, grads, stats, score_scale):
     columns, _, own, share, width = pairs[0].shape
-    pieces = len(pairs)
-    positions = pieces * columns * share
+    positions = len(pairs) * columns * share
     tiles, row_tile, _ = queries.shape
-    rows = tiles * row_tile
-    half = (pieces // 2, columns, 2, own, share, width)
+    stat = jax.ShapeDtypeStruct((tiles, 1, row_tile), jnp.float32)
     buffers = [
         pltpu.VMEM((positions, row_tile), jnp.float32),
         pltpu.VMEM((positions, row_tile), jnp.float32),
@@ -161,10 +255,11 @@
         pltpu.VMEM((positions, row_tile), jnp.bfloat16),
     ]
     return pl.pallas_call(
-        functools.partial(attend_kernel, score_scale, tiles // own, pieces),
+        functools.partial(second_half_kernel, score_scale, tiles // own, len(pairs)),
         out_shape=(
-            jax.ShapeDtypeStruct(half, jnp.float32),
-            jax.ShapeDtypeStruct(half, jnp.bfloat16),
+            jax.ShapeDtypeStruct((len(pairs),) + pairs[0].shape, jnp.bfloat16),
+            stat,
+            stat,
         ),
         scratch_shapes=[
             pltpu.VMEM((own, positions, width), jnp.bfloat16),
@@ -174,14 +269,86 @@
         ]
         + buffers
         + buffers,
-        compiler_params=pltpu.CompilerParams(vmem_limit_bytes=44 * MIB),
+        compiler_params=pltpu.CompilerParams(vmem_limit_bytes=30 * MIB),
         cost_estimate=pl.CostEstimate(
-            flops=8 * rows * positions * width,
-            bytes_accessed=4 * rows * width + 8 * own * positions * width,
-            transcendentals=rows * positions,
+            flops=8 * tiles * row_tile * positions * width,
+            bytes_accessed=4 * tiles * row_tile * width,
+            transcendentals=tiles * row_tile * positions,
         ),
-        name="attend",
-    )(*pairs, queries, grads, lse_rows, dot_rows)
+        name="second_half",
+    )(*pairs, queries, grads, *stats)
+
+
+def finish_kernel(score_scale, per_group, *refs):
+    kept, refs = refs[:4], refs[4:]
+    queries_ref, grads_ref, inverse_ref, delta_ref, out_ref = refs[:5]
+    key_total, value_total = refs[5:7]
+    even, odd = refs[7:9], refs[9:11]
+    _, columns, _, own, share, width = out_ref.shape
+    tiles = queries_ref.shape[0]
+    key_total[...] = jnp.zeros_like(key_total)
+    value_total[...] = jnp.zeros_like(value_total)
+
+    def spread(tile, parity, step, buffers):
+        weigh(
+            kept[2 * parity].at[step],
+            kept[2 * parity + 1].at[step],
+            inverse_ref[tile],
+            delta_ref[tile],
+            *buffers,
+        )
+
+    def gather(tile, buffers):
+        accumulate(
+            key_total,
+            value_total,
+            tile // per_group,
+            *buffers,
+            queries_ref[tile],
+            grads_ref[tile],
+        )
+
+    spread(0, 0, 0, even)
+
+    def two_tiles(step, carry):
+        spread(2 * step + 1, 1, step, odd)
+        gather(2 * step, even)
+        spread(2 * step + 2, 0, step + 1, even)
+        gather(2 * step + 1, odd)
+        return carry
+
+    last = tiles // 2 - 1
+    lax.fori_loop(0, last, two_tiles, 0)
+    spread(tiles - 1, 1, last, odd)
+    gather(tiles - 2, even)
+    gather(tiles - 1, odd)
+    shape = out_ref.shape[:2] + (share, width)
+    for slot in range(own):
+        out_ref[:, :, 0, slot] = (key_total[slot] * score_scale).reshape(shape)
+        out_ref[:, :, 1, slot] = value_total[slot].reshape(shape)
+
+
+def finish(kept, queries, grads, inverse, delta, shape, score_scale):
+    _, positions, row_tile = kept[0].shape
+    own, width = shape[3], shape[5]
+    tiles = queries.shape[0]
+    buffers = [pltpu.VMEM((positions, row_tile), jnp.bfloat16)] * 4
+    return pl.pallas_call(
+        functools.partial(finish_kernel, score_scale, tiles // own),
+        out_shape=jax.ShapeDtypeStruct(shape, jnp.float32),
+        scratch_shapes=[
+            pltpu.VMEM((own, positions, width), jnp.float32),
+            pltpu.VMEM((own, positions, width), jnp.float32),
+        ]
+        + buffers,
+        compiler_params=pltpu.CompilerParams(vmem_limit_bytes=30 * MIB),
+        cost_estimate=pl.CostEstimate(
+            flops=4 * tiles * row_tile * positions * width,
+            bytes_accessed=8 * tiles * row_tile * positions,
+            transcendentals=0,
+        ),
+        name="finish",
+    )(*kept, queries, grads, inverse, delta)
 
 
 def chip_sum_kernel(mine_ref, mate_ref, *outs):
@@ -296,23 +463,26 @@
     slices = pack(cache, columns, own)
     gathered = jnp.stack(swap_all(slices, "cache", columns, 1))
     pairs = swap_all([gathered] * chips, "dp", dp_size, 2)
-    pairs = pairs + [swap(pair, "dp", dp_size, 1) for pair in pairs]
-
     def tiles_of(array):
         parts = array.reshape((tokens, groups, group_size) + array.shape[2:])
         part = lax.dynamic_slice_in_dim(parts, first_token, own_tokens, 0)
         part = lax.dynamic_slice_in_dim(part, first_group, own, 1)
         return jnp.moveaxis(part, 1, 0).reshape((-1, ROW_TILE) + array.shape[2:])
 
-    mine, mate = attend(
-        pairs,
-        tiles_of(queries),
-        tiles_of(out_grad),
-        tiles_of(self_lse)[:, None],
-        tiles_of(self_dot)[:, None],
-        score_scale,
-    )
-    by_chip = chip_sum(mine, swap(mate, "dp", dp_size, 1))
+    tiles = [tiles_of(queries), tiles_of(out_grad)]
+    tiles += [tiles_of(self_lse), tiles_of(self_dot)]
+    own_pair, tiles = lax.optimization_barrier((pairs[-1], tiles))
+    query_tiles, grad_tiles, lse_rows, dot_rows = tiles
+    mate_pairs = [swap(pair, "dp", dp_size, 1) for pair in pairs[:-1] + [own_pair]]
+    *kept, peak, total, dotted = first_half(
+        pairs, query_tiles, grad_tiles, lse_rows, dot_rows, score_scale
+    )
+    mate, inverse, delta = second_half(
+        mate_pairs, query_tiles, grad_tiles, (peak, total, dotted), score_scale
+    )
+    from_mate = swap(mate, "dp", dp_size, 1)
+    mine = finish(kept, query_tiles, grad_tiles, inverse, delta, mate.shape, score_scale)
+    by_chip = chip_sum(mine, from_mate)
     *away, home = swap_all(by_chip, "dp", dp_size, 2)
     by_column = column_sum(home, away)
     parts = swap_all(by_column, "cache", columns, 1)

time: 44.7 us -> 44 us (0.984)
  waiting for transfers between devices: 11.4 us -> 9.47 us
  Pallas kernels: 9.42 us -> 10.6 us
    ppermute x17, waiting for transfers between devices: 11.4 us -> 9.47 us  [swap(): lax.ppermute(value, axis, [(place, place ^ flip) for place in range(size)])]
    pallas_call x1 -> x3, Pallas kernels: 7.93 us -> 9.09 us  [the longest x1 4.51 us: second_half(): pl.pallas_call(functools.partial(second_half_kernel, score_scale, tiles /...]
  transfers between devices with their start and end apart: 17 -> 17, of which waited for: 11 -> 7; matrix products, arithmetic and copies ran while one was open for 8% -> 8% of each run, Pallas kernels for 0% -> 11%
where the time goes in v8:
time: 44 us; the launch traced here: 43.6 us
  starting transfers between devices  18.4 us (42%)
  Pallas kernels  10.6 us (24%)
  waiting for transfers between devices  9.47 us (22%)
  local copies, waits for them, and re-layouts  4.31 us (10%)
  between operations  0.8 us (2%)
    ppermute x17, starting transfers between devices, swap(): lax.ppermute(value, axis, [(place, place ^ flip) for place in range(size)])  18.4 us
    ppermute x17, waiting for transfers between devices, swap(): lax.ppermute(value, axis, [(place, place ^ flip) for place in range(size)])  9.47 us
    pallas_call x1, Pallas kernels, second_half(): pl.pallas_call(functools.partial(second_half_kernel, score_scale, tiles /...  4.51 us
    pallas_call x1, Pallas kernels, first_half(): pl.pallas_call(functools.partial(first_half_kernel, score_scale, tiles //...  2.7 us
    dynamic_slice x2, local copies, waits for them, and re-layouts, tiles_of(): part = lax.dynamic_slice_in_dim(part, first_group, own, 1)  2.69 us
    pallas_call x1, Pallas kernels, finish(): pl.pallas_call(functools.partial(finish_kernel, score_scale, tiles // own...  1.89 us
    unnamed x12, local copies, waits for them, and re-layouts  1.3 us
    pallas_call x1, Pallas kernels, adam(): pl.pallas_call(functools.partial(adam_kernel, len(parts)), out_shape=(sha...  1.27 us
  transfers between devices with their start and end apart: 17, of which 7 were waited for; matrix products, arithmetic and copies ran while one was open for 8% of the time, Pallas kernels for 11%

profile of v8, /device:TPU:0, one launch (start us, length us, event | category | flops | bytes accessed | tf_op | source)
XLA Modules:
  0.0 43.6 jit_solution(9054909194207567309)
XLA Ops:
  0.6 0.0 copy-start
  0.6 0.9 %copy-done = f32[16,2,8,128]{3,2,1,0:T(8,128)S(1)} copy-done((f32[16,2,8,128]{3,2,1,0:T(8,128)S(1)}, f32[16,2,8,128]{3,2,1,0:T(8,128)}, u32[]{:S(2)}) %copy-start) | copy-done | bytes 131096
  1.5 0.1 pack.1
  1.7 5.1 %collective-permute-start = (bf16[2,2,16,128]{3,2,1,0:T(8,128)(2,1)S(1)}, bf16[2,2,16,128]{3,2,1,0:T(8,128)(2,1)S(1)}, u32[]{:S(2)}, u32[]{:S(2)}) collective-permute-start(bf16[2,2,16,128]{3,2,1,0:T(8,128)(2,1)S(1)} %get-tuple-element.30), channel_id=1, source_target_pairs={{0,3},{1,2},{2,1},{3,0},{4,7},{5,6},{6,5},{7,4},{8,11},{9,10},{10,... | collective-permute-start | bytes 49160 | tf_op jit(solution)/shard_map/ppermute | solution.py:438
  6.8 0.0 collective-permute-start.1
  6.8 0.6 %collective-permute-start.2 = (bf16[2,2,16,128]{3,2,1,0:T(8,128)(2,1)S(1)}, bf16[2,2,16,128]{3,2,1,0:T(8,128)(2,1)S(1)}, u32[]{:S(2)}, u32[]{:S(2)}) collective-permute-start(bf16[2,2,16,128]{3,2,1,0:T(8,128)(2,1)S(1)} %get-tuple-element.32), channel_id=1, source_target_pairs={{0,1},{1,0},{2,3},{3,2},{4,5},{5,4},{6,7},{7,6},{8,9},{9,8},{10,11... | collective-permute-start | bytes 49160 | tf_op jit(solution)/shard_map/ppermute | solution.py:438
  7.4 2.0 %constant_dynamic-slice_fusion.2 = (bf16[256,2,8,128]{3,2,1,0:T(8,128)(2,1)S(1)}, bf16[256,2,8,128]{3,2,1,0:T(8,128)(2,1)S(1)}) fusion(bf16[256,8,8,128]{3,2,1,0:T(8,128)(2,1)} %bitcast.25, s32[]{:T(128)S(6)} %select_n.9, bf16[256,8,8,128]{3,2,1,0:T(8,128)(2,1)} %bitcast.26), kind=kLoop, calls=%fused_computation.3 | loop fusion | bytes 4194308 | tf_op jit(solution)/shard_map/dynamic_slice | solution.py:469
  9.4 0.0 collective-permute-done
  9.4 2.0 %collective-permute-done.1 = bf16[2,2,16,128]{3,2,1,0:T(8,128)(2,1)S(1)} collective-permute-done((bf16[2,2,16,128]{3,2,1,0:T(8,128)(2,1)S(1)}, bf16[2,2,16,128]{3,2,1,0:T(8,128)(2,1)S(1)}, u32[]{:S(2)}, u32[]{:S(2)}) %collective-permute-start.1) | collective-permute-done | bytes 16416 | tf_op jit(solution)/shard_map/ppermute | solution.py:438
  11.4 0.0 collective-permute-done.2
  11.5 1.6 %collective-permute-start.5 = (bf16[4,2,2,16,128]{4,3,2,1,0:T(8,128)(2,1)S(1)}, bf16[4,2,2,16,128]{4,3,2,1,0:T(8,128)(2,1)S(1)}, u32[]{:S(2)}, u32[]{:S(2)}) collective-permute-start(bf16[4,2,2,16,128]{4,3,2,1,0:T(8,128)(2,1)S(1)} %pad_maximum_fusion.refs_3_), channel_id=1, source_target_pairs={{0,8},{4,12},{8,0},{12,4},{16,24},{20,28},{24,16},{28,20},{1,9},{5... | collective-permute-start | bytes 196616 | tf_op jit(solution)/shard_map/ppermute | solution.py:438
  13.0 1.5 %collective-permute-start.4 = (bf16[4,2,2,16,128]{4,3,2,1,0:T(8,128)(2,1)S(1)}, bf16[4,2,2,16,128]{4,3,2,1,0:T(8,128)(2,1)S(1)}, u32[]{:S(2)}, u32[]{:S(2)}) collective-permute-start(bf16[4,2,2,16,128]{4,3,2,1,0:T(8,128)(2,1)S(1)} %pad_maximum_fusion.refs_3_), channel_id=1, source_target_pairs={{0,16},{4,20},{8,24},{12,28},{16,0},{20,4},{24,8},{28,12},{1,17},{... | collective-permute-start | bytes 196616 | tf_op jit(solution)/shard_map/ppermute | solution.py:438
  14.5 0.5 %collective-permute-start.3 = (bf16[4,2,2,16,128]{4,3,2,1,0:T(8,128)(2,1)S(1)}, bf16[4,2,2,16,128]{4,3,2,1,0:T(8,128)(2,1)S(1)}, u32[]{:S(2)}, u32[]{:S(2)}) collective-permute-start(bf16[4,2,2,16,128]{4,3,2,1,0:T(8,128)(2,1)S(1)} %pad_maximum_fusion.refs_3_), channel_id=1, source_target_pairs={{0,24},{4,28},{8,16},{12,20},{16,8},{20,12},{24,0},{28,4},{1,25},{... | collective-permute-start | bytes 196616 | tf_op jit(solution)/shard_map/ppermute | solution.py:438
  15.0 0.7 %constant_dynamic-slice_fusion = (f32[256,2,8]{0,2,1:T(8,128)S(1)}, f32[256,2,8]{0,2,1:T(8,128)S(1)}) fusion(f32[256,8,8]{0,2,1:T(8,128)} %bitcast.30, s32[]{:T(128)S(6)} %select_n.9, f32[256,8,8]{0,2,1:T(8,128)} %bitcast.31), kind=kLoop, calls=%fused_computation.1 | loop fusion | bytes 65540 | tf_op jit(solution)/shard_map/dynamic_slice | solution.py:469
  15.7 0.1 copy.21
  15.9 0.2 reshape.37.refs_7_
  16.0 0.1 copy.20
  16.2 0.2 reshape.35.refs_6_
  16.3 0.1 copy.19
  16.4 0.1 copy.18
  16.5 0.1 collective-permute-start.9
  16.6 0.0 collective-permute-done.5.refs_2_
  16.6 0.5 %collective-permute-start.8 = (bf16[4,2,2,16,128]{4,3,2,1,0:T(8,128)(2,1)S(1)}, bf16[4,2,2,16,128]{4,3,2,1,0:T(8,128)(2,1)S(1)}, u32[]{:S(2)}, u32[]{:S(2)}) collective-permute-start(bf16[4,2,2,16,128]{4,3,2,1,0:T(8,128)(2,1)S(1)} %collective-permute-done.5.refs_2_), channel_id=1, source_target_pairs={{0,4},{4,0},{8,12},{12,8},{16,20},{20,16},{24,28},{28,24},{1,5},{5... | collective-permute-start | bytes 196616 | tf_op jit(solution)/shard_map/ppermute | solution.py:438
  17.1 0.5 %collective-permute-done.4.refs_1_ = bf16[4,2,2,16,128]{4,3,2,1,0:T(8,128)(2,1)S(1)} collective-permute-done((bf16[4,2,2,16,128]{4,3,2,1,0:T(8,128)(2,1)S(1)}, bf16[4,2,2,16,128]{4,3,2,1,0:T(8,128)(2,1)S(1)}, u32[]{:S(2)}, u32[]{:S(2)}) %collective-permute-start.4) | collective-permute-done | bytes 65568 | tf_op jit(solution)/shard_map/ppermute | solution.py:438
  17.5 0.0 collective-permute-start.7
  17.5 2.1 %collective-permute-done.3.refs_0_ = bf16[4,2,2,16,128]{4,3,2,1,0:T(8,128)(2,1)S(1)} collective-permute-done((bf16[4,2,2,16,128]{4,3,2,1,0:T(8,128)(2,1)S(1)}, bf16[4,2,2,16,128]{4,3,2,1,0:T(8,128)(2,1)S(1)}, u32[]{:S(2)}, u32[]{:S(2)}) %collective-permute-start.3) | collective-permute-done | bytes 65568 | tf_op jit(solution)/shard_map/ppermute | solution.py:438
  19.7 0.0 collective-permute-start.6
  19.7 2.7 %first_half.1 = (f32[4,256,512]{2,1,0:T(8,128)S(1)}, f32[4,256,512]{2,1,0:T(8,128)S(1)}, f32[4,256,512]{2,1,0:T(8,128)S(1)}, f32[4,256,512]{2,1,0:T(8,128)S(1)},...) custom-call(bf16[4,2,2,16,128]{4,3,2,1,0:T(8,128)(2,1)S(1)} %collective-permute-done.3.refs_0_, ...), custom_call_target="tpu_custom_call" | custom-call | flops 536870912 | bytes 8388608 | tf_op jit(solution)/shard_map/first_half/pallas_call | solution.py:164
  22.4 0.0 collective-permute-done.9.refs_3_
  22.4 0.0 collective-permute-done.8.refs_2_
  22.4 0.0 collective-permute-done.7.refs_1_
  22.4 0.0 collective-permute-done.6.refs_0_
  22.4 4.5 %second_half.1 = (bf16[4,4,2,2,16,128]{5,4,3,2,1,0:T(8,128)(2,1)S(1)}, f32[8,1,512]{2,1,0:T(1,128)S(1)}, f32[8,1,512]{2,1,0:T(1,128)S(1)}) custom-call(bf16[4,2,2,16,128]{4,3,2,1,0:T(8,128)(2,1)S(1)} %collective-permute-done.6.refs_0_, bf16[4,2,2,16,128]{4,3,2,1,0:T(8,128)(2,1)S(1)} %collective-permute-done.7.refs_1_, ...), custom_call_target="tpu_custom_call" | custom-call | flops 1073741824 | bytes 2097152 | tf_op jit(solution)/shard_map/second_half/pallas_call | solution.py:257
  27.0 0.6 %collective-permute-start.10 = (bf16[4,4,2,2,16,128]{5,4,3,2,1,0:T(8,128)(2,1)S(1)}, bf16[4,4,2,2,16,128]{5,4,3,2,1,0:T(8,128)(2,1)S(1)}, u32[]{:S(2)}, u32[]{:S(2)}) collective-permute-start(bf16[4,4,2,2,16,128]{5,4,3,2,1,0:T(8,128)(2,1)S(1)} %get-tuple-element.48), channel_id=1, source_target_pairs={{0,4},{4,0},{8,12},{12,8},{16,20},{20,16},{24,28},{28,24},{1,5},{5... | collective-permute-start | bytes 786440 | tf_op jit(solution)/shard_map/ppermute | solution.py:438
  27.5 0.0 copy-start.1
  27.5 0.0 copy-start.2
  27.5 0.0 copy-start.3
  27.5 1.9 %finish.1.mine_ref = f32[4,4,2,2,16,128]{5,4,3,2,1,0:T(8,128)S(1)} custom-call(f32[4,256,512]{2,1,0:T(8,128)S(1)} %get-tuple-element.38.refs_0_, f32[4,256,512]{2,1,0:T(8,128)S(1)} %get-tuple-element.39.refs_1_, f32[4,256,512]{2,1,0:T(8,128)S(1)} %get-tuple-element.40.refs_2_, f32[4,256,512]{2,1,0:T(8,128)S(1)} %get-tuple-element.41.refs_3_, ...), custom_call_target="tpu_custom_call" | custom-call | flops 536870912 | bytes 8388608 | tf_op jit(solution)/shard_map/finish/pallas_call | solution.py:336
  29.4 0.0 collective-permute-done.10.mate_ref
  29.5 0.5 %collective-permute-start.11 = (bf16[4,2,2,16,128]{4,3,2,1,0:T(8,128)(2,1)S(1)}, bf16[4,2,2,16,128]{4,3,2,1,0:T(8,128)(2,1)S(1)}, u32[]{:S(2)}, u32[]{:S(2)}) collective-permute-start(bf16[4,2,2,16,128]{4,3,2,1,0:T(8,128)(2,1)S(1)} %get-tuple-element.50), channel_id=1, source_target_pairs={{0,24},{4,28},{8,16},{12,20},{16,8},{20,12},{24,0},{28,4},{1,25},{... | collective-permute-start | bytes 196616 | tf_op jit(solution)/shard_map/ppermute | solution.py:438
  30.0 1.5 %collective-permute-start.12 = (bf16[4,2,2,16,128]{4,3,2,1,0:T(8,128)(2,1)S(1)}, bf16[4,2,2,16,128]{4,3,2,1,0:T(8,128)(2,1)S(1)}, u32[]{:S(2)}, u32[]{:S(2)}) collective-permute-start(bf16[4,2,2,16,128]{4,3,2,1,0:T(8,128)(2,1)S(1)} %get-tuple-element.51), channel_id=1, source_target_pairs={{0,16},{4,20},{8,24},{12,28},{16,0},{20,4},{24,8},{28,12},{1,17},{... | collective-permute-start | bytes 196616 | tf_op jit(solution)/shard_map/ppermute | solution.py:438
  31.6 1.5 %collective-permute-start.13 = (bf16[4,2,2,16,128]{4,3,2,1,0:T(8,128)(2,1)S(1)}, bf16[4,2,2,16,128]{4,3,2,1,0:T(8,128)(2,1)S(1)}, u32[]{:S(2)}, u32[]{:S(2)}) collective-permute-start(bf16[4,2,2,16,128]{4,3,2,1,0:T(8,128)(2,1)S(1)} %get-tuple-element.52), channel_id=1, source_target_pairs={{0,8},{4,12},{8,0},{12,4},{16,24},{20,28},{24,16},{28,20},{1,9},{5... | collective-permute-start | bytes 196616 | tf_op jit(solution)/shard_map/ppermute | solution.py:438
  33.0 2.2 %collective-permute-done.11.refs_0_ = bf16[4,2,2,16,128]{4,3,2,1,0:T(8,128)(2,1)S(1)} collective-permute-done((bf16[4,2,2,16,128]{4,3,2,1,0:T(8,128)(2,1)S(1)}, bf16[4,2,2,16,128]{4,3,2,1,0:T(8,128)(2,1)S(1)}, u32[]{:S(2)}, u32[]{:S(2)}) %collective-permute-start.11) | collective-permute-done | bytes 65568 | tf_op jit(solution)/shard_map/ppermute | solution.py:438
  35.2 0.0 collective-permute-done.12.refs_1_
  35.2 0.6 %collective-permute-done.13.refs_2_ = bf16[4,2,2,16,128]{4,3,2,1,0:T(8,128)(2,1)S(1)} collective-permute-done((bf16[4,2,2,16,128]{4,3,2,1,0:T(8,128)(2,1)S(1)}, bf16[4,2,2,16,128]{4,3,2,1,0:T(8,128)(2,1)S(1)}, u32[]{:S(2)}, u32[]{:S(2)}) %collective-permute-start.13) | collective-permute-done | bytes 65568 | tf_op jit(solution)/shard_map/ppermute | solution.py:438
  35.9 1.8 %collective-permute-start.14 = (bf16[2,2,16,128]{3,2,1,0:T(8,128)(2,1)S(1)}, bf16[2,2,16,128]{3,2,1,0:T(8,128)(2,1)S(1)}, u32[]{:S(2)}, u32[]{:S(2)}) collective-permute-start(bf16[2,2,16,128]{3,2,1,0:T(8,128)(2,1)S(1)} %get-tuple-element.53), channel_id=1, source_target_pairs={{0,3},{1,2},{2,1},{3,0},{4,7},{5,6},{6,5},{7,4},{8,11},{9,10},{10,... | collective-permute-start | bytes 49160 | tf_op jit(solution)/shard_map/ppermute | solution.py:438
  37.7 0.3 collective-permute-start.15
  38.0 2.3 %collective-permute-start.16 = (bf16[2,2,16,128]{3,2,1,0:T(8,128)(2,1)S(1)}, bf16[2,2,16,128]{3,2,1,0:T(8,128)(2,1)S(1)}, u32[]{:S(2)}, u32[]{:S(2)}) collective-permute-start(bf16[2,2,16,128]{3,2,1,0:T(8,128)(2,1)S(1)} %get-tuple-element.55), channel_id=1, source_target_pairs={{0,1},{1,0},{2,3},{3,2},{4,5},{5,4},{6,7},{7,6},{8,9},{9,8},{10,11... | collective-permute-start | bytes 49160 | tf_op jit(solution)/shard_map/ppermute | solution.py:438
  40.3 1.1 %collective-permute-done.14.refs_0_ = bf16[2,2,16,128]{3,2,1,0:T(8,128)(2,1)S(1)} collective-permute-done((bf16[2,2,16,128]{3,2,1,0:T(8,128)(2,1)S(1)}, bf16[2,2,16,128]{3,2,1,0:T(8,128)(2,1)S(1)}, u32[]{:S(2)}, u32[]{:S(2)}) %collective-permute-start.14) | collective-permute-done | bytes 16416 | tf_op jit(solution)/shard_map/ppermute | solution.py:438
  41.5 0.9 %collective-permute-done.15.refs_1_ = bf16[2,2,16,128]{3,2,1,0:T(8,128)(2,1)S(1)} collective-permute-done((bf16[2,2,16,128]{3,2,1,0:T(8,128)(2,1)S(1)}, bf16[2,2,16,128]{3,2,1,0:T(8,128)(2,1)S(1)}, u32[]{:S(2)}, u32[]{:S(2)}) %collective-permute-start.15) | collective-permute-done | bytes 16416 | tf_op jit(solution)/shard_map/ppermute | solution.py:438
  42.3 0.0 collective-permute-done.16.refs_2_
  42.3 0.0 copy-done.1
  42.3 0.0 copy-done.2
  42.3 0.0 copy-done.3
  42.4 1.3 %adam.1 = (f32[16,2,8,128]{3,2,1,0:T(8,128)}, f32[16,2,8,128]{3,2,1,0:T(8,128)}, f32[16,2,8,128]{3,2,1,0:T(8,128)}) custom-call(bf16[2,2,16,128]{3,2,1,0:T(8,128)(2,1)S(1)} %collective-permute-done.14.refs_0_, bf16[2,2,16,128]{3,2,1,0:T(8,128)(2,1)S(1)} %collective-permute-done.15.refs_1_, bf16[2,2,16,128]{3,2,1,0:T(8,128)(2,1)S(1)} %collective-permute-done.16.refs_2_, ...), custom_call_target="tpu_custom_call" | custom-call | tf_op jit(solution)/shard_map/adam/pallas_call | solution.py:428
  (3 shorter events, 0.1 us)
Async XLA Ops:
  0.6 0.9 %copy-start = (f32[16,2,8,128]{3,2,1,0:T(8,128)S(1)}, f32[16,2,8,128]{3,2,1,0:T(8,128)}, u32[]{:S(2)}) copy-start(f32[16,2,8,128]{3,2,1,0:T(8,128)} %refs_4_.1) | copy-start | bytes 393220
  1.7 7.7 %collective-permute-start = (bf16[2,2,16,128]{3,2,1,0:T(8,128)(2,1)S(1)}, bf16[2,2,16,128]{3,2,1,0:T(8,128)(2,1)S(1)}, u32[]{:S(2)}, u32[]{:S(2)}) collective-permute-start(bf16[2,2,16,128]{3,2,1,0:T(8,128)(2,1)S(1)} %get-tuple-element.30), channel_id=1, source_target_pairs={{0,3},{1,2},{2,1},{3,0},{4,7},{5,6},{6,5},{7,4},{8,11},{9,10},{10,... | collective-permute-start | bytes 49160 | tf_op jit(solution)/shard_map/ppermute | solution.py:438
  6.8 4.6 %collective-permute-start.1 = (bf16[2,2,16,128]{3,2,1,0:T(8,128)(2,1)S(1)}, bf16[2,2,16,128]{3,2,1,0:T(8,128)(2,1)S(1)}, u32[]{:S(2)}, u32[]{:S(2)}) collective-permute-start(bf16[2,2,16,128]{3,2,1,0:T(8,128)(2,1)S(1)} %get-tuple-element.31), channel_id=1, source_target_pairs={{0,2},{1,3},{2,0},{3,1},{4,6},{5,7},{6,4},{7,5},{8,10},{9,11},{10,... | collective-permute-start | bytes 49160 | tf_op jit(solution)/shard_map/ppermute | solution.py:438
  6.8 4.6 %collective-permute-start.2 = (bf16[2,2,16,128]{3,2,1,0:T(8,128)(2,1)S(1)}, bf16[2,2,16,128]{3,2,1,0:T(8,128)(2,1)S(1)}, u32[]{:S(2)}, u32[]{:S(2)}) collective-permute-start(bf16[2,2,16,128]{3,2,1,0:T(8,128)(2,1)S(1)} %get-tuple-element.32), channel_id=1, source_target_pairs={{0,1},{1,0},{2,3},{3,2},{4,5},{5,4},{6,7},{7,6},{8,9},{9,8},{10,11... | collective-permute-start | bytes 49160 | tf_op jit(solution)/shard_map/ppermute | solution.py:438
  11.5 5.1 %collective-permute-start.5 = (bf16[4,2,2,16,128]{4,3,2,1,0:T(8,128)(2,1)S(1)}, bf16[4,2,2,16,128]{4,3,2,1,0:T(8,128)(2,1)S(1)}, u32[]{:S(2)}, u32[]{:S(2)}) collective-permute-start(bf16[4,2,2,16,128]{4,3,2,1,0:T(8,128)(2,1)S(1)} %pad_maximum_fusion.refs_3_), channel_id=1, source_target_pairs={{0,8},{4,12},{8,0},{12,4},{16,24},{20,28},{24,16},{28,20},{1,9},{5... | collective-permute-start | bytes 196616 | tf_op jit(solution)/shard_map/ppermute | solution.py:438
  13.0 4.5 %collective-permute-start.4 = (bf16[4,2,2,16,128]{4,3,2,1,0:T(8,128)(2,1)S(1)}, bf16[4,2,2,16,128]{4,3,2,1,0:T(8,128)(2,1)S(1)}, u32[]{:S(2)}, u32[]{:S(2)}) collective-permute-start(bf16[4,2,2,16,128]{4,3,2,1,0:T(8,128)(2,1)S(1)} %pad_maximum_fusion.refs_3_), channel_id=1, source_target_pairs={{0,16},{4,20},{8,24},{12,28},{16,0},{20,4},{24,8},{28,12},{1,17},{... | collective-permute-start | bytes 196616 | tf_op jit(solution)/shard_map/ppermute | solution.py:438
  14.5 5.2 %collective-permute-start.3 = (bf16[4,2,2,16,128]{4,3,2,1,0:T(8,128)(2,1)S(1)}, bf16[4,2,2,16,128]{4,3,2,1,0:T(8,128)(2,1)S(1)}, u32[]{:S(2)}, u32[]{:S(2)}) collective-permute-start(bf16[4,2,2,16,128]{4,3,2,1,0:T(8,128)(2,1)S(1)} %pad_maximum_fusion.refs_3_), channel_id=1, source_target_pairs={{0,24},{4,28},{8,16},{12,20},{16,8},{20,12},{24,0},{28,4},{1,25},{... | collective-permute-start | bytes 196616 | tf_op jit(solution)/shard_map/ppermute | solution.py:438
  16.5 5.9 %collective-permute-start.9 = (bf16[4,2,2,16,128]{4,3,2,1,0:T(8,128)(2,1)S(1)}, bf16[4,2,2,16,128]{4,3,2,1,0:T(8,128)(2,1)S(1)}, u32[]{:S(2)}, u32[]{:S(2)}) collective-permute-start(bf16[4,2,2,16,128]{4,3,2,1,0:T(8,128)(2,1)S(1)} %pad_maximum_fusion.refs_3_), channel_id=1, source_target_pairs={{0,4},{4,0},{8,12},{12,8},{16,20},{20,16},{24,28},{28,24},{1,5},{5... | collective-permute-start | bytes 196616 | tf_op jit(solution)/shard_map/ppermute | solution.py:438
  16.6 5.8 %collective-permute-start.8 = (bf16[4,2,2,16,128]{4,3,2,1,0:T(8,128)(2,1)S(1)}, bf16[4,2,2,16,128]{4,3,2,1,0:T(8,128)(2,1)S(1)}, u32[]{:S(2)}, u32[]{:S(2)}) collective-permute-start(bf16[4,2,2,16,128]{4,3,2,1,0:T(8,128)(2,1)S(1)} %collective-permute-done.5.refs_2_), channel_id=1, source_target_pairs={{0,4},{4,0},{8,12},{12,8},{16,20},{20,16},{24,28},{28,24},{1,5},{5... | collective-permute-start | bytes 196616 | tf_op jit(solution)/shard_map/ppermute | solution.py:438
  17.5 4.9 %collective-permute-start.7 = (bf16[4,2,2,16,128]{4,3,2,1,0:T(8,128)(2,1)S(1)}, bf16[4,2,2,16,128]{4,3,2,1,0:T(8,128)(2,1)S(1)}, u32[]{:S(2)}, u32[]{:S(2)}) collective-permute-start(bf16[4,2,2,16,128]{4,3,2,1,0:T(8,128)(2,1)S(1)} %collective-permute-done.4.refs_1_), channel_id=1, source_target_pairs={{0,4},{4,0},{8,12},{12,8},{16,20},{20,16},{24,28},{28,24},{1,5},{5... | collective-permute-start | bytes 196616 | tf_op jit(solution)/shard_map/ppermute | solution.py:438
  19.7 2.7 %collective-permute-start.6 = (bf16[4,2,2,16,128]{4,3,2,1,0:T(8,128)(2,1)S(1)}, bf16[4,2,2,16,128]{4,3,2,1,0:T(8,128)(2,1)S(1)}, u32[]{:S(2)}, u32[]{:S(2)}) collective-permute-start(bf16[4,2,2,16,128]{4,3,2,1,0:T(8,128)(2,1)S(1)} %collective-permute-done.3.refs_0_), channel_id=1, source_target_pairs={{0,4},{4,0},{8,12},{12,8},{16,20},{20,16},{24,28},{28,24},{1,5},{5... | collective-permute-start | bytes 196616 | tf_op jit(solution)/shard_map/ppermute | solution.py:438
  27.0 2.5 %collective-permute-start.10 = (bf16[4,4,2,2,16,128]{5,4,3,2,1,0:T(8,128)(2,1)S(1)}, bf16[4,4,2,2,16,128]{5,4,3,2,1,0:T(8,128)(2,1)S(1)}, u32[]{:S(2)}, u32[]{:S(2)}) collective-permute-start(bf16[4,4,2,2,16,128]{5,4,3,2,1,0:T(8,128)(2,1)S(1)} %get-tuple-element.48), channel_id=1, source_target_pairs={{0,4},{4,0},{8,12},{12,8},{16,20},{20,16},{24,28},{28,24},{1,5},{5... | collective-permute-start | bytes 786440 | tf_op jit(solution)/shard_map/ppermute | solution.py:438
  27.5 14.8 %copy-start.1 = (f32[16,2,8,128]{3,2,1,0:T(8,128)S(1)}, f32[16,2,8,128]{3,2,1,0:T(8,128)}, u32[]{:S(2)}) copy-start(f32[16,2,8,128]{3,2,1,0:T(8,128)} %refs_4_.1) | copy-start | bytes 393220
  27.5 14.8 %copy-start.2 = (f32[16,2,8,128]{3,2,1,0:T(8,128)S(1)}, f32[16,2,8,128]{3,2,1,0:T(8,128)}, u32[]{:S(2)}) copy-start(f32[16,2,8,128]{3,2,1,0:T(8,128)} %refs_5_.1) | copy-start | bytes 393220
  27.5 14.8 %copy-start.3 = (f32[16,2,8,128]{3,2,1,0:T(8,128)S(1)}, f32[16,2,8,128]{3,2,1,0:T(8,128)}, u32[]{:S(2)}) copy-start(f32[16,2,8,128]{3,2,1,0:T(8,128)} %refs_6_.1) | copy-start | bytes 393220
  29.5 5.7 %collective-permute-start.11 = (bf16[4,2,2,16,128]{4,3,2,1,0:T(8,128)(2,1)S(1)}, bf16[4,2,2,16,128]{4,3,2,1,0:T(8,128)(2,1)S(1)}, u32[]{:S(2)}, u32[]{:S(2)}) collective-permute-start(bf16[4,2,2,16,128]{4,3,2,1,0:T(8,128)(2,1)S(1)} %get-tuple-element.50), channel_id=1, source_target_pairs={{0,24},{4,28},{8,16},{12,20},{16,8},{20,12},{24,0},{28,4},{1,25},{... | collective-permute-start | bytes 196616 | tf_op jit(solution)/shard_map/ppermute | solution.py:438
  30.0 5.2 %collective-permute-start.12 = (bf16[4,2,2,16,128]{4,3,2,1,0:T(8,128)(2,1)S(1)}, bf16[4,2,2,16,128]{4,3,2,1,0:T(8,128)(2,1)S(1)}, u32[]{:S(2)}, u32[]{:S(2)}) collective-permute-start(bf16[4,2,2,16,128]{4,3,2,1,0:T(8,128)(2,1)S(1)} %get-tuple-element.51), channel_id=1, source_target_pairs={{0,16},{4,20},{8,24},{12,28},{16,0},{20,4},{24,8},{28,12},{1,17},{... | collective-permute-start | bytes 196616 | tf_op jit(solution)/shard_map/ppermute | solution.py:438
  31.6 4.3 %collective-permute-start.13 = (bf16[4,2,2,16,128]{4,3,2,1,0:T(8,128)(2,1)S(1)}, bf16[4,2,2,16,128]{4,3,2,1,0:T(8,128)(2,1)S(1)}, u32[]{:S(2)}, u32[]{:S(2)}) collective-permute-start(bf16[4,2,2,16,128]{4,3,2,1,0:T(8,128)(2,1)S(1)} %get-tuple-element.52), channel_id=1, source_target_pairs={{0,8},{4,12},{8,0},{12,4},{16,24},{20,28},{24,16},{28,20},{1,9},{5... | collective-permute-start | bytes 196616 | tf_op jit(solution)/shard_map/ppermute | solution.py:438
  35.9 5.6 %collective-permute-start.14 = (bf16[2,2,16,128]{3,2,1,0:T(8,128)(2,1)S(1)}, bf16[2,2,16,128]{3,2,1,0:T(8,128)(2,1)S(1)}, u32[]{:S(2)}, u32[]{:S(2)}) collective-permute-start(bf16[2,2,16,128]{3,2,1,0:T(8,128)(2,1)S(1)} %get-tuple-element.53), channel_id=1, source_target_pairs={{0,3},{1,2},{2,1},{3,0},{4,7},{5,6},{6,5},{7,4},{8,11},{9,10},{10,... | collective-permute-start | bytes 49160 | tf_op jit(solution)/shard_map/ppermute | solution.py:438
  37.7 4.6 %collective-permute-start.15 = (bf16[2,2,16,128]{3,2,1,0:T(8,128)(2,1)S(1)}, bf16[2,2,16,128]{3,2,1,0:T(8,128)(2,1)S(1)}, u32[]{:S(2)}, u32[]{:S(2)}) collective-permute-start(bf16[2,2,16,128]{3,2,1,0:T(8,128)(2,1)S(1)} %get-tuple-element.54), channel_id=1, source_target_pairs={{0,2},{1,3},{2,0},{3,1},{4,6},{5,7},{6,4},{7,5},{8,10},{9,11},{10,... | collective-permute-start | bytes 49160 | tf_op jit(solution)/shard_map/ppermute | solution.py:438
  38.0 4.3 %collective-permute-start.16 = (bf16[2,2,16,128]{3,2,1,0:T(8,128)(2,1)S(1)}, bf16[2,2,16,128]{3,2,1,0:T(8,128)(2,1)S(1)}, u32[]{:S(2)}, u32[]{:S(2)}) collective-permute-start(bf16[2,2,16,128]{3,2,1,0:T(8,128)(2,1)S(1)} %get-tuple-element.55), channel_id=1, source_target_pairs={{0,1},{1,0},{2,3},{3,2},{4,5},{5,4},{6,7},{7,6},{8,9},{9,8},{10,11... | collective-permute-start | bytes 49160 | tf_op jit(solution)/shard_map/ppermute | solution.py:438

commit v9 on v8

--- a/solution.py
+++ b/solution.py
@@ -113,7 +113,7 @@
 
 
 def first_half_kernel(score_scale, per_group, pieces, *refs):
-    pair_refs, refs = refs[:pieces], refs[pieces:]
+    pair_refs, refs = refs[:pieces][::-1], refs[pieces:]
     queries_ref, grads_ref, lse_ref, dot_ref = refs[:4]
     kept, (peak_ref, total_ref, dotted_ref, keys, values) = refs[4:8], refs[8:]
     tiles = queries_ref.shape[0]
@@ -175,7 +175,7 @@
             transcendentals=tiles * row_tile * positions,
         ),
         name="first_half",
-    )(*pairs, queries, grads, lse_rows, dot_rows)
+    )(*pairs[::-1], queries, grads, lse_rows, dot_rows)
 
 
 def second_half_kernel(score_scale, per_group, pieces, *refs):
@@ -395,7 +395,8 @@
 
 def adam_kernel(columns, *refs):
     parts, refs = refs[:columns], refs[columns:]
-    cache_ref, first_ref, second_ref, new_cache, new_first, new_second, by_flip = refs
+    cache_ref, first_ref, second_ref, new_cache, new_first, new_second = refs[:6]
+    by_flip, gathered = refs[6:]
     groups = cache_ref.shape[2]
     own = parts[0].shape[1]
     repeat = own * columns // groups
@@ -406,21 +407,18 @@
         for group in range(groups):
             first_owner = group // own * repeat
             slot = group % own
-            gradient = by_flip[column ^ first_owner, side, slot]
+            total = by_flip[column ^ first_owner, side, slot]
             for owner in range(first_owner + 1, first_owner + repeat):
-                gradient = gradient + by_flip[column ^ owner, side, slot]
-            first = beta_first * first_ref[:, side, group] + (1.0 - beta_first) * gradient
-            second = (
-                beta_second * second_ref[:, side, group]
-                + (1.0 - beta_second) * gradient * gradient
-            )
-            first_hat = first / (1.0 - beta_first**STEP)
-            second_hat = second / (1.0 - beta_second**STEP)
-            new_cache[:, side, group] = cache_ref[
-                :, side, group
-            ] - learn_rate * first_hat / (jnp.sqrt(second_hat) + epsilon)
-            new_first[:, side, group] = first
-            new_second[:, side, group] = second
+                total = total + by_flip[column ^ owner, side, slot]
+            gathered[:, side, group] = total
+    gradient = gathered[...]
+    first = beta_first * first_ref[...] + (1.0 - beta_first) * gradient
+    second = beta_second * second_ref[...] + (1.0 - beta_second) * gradient * gradient
+    first_hat = first / (1.0 - beta_first**STEP)
+    second_hat = second / (1.0 - beta_second**STEP)
+    new_cache[...] = cache_ref[...] - learn_rate * first_hat / (jnp.sqrt(second_hat) + epsilon)
+    new_first[...] = first
+    new_second[...] = second
 
 
 def adam(parts, cache, first_moment, second_moment):
@@ -428,7 +426,10 @@
     return pl.pallas_call(
         functools.partial(adam_kernel, len(parts)),
         out_shape=(shape, shape, shape),
-        scratch_shapes=[pltpu.VMEM((len(parts),) + parts[0].shape, jnp.float32)],
+        scratch_shapes=[
+            pltpu.VMEM((len(parts),) + parts[0].shape, jnp.float32),
+            pltpu.VMEM(cache.shape, jnp.float32),
+        ],
         compiler_params=pltpu.CompilerParams(vmem_limit_bytes=16 * MIB),
         name="adam",
     )(*parts, cache, first_moment, second_moment)

time: 44 us -> 42.9 us (0.975)
    ppermute x17, starting transfers between devices: 18.4 us -> 18 us  [swap(): lax.ppermute(value, axis, [(place, place ^ flip) for place in range(size)])]
  transfers between devices with their start and end apart: 17 -> 17, of which waited for: 7 -> 9; matrix products, arithmetic and copies ran while one was open for 8% -> 8% of each run, Pallas kernels for 11% -> 11%
where the time goes in v9:
time: 42.9 us; the launch traced here: 42.5 us
  starting transfers between devices  18 us (42%)
  Pallas kernels  10.2 us (24%)
  waiting for transfers between devices  9.24 us (22%)
  local copies, waits for them, and re-layouts  4.31 us (10%)
  between operations  0.79 us (2%)
    ppermute x17, starting transfers between devices, swap(): lax.ppermute(value, axis, [(place, place ^ flip) for place in range(size)])  18 us
    ppermute x17, waiting for transfers between devices, swap(): lax.ppermute(value, axis, [(place, place ^ flip) for place in range(size)])  9.24 us
    pallas_call x1, Pallas kernels, second_half(): pl.pallas_call(functools.partial(second_half_kernel, score_scale, tiles /...  4.51 us
    pallas_call x1, Pallas kernels, first_half(): pl.pallas_call(functools.partial(first_half_kernel, score_scale, tiles //...  2.7 us
    dynamic_slice x2, local copies, waits for them, and re-layouts, tiles_of(): part = lax.dynamic_slice_in_dim(part, first_group, own, 1)  2.69 us
    pallas_call x1, Pallas kernels, finish(): pl.pallas_call(functools.partial(finish_kernel, score_scale, tiles // own...  1.89 us
    unnamed x12, local copies, waits for them, and re-layouts  1.3 us
    pallas_call x1, Pallas kernels, adam(): pl.pallas_call(functools.partial(adam_kernel, len(parts)), out_shape=(sha...  0.89 us
  transfers between devices with their start and end apart: 17, of which 9 were waited for; matrix products, arithmetic and copies ran while one was open for 8% of the time, Pallas kernels for 11%

profile of v9, /device:TPU:0, one launch (start us, length us, event | category | flops | bytes accessed | tf_op | source)
XLA Modules:
  0.0 42.5 jit_solution(15942515949975723046)
XLA Ops:
  0.6 0.0 copy-start
  0.6 0.9 %copy-done = f32[16,2,8,128]{3,2,1,0:T(8,128)S(1)} copy-done((f32[16,2,8,128]{3,2,1,0:T(8,128)S(1)}, f32[16,2,8,128]{3,2,1,0:T(8,128)}, u32[]{:S(2)}) %copy-start) | copy-done | bytes 131096
  1.5 0.1 pack.1
  1.7 5.1 %collective-permute-start = (bf16[2,2,16,128]{3,2,1,0:T(8,128)(2,1)S(1)}, bf16[2,2,16,128]{3,2,1,0:T(8,128)(2,1)S(1)}, u32[]{:S(2)}, u32[]{:S(2)}) collective-permute-start(bf16[2,2,16,128]{3,2,1,0:T(8,128)(2,1)S(1)} %get-tuple-element.30), channel_id=1, source_target_pairs={{0,3},{1,2},{2,1},{3,0},{4,7},{5,6},{6,5},{7,4},{8,11},{9,10},{10,... | collective-permute-start | bytes 49160 | tf_op jit(solution)/shard_map/ppermute | solution.py:439
  6.8 0.0 collective-permute-start.1
  6.8 0.6 %collective-permute-start.2 = (bf16[2,2,16,128]{3,2,1,0:T(8,128)(2,1)S(1)}, bf16[2,2,16,128]{3,2,1,0:T(8,128)(2,1)S(1)}, u32[]{:S(2)}, u32[]{:S(2)}) collective-permute-start(bf16[2,2,16,128]{3,2,1,0:T(8,128)(2,1)S(1)} %get-tuple-element.32), channel_id=1, source_target_pairs={{0,1},{1,0},{2,3},{3,2},{4,5},{5,4},{6,7},{7,6},{8,9},{9,8},{10,11... | collective-permute-start | bytes 49160 | tf_op jit(solution)/shard_map/ppermute | solution.py:439
  7.4 2.0 %constant_dynamic-slice_fusion.2 = (bf16[256,2,8,128]{3,2,1,0:T(8,128)(2,1)S(1)}, bf16[256,2,8,128]{3,2,1,0:T(8,128)(2,1)S(1)}) fusion(bf16[256,8,8,128]{3,2,1,0:T(8,128)(2,1)} %bitcast.25, s32[]{:T(128)S(6)} %select_n.9, bf16[256,8,8,128]{3,2,1,0:T(8,128)(2,1)} %bitcast.26), kind=kLoop, calls=%fused_computation.3 | loop fusion | bytes 4194308 | tf_op jit(solution)/shard_map/dynamic_slice | solution.py:470
  9.4 0.0 collective-permute-done
  9.4 2.0 %collective-permute-done.1 = bf16[2,2,16,128]{3,2,1,0:T(8,128)(2,1)S(1)} collective-permute-done((bf16[2,2,16,128]{3,2,1,0:T(8,128)(2,1)S(1)}, bf16[2,2,16,128]{3,2,1,0:T(8,128)(2,1)S(1)}, u32[]{:S(2)}, u32[]{:S(2)}) %collective-permute-start.1) | collective-permute-done | bytes 16416 | tf_op jit(solution)/shard_map/ppermute | solution.py:439
  11.4 0.0 collective-permute-done.2
  11.5 2.5 %collective-permute-start.5 = (bf16[4,2,2,16,128]{4,3,2,1,0:T(8,128)(2,1)S(1)}, bf16[4,2,2,16,128]{4,3,2,1,0:T(8,128)(2,1)S(1)}, u32[]{:S(2)}, u32[]{:S(2)}) collective-permute-start(bf16[4,2,2,16,128]{4,3,2,1,0:T(8,128)(2,1)S(1)} %pad_maximum_fusion.refs_0_), channel_id=1, source_target_pairs={{0,24},{4,28},{8,16},{12,20},{16,8},{20,12},{24,0},{28,4},{1,25},{... | collective-permute-start | bytes 196616 | tf_op jit(solution)/shard_map/ppermute | solution.py:439
  14.0 0.5 %collective-permute-start.4 = (bf16[4,2,2,16,128]{4,3,2,1,0:T(8,128)(2,1)S(1)}, bf16[4,2,2,16,128]{4,3,2,1,0:T(8,128)(2,1)S(1)}, u32[]{:S(2)}, u32[]{:S(2)}) collective-permute-start(bf16[4,2,2,16,128]{4,3,2,1,0:T(8,128)(2,1)S(1)} %pad_maximum_fusion.refs_0_), channel_id=1, source_target_pairs={{0,16},{4,20},{8,24},{12,28},{16,0},{20,4},{24,8},{28,12},{1,17},{... | collective-permute-start | bytes 196616 | tf_op jit(solution)/shard_map/ppermute | solution.py:439
  14.5 0.5 %collective-permute-start.3 = (bf16[4,2,2,16,128]{4,3,2,1,0:T(8,128)(2,1)S(1)}, bf16[4,2,2,16,128]{4,3,2,1,0:T(8,128)(2,1)S(1)}, u32[]{:S(2)}, u32[]{:S(2)}) collective-permute-start(bf16[4,2,2,16,128]{4,3,2,1,0:T(8,128)(2,1)S(1)} %pad_maximum_fusion.refs_0_), channel_id=1, source_target_pairs={{0,8},{4,12},{8,0},{12,4},{16,24},{20,28},{24,16},{28,20},{1,9},{5... | collective-permute-start | bytes 196616 | tf_op jit(solution)/shard_map/ppermute | solution.py:439
  15.0 0.7 %constant_dynamic-slice_fusion = (f32[256,2,8]{0,2,1:T(8,128)S(1)}, f32[256,2,8]{0,2,1:T(8,128)S(1)}) fusion(f32[256,8,8]{0,2,1:T(8,128)} %bitcast.30, s32[]{:T(128)S(6)} %select_n.9, f32[256,8,8]{0,2,1:T(8,128)} %bitcast.31), kind=kLoop, calls=%fused_computation.1 | loop fusion | bytes 65540 | tf_op jit(solution)/shard_map/dynamic_slice | solution.py:470
  15.7 0.1 copy.21
  15.9 0.2 reshape.37.refs_7_
  16.0 0.1 copy.20
  16.2 0.2 reshape.35.refs_6_
  16.3 0.1 copy.19
  16.4 0.1 copy.18
  16.5 0.1 collective-permute-start.9
  16.6 0.7 %collective-permute-done.5.refs_3_ = bf16[4,2,2,16,128]{4,3,2,1,0:T(8,128)(2,1)S(1)} collective-permute-done((bf16[4,2,2,16,128]{4,3,2,1,0:T(8,128)(2,1)S(1)}, bf16[4,2,2,16,128]{4,3,2,1,0:T(8,128)(2,1)S(1)}, u32[]{:S(2)}, u32[]{:S(2)}) %collective-permute-start.5) | collective-permute-done | bytes 65568 | tf_op jit(solution)/shard_map/ppermute | solution.py:439
  17.3 0.0 collective-permute-start.6
  17.3 1.0 %collective-permute-done.4.refs_2_ = bf16[4,2,2,16,128]{4,3,2,1,0:T(8,128)(2,1)S(1)} collective-permute-done((bf16[4,2,2,16,128]{4,3,2,1,0:T(8,128)(2,1)S(1)}, bf16[4,2,2,16,128]{4,3,2,1,0:T(8,128)(2,1)S(1)}, u32[]{:S(2)}, u32[]{:S(2)}) %collective-permute-start.4) | collective-permute-done | bytes 65568 | tf_op jit(solution)/shard_map/ppermute | solution.py:439
  18.2 0.0 collective-permute-start.7
  18.2 0.5 %collective-permute-done.3.refs_1_ = bf16[4,2,2,16,128]{4,3,2,1,0:T(8,128)(2,1)S(1)} collective-permute-done((bf16[4,2,2,16,128]{4,3,2,1,0:T(8,128)(2,1)S(1)}, bf16[4,2,2,16,128]{4,3,2,1,0:T(8,128)(2,1)S(1)}, u32[]{:S(2)}, u32[]{:S(2)}) %collective-permute-start.3) | collective-permute-done | bytes 65568 | tf_op jit(solution)/shard_map/ppermute | solution.py:439
  18.7 0.0 collective-permute-start.8
  18.7 2.7 %first_half.1 = (f32[4,256,512]{2,1,0:T(8,128)S(1)}, f32[4,256,512]{2,1,0:T(8,128)S(1)}, f32[4,256,512]{2,1,0:T(8,128)S(1)}, f32[4,256,512]{2,1,0:T(8,128)S(1)},...) custom-call(bf16[4,2,2,16,128]{4,3,2,1,0:T(8,128)(2,1)S(1)} %pad_maximum_fusion.refs_0_, ...), custom_call_target="tpu_custom_call" | custom-call | flops 536870912 | bytes 8388608 | tf_op jit(solution)/shard_map/first_half/pallas_call | solution.py:164
  21.5 0.0 collective-permute-done.9.refs_3_
  21.5 0.0 collective-permute-done.6.refs_0_
  21.5 0.0 collective-permute-done.7.refs_1_
  21.5 0.0 collective-permute-done.8.refs_2_
  21.5 4.5 %second_half.1 = (bf16[4,4,2,2,16,128]{5,4,3,2,1,0:T(8,128)(2,1)S(1)}, f32[8,1,512]{2,1,0:T(1,128)S(1)}, f32[8,1,512]{2,1,0:T(1,128)S(1)}) custom-call(bf16[4,2,2,16,128]{4,3,2,1,0:T(8,128)(2,1)S(1)} %collective-permute-done.6.refs_0_, bf16[4,2,2,16,128]{4,3,2,1,0:T(8,128)(2,1)S(1)} %collective-permute-done.7.refs_1_, ...), custom_call_target="tpu_custom_call" | custom-call | flops 1073741824 | bytes 2097152 | tf_op jit(solution)/shard_map/second_half/pallas_call | solution.py:257
  26.0 0.6 %collective-permute-start.10 = (bf16[4,4,2,2,16,128]{5,4,3,2,1,0:T(8,128)(2,1)S(1)}, bf16[4,4,2,2,16,128]{5,4,3,2,1,0:T(8,128)(2,1)S(1)}, u32[]{:S(2)}, u32[]{:S(2)}) collective-permute-start(bf16[4,4,2,2,16,128]{5,4,3,2,1,0:T(8,128)(2,1)S(1)} %get-tuple-element.48), channel_id=1, source_target_pairs={{0,4},{4,0},{8,12},{12,8},{16,20},{20,16},{24,28},{28,24},{1,5},{5... | collective-permute-start | bytes 786440 | tf_op jit(solution)/shard_map/ppermute | solution.py:439
  26.6 0.0 copy-start.1
  26.6 0.0 copy-start.2
  26.6 0.0 copy-start.3
  26.6 1.9 %finish.1.mine_ref = f32[4,4,2,2,16,128]{5,4,3,2,1,0:T(8,128)S(1)} custom-call(f32[4,256,512]{2,1,0:T(8,128)S(1)} %get-tuple-element.38.refs_0_, f32[4,256,512]{2,1,0:T(8,128)S(1)} %get-tuple-element.39.refs_1_, f32[4,256,512]{2,1,0:T(8,128)S(1)} %get-tuple-element.40.refs_2_, f32[4,256,512]{2,1,0:T(8,128)S(1)} %get-tuple-element.41.refs_3_, ...), custom_call_target="tpu_custom_call" | custom-call | flops 536870912 | bytes 8388608 | tf_op jit(solution)/shard_map/finish/pallas_call | solution.py:336
  28.5 0.0 collective-permute-done.10.mate_ref
  28.5 1.6 %collective-permute-start.11 = (bf16[4,2,2,16,128]{4,3,2,1,0:T(8,128)(2,1)S(1)}, bf16[4,2,2,16,128]{4,3,2,1,0:T(8,128)(2,1)S(1)}, u32[]{:S(2)}, u32[]{:S(2)}) collective-permute-start(bf16[4,2,2,16,128]{4,3,2,1,0:T(8,128)(2,1)S(1)} %get-tuple-element.50), channel_id=1, source_target_pairs={{0,24},{4,28},{8,16},{12,20},{16,8},{20,12},{24,0},{28,4},{1,25},{... | collective-permute-start | bytes 196616 | tf_op jit(solution)/shard_map/ppermute | solution.py:439
  30.1 0.5 %collective-permute-start.12 = (bf16[4,2,2,16,128]{4,3,2,1,0:T(8,128)(2,1)S(1)}, bf16[4,2,2,16,128]{4,3,2,1,0:T(8,128)(2,1)S(1)}, u32[]{:S(2)}, u32[]{:S(2)}) collective-permute-start(bf16[4,2,2,16,128]{4,3,2,1,0:T(8,128)(2,1)S(1)} %get-tuple-element.51), channel_id=1, source_target_pairs={{0,16},{4,20},{8,24},{12,28},{16,0},{20,4},{24,8},{28,12},{1,17},{... | collective-permute-start | bytes 196616 | tf_op jit(solution)/shard_map/ppermute | solution.py:439
  30.6 1.5 %collective-permute-start.13 = (bf16[4,2,2,16,128]{4,3,2,1,0:T(8,128)(2,1)S(1)}, bf16[4,2,2,16,128]{4,3,2,1,0:T(8,128)(2,1)S(1)}, u32[]{:S(2)}, u32[]{:S(2)}) collective-permute-start(bf16[4,2,2,16,128]{4,3,2,1,0:T(8,128)(2,1)S(1)} %get-tuple-element.52), channel_id=1, source_target_pairs={{0,8},{4,12},{8,0},{12,4},{16,24},{20,28},{24,16},{28,20},{1,9},{5... | collective-permute-start | bytes 196616 | tf_op jit(solution)/shard_map/ppermute | solution.py:439
  32.1 1.9 %collective-permute-done.11.refs_0_ = bf16[4,2,2,16,128]{4,3,2,1,0:T(8,128)(2,1)S(1)} collective-permute-done((bf16[4,2,2,16,128]{4,3,2,1,0:T(8,128)(2,1)S(1)}, bf16[4,2,2,16,128]{4,3,2,1,0:T(8,128)(2,1)S(1)}, u32[]{:S(2)}, u32[]{:S(2)}) %collective-permute-start.11) | collective-permute-done | bytes 65568 | tf_op jit(solution)/shard_map/ppermute | solution.py:439
  34.0 1.0 %collective-permute-done.12.refs_1_ = bf16[4,2,2,16,128]{4,3,2,1,0:T(8,128)(2,1)S(1)} collective-permute-done((bf16[4,2,2,16,128]{4,3,2,1,0:T(8,128)(2,1)S(1)}, bf16[4,2,2,16,128]{4,3,2,1,0:T(8,128)(2,1)S(1)}, u32[]{:S(2)}, u32[]{:S(2)}) %collective-permute-start.12) | collective-permute-done | bytes 65568 | tf_op jit(solution)/shard_map/ppermute | solution.py:439
  35.0 0.1 collective-permute-done.13.refs_2_
  35.0 1.9 %collective-permute-start.14 = (bf16[2,2,16,128]{3,2,1,0:T(8,128)(2,1)S(1)}, bf16[2,2,16,128]{3,2,1,0:T(8,128)(2,1)S(1)}, u32[]{:S(2)}, u32[]{:S(2)}) collective-permute-start(bf16[2,2,16,128]{3,2,1,0:T(8,128)(2,1)S(1)} %get-tuple-element.53), channel_id=1, source_target_pairs={{0,3},{1,2},{2,1},{3,0},{4,7},{5,6},{6,5},{7,4},{8,11},{9,10},{10,... | collective-permute-start | bytes 49160 | tf_op jit(solution)/shard_map/ppermute | solution.py:439
  37.0 0.2 collective-permute-start.15
  37.2 2.3 %collective-permute-start.16 = (bf16[2,2,16,128]{3,2,1,0:T(8,128)(2,1)S(1)}, bf16[2,2,16,128]{3,2,1,0:T(8,128)(2,1)S(1)}, u32[]{:S(2)}, u32[]{:S(2)}) collective-permute-start(bf16[2,2,16,128]{3,2,1,0:T(8,128)(2,1)S(1)} %get-tuple-element.55), channel_id=1, source_target_pairs={{0,1},{1,0},{2,3},{3,2},{4,5},{5,4},{6,7},{7,6},{8,9},{9,8},{10,11... | collective-permute-start | bytes 49160 | tf_op jit(solution)/shard_map/ppermute | solution.py:439
  39.5 1.1 %collective-permute-done.14.refs_0_ = bf16[2,2,16,128]{3,2,1,0:T(8,128)(2,1)S(1)} collective-permute-done((bf16[2,2,16,128]{3,2,1,0:T(8,128)(2,1)S(1)}, bf16[2,2,16,128]{3,2,1,0:T(8,128)(2,1)S(1)}, u32[]{:S(2)}, u32[]{:S(2)}) %collective-permute-start.14) | collective-permute-done | bytes 16416 | tf_op jit(solution)/shard_map/ppermute | solution.py:439
  40.6 1.0 %collective-permute-done.15.refs_1_ = bf16[2,2,16,128]{3,2,1,0:T(8,128)(2,1)S(1)} collective-permute-done((bf16[2,2,16,128]{3,2,1,0:T(8,128)(2,1)S(1)}, bf16[2,2,16,128]{3,2,1,0:T(8,128)(2,1)S(1)}, u32[]{:S(2)}, u32[]{:S(2)}) %collective-permute-start.15) | collective-permute-done | bytes 16416 | tf_op jit(solution)/shard_map/ppermute | solution.py:439
  41.6 0.0 collective-permute-done.16.refs_2_
  41.6 0.0 copy-done.1
  41.6 0.0 copy-done.2
  41.6 0.0 copy-done.3
  41.6 0.9 %adam.1 = (f32[16,2,8,128]{3,2,1,0:T(8,128)}, f32[16,2,8,128]{3,2,1,0:T(8,128)}, f32[16,2,8,128]{3,2,1,0:T(8,128)}) custom-call(bf16[2,2,16,128]{3,2,1,0:T(8,128)(2,1)S(1)} %collective-permute-done.14.refs_0_, bf16[2,2,16,128]{3,2,1,0:T(8,128)(2,1)S(1)} %collective-permute-done.15.refs_1_, bf16[2,2,16,128]{3,2,1,0:T(8,128)(2,1)S(1)} %collective-permute-done.16.refs_2_, ...), custom_call_target="tpu_custom_call" | custom-call | tf_op jit(solution)/shard_map/adam/pallas_call | solution.py:426
  (3 shorter events, 0.1 us)
Async XLA Ops:
  0.6 0.9 %copy-start = (f32[16,2,8,128]{3,2,1,0:T(8,128)S(1)}, f32[16,2,8,128]{3,2,1,0:T(8,128)}, u32[]{:S(2)}) copy-start(f32[16,2,8,128]{3,2,1,0:T(8,128)} %refs_4_.1) | copy-start | bytes 393220
  1.7 7.7 %collective-permute-start = (bf16[2,2,16,128]{3,2,1,0:T(8,128)(2,1)S(1)}, bf16[2,2,16,128]{3,2,1,0:T(8,128)(2,1)S(1)}, u32[]{:S(2)}, u32[]{:S(2)}) collective-permute-start(bf16[2,2,16,128]{3,2,1,0:T(8,128)(2,1)S(1)} %get-tuple-element.30), channel_id=1, source_target_pairs={{0,3},{1,2},{2,1},{3,0},{4,7},{5,6},{6,5},{7,4},{8,11},{9,10},{10,... | collective-permute-start | bytes 49160 | tf_op jit(solution)/shard_map/ppermute | solution.py:439
  6.8 4.6 %collective-permute-start.1 = (bf16[2,2,16,128]{3,2,1,0:T(8,128)(2,1)S(1)}, bf16[2,2,16,128]{3,2,1,0:T(8,128)(2,1)S(1)}, u32[]{:S(2)}, u32[]{:S(2)}) collective-permute-start(bf16[2,2,16,128]{3,2,1,0:T(8,128)(2,1)S(1)} %get-tuple-element.31), channel_id=1, source_target_pairs={{0,2},{1,3},{2,0},{3,1},{4,6},{5,7},{6,4},{7,5},{8,10},{9,11},{10,... | collective-permute-start | bytes 49160 | tf_op jit(solution)/shard_map/ppermute | solution.py:439
  6.8 4.6 %collective-permute-start.2 = (bf16[2,2,16,128]{3,2,1,0:T(8,128)(2,1)S(1)}, bf16[2,2,16,128]{3,2,1,0:T(8,128)(2,1)S(1)}, u32[]{:S(2)}, u32[]{:S(2)}) collective-permute-start(bf16[2,2,16,128]{3,2,1,0:T(8,128)(2,1)S(1)} %get-tuple-element.32), channel_id=1, source_target_pairs={{0,1},{1,0},{2,3},{3,2},{4,5},{5,4},{6,7},{7,6},{8,9},{9,8},{10,11... | collective-permute-start | bytes 49160 | tf_op jit(solution)/shard_map/ppermute | solution.py:439
  11.5 5.8 %collective-permute-start.5 = (bf16[4,2,2,16,128]{4,3,2,1,0:T(8,128)(2,1)S(1)}, bf16[4,2,2,16,128]{4,3,2,1,0:T(8,128)(2,1)S(1)}, u32[]{:S(2)}, u32[]{:S(2)}) collective-permute-start(bf16[4,2,2,16,128]{4,3,2,1,0:T(8,128)(2,1)S(1)} %pad_maximum_fusion.refs_0_), channel_id=1, source_target_pairs={{0,24},{4,28},{8,16},{12,20},{16,8},{20,12},{24,0},{28,4},{1,25},{... | collective-permute-start | bytes 196616 | tf_op jit(solution)/shard_map/ppermute | solution.py:439
  14.0 4.3 %collective-permute-start.4 = (bf16[4,2,2,16,128]{4,3,2,1,0:T(8,128)(2,1)S(1)}, bf16[4,2,2,16,128]{4,3,2,1,0:T(8,128)(2,1)S(1)}, u32[]{:S(2)}, u32[]{:S(2)}) collective-permute-start(bf16[4,2,2,16,128]{4,3,2,1,0:T(8,128)(2,1)S(1)} %pad_maximum_fusion.refs_0_), channel_id=1, source_target_pairs={{0,16},{4,20},{8,24},{12,28},{16,0},{20,4},{24,8},{28,12},{1,17},{... | collective-permute-start | bytes 196616 | tf_op jit(solution)/shard_map/ppermute | solution.py:439
  14.5 4.3 %collective-permute-start.3 = (bf16[4,2,2,16,128]{4,3,2,1,0:T(8,128)(2,1)S(1)}, bf16[4,2,2,16,128]{4,3,2,1,0:T(8,128)(2,1)S(1)}, u32[]{:S(2)}, u32[]{:S(2)}) collective-permute-start(bf16[4,2,2,16,128]{4,3,2,1,0:T(8,128)(2,1)S(1)} %pad_maximum_fusion.refs_0_), channel_id=1, source_target_pairs={{0,8},{4,12},{8,0},{12,4},{16,24},{20,28},{24,16},{28,20},{1,9},{5... | collective-permute-start | bytes 196616 | tf_op jit(solution)/shard_map/ppermute | solution.py:439
  16.5 5.0 %collective-permute-start.9 = (bf16[4,2,2,16,128]{4,3,2,1,0:T(8,128)(2,1)S(1)}, bf16[4,2,2,16,128]{4,3,2,1,0:T(8,128)(2,1)S(1)}, u32[]{:S(2)}, u32[]{:S(2)}) collective-permute-start(bf16[4,2,2,16,128]{4,3,2,1,0:T(8,128)(2,1)S(1)} %pad_maximum_fusion.refs_0_), channel_id=1, source_target_pairs={{0,4},{4,0},{8,12},{12,8},{16,20},{20,16},{24,28},{28,24},{1,5},{5... | collective-permute-start | bytes 196616 | tf_op jit(solution)/shard_map/ppermute | solution.py:439
  17.3 4.2 %collective-permute-start.6 = (bf16[4,2,2,16,128]{4,3,2,1,0:T(8,128)(2,1)S(1)}, bf16[4,2,2,16,128]{4,3,2,1,0:T(8,128)(2,1)S(1)}, u32[]{:S(2)}, u32[]{:S(2)}) collective-permute-start(bf16[4,2,2,16,128]{4,3,2,1,0:T(8,128)(2,1)S(1)} %collective-permute-done.5.refs_3_), channel_id=1, source_target_pairs={{0,4},{4,0},{8,12},{12,8},{16,20},{20,16},{24,28},{28,24},{1,5},{5... | collective-permute-start | bytes 196616 | tf_op jit(solution)/shard_map/ppermute | solution.py:439
  18.2 3.2 %collective-permute-start.7 = (bf16[4,2,2,16,128]{4,3,2,1,0:T(8,128)(2,1)S(1)}, bf16[4,2,2,16,128]{4,3,2,1,0:T(8,128)(2,1)S(1)}, u32[]{:S(2)}, u32[]{:S(2)}) collective-permute-start(bf16[4,2,2,16,128]{4,3,2,1,0:T(8,128)(2,1)S(1)} %collective-permute-done.4.refs_2_), channel_id=1, source_target_pairs={{0,4},{4,0},{8,12},{12,8},{16,20},{20,16},{24,28},{28,24},{1,5},{5... | collective-permute-start | bytes 196616 | tf_op jit(solution)/shard_map/ppermute | solution.py:439
  18.7 2.7 %collective-permute-start.8 = (bf16[4,2,2,16,128]{4,3,2,1,0:T(8,128)(2,1)S(1)}, bf16[4,2,2,16,128]{4,3,2,1,0:T(8,128)(2,1)S(1)}, u32[]{:S(2)}, u32[]{:S(2)}) collective-permute-start(bf16[4,2,2,16,128]{4,3,2,1,0:T(8,128)(2,1)S(1)} %collective-permute-done.3.refs_1_), channel_id=1, source_target_pairs={{0,4},{4,0},{8,12},{12,8},{16,20},{20,16},{24,28},{28,24},{1,5},{5... | collective-permute-start | bytes 196616 | tf_op jit(solution)/shard_map/ppermute | solution.py:439
  26.0 2.5 %collective-permute-start.10 = (bf16[4,4,2,2,16,128]{5,4,3,2,1,0:T(8,128)(2,1)S(1)}, bf16[4,4,2,2,16,128]{5,4,3,2,1,0:T(8,128)(2,1)S(1)}, u32[]{:S(2)}, u32[]{:S(2)}) collective-permute-start(bf16[4,4,2,2,16,128]{5,4,3,2,1,0:T(8,128)(2,1)S(1)} %get-tuple-element.48), channel_id=1, source_target_pairs={{0,4},{4,0},{8,12},{12,8},{16,20},{20,16},{24,28},{28,24},{1,5},{5... | collective-permute-start | bytes 786440 | tf_op jit(solution)/shard_map/ppermute | solution.py:439
  26.6 15.0 %copy-start.1 = (f32[16,2,8,128]{3,2,1,0:T(8,128)S(1)}, f32[16,2,8,128]{3,2,1,0:T(8,128)}, u32[]{:S(2)}) copy-start(f32[16,2,8,128]{3,2,1,0:T(8,128)} %refs_4_.1) | copy-start | bytes 393220
  26.6 15.0 %copy-start.2 = (f32[16,2,8,128]{3,2,1,0:T(8,128)S(1)}, f32[16,2,8,128]{3,2,1,0:T(8,128)}, u32[]{:S(2)}) copy-start(f32[16,2,8,128]{3,2,1,0:T(8,128)} %refs_5_.1) | copy-start | bytes 393220
  26.6 15.0 %copy-start.3 = (f32[16,2,8,128]{3,2,1,0:T(8,128)S(1)}, f32[16,2,8,128]{3,2,1,0:T(8,128)}, u32[]{:S(2)}) copy-start(f32[16,2,8,128]{3,2,1,0:T(8,128)} %refs_6_.1) | copy-start | bytes 393220
  28.5 5.4 %collective-permute-start.11 = (bf16[4,2,2,16,128]{4,3,2,1,0:T(8,128)(2,1)S(1)}, bf16[4,2,2,16,128]{4,3,2,1,0:T(8,128)(2,1)S(1)}, u32[]{:S(2)}, u32[]{:S(2)}) collective-permute-start(bf16[4,2,2,16,128]{4,3,2,1,0:T(8,128)(2,1)S(1)} %get-tuple-element.50), channel_id=1, source_target_pairs={{0,24},{4,28},{8,16},{12,20},{16,8},{20,12},{24,0},{28,4},{1,25},{... | collective-permute-start | bytes 196616 | tf_op jit(solution)/shard_map/ppermute | solution.py:439
  30.1 4.9 %collective-permute-start.12 = (bf16[4,2,2,16,128]{4,3,2,1,0:T(8,128)(2,1)S(1)}, bf16[4,2,2,16,128]{4,3,2,1,0:T(8,128)(2,1)S(1)}, u32[]{:S(2)}, u32[]{:S(2)}) collective-permute-start(bf16[4,2,2,16,128]{4,3,2,1,0:T(8,128)(2,1)S(1)} %get-tuple-element.51), channel_id=1, source_target_pairs={{0,16},{4,20},{8,24},{12,28},{16,0},{20,4},{24,8},{28,12},{1,17},{... | collective-permute-start | bytes 196616 | tf_op jit(solution)/shard_map/ppermute | solution.py:439
  30.6 4.4 %collective-permute-start.13 = (bf16[4,2,2,16,128]{4,3,2,1,0:T(8,128)(2,1)S(1)}, bf16[4,2,2,16,128]{4,3,2,1,0:T(8,128)(2,1)S(1)}, u32[]{:S(2)}, u32[]{:S(2)}) collective-permute-start(bf16[4,2,2,16,128]{4,3,2,1,0:T(8,128)(2,1)S(1)} %get-tuple-element.52), channel_id=1, source_target_pairs={{0,8},{4,12},{8,0},{12,4},{16,24},{20,28},{24,16},{28,20},{1,9},{5... | collective-permute-start | bytes 196616 | tf_op jit(solution)/shard_map/ppermute | solution.py:439
  35.0 5.6 %collective-permute-start.14 = (bf16[2,2,16,128]{3,2,1,0:T(8,128)(2,1)S(1)}, bf16[2,2,16,128]{3,2,1,0:T(8,128)(2,1)S(1)}, u32[]{:S(2)}, u32[]{:S(2)}) collective-permute-start(bf16[2,2,16,128]{3,2,1,0:T(8,128)(2,1)S(1)} %get-tuple-element.53), channel_id=1, source_target_pairs={{0,3},{1,2},{2,1},{3,0},{4,7},{5,6},{6,5},{7,4},{8,11},{9,10},{10,... | collective-permute-start | bytes 49160 | tf_op jit(solution)/shard_map/ppermute | solution.py:439
  37.0 4.6 %collective-permute-start.15 = (bf16[2,2,16,128]{3,2,1,0:T(8,128)(2,1)S(1)}, bf16[2,2,16,128]{3,2,1,0:T(8,128)(2,1)S(1)}, u32[]{:S(2)}, u32[]{:S(2)}) collective-permute-start(bf16[2,2,16,128]{3,2,1,0:T(8,128)(2,1)S(1)} %get-tuple-element.54), channel_id=1, source_target_pairs={{0,2},{1,3},{2,0},{3,1},{4,6},{5,7},{6,4},{7,5},{8,10},{9,11},{10,... | collective-permute-start | bytes 49160 | tf_op jit(solution)/shard_map/ppermute | solution.py:439
  37.2 4.4 %collective-permute-start.16 = (bf16[2,2,16,128]{3,2,1,0:T(8,128)(2,1)S(1)}, bf16[2,2,16,128]{3,2,1,0:T(8,128)(2,1)S(1)}, u32[]{:S(2)}, u32[]{:S(2)}) collective-permute-start(bf16[2,2,16,128]{3,2,1,0:T(8,128)(2,1)S(1)} %get-tuple-element.55), channel_id=1, source_target_pairs={{0,1},{1,0},{2,3},{3,2},{4,5},{5,4},{6,7},{7,6},{8,9},{9,8},{10,11... | collective-permute-start | bytes 49160 | tf_op jit(solution)/shard_map/ppermute | solution.py:439

commit v10 on v9

--- a/solution.py
+++ b/solution.py
@@ -17,6 +17,7 @@
 
 ROW_TILE = 512
 CHUNK = 16
+DOT_ROWS = 256
 MIB = 1024 * 1024
 
 
@@ -67,24 +68,63 @@
             values[slot, at] = pair_ref[:, 1, slot].reshape(length, width)
 
 
-def multiply(keys, values, queries, grads, scores, slopes):
-    scores[...] = lax.dot_general(keys, queries, ACROSS, preferred_element_type=jnp.float32)
-    slopes[...] = lax.dot_general(values, grads, ACROSS, preferred_element_type=jnp.float32)
+def interleave(passes, *products):
+    products = [product for some in products for product in some]
+    steps = passes[0]
+    done = 0
+    for number, step in enumerate(passes[1]):
+        while done < len(products) and done * steps <= number * len(products):
+            products[done]()
+            done += 1
+    for product in products[done:]:
+        product()
+
+
+def score_products(keys, values, slot, queries_ref, grads_ref, tile, scores, slopes):
+    def product(rows, left, right_ref, out):
+        def run():
+            out[:, rows] = lax.dot_general(
+                left[slot], right_ref[tile, rows], ACROSS, preferred_element_type=jnp.float32
+            )
+
+        return run
+
+    products = []
+    for start in range(0, scores.shape[1], DOT_ROWS):
+        rows = pl.ds(start, DOT_ROWS)
+        products.append(product(rows, keys, queries_ref, scores))
+        products.append(product(rows, values, grads_ref, slopes))
+    return products
+
+
+def gradient_products(key_total, value_total, slot, weights, dscores, queries_ref, grads_ref, tile):
+    def product(total, left, right_ref):
+        def run():
+            total[slot] += lax.dot_general(
+                left[...], right_ref[tile], ALONG, preferred_element_type=jnp.float32
+            )
+
+        return run
+
+    return [
+        product(key_total, dscores, queries_ref),
+        product(value_total, weights, grads_ref),
+    ]
 
 
 def cuts_of(ref):
     return [pl.ds(start, CHUNK) for start in range(0, ref.shape[0], CHUNK)]
 
 
-def largest(scores):
-    cuts = cuts_of(scores)
-    top = scores[cuts[0]]
-    for cut in cuts[1:]:
-        top = jnp.maximum(top, scores[cut])
-    return jnp.max(top, axis=0, keepdims=True)
-
-
-def exponentiate(scores, slopes, factor, peak):
+def largest(scores, result):
+    top = None
+    for cut in cuts_of(scores):
+        top = scores[cut] if top is None else jnp.maximum(top, scores[cut])
+        yield
+    result.append(jnp.max(top, axis=0, keepdims=True))
+
+
+def exponentiate(scores, slopes, factor, peak, result):
     total = None
     dotted = None
     for cut in cuts_of(scores):
@@ -93,7 +133,9 @@
         scores[cut] = shifted
         total = shifted if total is None else total + shifted
         dotted = product if dotted is None else dotted + product
-    return jnp.sum(total, axis=0, keepdims=True), jnp.sum(dotted, axis=0, keepdims=True)
+        yield
+    result.append(jnp.sum(total, axis=0, keepdims=True))
+    result.append(jnp.sum(dotted, axis=0, keepdims=True))
 
 
 def weigh(shifted, slopes, inverse, delta, weights, dscores):
@@ -101,15 +143,7 @@
         probability = shifted[cut] * inverse
         weights[cut] = probability.astype(jnp.bfloat16)
         dscores[cut] = (probability * (slopes[cut] - delta)).astype(jnp.bfloat16)
-
-
-def accumulate(key_total, value_total, slot, weights, dscores, queries, grads):
-    key_total[slot] += lax.dot_general(
-        dscores[...], queries, ALONG, preferred_element_type=jnp.float32
-    )
-    value_total[slot] += lax.dot_general(
-        weights[...], grads, ALONG, preferred_element_type=jnp.float32
-    )
+        yield
 
 
 def first_half_kernel(score_scale, per_group, pieces, *refs):
@@ -125,34 +159,39 @@
 
     def products(tile, parity, step):
         slot = tile // per_group
-        multiply(
-            keys[slot], values[slot], queries_ref[tile], grads_ref[tile], *place(tile, parity, step)
+        return score_products(
+            keys, values, slot, queries_ref, grads_ref, tile, *place(tile, parity, step)
         )
 
     def normalize(tile, parity, step):
         scores, slopes = place(tile, parity, step)
-        side_lse = lse_ref[pl.ds(tile, 1)] * LOG2E
-        peak = jnp.maximum(largest(scores) * factor, side_lse)
-        total, dotted = exponentiate(scores, slopes, factor, peak)
-        side = jnp.exp2(side_lse - peak)
-        peak_ref[tile] = peak
-        total_ref[tile] = total + side
-        dotted_ref[tile] = dotted + side * dot_ref[pl.ds(tile, 1)]
-
-    products(0, 0, 0)
+
+        def passes():
+            side_lse = lse_ref[pl.ds(tile, 1)] * LOG2E
+            found = []
+            yield from largest(scores, found)
+            peak = jnp.maximum(found[0] * factor, side_lse)
+            sums = []
+            yield from exponentiate(scores, slopes, factor, peak, sums)
+            side = jnp.exp2(side_lse - peak)
+            peak_ref[tile] = peak
+            total_ref[tile] = sums[0] + side
+            dotted_ref[tile] = sums[1] + side * dot_ref[pl.ds(tile, 1)]
+
+        return 2 * len(cuts_of(scores)), passes()
+
+    for product in products(0, 0, 0):
+        product()
 
     def two_tiles(step, carry):
-        products(2 * step + 1, 1, step)
-        normalize(2 * step, 0, step)
-        products(2 * step + 2, 0, step + 1)
-        normalize(2 * step + 1, 1, step)
+        interleave(normalize(2 * step, 0, step), products(2 * step + 1, 1, step))
+        interleave(normalize(2 * step + 1, 1, step), products(2 * step + 2, 0, step + 1))
         return carry
 
     last = tiles // 2 - 1
     lax.fori_loop(0, last, two_tiles, 0)
-    products(tiles - 1, 1, last)
-    normalize(tiles - 2, 0, last)
-    normalize(tiles - 1, 1, last)
+    interleave(normalize(tiles - 2, 0, last), products(tiles - 1, 1, last))
+    interleave(normalize(tiles - 1, 1, last))
 
 
 def first_half(pairs, queries, grads, lse_rows, dot_rows, score_scale):
@@ -193,49 +232,53 @@
 
     def products(tile, buffers):
         slot = tile // per_group
-        multiply(keys[slot], values[slot], queries_ref[tile], grads_ref[tile], *buffers[:2])
+        return score_products(keys, values, slot, queries_ref, grads_ref, tile, *buffers[:2])
 
     def normalize(tile, buffers):
         scores, slopes, weights, dscores = buffers
-        first_peak = peak_ref[tile]
-        peak = jnp.maximum(largest(scores) * factor, first_peak)
-        total, dotted = exponentiate(scores, slopes, factor, peak)
-        rescale = jnp.exp2(first_peak - peak)
-        inverse = 1.0 / (total + total_ref[tile] * rescale)
-        delta = (dotted + dotted_ref[tile] * rescale) * inverse
-        inverse_ref[tile] = inverse * rescale
-        delta_ref[tile] = delta
-        weigh(scores, slopes, inverse, delta, weights, dscores)
+
+        def passes():
+            found = []
+            yield from largest(scores, found)
+            first_peak = peak_ref[tile]
+            peak = jnp.maximum(found[0] * factor, first_peak)
+            sums = []
+            yield from exponentiate(scores, slopes, factor, peak, sums)
+            rescale = jnp.exp2(first_peak - peak)
+            inverse = 1.0 / (sums[0] + total_ref[tile] * rescale)
+            delta = (sums[1] + dotted_ref[tile] * rescale) * inverse
+            inverse_ref[tile] = inverse * rescale
+            delta_ref[tile] = delta
+            yield from weigh(scores, slopes, inverse, delta, weights, dscores)
+
+        return 3 * len(cuts_of(scores)), passes()
 
     def gather(tile, buffers):
-        accumulate(
+        return gradient_products(
             key_total,
             value_total,
             tile // per_group,
             buffers[2],
             buffers[3],
-            queries_ref[tile],
-            grads_ref[tile],
+            queries_ref,
+            grads_ref,
+            tile,
         )
 
-    products(0, even)
-    products(1, odd)
-    normalize(0, even)
+    for product in products(0, even):
+        product()
+    interleave(normalize(0, even), products(1, odd))
 
     def two_tiles(step, carry):
         tile = step * 2
-        products(tile + 2, even)
-        normalize(tile + 1, odd)
-        gather(tile, even)
-        products(tile + 3, odd)
-        normalize(tile + 2, even)
-        gather(tile + 1, odd)
+        interleave(normalize(tile + 1, odd), products(tile + 2, even), gather(tile, even))
+        interleave(normalize(tile + 2, even), products(tile + 3, odd), gather(tile + 1, odd))
         return carry
 
     lax.fori_loop(0, tiles // 2 - 1, two_tiles, 0)
-    normalize(tiles - 1, odd)
-    gather(tiles - 2, even)
-    gather(tiles - 1, odd)
+    interleave(normalize(tiles - 1, odd), gather(tiles - 2, even))
+    for product in gather(tiles - 1, odd):
+        product()
     shape = out_ref.shape[:2] + (share, width)
     for slot in range(own):
         key_sum = key_total[slot] * score_scale
@@ -290,38 +333,32 @@
     value_total[...] = jnp.zeros_like(value_total)
 
     def spread(tile, parity, step, buffers):
-        weigh(
+        steps = weigh(
             kept[2 * parity].at[step],
             kept[2 * parity + 1].at[step],
             inverse_ref[tile],
             delta_ref[tile],
             *buffers,
         )
+        return len(cuts_of(buffers[0])), steps
 
     def gather(tile, buffers):
-        accumulate(
-            key_total,
-            value_total,
-            tile // per_group,
-            *buffers,
-            queries_ref[tile],
-            grads_ref[tile],
+        return gradient_products(
+            key_total, value_total, tile // per_group, *buffers, queries_ref, grads_ref, tile
         )
 
-    spread(0, 0, 0, even)
+    interleave(spread(0, 0, 0, even))
 
     def two_tiles(step, carry):
-        spread(2 * step + 1, 1, step, odd)
-        gather(2 * step, even)
-        spread(2 * step + 2, 0, step + 1, even)
-        gather(2 * step + 1, odd)
+        interleave(spread(2 * step + 1, 1, step, odd), gather(2 * step, even))
+        interleave(spread(2 * step + 2, 0, step + 1, even), gather(2 * step + 1, odd))
         return carry
 
     last = tiles // 2 - 1
     lax.fori_loop(0, last, two_tiles, 0)
-    spread(tiles - 1, 1, last, odd)
-    gather(tiles - 2, even)
-    gather(tiles - 1, odd)
+    interleave(spread(tiles - 1, 1, last, odd), gather(tiles - 2, even))
+    for product in gather(tiles - 1, odd):
+        product()
     shape = out_ref.shape[:2] + (share, width)
     for slot in range(own):
         out_ref[:, :, 0, slot] = (key_total[slot] * score_scale).reshape(shape)

time: 42.9 us -> 42.2 us (0.984)
  Pallas kernels: 10.2 us -> 9.54 us
    pallas_call x1, Pallas kernels: 4.51 us -> 4.05 us  [second_half(): pl.pallas_call(functools.partial(second_half_kernel, score_scale, tiles /...]
  transfers between devices with their start and end apart: 17 -> 17, of which waited for: 9 -> 9; matrix products, arithmetic and copies ran while one was open for 8% -> 8% of each run, Pallas kernels for 11% -> 10%
where the time goes in v10:
time: 42.2 us; the launch traced here: 41.8 us
  starting transfers between devices  18 us (43%)
  Pallas kernels  9.54 us (23%)
  waiting for transfers between devices  9.22 us (22%)
  local copies, waits for them, and re-layouts  4.31 us (10%)
  between operations  0.79 us (2%)
    ppermute x17, starting transfers between devices, swap(): lax.ppermute(value, axis, [(place, place ^ flip) for place in range(size)])  18 us
    ppermute x17, waiting for transfers between devices, swap(): lax.ppermute(value, axis, [(place, place ^ flip) for place in range(size)])  9.22 us
    pallas_call x1, Pallas kernels, second_half(): pl.pallas_call(functools.partial(second_half_kernel, score_scale, tiles /...  4.05 us
    dynamic_slice x2, local copies, waits for them, and re-layouts, tiles_of(): part = lax.dynamic_slice_in_dim(part, first_group, own, 1)  2.69 us
    pallas_call x1, Pallas kernels, first_half(): pl.pallas_call(functools.partial(first_half_kernel, score_scale, tiles //...  2.49 us
    pallas_call x1, Pallas kernels, finish(): pl.pallas_call(functools.partial(finish_kernel, score_scale, tiles // own...  1.89 us
    unnamed x12, local copies, waits for them, and re-layouts  1.3 us
    pallas_call x1, Pallas kernels, adam(): pl.pallas_call(functools.partial(adam_kernel, len(parts)), out_shape=(sha...  0.89 us
  transfers between devices with their start and end apart: 17, of which 9 were waited for; matrix products, arithmetic and copies ran while one was open for 8% of the time, Pallas kernels for 10%

profile of v10, /device:TPU:0, one launch (start us, length us, event | category | flops | bytes accessed | tf_op | source)
XLA Modules:
  0.0 41.8 jit_solution(18008198570815739760)
XLA Ops:
  0.6 0.0 copy-start
  0.6 0.9 %copy-done = f32[16,2,8,128]{3,2,1,0:T(8,128)S(1)} copy-done((f32[16,2,8,128]{3,2,1,0:T(8,128)S(1)}, f32[16,2,8,128]{3,2,1,0:T(8,128)}, u32[]{:S(2)}) %copy-start) | copy-done | bytes 131096
  1.5 0.1 pack.1
  1.7 5.1 %collective-permute-start = (bf16[2,2,16,128]{3,2,1,0:T(8,128)(2,1)S(1)}, bf16[2,2,16,128]{3,2,1,0:T(8,128)(2,1)S(1)}, u32[]{:S(2)}, u32[]{:S(2)}) collective-permute-start(bf16[2,2,16,128]{3,2,1,0:T(8,128)(2,1)S(1)} %get-tuple-element.30), channel_id=1, source_target_pairs={{0,3},{1,2},{2,1},{3,0},{4,7},{5,6},{6,5},{7,4},{8,11},{9,10},{10,... | collective-permute-start | bytes 49160 | tf_op jit(solution)/shard_map/ppermute | solution.py:476
  6.8 0.0 collective-permute-start.1
  6.8 0.6 %collective-permute-start.2 = (bf16[2,2,16,128]{3,2,1,0:T(8,128)(2,1)S(1)}, bf16[2,2,16,128]{3,2,1,0:T(8,128)(2,1)S(1)}, u32[]{:S(2)}, u32[]{:S(2)}) collective-permute-start(bf16[2,2,16,128]{3,2,1,0:T(8,128)(2,1)S(1)} %get-tuple-element.32), channel_id=1, source_target_pairs={{0,1},{1,0},{2,3},{3,2},{4,5},{5,4},{6,7},{7,6},{8,9},{9,8},{10,11... | collective-permute-start | bytes 49160 | tf_op jit(solution)/shard_map/ppermute | solution.py:476
  7.4 2.0 %constant_dynamic-slice_fusion.2 = (bf16[256,2,8,128]{3,2,1,0:T(8,128)(2,1)S(1)}, bf16[256,2,8,128]{3,2,1,0:T(8,128)(2,1)S(1)}) fusion(bf16[256,8,8,128]{3,2,1,0:T(8,128)(2,1)} %bitcast.25, s32[]{:T(128)S(6)} %select_n.9, bf16[256,8,8,128]{3,2,1,0:T(8,128)(2,1)} %bitcast.26), kind=kLoop, calls=%fused_computation.3 | loop fusion | bytes 4194308 | tf_op jit(solution)/shard_map/dynamic_slice | solution.py:507
  9.4 0.0 collective-permute-done
  9.4 2.0 %collective-permute-done.1 = bf16[2,2,16,128]{3,2,1,0:T(8,128)(2,1)S(1)} collective-permute-done((bf16[2,2,16,128]{3,2,1,0:T(8,128)(2,1)S(1)}, bf16[2,2,16,128]{3,2,1,0:T(8,128)(2,1)S(1)}, u32[]{:S(2)}, u32[]{:S(2)}) %collective-permute-start.1) | collective-permute-done | bytes 16416 | tf_op jit(solution)/shard_map/ppermute | solution.py:476
  11.4 0.0 collective-permute-done.2
  11.5 2.5 %collective-permute-start.5 = (bf16[4,2,2,16,128]{4,3,2,1,0:T(8,128)(2,1)S(1)}, bf16[4,2,2,16,128]{4,3,2,1,0:T(8,128)(2,1)S(1)}, u32[]{:S(2)}, u32[]{:S(2)}) collective-permute-start(bf16[4,2,2,16,128]{4,3,2,1,0:T(8,128)(2,1)S(1)} %pad_maximum_fusion.refs_0_), channel_id=1, source_target_pairs={{0,24},{4,28},{8,16},{12,20},{16,8},{20,12},{24,0},{28,4},{1,25},{... | collective-permute-start | bytes 196616 | tf_op jit(solution)/shard_map/ppermute | solution.py:476
  14.0 0.5 %collective-permute-start.4 = (bf16[4,2,2,16,128]{4,3,2,1,0:T(8,128)(2,1)S(1)}, bf16[4,2,2,16,128]{4,3,2,1,0:T(8,128)(2,1)S(1)}, u32[]{:S(2)}, u32[]{:S(2)}) collective-permute-start(bf16[4,2,2,16,128]{4,3,2,1,0:T(8,128)(2,1)S(1)} %pad_maximum_fusion.refs_0_), channel_id=1, source_target_pairs={{0,16},{4,20},{8,24},{12,28},{16,0},{20,4},{24,8},{28,12},{1,17},{... | collective-permute-start | bytes 196616 | tf_op jit(solution)/shard_map/ppermute | solution.py:476
  14.5 0.5 %collective-permute-start.3 = (bf16[4,2,2,16,128]{4,3,2,1,0:T(8,128)(2,1)S(1)}, bf16[4,2,2,16,128]{4,3,2,1,0:T(8,128)(2,1)S(1)}, u32[]{:S(2)}, u32[]{:S(2)}) collective-permute-start(bf16[4,2,2,16,128]{4,3,2,1,0:T(8,128)(2,1)S(1)} %pad_maximum_fusion.refs_0_), channel_id=1, source_target_pairs={{0,8},{4,12},{8,0},{12,4},{16,24},{20,28},{24,16},{28,20},{1,9},{5... | collective-permute-start | bytes 196616 | tf_op jit(solution)/shard_map/ppermute | solution.py:476
  15.0 0.7 %constant_dynamic-slice_fusion = (f32[256,2,8]{0,2,1:T(8,128)S(1)}, f32[256,2,8]{0,2,1:T(8,128)S(1)}) fusion(f32[256,8,8]{0,2,1:T(8,128)} %bitcast.30, s32[]{:T(128)S(6)} %select_n.9, f32[256,8,8]{0,2,1:T(8,128)} %bitcast.31), kind=kLoop, calls=%fused_computation.1 | loop fusion | bytes 65540 | tf_op jit(solution)/shard_map/dynamic_slice | solution.py:507
  15.7 0.1 copy.21
  15.9 0.2 reshape.37.refs_7_
  16.0 0.1 copy.20
  16.2 0.2 reshape.35.refs_6_
  16.3 0.1 copy.19
  16.4 0.1 copy.18
  16.5 0.1 collective-permute-start.9
  16.6 0.7 %collective-permute-done.5.refs_3_ = bf16[4,2,2,16,128]{4,3,2,1,0:T(8,128)(2,1)S(1)} collective-permute-done((bf16[4,2,2,16,128]{4,3,2,1,0:T(8,128)(2,1)S(1)}, bf16[4,2,2,16,128]{4,3,2,1,0:T(8,128)(2,1)S(1)}, u32[]{:S(2)}, u32[]{:S(2)}) %collective-permute-start.5) | collective-permute-done | bytes 65568 | tf_op jit(solution)/shard_map/ppermute | solution.py:476
  17.3 0.0 collective-permute-start.6
  17.3 1.0 %collective-permute-done.4.refs_2_ = bf16[4,2,2,16,128]{4,3,2,1,0:T(8,128)(2,1)S(1)} collective-permute-done((bf16[4,2,2,16,128]{4,3,2,1,0:T(8,128)(2,1)S(1)}, bf16[4,2,2,16,128]{4,3,2,1,0:T(8,128)(2,1)S(1)}, u32[]{:S(2)}, u32[]{:S(2)}) %collective-permute-start.4) | collective-permute-done | bytes 65568 | tf_op jit(solution)/shard_map/ppermute | solution.py:476
  18.2 0.0 collective-permute-start.7
  18.2 0.5 %collective-permute-done.3.refs_1_ = bf16[4,2,2,16,128]{4,3,2,1,0:T(8,128)(2,1)S(1)} collective-permute-done((bf16[4,2,2,16,128]{4,3,2,1,0:T(8,128)(2,1)S(1)}, bf16[4,2,2,16,128]{4,3,2,1,0:T(8,128)(2,1)S(1)}, u32[]{:S(2)}, u32[]{:S(2)}) %collective-permute-start.3) | collective-permute-done | bytes 65568 | tf_op jit(solution)/shard_map/ppermute | solution.py:476
  18.7 0.0 collective-permute-start.8
  18.7 2.5 %first_half.1 = (f32[4,256,512]{2,1,0:T(8,128)S(1)}, f32[4,256,512]{2,1,0:T(8,128)S(1)}, f32[4,256,512]{2,1,0:T(8,128)S(1)}, f32[4,256,512]{2,1,0:T(8,128)S(1)},...) custom-call(bf16[4,2,2,16,128]{4,3,2,1,0:T(8,128)(2,1)S(1)} %pad_maximum_fusion.refs_0_, ...), custom_call_target="tpu_custom_call" | custom-call | flops 536870912 | bytes 8388608 | tf_op jit(solution)/shard_map/first_half/pallas_call | solution.py:203
  21.2 0.0 collective-permute-done.9.refs_3_
  21.3 0.0 collective-permute-done.6.refs_0_
  21.3 0.0 collective-permute-done.7.refs_1_
  21.3 0.0 collective-permute-done.8.refs_2_
  21.3 4.0 %second_half.1 = (bf16[4,4,2,2,16,128]{5,4,3,2,1,0:T(8,128)(2,1)S(1)}, f32[8,1,512]{2,1,0:T(1,128)S(1)}, f32[8,1,512]{2,1,0:T(1,128)S(1)}) custom-call(bf16[4,2,2,16,128]{4,3,2,1,0:T(8,128)(2,1)S(1)} %collective-permute-done.6.refs_0_, bf16[4,2,2,16,128]{4,3,2,1,0:T(8,128)(2,1)S(1)} %collective-permute-done.7.refs_1_, ...), custom_call_target="tpu_custom_call" | custom-call | flops 1073741824 | bytes 2097152 | tf_op jit(solution)/shard_map/second_half/pallas_call | solution.py:300
  25.3 0.6 %collective-permute-start.10 = (bf16[4,4,2,2,16,128]{5,4,3,2,1,0:T(8,128)(2,1)S(1)}, bf16[4,4,2,2,16,128]{5,4,3,2,1,0:T(8,128)(2,1)S(1)}, u32[]{:S(2)}, u32[]{:S(2)}) collective-permute-start(bf16[4,4,2,2,16,128]{5,4,3,2,1,0:T(8,128)(2,1)S(1)} %get-tuple-element.48), channel_id=1, source_target_pairs={{0,4},{4,0},{8,12},{12,8},{16,20},{20,16},{24,28},{28,24},{1,5},{5... | collective-permute-start | bytes 786440 | tf_op jit(solution)/shard_map/ppermute | solution.py:476
  25.9 0.0 copy-start.1
  25.9 0.0 copy-start.2
  25.9 0.0 copy-start.3
  25.9 1.9 %finish.1.mine_ref = f32[4,4,2,2,16,128]{5,4,3,2,1,0:T(8,128)S(1)} custom-call(f32[4,256,512]{2,1,0:T(8,128)S(1)} %get-tuple-element.38.refs_0_, f32[4,256,512]{2,1,0:T(8,128)S(1)} %get-tuple-element.39.refs_1_, f32[4,256,512]{2,1,0:T(8,128)S(1)} %get-tuple-element.40.refs_2_, f32[4,256,512]{2,1,0:T(8,128)S(1)} %get-tuple-element.41.refs_3_, ...), custom_call_target="tpu_custom_call" | custom-call | flops 536870912 | bytes 8388608 | tf_op jit(solution)/shard_map/finish/pallas_call | solution.py:373
  27.8 0.0 collective-permute-done.10.mate_ref
  27.9 1.6 %collective-permute-start.11 = (bf16[4,2,2,16,128]{4,3,2,1,0:T(8,128)(2,1)S(1)}, bf16[4,2,2,16,128]{4,3,2,1,0:T(8,128)(2,1)S(1)}, u32[]{:S(2)}, u32[]{:S(2)}) collective-permute-start(bf16[4,2,2,16,128]{4,3,2,1,0:T(8,128)(2,1)S(1)} %get-tuple-element.50), channel_id=1, source_target_pairs={{0,24},{4,28},{8,16},{12,20},{16,8},{20,12},{24,0},{28,4},{1,25},{... | collective-permute-start | bytes 196616 | tf_op jit(solution)/shard_map/ppermute | solution.py:476
  29.4 0.5 %collective-permute-start.12 = (bf16[4,2,2,16,128]{4,3,2,1,0:T(8,128)(2,1)S(1)}, bf16[4,2,2,16,128]{4,3,2,1,0:T(8,128)(2,1)S(1)}, u32[]{:S(2)}, u32[]{:S(2)}) collective-permute-start(bf16[4,2,2,16,128]{4,3,2,1,0:T(8,128)(2,1)S(1)} %get-tuple-element.51), channel_id=1, source_target_pairs={{0,16},{4,20},{8,24},{12,28},{16,0},{20,4},{24,8},{28,12},{1,17},{... | collective-permute-start | bytes 196616 | tf_op jit(solution)/shard_map/ppermute | solution.py:476
  29.9 1.5 %collective-permute-start.13 = (bf16[4,2,2,16,128]{4,3,2,1,0:T(8,128)(2,1)S(1)}, bf16[4,2,2,16,128]{4,3,2,1,0:T(8,128)(2,1)S(1)}, u32[]{:S(2)}, u32[]{:S(2)}) collective-permute-start(bf16[4,2,2,16,128]{4,3,2,1,0:T(8,128)(2,1)S(1)} %get-tuple-element.52), channel_id=1, source_target_pairs={{0,8},{4,12},{8,0},{12,4},{16,24},{20,28},{24,16},{28,20},{1,9},{5... | collective-permute-start | bytes 196616 | tf_op jit(solution)/shard_map/ppermute | solution.py:476
  31.4 1.9 %collective-permute-done.11.refs_0_ = bf16[4,2,2,16,128]{4,3,2,1,0:T(8,128)(2,1)S(1)} collective-permute-done((bf16[4,2,2,16,128]{4,3,2,1,0:T(8,128)(2,1)S(1)}, bf16[4,2,2,16,128]{4,3,2,1,0:T(8,128)(2,1)S(1)}, u32[]{:S(2)}, u32[]{:S(2)}) %collective-permute-start.11) | collective-permute-done | bytes 65568 | tf_op jit(solution)/shard_map/ppermute | solution.py:476
  33.3 1.0 %collective-permute-done.12.refs_1_ = bf16[4,2,2,16,128]{4,3,2,1,0:T(8,128)(2,1)S(1)} collective-permute-done((bf16[4,2,2,16,128]{4,3,2,1,0:T(8,128)(2,1)S(1)}, bf16[4,2,2,16,128]{4,3,2,1,0:T(8,128)(2,1)S(1)}, u32[]{:S(2)}, u32[]{:S(2)}) %collective-permute-start.12) | collective-permute-done | bytes 65568 | tf_op jit(solution)/shard_map/ppermute | solution.py:476
  34.3 0.1 collective-permute-done.13.refs_2_
  34.4 1.9 %collective-permute-start.14 = (bf16[2,2,16,128]{3,2,1,0:T(8,128)(2,1)S(1)}, bf16[2,2,16,128]{3,2,1,0:T(8,128)(2,1)S(1)}, u32[]{:S(2)}, u32[]{:S(2)}) collective-permute-start(bf16[2,2,16,128]{3,2,1,0:T(8,128)(2,1)S(1)} %get-tuple-element.53), channel_id=1, source_target_pairs={{0,3},{1,2},{2,1},{3,0},{4,7},{5,6},{6,5},{7,4},{8,11},{9,10},{10,... | collective-permute-start | bytes 49160 | tf_op jit(solution)/shard_map/ppermute | solution.py:476
  36.3 0.2 collective-permute-start.15
  36.5 2.3 %collective-permute-start.16 = (bf16[2,2,16,128]{3,2,1,0:T(8,128)(2,1)S(1)}, bf16[2,2,16,128]{3,2,1,0:T(8,128)(2,1)S(1)}, u32[]{:S(2)}, u32[]{:S(2)}) collective-permute-start(bf16[2,2,16,128]{3,2,1,0:T(8,128)(2,1)S(1)} %get-tuple-element.55), channel_id=1, source_target_pairs={{0,1},{1,0},{2,3},{3,2},{4,5},{5,4},{6,7},{7,6},{8,9},{9,8},{10,11... | collective-permute-start | bytes 49160 | tf_op jit(solution)/shard_map/ppermute | solution.py:476
  38.8 1.1 %collective-permute-done.14.refs_0_ = bf16[2,2,16,128]{3,2,1,0:T(8,128)(2,1)S(1)} collective-permute-done((bf16[2,2,16,128]{3,2,1,0:T(8,128)(2,1)S(1)}, bf16[2,2,16,128]{3,2,1,0:T(8,128)(2,1)S(1)}, u32[]{:S(2)}, u32[]{:S(2)}) %collective-permute-start.14) | collective-permute-done | bytes 16416 | tf_op jit(solution)/shard_map/ppermute | solution.py:476
  40.0 0.9 %collective-permute-done.15.refs_1_ = bf16[2,2,16,128]{3,2,1,0:T(8,128)(2,1)S(1)} collective-permute-done((bf16[2,2,16,128]{3,2,1,0:T(8,128)(2,1)S(1)}, bf16[2,2,16,128]{3,2,1,0:T(8,128)(2,1)S(1)}, u32[]{:S(2)}, u32[]{:S(2)}) %collective-permute-start.15) | collective-permute-done | bytes 16416 | tf_op jit(solution)/shard_map/ppermute | solution.py:476
  40.9 0.0 collective-permute-done.16.refs_2_
  40.9 0.0 copy-done.1
  40.9 0.0 copy-done.2
  40.9 0.0 copy-done.3
  40.9 0.9 %adam.1 = (f32[16,2,8,128]{3,2,1,0:T(8,128)}, f32[16,2,8,128]{3,2,1,0:T(8,128)}, f32[16,2,8,128]{3,2,1,0:T(8,128)}) custom-call(bf16[2,2,16,128]{3,2,1,0:T(8,128)(2,1)S(1)} %collective-permute-done.14.refs_0_, bf16[2,2,16,128]{3,2,1,0:T(8,128)(2,1)S(1)} %collective-permute-done.15.refs_1_, bf16[2,2,16,128]{3,2,1,0:T(8,128)(2,1)S(1)} %collective-permute-done.16.refs_2_, ...), custom_call_target="tpu_custom_call" | custom-call | tf_op jit(solution)/shard_map/adam/pallas_call | solution.py:463
  (3 shorter events, 0.1 us)
Async XLA Ops:
  0.6 0.9 %copy-start = (f32[16,2,8,128]{3,2,1,0:T(8,128)S(1)}, f32[16,2,8,128]{3,2,1,0:T(8,128)}, u32[]{:S(2)}) copy-start(f32[16,2,8,128]{3,2,1,0:T(8,128)} %refs_4_.1) | copy-start | bytes 393220
  1.7 7.7 %collective-permute-start = (bf16[2,2,16,128]{3,2,1,0:T(8,128)(2,1)S(1)}, bf16[2,2,16,128]{3,2,1,0:T(8,128)(2,1)S(1)}, u32[]{:S(2)}, u32[]{:S(2)}) collective-permute-start(bf16[2,2,16,128]{3,2,1,0:T(8,128)(2,1)S(1)} %get-tuple-element.30), channel_id=1, source_target_pairs={{0,3},{1,2},{2,1},{3,0},{4,7},{5,6},{6,5},{7,4},{8,11},{9,10},{10,... | collective-permute-start | bytes 49160 | tf_op jit(solution)/shard_map/ppermute | solution.py:476
  6.8 4.6 %collective-permute-start.1 = (bf16[2,2,16,128]{3,2,1,0:T(8,128)(2,1)S(1)}, bf16[2,2,16,128]{3,2,1,0:T(8,128)(2,1)S(1)}, u32[]{:S(2)}, u32[]{:S(2)}) collective-permute-start(bf16[2,2,16,128]{3,2,1,0:T(8,128)(2,1)S(1)} %get-tuple-element.31), channel_id=1, source_target_pairs={{0,2},{1,3},{2,0},{3,1},{4,6},{5,7},{6,4},{7,5},{8,10},{9,11},{10,... | collective-permute-start | bytes 49160 | tf_op jit(solution)/shard_map/ppermute | solution.py:476
  6.8 4.6 %collective-permute-start.2 = (bf16[2,2,16,128]{3,2,1,0:T(8,128)(2,1)S(1)}, bf16[2,2,16,128]{3,2,1,0:T(8,128)(2,1)S(1)}, u32[]{:S(2)}, u32[]{:S(2)}) collective-permute-start(bf16[2,2,16,128]{3,2,1,0:T(8,128)(2,1)S(1)} %get-tuple-element.32), channel_id=1, source_target_pairs={{0,1},{1,0},{2,3},{3,2},{4,5},{5,4},{6,7},{7,6},{8,9},{9,8},{10,11... | collective-permute-start | bytes 49160 | tf_op jit(solution)/shard_map/ppermute | solution.py:476
  11.5 5.8 %collective-permute-start.5 = (bf16[4,2,2,16,128]{4,3,2,1,0:T(8,128)(2,1)S(1)}, bf16[4,2,2,16,128]{4,3,2,1,0:T(8,128)(2,1)S(1)}, u32[]{:S(2)}, u32[]{:S(2)}) collective-permute-start(bf16[4,2,2,16,128]{4,3,2,1,0:T(8,128)(2,1)S(1)} %pad_maximum_fusion.refs_0_), channel_id=1, source_target_pairs={{0,24},{4,28},{8,16},{12,20},{16,8},{20,12},{24,0},{28,4},{1,25},{... | collective-permute-start | bytes 196616 | tf_op jit(solution)/shard_map/ppermute | solution.py:476
  14.0 4.3 %collective-permute-start.4 = (bf16[4,2,2,16,128]{4,3,2,1,0:T(8,128)(2,1)S(1)}, bf16[4,2,2,16,128]{4,3,2,1,0:T(8,128)(2,1)S(1)}, u32[]{:S(2)}, u32[]{:S(2)}) collective-permute-start(bf16[4,2,2,16,128]{4,3,2,1,0:T(8,128)(2,1)S(1)} %pad_maximum_fusion.refs_0_), channel_id=1, source_target_pairs={{0,16},{4,20},{8,24},{12,28},{16,0},{20,4},{24,8},{28,12},{1,17},{... | collective-permute-start | bytes 196616 | tf_op jit(solution)/shard_map/ppermute | solution.py:476
  14.5 4.3 %collective-permute-start.3 = (bf16[4,2,2,16,128]{4,3,2,1,0:T(8,128)(2,1)S(1)}, bf16[4,2,2,16,128]{4,3,2,1,0:T(8,128)(2,1)S(1)}, u32[]{:S(2)}, u32[]{:S(2)}) collective-permute-start(bf16[4,2,2,16,128]{4,3,2,1,0:T(8,128)(2,1)S(1)} %pad_maximum_fusion.refs_0_), channel_id=1, source_target_pairs={{0,8},{4,12},{8,0},{12,4},{16,24},{20,28},{24,16},{28,20},{1,9},{5... | collective-permute-start | bytes 196616 | tf_op jit(solution)/shard_map/ppermute | solution.py:476
  16.5 4.8 %collective-permute-start.9 = (bf16[4,2,2,16,128]{4,3,2,1,0:T(8,128)(2,1)S(1)}, bf16[4,2,2,16,128]{4,3,2,1,0:T(8,128)(2,1)S(1)}, u32[]{:S(2)}, u32[]{:S(2)}) collective-permute-start(bf16[4,2,2,16,128]{4,3,2,1,0:T(8,128)(2,1)S(1)} %pad_maximum_fusion.refs_0_), channel_id=1, source_target_pairs={{0,4},{4,0},{8,12},{12,8},{16,20},{20,16},{24,28},{28,24},{1,5},{5... | collective-permute-start | bytes 196616 | tf_op jit(solution)/shard_map/ppermute | solution.py:476
  17.3 4.0 %collective-permute-start.6 = (bf16[4,2,2,16,128]{4,3,2,1,0:T(8,128)(2,1)S(1)}, bf16[4,2,2,16,128]{4,3,2,1,0:T(8,128)(2,1)S(1)}, u32[]{:S(2)}, u32[]{:S(2)}) collective-permute-start(bf16[4,2,2,16,128]{4,3,2,1,0:T(8,128)(2,1)S(1)} %collective-permute-done.5.refs_3_), channel_id=1, source_target_pairs={{0,4},{4,0},{8,12},{12,8},{16,20},{20,16},{24,28},{28,24},{1,5},{5... | collective-permute-start | bytes 196616 | tf_op jit(solution)/shard_map/ppermute | solution.py:476
  18.2 3.0 %collective-permute-start.7 = (bf16[4,2,2,16,128]{4,3,2,1,0:T(8,128)(2,1)S(1)}, bf16[4,2,2,16,128]{4,3,2,1,0:T(8,128)(2,1)S(1)}, u32[]{:S(2)}, u32[]{:S(2)}) collective-permute-start(bf16[4,2,2,16,128]{4,3,2,1,0:T(8,128)(2,1)S(1)} %collective-permute-done.4.refs_2_), channel_id=1, source_target_pairs={{0,4},{4,0},{8,12},{12,8},{16,20},{20,16},{24,28},{28,24},{1,5},{5... | collective-permute-start | bytes 196616 | tf_op jit(solution)/shard_map/ppermute | solution.py:476
  18.7 2.5 %collective-permute-start.8 = (bf16[4,2,2,16,128]{4,3,2,1,0:T(8,128)(2,1)S(1)}, bf16[4,2,2,16,128]{4,3,2,1,0:T(8,128)(2,1)S(1)}, u32[]{:S(2)}, u32[]{:S(2)}) collective-permute-start(bf16[4,2,2,16,128]{4,3,2,1,0:T(8,128)(2,1)S(1)} %collective-permute-done.3.refs_1_), channel_id=1, source_target_pairs={{0,4},{4,0},{8,12},{12,8},{16,20},{20,16},{24,28},{28,24},{1,5},{5... | collective-permute-start | bytes 196616 | tf_op jit(solution)/shard_map/ppermute | solution.py:476
  25.3 2.5 %collective-permute-start.10 = (bf16[4,4,2,2,16,128]{5,4,3,2,1,0:T(8,128)(2,1)S(1)}, bf16[4,4,2,2,16,128]{5,4,3,2,1,0:T(8,128)(2,1)S(1)}, u32[]{:S(2)}, u32[]{:S(2)}) collective-permute-start(bf16[4,4,2,2,16,128]{5,4,3,2,1,0:T(8,128)(2,1)S(1)} %get-tuple-element.48), channel_id=1, source_target_pairs={{0,4},{4,0},{8,12},{12,8},{16,20},{20,16},{24,28},{28,24},{1,5},{5... | collective-permute-start | bytes 786440 | tf_op jit(solution)/shard_map/ppermute | solution.py:476
  25.9 15.0 %copy-start.1 = (f32[16,2,8,128]{3,2,1,0:T(8,128)S(1)}, f32[16,2,8,128]{3,2,1,0:T(8,128)}, u32[]{:S(2)}) copy-start(f32[16,2,8,128]{3,2,1,0:T(8,128)} %refs_4_.1) | copy-start | bytes 393220
  25.9 15.0 %copy-start.2 = (f32[16,2,8,128]{3,2,1,0:T(8,128)S(1)}, f32[16,2,8,128]{3,2,1,0:T(8,128)}, u32[]{:S(2)}) copy-start(f32[16,2,8,128]{3,2,1,0:T(8,128)} %refs_5_.1) | copy-start | bytes 393220
  25.9 15.0 %copy-start.3 = (f32[16,2,8,128]{3,2,1,0:T(8,128)S(1)}, f32[16,2,8,128]{3,2,1,0:T(8,128)}, u32[]{:S(2)}) copy-start(f32[16,2,8,128]{3,2,1,0:T(8,128)} %refs_6_.1) | copy-start | bytes 393220
  27.9 5.4 %collective-permute-start.11 = (bf16[4,2,2,16,128]{4,3,2,1,0:T(8,128)(2,1)S(1)}, bf16[4,2,2,16,128]{4,3,2,1,0:T(8,128)(2,1)S(1)}, u32[]{:S(2)}, u32[]{:S(2)}) collective-permute-start(bf16[4,2,2,16,128]{4,3,2,1,0:T(8,128)(2,1)S(1)} %get-tuple-element.50), channel_id=1, source_target_pairs={{0,24},{4,28},{8,16},{12,20},{16,8},{20,12},{24,0},{28,4},{1,25},{... | collective-permute-start | bytes 196616 | tf_op jit(solution)/shard_map/ppermute | solution.py:476
  29.4 4.9 %collective-permute-start.12 = (bf16[4,2,2,16,128]{4,3,2,1,0:T(8,128)(2,1)S(1)}, bf16[4,2,2,16,128]{4,3,2,1,0:T(8,128)(2,1)S(1)}, u32[]{:S(2)}, u32[]{:S(2)}) collective-permute-start(bf16[4,2,2,16,128]{4,3,2,1,0:T(8,128)(2,1)S(1)} %get-tuple-element.51), channel_id=1, source_target_pairs={{0,16},{4,20},{8,24},{12,28},{16,0},{20,4},{24,8},{28,12},{1,17},{... | collective-permute-start | bytes 196616 | tf_op jit(solution)/shard_map/ppermute | solution.py:476
  29.9 4.4 %collective-permute-start.13 = (bf16[4,2,2,16,128]{4,3,2,1,0:T(8,128)(2,1)S(1)}, bf16[4,2,2,16,128]{4,3,2,1,0:T(8,128)(2,1)S(1)}, u32[]{:S(2)}, u32[]{:S(2)}) collective-permute-start(bf16[4,2,2,16,128]{4,3,2,1,0:T(8,128)(2,1)S(1)} %get-tuple-element.52), channel_id=1, source_target_pairs={{0,8},{4,12},{8,0},{12,4},{16,24},{20,28},{24,16},{28,20},{1,9},{5... | collective-permute-start | bytes 196616 | tf_op jit(solution)/shard_map/ppermute | solution.py:476
  34.4 5.6 %collective-permute-start.14 = (bf16[2,2,16,128]{3,2,1,0:T(8,128)(2,1)S(1)}, bf16[2,2,16,128]{3,2,1,0:T(8,128)(2,1)S(1)}, u32[]{:S(2)}, u32[]{:S(2)}) collective-permute-start(bf16[2,2,16,128]{3,2,1,0:T(8,128)(2,1)S(1)} %get-tuple-element.53), channel_id=1, source_target_pairs={{0,3},{1,2},{2,1},{3,0},{4,7},{5,6},{6,5},{7,4},{8,11},{9,10},{10,... | collective-permute-start | bytes 49160 | tf_op jit(solution)/shard_map/ppermute | solution.py:476
  36.3 4.6 %collective-permute-start.15 = (bf16[2,2,16,128]{3,2,1,0:T(8,128)(2,1)S(1)}, bf16[2,2,16,128]{3,2,1,0:T(8,128)(2,1)S(1)}, u32[]{:S(2)}, u32[]{:S(2)}) collective-permute-start(bf16[2,2,16,128]{3,2,1,0:T(8,128)(2,1)S(1)} %get-tuple-element.54), channel_id=1, source_target_pairs={{0,2},{1,3},{2,0},{3,1},{4,6},{5,7},{6,4},{7,5},{8,10},{9,11},{10,... | collective-permute-start | bytes 49160 | tf_op jit(solution)/shard_map/ppermute | solution.py:476
  36.5 4.4 %collective-permute-start.16 = (bf16[2,2,16,128]{3,2,1,0:T(8,128)(2,1)S(1)}, bf16[2,2,16,128]{3,2,1,0:T(8,128)(2,1)S(1)}, u32[]{:S(2)}, u32[]{:S(2)}) collective-permute-start(bf16[2,2,16,128]{3,2,1,0:T(8,128)(2,1)S(1)} %get-tuple-element.55), channel_id=1, source_target_pairs={{0,1},{1,0},{2,3},{3,2},{4,5},{5,4},{6,7},{7,6},{8,9},{9,8},{10,11... | collective-permute-start | bytes 49160 | tf_op jit(solution)/shard_map/ppermute | solution.py:476

commit v11 on v10

--- a/solution.py
+++ b/solution.py
@@ -80,12 +80,15 @@
         product()
 
 
-def score_products(keys, values, slot, queries_ref, grads_ref, tile, scores, slopes):
+def score_products(keys, values, slot, queries_ref, grads_ref, tile, scores, slopes, tops):
     def product(rows, left, right_ref, out):
         def run():
-            out[:, rows] = lax.dot_general(
+            found = lax.dot_general(
                 left[slot], right_ref[tile, rows], ACROSS, preferred_element_type=jnp.float32
             )
+            out[:, rows] = found
+            if out is scores:
+                tops[:, rows] = jnp.max(found.reshape(-1, 8, found.shape[1]), axis=0)
 
         return run
 
@@ -116,21 +119,13 @@
     return [pl.ds(start, CHUNK) for start in range(0, ref.shape[0], CHUNK)]
 
 
-def largest(scores, result):
-    top = None
-    for cut in cuts_of(scores):
-        top = scores[cut] if top is None else jnp.maximum(top, scores[cut])
-        yield
-    result.append(jnp.max(top, axis=0, keepdims=True))
-
-
-def exponentiate(scores, slopes, factor, peak, result):
+def exponentiate(scores, slopes, factor, peak, kept, result):
     total = None
     dotted = None
     for cut in cuts_of(scores):
         shifted = jnp.exp2(scores[cut] * factor - peak)
         product = shifted * slopes[cut]
-        scores[cut] = shifted
+        kept[cut] = shifted.astype(jnp.bfloat16)
         total = shifted if total is None else total + shifted
         dotted = product if dotted is None else dotted + product
         yield
@@ -138,9 +133,9 @@
     result.append(jnp.sum(dotted, axis=0, keepdims=True))
 
 
-def weigh(shifted, slopes, inverse, delta, weights, dscores):
+def weigh(kept, slopes, inverse, delta, weights, dscores):
     for cut in cuts_of(weights):
-        probability = shifted[cut] * inverse
+        probability = kept[cut].astype(jnp.float32) * inverse
         weights[cut] = probability.astype(jnp.bfloat16)
         dscores[cut] = (probability * (slopes[cut] - delta)).astype(jnp.bfloat16)
         yield
@@ -149,36 +144,38 @@
 def first_half_kernel(score_scale, per_group, pieces, *refs):
     pair_refs, refs = refs[:pieces][::-1], refs[pieces:]
     queries_ref, grads_ref, lse_ref, dot_ref = refs[:4]
-    kept, (peak_ref, total_ref, dotted_ref, keys, values) = refs[4:8], refs[8:]
+    kept, (peak_ref, total_ref, dotted_ref, keys, values) = refs[4:8], refs[8:13]
+    even, odd = refs[13:15], refs[15:17]
     tiles = queries_ref.shape[0]
     factor = score_scale * LOG2E
     load_pairs(pair_refs, keys, values)
 
-    def place(tile, parity, step):
-        return kept[2 * parity].at[step], kept[2 * parity + 1].at[step]
+    def place(parity, step):
+        scores, tops = odd if parity else even
+        return scores, kept[2 * parity].at[step], kept[2 * parity + 1].at[step], tops
 
     def products(tile, parity, step):
+        scores, _, slopes, tops = place(parity, step)
         slot = tile // per_group
         return score_products(
-            keys, values, slot, queries_ref, grads_ref, tile, *place(tile, parity, step)
+            keys, values, slot, queries_ref, grads_ref, tile, scores, slopes, tops
         )
 
     def normalize(tile, parity, step):
-        scores, slopes = place(tile, parity, step)
+        scores, shifted, slopes, tops = place(parity, step)
 
         def passes():
             side_lse = lse_ref[pl.ds(tile, 1)] * LOG2E
-            found = []
-            yield from largest(scores, found)
-            peak = jnp.maximum(found[0] * factor, side_lse)
+            peak = jnp.max(tops[...], axis=0, keepdims=True) * factor
+            peak = jnp.maximum(peak, side_lse)
             sums = []
-            yield from exponentiate(scores, slopes, factor, peak, sums)
+            yield from exponentiate(scores, slopes, factor, peak, shifted, sums)
             side = jnp.exp2(side_lse - peak)
             peak_ref[tile] = peak
             total_ref[tile] = sums[0] + side
             dotted_ref[tile] = sums[1] + side * dot_ref[pl.ds(tile, 1)]
 
-        return 2 * len(cuts_of(scores)), passes()
+        return len(cuts_of(scores)), passes()
 
     for product in products(0, 0, 0):
         product()
@@ -198,15 +195,24 @@
     columns, _, own, share, width = pairs[0].shape
     positions = len(pairs) * columns * share
     tiles, row_tile, _ = queries.shape
-    kept = jax.ShapeDtypeStruct((tiles // 2, positions, row_tile), jnp.float32)
+    kept = [
+        jax.ShapeDtypeStruct((tiles // 2, positions, row_tile), kind)
+        for kind in (jnp.bfloat16, jnp.float32)
+    ]
+    buffers = [
+        pltpu.VMEM((positions, row_tile), jnp.float32),
+        pltpu.VMEM((8, row_tile), jnp.float32),
+    ]
     stat = jax.ShapeDtypeStruct((tiles, 1, row_tile), jnp.float32)
     return pl.pallas_call(
         functools.partial(first_half_kernel, score_scale, tiles // own, len(pairs)),
-        out_shape=[kept] * 4 + [stat] * 3,
+        out_shape=kept + kept + [stat] * 3,
         scratch_shapes=[
             pltpu.VMEM((own, positions, width), jnp.bfloat16),
             pltpu.VMEM((own, positions, width), jnp.bfloat16),
-        ],
+        ]
+        + buffers
+        + buffers,
         compiler_params=pltpu.CompilerParams(vmem_limit_bytes=30 * MIB),
         cost_estimate=pl.CostEstimate(
             flops=4 * tiles * row_tile * positions * width,
@@ -222,7 +228,7 @@
     queries_ref, grads_ref, peak_ref, total_ref, dotted_ref = refs[:5]
     out_ref, inverse_ref, delta_ref = refs[5:8]
     keys, values, key_total, value_total = refs[8:12]
-    even, odd = refs[12:16], refs[16:20]
+    even, odd = refs[12:18], refs[18:24]
     _, columns, _, own, share, width = out_ref.shape
     tiles = queries_ref.shape[0]
     factor = score_scale * LOG2E
@@ -232,34 +238,32 @@
 
     def products(tile, buffers):
         slot = tile // per_group
-        return score_products(keys, values, slot, queries_ref, grads_ref, tile, *buffers[:2])
+        return score_products(keys, values, slot, queries_ref, grads_ref, tile, *buffers[:3])
 
     def normalize(tile, buffers):
-        scores, slopes, weights, dscores = buffers
+        scores, slopes, tops, shifted, weights, dscores = buffers
 
         def passes():
-            found = []
-            yield from largest(scores, found)
             first_peak = peak_ref[tile]
-            peak = jnp.maximum(found[0] * factor, first_peak)
+            peak = jnp.max(tops[...], axis=0, keepdims=True) * factor
+            peak = jnp.maximum(peak, first_peak)
             sums = []
-            yield from exponentiate(scores, slopes, factor, peak, sums)
+            yield from exponentiate(scores, slopes, factor, peak, shifted, sums)
             rescale = jnp.exp2(first_peak - peak)
             inverse = 1.0 / (sums[0] + total_ref[tile] * rescale)
             delta = (sums[1] + dotted_ref[tile] * rescale) * inverse
             inverse_ref[tile] = inverse * rescale
             delta_ref[tile] = delta
-            yield from weigh(scores, slopes, inverse, delta, weights, dscores)
-
-        return 3 * len(cuts_of(scores)), passes()
+            yield from weigh(shifted, slopes, inverse, delta, weights, dscores)
+
+        return 2 * len(cuts_of(scores)), passes()
 
     def gather(tile, buffers):
         return gradient_products(
             key_total,
             value_total,
             tile // per_group,
-            buffers[2],
-            buffers[3],
+            *buffers[4:],
             queries_ref,
             grads_ref,
             tile,
@@ -294,6 +298,8 @@
     buffers = [
         pltpu.VMEM((positions, row_tile), jnp.float32),
         pltpu.VMEM((positions, row_tile), jnp.float32),
+        pltpu.VMEM((8, row_tile), jnp.float32),
+        pltpu.VMEM((positions, row_tile), jnp.bfloat16),
         pltpu.VMEM((positions, row_tile), jnp.bfloat16),
         pltpu.VMEM((positions, row_tile), jnp.bfloat16),
     ]

time: 42.2 us -> 42.5 us (level)
  transfers between devices with their start and end apart: 17 -> 17, of which waited for: 9 -> 9; matrix products, arithmetic and copies ran while one was open for 8% -> 8% of each run, Pallas kernels for 10% -> 11%
where the time goes in v11:
time: 42.5 us; the launch traced here: 42.2 us
  starting transfers between devices  18 us (42%)
  Pallas kernels  9.82 us (23%)
  waiting for transfers between devices  9.25 us (22%)
  local copies, waits for them, and re-layouts  4.31 us (10%)
  between operations  0.79 us (2%)
    ppermute x17, starting transfers between devices, swap(): lax.ppermute(value, axis, [(place, place ^ flip) for place in range(size)])  18 us
    ppermute x17, waiting for transfers between devices, swap(): lax.ppermute(value, axis, [(place, place ^ flip) for place in range(size)])  9.25 us
    pallas_call x1, Pallas kernels, second_half(): pl.pallas_call(functools.partial(second_half_kernel, score_scale, tiles /...  4.24 us
    dynamic_slice x2, local copies, waits for them, and re-layouts, tiles_of(): part = lax.dynamic_slice_in_dim(part, first_group, own, 1)  2.69 us
    pallas_call x1, Pallas kernels, first_half(): pl.pallas_call(functools.partial(first_half_kernel, score_scale, tiles //...  2.46 us
    pallas_call x1, Pallas kernels, finish(): pl.pallas_call(functools.partial(finish_kernel, score_scale, tiles // own...  2.01 us
    unnamed x12, local copies, waits for them, and re-layouts  1.3 us
    pallas_call x1, Pallas kernels, adam(): pl.pallas_call(functools.partial(adam_kernel, len(parts)), out_shape=(sha...  0.89 us
  transfers between devices with their start and end apart: 17, of which 9 were waited for; matrix products, arithmetic and copies ran while one was open for 8% of the time, Pallas kernels for 11%

profile of v11, /device:TPU:0, one launch (start us, length us, event | category | flops | bytes accessed | tf_op | source)
XLA Modules:
  0.0 42.2 jit_solution(16583302226039554839)
XLA Ops:
  0.6 0.0 copy-start
  0.6 0.9 %copy-done = f32[16,2,8,128]{3,2,1,0:T(8,128)S(1)} copy-done((f32[16,2,8,128]{3,2,1,0:T(8,128)S(1)}, f32[16,2,8,128]{3,2,1,0:T(8,128)}, u32[]{:S(2)}) %copy-start) | copy-done | bytes 131096
  1.5 0.1 pack.1
  1.7 5.1 %collective-permute-start = (bf16[2,2,16,128]{3,2,1,0:T(8,128)(2,1)S(1)}, bf16[2,2,16,128]{3,2,1,0:T(8,128)(2,1)S(1)}, u32[]{:S(2)}, u32[]{:S(2)}) collective-permute-start(bf16[2,2,16,128]{3,2,1,0:T(8,128)(2,1)S(1)} %get-tuple-element.30), channel_id=1, source_target_pairs={{0,3},{1,2},{2,1},{3,0},{4,7},{5,6},{6,5},{7,4},{8,11},{9,10},{10,... | collective-permute-start | bytes 49160 | tf_op jit(solution)/shard_map/ppermute | solution.py:482
  6.8 0.0 collective-permute-start.1
  6.8 0.6 %collective-permute-start.2 = (bf16[2,2,16,128]{3,2,1,0:T(8,128)(2,1)S(1)}, bf16[2,2,16,128]{3,2,1,0:T(8,128)(2,1)S(1)}, u32[]{:S(2)}, u32[]{:S(2)}) collective-permute-start(bf16[2,2,16,128]{3,2,1,0:T(8,128)(2,1)S(1)} %get-tuple-element.32), channel_id=1, source_target_pairs={{0,1},{1,0},{2,3},{3,2},{4,5},{5,4},{6,7},{7,6},{8,9},{9,8},{10,11... | collective-permute-start | bytes 49160 | tf_op jit(solution)/shard_map/ppermute | solution.py:482
  7.4 2.0 %constant_dynamic-slice_fusion.2 = (bf16[256,2,8,128]{3,2,1,0:T(8,128)(2,1)S(1)}, bf16[256,2,8,128]{3,2,1,0:T(8,128)(2,1)S(1)}) fusion(bf16[256,8,8,128]{3,2,1,0:T(8,128)(2,1)} %bitcast.25, s32[]{:T(128)S(6)} %select_n.9, bf16[256,8,8,128]{3,2,1,0:T(8,128)(2,1)} %bitcast.26), kind=kLoop, calls=%fused_computation.3 | loop fusion | bytes 4194308 | tf_op jit(solution)/shard_map/dynamic_slice | solution.py:513
  9.4 0.0 collective-permute-done
  9.4 2.0 %collective-permute-done.1 = bf16[2,2,16,128]{3,2,1,0:T(8,128)(2,1)S(1)} collective-permute-done((bf16[2,2,16,128]{3,2,1,0:T(8,128)(2,1)S(1)}, bf16[2,2,16,128]{3,2,1,0:T(8,128)(2,1)S(1)}, u32[]{:S(2)}, u32[]{:S(2)}) %collective-permute-start.1) | collective-permute-done | bytes 16416 | tf_op jit(solution)/shard_map/ppermute | solution.py:482
  11.4 0.0 collective-permute-done.2
  11.5 2.5 %collective-permute-start.5 = (bf16[4,2,2,16,128]{4,3,2,1,0:T(8,128)(2,1)S(1)}, bf16[4,2,2,16,128]{4,3,2,1,0:T(8,128)(2,1)S(1)}, u32[]{:S(2)}, u32[]{:S(2)}) collective-permute-start(bf16[4,2,2,16,128]{4,3,2,1,0:T(8,128)(2,1)S(1)} %pad_maximum_fusion.refs_0_), channel_id=1, source_target_pairs={{0,24},{4,28},{8,16},{12,20},{16,8},{20,12},{24,0},{28,4},{1,25},{... | collective-permute-start | bytes 196616 | tf_op jit(solution)/shard_map/ppermute | solution.py:482
  14.0 0.5 %collective-permute-start.4 = (bf16[4,2,2,16,128]{4,3,2,1,0:T(8,128)(2,1)S(1)}, bf16[4,2,2,16,128]{4,3,2,1,0:T(8,128)(2,1)S(1)}, u32[]{:S(2)}, u32[]{:S(2)}) collective-permute-start(bf16[4,2,2,16,128]{4,3,2,1,0:T(8,128)(2,1)S(1)} %pad_maximum_fusion.refs_0_), channel_id=1, source_target_pairs={{0,16},{4,20},{8,24},{12,28},{16,0},{20,4},{24,8},{28,12},{1,17},{... | collective-permute-start | bytes 196616 | tf_op jit(solution)/shard_map/ppermute | solution.py:482
  14.5 0.5 %collective-permute-start.3 = (bf16[4,2,2,16,128]{4,3,2,1,0:T(8,128)(2,1)S(1)}, bf16[4,2,2,16,128]{4,3,2,1,0:T(8,128)(2,1)S(1)}, u32[]{:S(2)}, u32[]{:S(2)}) collective-permute-start(bf16[4,2,2,16,128]{4,3,2,1,0:T(8,128)(2,1)S(1)} %pad_maximum_fusion.refs_0_), channel_id=1, source_target_pairs={{0,8},{4,12},{8,0},{12,4},{16,24},{20,28},{24,16},{28,20},{1,9},{5... | collective-permute-start | bytes 196616 | tf_op jit(solution)/shard_map/ppermute | solution.py:482
  15.0 0.7 %constant_dynamic-slice_fusion = (f32[256,2,8]{0,2,1:T(8,128)S(1)}, f32[256,2,8]{0,2,1:T(8,128)S(1)}) fusion(f32[256,8,8]{0,2,1:T(8,128)} %bitcast.30, s32[]{:T(128)S(6)} %select_n.9, f32[256,8,8]{0,2,1:T(8,128)} %bitcast.31), kind=kLoop, calls=%fused_computation.1 | loop fusion | bytes 65540 | tf_op jit(solution)/shard_map/dynamic_slice | solution.py:513
  15.7 0.1 copy.21
  15.9 0.2 reshape.37.refs_7_
  16.0 0.1 copy.20
  16.2 0.2 reshape.35.refs_6_
  16.3 0.1 copy.19
  16.4 0.1 copy.18
  16.5 0.1 collective-permute-start.9
  16.6 0.7 %collective-permute-done.5.refs_3_ = bf16[4,2,2,16,128]{4,3,2,1,0:T(8,128)(2,1)S(1)} collective-permute-done((bf16[4,2,2,16,128]{4,3,2,1,0:T(8,128)(2,1)S(1)}, bf16[4,2,2,16,128]{4,3,2,1,0:T(8,128)(2,1)S(1)}, u32[]{:S(2)}, u32[]{:S(2)}) %collective-permute-start.5) | collective-permute-done | bytes 65568 | tf_op jit(solution)/shard_map/ppermute | solution.py:482
  17.3 0.0 collective-permute-start.6
  17.3 1.0 %collective-permute-done.4.refs_2_ = bf16[4,2,2,16,128]{4,3,2,1,0:T(8,128)(2,1)S(1)} collective-permute-done((bf16[4,2,2,16,128]{4,3,2,1,0:T(8,128)(2,1)S(1)}, bf16[4,2,2,16,128]{4,3,2,1,0:T(8,128)(2,1)S(1)}, u32[]{:S(2)}, u32[]{:S(2)}) %collective-permute-start.4) | collective-permute-done | bytes 65568 | tf_op jit(solution)/shard_map/ppermute | solution.py:482
  18.2 0.0 collective-permute-start.7
  18.2 0.5 %collective-permute-done.3.refs_1_ = bf16[4,2,2,16,128]{4,3,2,1,0:T(8,128)(2,1)S(1)} collective-permute-done((bf16[4,2,2,16,128]{4,3,2,1,0:T(8,128)(2,1)S(1)}, bf16[4,2,2,16,128]{4,3,2,1,0:T(8,128)(2,1)S(1)}, u32[]{:S(2)}, u32[]{:S(2)}) %collective-permute-start.3) | collective-permute-done | bytes 65568 | tf_op jit(solution)/shard_map/ppermute | solution.py:482
  18.7 0.0 collective-permute-start.8
  18.7 2.5 %first_half.1 = (bf16[4,256,512]{2,1,0:T(8,128)(2,1)S(1)}, f32[4,256,512]{2,1,0:T(8,128)S(1)}, bf16[4,256,512]{2,1,0:T(8,128)(2,1)S(1)}, f32[4,256,512]{2,1,0:T(...) custom-call(bf16[4,2,2,16,128]{4,3,2,1,0:T(8,128)(2,1)S(1)} %pad_maximum_fusion.refs_0_, ...), custom_call_target="tpu_custom_call" | custom-call | flops 536870912 | bytes 8388608 | tf_op jit(solution)/shard_map/first_half/pallas_call | solution.py:207
  21.2 0.0 collective-permute-done.9.refs_3_
  21.2 0.0 collective-permute-done.6.refs_0_
  21.2 0.0 collective-permute-done.7.refs_1_
  21.2 0.0 collective-permute-done.8.refs_2_
  21.3 4.2 %second_half.1 = (bf16[4,4,2,2,16,128]{5,4,3,2,1,0:T(8,128)(2,1)S(1)}, f32[8,1,512]{2,1,0:T(1,128)S(1)}, f32[8,1,512]{2,1,0:T(1,128)S(1)}) custom-call(bf16[4,2,2,16,128]{4,3,2,1,0:T(8,128)(2,1)S(1)} %collective-permute-done.6.refs_0_, bf16[4,2,2,16,128]{4,3,2,1,0:T(8,128)(2,1)S(1)} %collective-permute-done.7.refs_1_, ...), custom_call_target="tpu_custom_call" | custom-call | flops 1073741824 | bytes 2097152 | tf_op jit(solution)/shard_map/second_half/pallas_call | solution.py:306
  25.5 0.6 %collective-permute-start.10 = (bf16[4,4,2,2,16,128]{5,4,3,2,1,0:T(8,128)(2,1)S(1)}, bf16[4,4,2,2,16,128]{5,4,3,2,1,0:T(8,128)(2,1)S(1)}, u32[]{:S(2)}, u32[]{:S(2)}) collective-permute-start(bf16[4,4,2,2,16,128]{5,4,3,2,1,0:T(8,128)(2,1)S(1)} %get-tuple-element.48), channel_id=1, source_target_pairs={{0,4},{4,0},{8,12},{12,8},{16,20},{20,16},{24,28},{28,24},{1,5},{5... | collective-permute-start | bytes 786440 | tf_op jit(solution)/shard_map/ppermute | solution.py:482
  26.1 0.0 copy-start.1
  26.1 0.0 copy-start.2
  26.1 0.0 copy-start.3
  26.1 2.0 %finish.1.mine_ref = f32[4,4,2,2,16,128]{5,4,3,2,1,0:T(8,128)S(1)} custom-call(bf16[4,256,512]{2,1,0:T(8,128)(2,1)S(1)} %get-tuple-element.38.refs_0_, f32[4,256,512]{2,1,0:T(8,128)S(1)} %get-tuple-element.39.refs_1_, bf16[4,256,512]{2,1,0:T(8,128)(2,1)S(1)} %get-tuple-element.40.refs_2_, f32[4,256,512]{2,1,0:T(8,128)S(1)} %get-tuple-element.41.refs_3_, ...), custom_call_target="tpu_custom_call" | custom-call | flops 536870912 | bytes 8388608 | tf_op jit(solution)/shard_map/finish/pallas_call | solution.py:379
  28.1 0.0 collective-permute-done.10.mate_ref
  28.2 1.5 %collective-permute-start.11 = (bf16[4,2,2,16,128]{4,3,2,1,0:T(8,128)(2,1)S(1)}, bf16[4,2,2,16,128]{4,3,2,1,0:T(8,128)(2,1)S(1)}, u32[]{:S(2)}, u32[]{:S(2)}) collective-permute-start(bf16[4,2,2,16,128]{4,3,2,1,0:T(8,128)(2,1)S(1)} %get-tuple-element.50), channel_id=1, source_target_pairs={{0,24},{4,28},{8,16},{12,20},{16,8},{20,12},{24,0},{28,4},{1,25},{... | collective-permute-start | bytes 196616 | tf_op jit(solution)/shard_map/ppermute | solution.py:482
  29.7 0.5 %collective-permute-start.12 = (bf16[4,2,2,16,128]{4,3,2,1,0:T(8,128)(2,1)S(1)}, bf16[4,2,2,16,128]{4,3,2,1,0:T(8,128)(2,1)S(1)}, u32[]{:S(2)}, u32[]{:S(2)}) collective-permute-start(bf16[4,2,2,16,128]{4,3,2,1,0:T(8,128)(2,1)S(1)} %get-tuple-element.51), channel_id=1, source_target_pairs={{0,16},{4,20},{8,24},{12,28},{16,0},{20,4},{24,8},{28,12},{1,17},{... | collective-permute-start | bytes 196616 | tf_op jit(solution)/shard_map/ppermute | solution.py:482
  30.2 1.5 %collective-permute-start.13 = (bf16[4,2,2,16,128]{4,3,2,1,0:T(8,128)(2,1)S(1)}, bf16[4,2,2,16,128]{4,3,2,1,0:T(8,128)(2,1)S(1)}, u32[]{:S(2)}, u32[]{:S(2)}) collective-permute-start(bf16[4,2,2,16,128]{4,3,2,1,0:T(8,128)(2,1)S(1)} %get-tuple-element.52), channel_id=1, source_target_pairs={{0,8},{4,12},{8,0},{12,4},{16,24},{20,28},{24,16},{28,20},{1,9},{5... | collective-permute-start | bytes 196616 | tf_op jit(solution)/shard_map/ppermute | solution.py:482
  31.7 1.9 %collective-permute-done.11.refs_0_ = bf16[4,2,2,16,128]{4,3,2,1,0:T(8,128)(2,1)S(1)} collective-permute-done((bf16[4,2,2,16,128]{4,3,2,1,0:T(8,128)(2,1)S(1)}, bf16[4,2,2,16,128]{4,3,2,1,0:T(8,128)(2,1)S(1)}, u32[]{:S(2)}, u32[]{:S(2)}) %collective-permute-start.11) | collective-permute-done | bytes 65568 | tf_op jit(solution)/shard_map/ppermute | solution.py:482
  33.6 1.0 %collective-permute-done.12.refs_1_ = bf16[4,2,2,16,128]{4,3,2,1,0:T(8,128)(2,1)S(1)} collective-permute-done((bf16[4,2,2,16,128]{4,3,2,1,0:T(8,128)(2,1)S(1)}, bf16[4,2,2,16,128]{4,3,2,1,0:T(8,128)(2,1)S(1)}, u32[]{:S(2)}, u32[]{:S(2)}) %collective-permute-start.12) | collective-permute-done | bytes 65568 | tf_op jit(solution)/shard_map/ppermute | solution.py:482
  34.6 0.1 collective-permute-done.13.refs_2_
  34.7 1.9 %collective-permute-start.14 = (bf16[2,2,16,128]{3,2,1,0:T(8,128)(2,1)S(1)}, bf16[2,2,16,128]{3,2,1,0:T(8,128)(2,1)S(1)}, u32[]{:S(2)}, u32[]{:S(2)}) collective-permute-start(bf16[2,2,16,128]{3,2,1,0:T(8,128)(2,1)S(1)} %get-tuple-element.53), channel_id=1, source_target_pairs={{0,3},{1,2},{2,1},{3,0},{4,7},{5,6},{6,5},{7,4},{8,11},{9,10},{10,... | collective-permute-start | bytes 49160 | tf_op jit(solution)/shard_map/ppermute | solution.py:482
  36.6 0.2 collective-permute-start.15
  36.8 2.3 %collective-permute-start.16 = (bf16[2,2,16,128]{3,2,1,0:T(8,128)(2,1)S(1)}, bf16[2,2,16,128]{3,2,1,0:T(8,128)(2,1)S(1)}, u32[]{:S(2)}, u32[]{:S(2)}) collective-permute-start(bf16[2,2,16,128]{3,2,1,0:T(8,128)(2,1)S(1)} %get-tuple-element.55), channel_id=1, source_target_pairs={{0,1},{1,0},{2,3},{3,2},{4,5},{5,4},{6,7},{7,6},{8,9},{9,8},{10,11... | collective-permute-start | bytes 49160 | tf_op jit(solution)/shard_map/ppermute | solution.py:482
  39.1 1.1 %collective-permute-done.14.refs_0_ = bf16[2,2,16,128]{3,2,1,0:T(8,128)(2,1)S(1)} collective-permute-done((bf16[2,2,16,128]{3,2,1,0:T(8,128)(2,1)S(1)}, bf16[2,2,16,128]{3,2,1,0:T(8,128)(2,1)S(1)}, u32[]{:S(2)}, u32[]{:S(2)}) %collective-permute-start.14) | collective-permute-done | bytes 16416 | tf_op jit(solution)/shard_map/ppermute | solution.py:482
  40.3 1.0 %collective-permute-done.15.refs_1_ = bf16[2,2,16,128]{3,2,1,0:T(8,128)(2,1)S(1)} collective-permute-done((bf16[2,2,16,128]{3,2,1,0:T(8,128)(2,1)S(1)}, bf16[2,2,16,128]{3,2,1,0:T(8,128)(2,1)S(1)}, u32[]{:S(2)}, u32[]{:S(2)}) %collective-permute-start.15) | collective-permute-done | bytes 16416 | tf_op jit(solution)/shard_map/ppermute | solution.py:482
  41.2 0.0 collective-permute-done.16.refs_2_
  41.3 0.0 copy-done.1
  41.3 0.0 copy-done.2
  41.3 0.0 copy-done.3
  41.3 0.9 %adam.1 = (f32[16,2,8,128]{3,2,1,0:T(8,128)}, f32[16,2,8,128]{3,2,1,0:T(8,128)}, f32[16,2,8,128]{3,2,1,0:T(8,128)}) custom-call(bf16[2,2,16,128]{3,2,1,0:T(8,128)(2,1)S(1)} %collective-permute-done.14.refs_0_, bf16[2,2,16,128]{3,2,1,0:T(8,128)(2,1)S(1)} %collective-permute-done.15.refs_1_, bf16[2,2,16,128]{3,2,1,0:T(8,128)(2,1)S(1)} %collective-permute-done.16.refs_2_, ...), custom_call_target="tpu_custom_call" | custom-call | tf_op jit(solution)/shard_map/adam/pallas_call | solution.py:469
  (3 shorter events, 0.1 us)
Async XLA Ops:
  0.6 0.9 %copy-start = (f32[16,2,8,128]{3,2,1,0:T(8,128)S(1)}, f32[16,2,8,128]{3,2,1,0:T(8,128)}, u32[]{:S(2)}) copy-start(f32[16,2,8,128]{3,2,1,0:T(8,128)} %refs_4_.1) | copy-start | bytes 393220
  1.7 7.7 %collective-permute-start = (bf16[2,2,16,128]{3,2,1,0:T(8,128)(2,1)S(1)}, bf16[2,2,16,128]{3,2,1,0:T(8,128)(2,1)S(1)}, u32[]{:S(2)}, u32[]{:S(2)}) collective-permute-start(bf16[2,2,16,128]{3,2,1,0:T(8,128)(2,1)S(1)} %get-tuple-element.30), channel_id=1, source_target_pairs={{0,3},{1,2},{2,1},{3,0},{4,7},{5,6},{6,5},{7,4},{8,11},{9,10},{10,... | collective-permute-start | bytes 49160 | tf_op jit(solution)/shard_map/ppermute | solution.py:482
  6.8 4.6 %collective-permute-start.1 = (bf16[2,2,16,128]{3,2,1,0:T(8,128)(2,1)S(1)}, bf16[2,2,16,128]{3,2,1,0:T(8,128)(2,1)S(1)}, u32[]{:S(2)}, u32[]{:S(2)}) collective-permute-start(bf16[2,2,16,128]{3,2,1,0:T(8,128)(2,1)S(1)} %get-tuple-element.31), channel_id=1, source_target_pairs={{0,2},{1,3},{2,0},{3,1},{4,6},{5,7},{6,4},{7,5},{8,10},{9,11},{10,... | collective-permute-start | bytes 49160 | tf_op jit(solution)/shard_map/ppermute | solution.py:482
  6.8 4.6 %collective-permute-start.2 = (bf16[2,2,16,128]{3,2,1,0:T(8,128)(2,1)S(1)}, bf16[2,2,16,128]{3,2,1,0:T(8,128)(2,1)S(1)}, u32[]{:S(2)}, u32[]{:S(2)}) collective-permute-start(bf16[2,2,16,128]{3,2,1,0:T(8,128)(2,1)S(1)} %get-tuple-element.32), channel_id=1, source_target_pairs={{0,1},{1,0},{2,3},{3,2},{4,5},{5,4},{6,7},{7,6},{8,9},{9,8},{10,11... | collective-permute-start | bytes 49160 | tf_op jit(solution)/shard_map/ppermute | solution.py:482
  11.5 5.8 %collective-permute-start.5 = (bf16[4,2,2,16,128]{4,3,2,1,0:T(8,128)(2,1)S(1)}, bf16[4,2,2,16,128]{4,3,2,1,0:T(8,128)(2,1)S(1)}, u32[]{:S(2)}, u32[]{:S(2)}) collective-permute-start(bf16[4,2,2,16,128]{4,3,2,1,0:T(8,128)(2,1)S(1)} %pad_maximum_fusion.refs_0_), channel_id=1, source_target_pairs={{0,24},{4,28},{8,16},{12,20},{16,8},{20,12},{24,0},{28,4},{1,25},{... | collective-permute-start | bytes 196616 | tf_op jit(solution)/shard_map/ppermute | solution.py:482
  14.0 4.3 %collective-permute-start.4 = (bf16[4,2,2,16,128]{4,3,2,1,0:T(8,128)(2,1)S(1)}, bf16[4,2,2,16,128]{4,3,2,1,0:T(8,128)(2,1)S(1)}, u32[]{:S(2)}, u32[]{:S(2)}) collective-permute-start(bf16[4,2,2,16,128]{4,3,2,1,0:T(8,128)(2,1)S(1)} %pad_maximum_fusion.refs_0_), channel_id=1, source_target_pairs={{0,16},{4,20},{8,24},{12,28},{16,0},{20,4},{24,8},{28,12},{1,17},{... | collective-permute-start | bytes 196616 | tf_op jit(solution)/shard_map/ppermute | solution.py:482
  14.5 4.3 %collective-permute-start.3 = (bf16[4,2,2,16,128]{4,3,2,1,0:T(8,128)(2,1)S(1)}, bf16[4,2,2,16,128]{4,3,2,1,0:T(8,128)(2,1)S(1)}, u32[]{:S(2)}, u32[]{:S(2)}) collective-permute-start(bf16[4,2,2,16,128]{4,3,2,1,0:T(8,128)(2,1)S(1)} %pad_maximum_fusion.refs_0_), channel_id=1, source_target_pairs={{0,8},{4,12},{8,0},{12,4},{16,24},{20,28},{24,16},{28,20},{1,9},{5... | collective-permute-start | bytes 196616 | tf_op jit(solution)/shard_map/ppermute | solution.py:482
  16.5 4.7 %collective-permute-start.9 = (bf16[4,2,2,16,128]{4,3,2,1,0:T(8,128)(2,1)S(1)}, bf16[4,2,2,16,128]{4,3,2,1,0:T(8,128)(2,1)S(1)}, u32[]{:S(2)}, u32[]{:S(2)}) collective-permute-start(bf16[4,2,2,16,128]{4,3,2,1,0:T(8,128)(2,1)S(1)} %pad_maximum_fusion.refs_0_), channel_id=1, source_target_pairs={{0,4},{4,0},{8,12},{12,8},{16,20},{20,16},{24,28},{28,24},{1,5},{5... | collective-permute-start | bytes 196616 | tf_op jit(solution)/shard_map/ppermute | solution.py:482
  17.3 4.0 %collective-permute-start.6 = (bf16[4,2,2,16,128]{4,3,2,1,0:T(8,128)(2,1)S(1)}, bf16[4,2,2,16,128]{4,3,2,1,0:T(8,128)(2,1)S(1)}, u32[]{:S(2)}, u32[]{:S(2)}) collective-permute-start(bf16[4,2,2,16,128]{4,3,2,1,0:T(8,128)(2,1)S(1)} %collective-permute-done.5.refs_3_), channel_id=1, source_target_pairs={{0,4},{4,0},{8,12},{12,8},{16,20},{20,16},{24,28},{28,24},{1,5},{5... | collective-permute-start | bytes 196616 | tf_op jit(solution)/shard_map/ppermute | solution.py:482
  18.2 3.0 %collective-permute-start.7 = (bf16[4,2,2,16,128]{4,3,2,1,0:T(8,128)(2,1)S(1)}, bf16[4,2,2,16,128]{4,3,2,1,0:T(8,128)(2,1)S(1)}, u32[]{:S(2)}, u32[]{:S(2)}) collective-permute-start(bf16[4,2,2,16,128]{4,3,2,1,0:T(8,128)(2,1)S(1)} %collective-permute-done.4.refs_2_), channel_id=1, source_target_pairs={{0,4},{4,0},{8,12},{12,8},{16,20},{20,16},{24,28},{28,24},{1,5},{5... | collective-permute-start | bytes 196616 | tf_op jit(solution)/shard_map/ppermute | solution.py:482
  18.7 2.5 %collective-permute-start.8 = (bf16[4,2,2,16,128]{4,3,2,1,0:T(8,128)(2,1)S(1)}, bf16[4,2,2,16,128]{4,3,2,1,0:T(8,128)(2,1)S(1)}, u32[]{:S(2)}, u32[]{:S(2)}) collective-permute-start(bf16[4,2,2,16,128]{4,3,2,1,0:T(8,128)(2,1)S(1)} %collective-permute-done.3.refs_1_), channel_id=1, source_target_pairs={{0,4},{4,0},{8,12},{12,8},{16,20},{20,16},{24,28},{28,24},{1,5},{5... | collective-permute-start | bytes 196616 | tf_op jit(solution)/shard_map/ppermute | solution.py:482
  25.5 2.6 %collective-permute-start.10 = (bf16[4,4,2,2,16,128]{5,4,3,2,1,0:T(8,128)(2,1)S(1)}, bf16[4,4,2,2,16,128]{5,4,3,2,1,0:T(8,128)(2,1)S(1)}, u32[]{:S(2)}, u32[]{:S(2)}) collective-permute-start(bf16[4,4,2,2,16,128]{5,4,3,2,1,0:T(8,128)(2,1)S(1)} %get-tuple-element.48), channel_id=1, source_target_pairs={{0,4},{4,0},{8,12},{12,8},{16,20},{20,16},{24,28},{28,24},{1,5},{5... | collective-permute-start | bytes 786440 | tf_op jit(solution)/shard_map/ppermute | solution.py:482
  26.1 15.2 %copy-start.1 = (f32[16,2,8,128]{3,2,1,0:T(8,128)S(1)}, f32[16,2,8,128]{3,2,1,0:T(8,128)}, u32[]{:S(2)}) copy-start(f32[16,2,8,128]{3,2,1,0:T(8,128)} %refs_4_.1) | copy-start | bytes 393220
  26.1 15.2 %copy-start.2 = (f32[16,2,8,128]{3,2,1,0:T(8,128)S(1)}, f32[16,2,8,128]{3,2,1,0:T(8,128)}, u32[]{:S(2)}) copy-start(f32[16,2,8,128]{3,2,1,0:T(8,128)} %refs_5_.1) | copy-start | bytes 393220
  26.1 15.2 %copy-start.3 = (f32[16,2,8,128]{3,2,1,0:T(8,128)S(1)}, f32[16,2,8,128]{3,2,1,0:T(8,128)}, u32[]{:S(2)}) copy-start(f32[16,2,8,128]{3,2,1,0:T(8,128)} %refs_6_.1) | copy-start | bytes 393220
  28.2 5.4 %collective-permute-start.11 = (bf16[4,2,2,16,128]{4,3,2,1,0:T(8,128)(2,1)S(1)}, bf16[4,2,2,16,128]{4,3,2,1,0:T(8,128)(2,1)S(1)}, u32[]{:S(2)}, u32[]{:S(2)}) collective-permute-start(bf16[4,2,2,16,128]{4,3,2,1,0:T(8,128)(2,1)S(1)} %get-tuple-element.50), channel_id=1, source_target_pairs={{0,24},{4,28},{8,16},{12,20},{16,8},{20,12},{24,0},{28,4},{1,25},{... | collective-permute-start | bytes 196616 | tf_op jit(solution)/shard_map/ppermute | solution.py:482
  29.7 4.9 %collective-permute-start.12 = (bf16[4,2,2,16,128]{4,3,2,1,0:T(8,128)(2,1)S(1)}, bf16[4,2,2,16,128]{4,3,2,1,0:T(8,128)(2,1)S(1)}, u32[]{:S(2)}, u32[]{:S(2)}) collective-permute-start(bf16[4,2,2,16,128]{4,3,2,1,0:T(8,128)(2,1)S(1)} %get-tuple-element.51), channel_id=1, source_target_pairs={{0,16},{4,20},{8,24},{12,28},{16,0},{20,4},{24,8},{28,12},{1,17},{... | collective-permute-start | bytes 196616 | tf_op jit(solution)/shard_map/ppermute | solution.py:482
  30.2 4.4 %collective-permute-start.13 = (bf16[4,2,2,16,128]{4,3,2,1,0:T(8,128)(2,1)S(1)}, bf16[4,2,2,16,128]{4,3,2,1,0:T(8,128)(2,1)S(1)}, u32[]{:S(2)}, u32[]{:S(2)}) collective-permute-start(bf16[4,2,2,16,128]{4,3,2,1,0:T(8,128)(2,1)S(1)} %get-tuple-element.52), channel_id=1, source_target_pairs={{0,8},{4,12},{8,0},{12,4},{16,24},{20,28},{24,16},{28,20},{1,9},{5... | collective-permute-start | bytes 196616 | tf_op jit(solution)/shard_map/ppermute | solution.py:482
  34.7 5.6 %collective-permute-start.14 = (bf16[2,2,16,128]{3,2,1,0:T(8,128)(2,1)S(1)}, bf16[2,2,16,128]{3,2,1,0:T(8,128)(2,1)S(1)}, u32[]{:S(2)}, u32[]{:S(2)}) collective-permute-start(bf16[2,2,16,128]{3,2,1,0:T(8,128)(2,1)S(1)} %get-tuple-element.53), channel_id=1, source_target_pairs={{0,3},{1,2},{2,1},{3,0},{4,7},{5,6},{6,5},{7,4},{8,11},{9,10},{10,... | collective-permute-start | bytes 49160 | tf_op jit(solution)/shard_map/ppermute | solution.py:482
  36.6 4.6 %collective-permute-start.15 = (bf16[2,2,16,128]{3,2,1,0:T(8,128)(2,1)S(1)}, bf16[2,2,16,128]{3,2,1,0:T(8,128)(2,1)S(1)}, u32[]{:S(2)}, u32[]{:S(2)}) collective-permute-start(bf16[2,2,16,128]{3,2,1,0:T(8,128)(2,1)S(1)} %get-tuple-element.54), channel_id=1, source_target_pairs={{0,2},{1,3},{2,0},{3,1},{4,6},{5,7},{6,4},{7,5},{8,10},{9,11},{10,... | collective-permute-start | bytes 49160 | tf_op jit(solution)/shard_map/ppermute | solution.py:482
  36.8 4.4 %collective-permute-start.16 = (bf16[2,2,16,128]{3,2,1,0:T(8,128)(2,1)S(1)}, bf16[2,2,16,128]{3,2,1,0:T(8,128)(2,1)S(1)}, u32[]{:S(2)}, u32[]{:S(2)}) collective-permute-start(bf16[2,2,16,128]{3,2,1,0:T(8,128)(2,1)S(1)} %get-tuple-element.55), channel_id=1, source_target_pairs={{0,1},{1,0},{2,3},{3,2},{4,5},{5,4},{6,7},{7,6},{8,9},{9,8},{10,11... | collective-permute-start | bytes 49160 | tf_op jit(solution)/shard_map/ppermute | solution.py:482

commit v12 on v11

--- a/solution.py
+++ b/solution.py
@@ -23,6 +23,10 @@
 
 def flips(size):
     return list(range(size - 1, -1, -1))
+
+
+def gather_flips(columns):
+    return flips(columns)[1::-1] + flips(columns)[2:]
 
 
 def pack_kernel(columns, cache_ref, *refs):
@@ -34,7 +38,7 @@
         for group in range(groups):
             by_group[group, side] = cache_ref[:, side, group].astype(jnp.bfloat16)
     column = lax.axis_index("cache")
-    for out, flip in zip(outs, flips(columns)):
+    for out, flip in zip(outs, gather_flips(columns)):
         first = (column ^ flip) // repeat * own
         for slot in range(own):
             for side in range(2):
@@ -125,7 +129,7 @@
     for cut in cuts_of(scores):
         shifted = jnp.exp2(scores[cut] * factor - peak)
         product = shifted * slopes[cut]
-        kept[cut] = shifted.astype(jnp.bfloat16)
+        kept[cut] = shifted
         total = shifted if total is None else total + shifted
         dotted = product if dotted is None else dotted + product
         yield
@@ -135,7 +139,7 @@
 
 def weigh(kept, slopes, inverse, delta, weights, dscores):
     for cut in cuts_of(weights):
-        probability = kept[cut].astype(jnp.float32) * inverse
+        probability = kept[cut] * inverse
         weights[cut] = probability.astype(jnp.bfloat16)
         dscores[cut] = (probability * (slopes[cut] - delta)).astype(jnp.bfloat16)
         yield
@@ -180,13 +184,13 @@
     for product in products(0, 0, 0):
         product()
 
-    def two_tiles(step, carry):
+    def two_tiles(step):
         interleave(normalize(2 * step, 0, step), products(2 * step + 1, 1, step))
         interleave(normalize(2 * step + 1, 1, step), products(2 * step + 2, 0, step + 1))
-        return carry
 
     last = tiles // 2 - 1
-    lax.fori_loop(0, last, two_tiles, 0)
+    for step in range(last):
+        two_tiles(step)
     interleave(normalize(tiles - 2, 0, last), products(tiles - 1, 1, last))
     interleave(normalize(tiles - 1, 1, last))
 
@@ -195,10 +199,7 @@
     columns, _, own, share, width = pairs[0].shape
     positions = len(pairs) * columns * share
     tiles, row_tile, _ = queries.shape
-    kept = [
-        jax.ShapeDtypeStruct((tiles // 2, positions, row_tile), kind)
-        for kind in (jnp.bfloat16, jnp.float32)
-    ]
+    kept = [jax.ShapeDtypeStruct((tiles // 2, positions, row_tile), jnp.float32)] * 2
     buffers = [
         pltpu.VMEM((positions, row_tile), jnp.float32),
         pltpu.VMEM((8, row_tile), jnp.float32),
@@ -228,7 +229,7 @@
     queries_ref, grads_ref, peak_ref, total_ref, dotted_ref = refs[:5]
     out_ref, inverse_ref, delta_ref = refs[5:8]
     keys, values, key_total, value_total = refs[8:12]
-    even, odd = refs[12:18], refs[18:24]
+    even, odd = refs[12:17], refs[17:22]
     _, columns, _, own, share, width = out_ref.shape
     tiles = queries_ref.shape[0]
     factor = score_scale * LOG2E
@@ -241,20 +242,20 @@
         return score_products(keys, values, slot, queries_ref, grads_ref, tile, *buffers[:3])
 
     def normalize(tile, buffers):
-        scores, slopes, tops, shifted, weights, dscores = buffers
+        scores, slopes, tops, weights, dscores = buffers
 
         def passes():
             first_peak = peak_ref[tile]
             peak = jnp.max(tops[...], axis=0, keepdims=True) * factor
             peak = jnp.maximum(peak, first_peak)
             sums = []
-            yield from exponentiate(scores, slopes, factor, peak, shifted, sums)
+            yield from exponentiate(scores, slopes, factor, peak, scores, sums)
             rescale = jnp.exp2(first_peak - peak)
             inverse = 1.0 / (sums[0] + total_ref[tile] * rescale)
             delta = (sums[1] + dotted_ref[tile] * rescale) * inverse
             inverse_ref[tile] = inverse * rescale
             delta_ref[tile] = delta
-            yield from weigh(shifted, slopes, inverse, delta, weights, dscores)
+            yield from weigh(scores, slopes, inverse, delta, weights, dscores)
 
         return 2 * len(cuts_of(scores)), passes()
 
@@ -263,7 +264,7 @@
             key_total,
             value_total,
             tile // per_group,
-            *buffers[4:],
+            *buffers[3:],
             queries_ref,
             grads_ref,
             tile,
@@ -273,13 +274,13 @@
         product()
     interleave(normalize(0, even), products(1, odd))
 
-    def two_tiles(step, carry):
+    def two_tiles(step):
         tile = step * 2
         interleave(normalize(tile + 1, odd), products(tile + 2, even), gather(tile, even))
         interleave(normalize(tile + 2, even), products(tile + 3, odd), gather(tile + 1, odd))
-        return carry
-
-    lax.fori_loop(0, tiles // 2 - 1, two_tiles, 0)
+
+    for step in range(tiles // 2 - 1):
+        two_tiles(step)
     interleave(normalize(tiles - 1, odd), gather(tiles - 2, even))
     for product in gather(tiles - 1, odd):
         product()
@@ -299,7 +300,6 @@
         pltpu.VMEM((positions, row_tile), jnp.float32),
         pltpu.VMEM((positions, row_tile), jnp.float32),
         pltpu.VMEM((8, row_tile), jnp.float32),
-        pltpu.VMEM((positions, row_tile), jnp.bfloat16),
         pltpu.VMEM((positions, row_tile), jnp.bfloat16),
         pltpu.VMEM((positions, row_tile), jnp.bfloat16),
     ]
@@ -355,13 +355,13 @@
 
     interleave(spread(0, 0, 0, even))
 
-    def two_tiles(step, carry):
+    def two_tiles(step):
         interleave(spread(2 * step + 1, 1, step, odd), gather(2 * step, even))
         interleave(spread(2 * step + 2, 0, step + 1, even), gather(2 * step + 1, odd))
-        return carry
 
     last = tiles // 2 - 1
-    lax.fori_loop(0, last, two_tiles, 0)
+    for step in range(last):
+        two_tiles(step)
     interleave(spread(tiles - 1, 1, last, odd), gather(tiles - 2, even))
     for product in gather(tiles - 1, odd):
         product()
@@ -415,10 +415,12 @@
 
 def column_sum_kernel(away, mine_ref, *refs):
     others, outs = refs[:away], refs[away:]
-    for offset, out in enumerate(outs):
-        total = mine_ref[offset]
+    columns = len(outs)
+    for out, flip in zip(outs, flips(columns)):
+        place = gather_flips(columns).index(flip)
+        total = mine_ref[place]
         for other in others:
-            total = total + other[offset].astype(jnp.float32)
+            total = total + other[place].astype(jnp.float32)
         out[...] = total.astype(out.dtype)
 
 
@@ -482,10 +484,10 @@
     return lax.ppermute(value, axis, [(place, place ^ flip) for place in range(size)])
 
 
-def swap_all(values, axis, size, stride):
+def swap_all(values, axis, size, stride, order=flips):
     return [
         swap(value, axis, size, flip * stride) if flip else value
-        for value, flip in zip(values, flips(len(values)))
+        for value, flip in zip(values, order(len(values)))
     ]
 
 
@@ -505,7 +507,7 @@
     first_token = column % repeat * own_tokens
 
     slices = pack(cache, columns, own)
-    gathered = jnp.stack(swap_all(slices, "cache", columns, 1))
+    gathered = jnp.stack(swap_all(slices, "cache", columns, 1, gather_flips))
     pairs = swap_all([gathered] * chips, "dp", dp_size, 2)
     def tiles_of(array):
         parts = array.reshape((tokens, groups, group_size) + array.shape[2:])

time: 42.5 us -> 40.6 us (0.955)
  Pallas kernels: 9.82 us -> 7.8 us
    pallas_call x1, Pallas kernels: 2.46 us -> 1.7 us  [first_half(): pl.pallas_call(functools.partial(first_half_kernel, score_scale, tiles //...]
    pallas_call x1, Pallas kernels: 2.01 us -> 1.32 us  [finish(): pl.pallas_call(functools.partial(finish_kernel, score_scale, tiles // own...]
    pallas_call x1, Pallas kernels: 4.24 us -> 3.68 us  [second_half(): pl.pallas_call(functools.partial(second_half_kernel, score_scale, tiles /...]
  transfers between devices with their start and end apart: 17 -> 17, of which waited for: 9 -> 9; matrix products, arithmetic and copies ran while one was open for 8% -> 8% of each run, Pallas kernels for 11% -> 7%
where the time goes in v12:
time: 40.6 us; the launch traced here: 40.3 us
  starting transfers between devices  17.9 us (44%)
  waiting for transfers between devices  9.5 us (23%)
  Pallas kernels  7.8 us (19%)
  local copies, waits for them, and re-layouts  4.31 us (11%)
  between operations  0.79 us (2%)
    ppermute x17, starting transfers between devices, swap(): lax.ppermute(value, axis, [(place, place ^ flip) for place in range(size)])  17.9 us
    ppermute x17, waiting for transfers between devices, swap(): lax.ppermute(value, axis, [(place, place ^ flip) for place in range(size)])  9.5 us
    pallas_call x1, Pallas kernels, second_half(): pl.pallas_call(functools.partial(second_half_kernel, score_scale, tiles /...  3.68 us
    dynamic_slice x2, local copies, waits for them, and re-layouts, tiles_of(): part = lax.dynamic_slice_in_dim(part, first_group, own, 1)  2.69 us
    pallas_call x1, Pallas kernels, first_half(): pl.pallas_call(functools.partial(first_half_kernel, score_scale, tiles //...  1.7 us
    pallas_call x1, Pallas kernels, finish(): pl.pallas_call(functools.partial(finish_kernel, score_scale, tiles // own...  1.32 us
    unnamed x12, local copies, waits for them, and re-layouts  1.3 us
    pallas_call x1, Pallas kernels, adam(): pl.pallas_call(functools.partial(adam_kernel, len(parts)), out_shape=(sha...  0.89 us
  transfers between devices with their start and end apart: 17, of which 9 were waited for; matrix products, arithmetic and copies ran while one was open for 8% of the time, Pallas kernels for 7%

profile of v12, /device:TPU:0, one launch (start us, length us, event | category | flops | bytes accessed | tf_op | source)
XLA Modules:
  0.0 40.3 jit_solution(3692188303000749742)
XLA Ops:
  0.6 0.0 copy-start
  0.6 0.9 %copy-done = f32[16,2,8,128]{3,2,1,0:T(8,128)S(1)} copy-done((f32[16,2,8,128]{3,2,1,0:T(8,128)S(1)}, f32[16,2,8,128]{3,2,1,0:T(8,128)}, u32[]{:S(2)}) %copy-start) | copy-done | bytes 131096
  1.5 0.1 pack.1
  1.7 4.1 %collective-permute-start = (bf16[2,2,16,128]{3,2,1,0:T(8,128)(2,1)S(1)}, bf16[2,2,16,128]{3,2,1,0:T(8,128)(2,1)S(1)}, u32[]{:S(2)}, u32[]{:S(2)}) collective-permute-start(bf16[2,2,16,128]{3,2,1,0:T(8,128)(2,1)S(1)} %get-tuple-element.30), channel_id=1, source_target_pairs={{0,2},{1,3},{2,0},{3,1},{4,6},{5,7},{6,4},{7,5},{8,10},{9,11},{10,... | collective-permute-start | bytes 49160 | tf_op jit(solution)/shard_map/ppermute | solution.py:484
  5.8 1.3 %collective-permute-start.1 = (bf16[2,2,16,128]{3,2,1,0:T(8,128)(2,1)S(1)}, bf16[2,2,16,128]{3,2,1,0:T(8,128)(2,1)S(1)}, u32[]{:S(2)}, u32[]{:S(2)}) collective-permute-start(bf16[2,2,16,128]{3,2,1,0:T(8,128)(2,1)S(1)} %get-tuple-element.31), channel_id=1, source_target_pairs={{0,3},{1,2},{2,1},{3,0},{4,7},{5,6},{6,5},{7,4},{8,11},{9,10},{10,... | collective-permute-start | bytes 49160 | tf_op jit(solution)/shard_map/ppermute | solution.py:484
  7.1 0.2 collective-permute-start.2
  7.4 2.0 %constant_dynamic-slice_fusion.2 = (bf16[256,2,8,128]{3,2,1,0:T(8,128)(2,1)S(1)}, bf16[256,2,8,128]{3,2,1,0:T(8,128)(2,1)S(1)}) fusion(bf16[256,8,8,128]{3,2,1,0:T(8,128)(2,1)} %bitcast.25, s32[]{:T(128)S(6)} %select_n.9, bf16[256,8,8,128]{3,2,1,0:T(8,128)(2,1)} %bitcast.26), kind=kLoop, calls=%fused_computation.3 | loop fusion | bytes 4194308 | tf_op jit(solution)/shard_map/dynamic_slice | solution.py:515
  9.3 0.0 collective-permute-done
  9.3 2.0 %collective-permute-done.1 = bf16[2,2,16,128]{3,2,1,0:T(8,128)(2,1)S(1)} collective-permute-done((bf16[2,2,16,128]{3,2,1,0:T(8,128)(2,1)S(1)}, bf16[2,2,16,128]{3,2,1,0:T(8,128)(2,1)S(1)}, u32[]{:S(2)}, u32[]{:S(2)}) %collective-permute-start.1) | collective-permute-done | bytes 16416 | tf_op jit(solution)/shard_map/ppermute | solution.py:484
  11.3 0.0 collective-permute-done.2
  11.3 2.5 %collective-permute-start.5 = (bf16[4,2,2,16,128]{4,3,2,1,0:T(8,128)(2,1)S(1)}, bf16[4,2,2,16,128]{4,3,2,1,0:T(8,128)(2,1)S(1)}, u32[]{:S(2)}, u32[]{:S(2)}) collective-permute-start(bf16[4,2,2,16,128]{4,3,2,1,0:T(8,128)(2,1)S(1)} %pad_maximum_fusion.refs_0_), channel_id=1, source_target_pairs={{0,24},{4,28},{8,16},{12,20},{16,8},{20,12},{24,0},{28,4},{1,25},{... | collective-permute-start | bytes 196616 | tf_op jit(solution)/shard_map/ppermute | solution.py:484
  13.9 0.5 %collective-permute-start.4 = (bf16[4,2,2,16,128]{4,3,2,1,0:T(8,128)(2,1)S(1)}, bf16[4,2,2,16,128]{4,3,2,1,0:T(8,128)(2,1)S(1)}, u32[]{:S(2)}, u32[]{:S(2)}) collective-permute-start(bf16[4,2,2,16,128]{4,3,2,1,0:T(8,128)(2,1)S(1)} %pad_maximum_fusion.refs_0_), channel_id=1, source_target_pairs={{0,16},{4,20},{8,24},{12,28},{16,0},{20,4},{24,8},{28,12},{1,17},{... | collective-permute-start | bytes 196616 | tf_op jit(solution)/shard_map/ppermute | solution.py:484
  14.4 0.5 %collective-permute-start.3 = (bf16[4,2,2,16,128]{4,3,2,1,0:T(8,128)(2,1)S(1)}, bf16[4,2,2,16,128]{4,3,2,1,0:T(8,128)(2,1)S(1)}, u32[]{:S(2)}, u32[]{:S(2)}) collective-permute-start(bf16[4,2,2,16,128]{4,3,2,1,0:T(8,128)(2,1)S(1)} %pad_maximum_fusion.refs_0_), channel_id=1, source_target_pairs={{0,8},{4,12},{8,0},{12,4},{16,24},{20,28},{24,16},{28,20},{1,9},{5... | collective-permute-start | bytes 196616 | tf_op jit(solution)/shard_map/ppermute | solution.py:484
  14.9 0.7 %constant_dynamic-slice_fusion = (f32[256,2,8]{0,2,1:T(8,128)S(1)}, f32[256,2,8]{0,2,1:T(8,128)S(1)}) fusion(f32[256,8,8]{0,2,1:T(8,128)} %bitcast.30, s32[]{:T(128)S(6)} %select_n.9, f32[256,8,8]{0,2,1:T(8,128)} %bitcast.31), kind=kLoop, calls=%fused_computation.1 | loop fusion | bytes 65540 | tf_op jit(solution)/shard_map/dynamic_slice | solution.py:515
  15.6 0.1 copy.21
  15.8 0.2 reshape.37.refs_7_
  15.9 0.1 copy.20
  16.1 0.2 reshape.35.refs_6_
  16.2 0.1 copy.19
  16.3 0.1 copy.18
  16.4 0.1 collective-permute-start.9
  16.5 0.7 %collective-permute-done.5.refs_3_ = bf16[4,2,2,16,128]{4,3,2,1,0:T(8,128)(2,1)S(1)} collective-permute-done((bf16[4,2,2,16,128]{4,3,2,1,0:T(8,128)(2,1)S(1)}, bf16[4,2,2,16,128]{4,3,2,1,0:T(8,128)(2,1)S(1)}, u32[]{:S(2)}, u32[]{:S(2)}) %collective-permute-start.5) | collective-permute-done | bytes 65568 | tf_op jit(solution)/shard_map/ppermute | solution.py:484
  17.2 0.0 collective-permute-start.6
  17.2 1.0 %collective-permute-done.4.refs_2_ = bf16[4,2,2,16,128]{4,3,2,1,0:T(8,128)(2,1)S(1)} collective-permute-done((bf16[4,2,2,16,128]{4,3,2,1,0:T(8,128)(2,1)S(1)}, bf16[4,2,2,16,128]{4,3,2,1,0:T(8,128)(2,1)S(1)}, u32[]{:S(2)}, u32[]{:S(2)}) %collective-permute-start.4) | collective-permute-done | bytes 65568 | tf_op jit(solution)/shard_map/ppermute | solution.py:484
  18.1 0.0 collective-permute-start.7
  18.1 0.5 %collective-permute-done.3.refs_1_ = bf16[4,2,2,16,128]{4,3,2,1,0:T(8,128)(2,1)S(1)} collective-permute-done((bf16[4,2,2,16,128]{4,3,2,1,0:T(8,128)(2,1)S(1)}, bf16[4,2,2,16,128]{4,3,2,1,0:T(8,128)(2,1)S(1)}, u32[]{:S(2)}, u32[]{:S(2)}) %collective-permute-start.3) | collective-permute-done | bytes 65568 | tf_op jit(solution)/shard_map/ppermute | solution.py:484
  18.6 0.0 collective-permute-start.8
  18.6 1.7 %first_half.1 = (f32[4,256,512]{2,1,0:T(8,128)S(1)}, f32[4,256,512]{2,1,0:T(8,128)S(1)}, f32[4,256,512]{2,1,0:T(8,128)S(1)}, f32[4,256,512]{2,1,0:T(8,128)S(1)},...) custom-call(bf16[4,2,2,16,128]{4,3,2,1,0:T(8,128)(2,1)S(1)} %pad_maximum_fusion.refs_0_, ...), custom_call_target="tpu_custom_call" | custom-call | flops 536870912 | bytes 8388608 | tf_op jit(solution)/shard_map/first_half/pallas_call | solution.py:208
  20.3 0.0 collective-permute-done.9.refs_3_
  20.3 0.0 collective-permute-done.6.refs_0_
  20.4 0.0 collective-permute-done.7.refs_1_
  20.4 0.0 collective-permute-done.8.refs_2_
  20.4 3.7 %second_half.1 = (bf16[4,4,2,2,16,128]{5,4,3,2,1,0:T(8,128)(2,1)S(1)}, f32[8,1,512]{2,1,0:T(1,128)S(1)}, f32[8,1,512]{2,1,0:T(1,128)S(1)}) custom-call(bf16[4,2,2,16,128]{4,3,2,1,0:T(8,128)(2,1)S(1)} %collective-permute-done.6.refs_0_, bf16[4,2,2,16,128]{4,3,2,1,0:T(8,128)(2,1)S(1)} %collective-permute-done.7.refs_1_, ...), custom_call_target="tpu_custom_call" | custom-call | flops 1073741824 | bytes 2097152 | tf_op jit(solution)/shard_map/second_half/pallas_call | solution.py:306
  24.1 0.6 %collective-permute-start.10 = (bf16[4,4,2,2,16,128]{5,4,3,2,1,0:T(8,128)(2,1)S(1)}, bf16[4,4,2,2,16,128]{5,4,3,2,1,0:T(8,128)(2,1)S(1)}, u32[]{:S(2)}, u32[]{:S(2)}) collective-permute-start(bf16[4,4,2,2,16,128]{5,4,3,2,1,0:T(8,128)(2,1)S(1)} %get-tuple-element.48), channel_id=1, source_target_pairs={{0,4},{4,0},{8,12},{12,8},{16,20},{20,16},{24,28},{28,24},{1,5},{5... | collective-permute-start | bytes 786440 | tf_op jit(solution)/shard_map/ppermute | solution.py:484
  24.6 0.0 copy-start.1
  24.6 0.0 copy-start.2
  24.6 0.0 copy-start.3
  24.6 1.3 %finish.1.mine_ref = f32[4,4,2,2,16,128]{5,4,3,2,1,0:T(8,128)S(1)} custom-call(f32[4,256,512]{2,1,0:T(8,128)S(1)} %get-tuple-element.38.refs_0_, f32[4,256,512]{2,1,0:T(8,128)S(1)} %get-tuple-element.39.refs_1_, f32[4,256,512]{2,1,0:T(8,128)S(1)} %get-tuple-element.40.refs_2_, f32[4,256,512]{2,1,0:T(8,128)S(1)} %get-tuple-element.41.refs_3_, ...), custom_call_target="tpu_custom_call" | custom-call | flops 536870912 | bytes 8388608 | tf_op jit(solution)/shard_map/finish/pallas_call | solution.py:379
  26.0 0.0 collective-permute-done.10.mate_ref
  26.0 1.5 %collective-permute-start.11 = (bf16[4,2,2,16,128]{4,3,2,1,0:T(8,128)(2,1)S(1)}, bf16[4,2,2,16,128]{4,3,2,1,0:T(8,128)(2,1)S(1)}, u32[]{:S(2)}, u32[]{:S(2)}) collective-permute-start(bf16[4,2,2,16,128]{4,3,2,1,0:T(8,128)(2,1)S(1)} %get-tuple-element.50), channel_id=1, source_target_pairs={{0,24},{4,28},{8,16},{12,20},{16,8},{20,12},{24,0},{28,4},{1,25},{... | collective-permute-start | bytes 196616 | tf_op jit(solution)/shard_map/ppermute | solution.py:484
  27.6 0.5 %collective-permute-start.12 = (bf16[4,2,2,16,128]{4,3,2,1,0:T(8,128)(2,1)S(1)}, bf16[4,2,2,16,128]{4,3,2,1,0:T(8,128)(2,1)S(1)}, u32[]{:S(2)}, u32[]{:S(2)}) collective-permute-start(bf16[4,2,2,16,128]{4,3,2,1,0:T(8,128)(2,1)S(1)} %get-tuple-element.51), channel_id=1, source_target_pairs={{0,16},{4,20},{8,24},{12,28},{16,0},{20,4},{24,8},{28,12},{1,17},{... | collective-permute-start | bytes 196616 | tf_op jit(solution)/shard_map/ppermute | solution.py:484
  28.1 1.5 %collective-permute-start.13 = (bf16[4,2,2,16,128]{4,3,2,1,0:T(8,128)(2,1)S(1)}, bf16[4,2,2,16,128]{4,3,2,1,0:T(8,128)(2,1)S(1)}, u32[]{:S(2)}, u32[]{:S(2)}) collective-permute-start(bf16[4,2,2,16,128]{4,3,2,1,0:T(8,128)(2,1)S(1)} %get-tuple-element.52), channel_id=1, source_target_pairs={{0,8},{4,12},{8,0},{12,4},{16,24},{20,28},{24,16},{28,20},{1,9},{5... | collective-permute-start | bytes 196616 | tf_op jit(solution)/shard_map/ppermute | solution.py:484
  29.6 1.7 %collective-permute-done.11.refs_0_ = bf16[4,2,2,16,128]{4,3,2,1,0:T(8,128)(2,1)S(1)} collective-permute-done((bf16[4,2,2,16,128]{4,3,2,1,0:T(8,128)(2,1)S(1)}, bf16[4,2,2,16,128]{4,3,2,1,0:T(8,128)(2,1)S(1)}, u32[]{:S(2)}, u32[]{:S(2)}) %collective-permute-start.11) | collective-permute-done | bytes 65568 | tf_op jit(solution)/shard_map/ppermute | solution.py:484
  31.3 1.3 %collective-permute-done.12.refs_1_ = bf16[4,2,2,16,128]{4,3,2,1,0:T(8,128)(2,1)S(1)} collective-permute-done((bf16[4,2,2,16,128]{4,3,2,1,0:T(8,128)(2,1)S(1)}, bf16[4,2,2,16,128]{4,3,2,1,0:T(8,128)(2,1)S(1)}, u32[]{:S(2)}, u32[]{:S(2)}) %collective-permute-start.12) | collective-permute-done | bytes 65568 | tf_op jit(solution)/shard_map/ppermute | solution.py:484
  32.6 0.1 collective-permute-done.13.refs_2_
  32.7 2.1 %collective-permute-start.14 = (bf16[2,2,16,128]{3,2,1,0:T(8,128)(2,1)S(1)}, bf16[2,2,16,128]{3,2,1,0:T(8,128)(2,1)S(1)}, u32[]{:S(2)}, u32[]{:S(2)}) collective-permute-start(bf16[2,2,16,128]{3,2,1,0:T(8,128)(2,1)S(1)} %get-tuple-element.53), channel_id=1, source_target_pairs={{0,3},{1,2},{2,1},{3,0},{4,7},{5,6},{6,5},{7,4},{8,11},{9,10},{10,... | collective-permute-start | bytes 49160 | tf_op jit(solution)/shard_map/ppermute | solution.py:484
  34.8 0.0 collective-permute-start.15
  34.8 2.4 %collective-permute-start.16 = (bf16[2,2,16,128]{3,2,1,0:T(8,128)(2,1)S(1)}, bf16[2,2,16,128]{3,2,1,0:T(8,128)(2,1)S(1)}, u32[]{:S(2)}, u32[]{:S(2)}) collective-permute-start(bf16[2,2,16,128]{3,2,1,0:T(8,128)(2,1)S(1)} %get-tuple-element.55), channel_id=1, source_target_pairs={{0,1},{1,0},{2,3},{3,2},{4,5},{5,4},{6,7},{7,6},{8,9},{9,8},{10,11... | collective-permute-start | bytes 49160 | tf_op jit(solution)/shard_map/ppermute | solution.py:484
  37.1 1.1 %collective-permute-done.14.refs_0_ = bf16[2,2,16,128]{3,2,1,0:T(8,128)(2,1)S(1)} collective-permute-done((bf16[2,2,16,128]{3,2,1,0:T(8,128)(2,1)S(1)}, bf16[2,2,16,128]{3,2,1,0:T(8,128)(2,1)S(1)}, u32[]{:S(2)}, u32[]{:S(2)}) %collective-permute-start.14) | collective-permute-done | bytes 16416 | tf_op jit(solution)/shard_map/ppermute | solution.py:484
  38.3 1.1 %collective-permute-done.15.refs_1_ = bf16[2,2,16,128]{3,2,1,0:T(8,128)(2,1)S(1)} collective-permute-done((bf16[2,2,16,128]{3,2,1,0:T(8,128)(2,1)S(1)}, bf16[2,2,16,128]{3,2,1,0:T(8,128)(2,1)S(1)}, u32[]{:S(2)}, u32[]{:S(2)}) %collective-permute-start.15) | collective-permute-done | bytes 16416 | tf_op jit(solution)/shard_map/ppermute | solution.py:484
  39.4 0.0 collective-permute-done.16.refs_2_
  39.4 0.0 copy-done.1
  39.4 0.0 copy-done.2
  39.4 0.0 copy-done.3
  39.4 0.9 %adam.1 = (f32[16,2,8,128]{3,2,1,0:T(8,128)}, f32[16,2,8,128]{3,2,1,0:T(8,128)}, f32[16,2,8,128]{3,2,1,0:T(8,128)}) custom-call(bf16[2,2,16,128]{3,2,1,0:T(8,128)(2,1)S(1)} %collective-permute-done.14.refs_0_, bf16[2,2,16,128]{3,2,1,0:T(8,128)(2,1)S(1)} %collective-permute-done.15.refs_1_, bf16[2,2,16,128]{3,2,1,0:T(8,128)(2,1)S(1)} %collective-permute-done.16.refs_2_, ...), custom_call_target="tpu_custom_call" | custom-call | tf_op jit(solution)/shard_map/adam/pallas_call | solution.py:471
  (3 shorter events, 0.1 us)
Async XLA Ops:
  0.6 0.9 %copy-start = (f32[16,2,8,128]{3,2,1,0:T(8,128)S(1)}, f32[16,2,8,128]{3,2,1,0:T(8,128)}, u32[]{:S(2)}) copy-start(f32[16,2,8,128]{3,2,1,0:T(8,128)} %refs_4_.1) | copy-start | bytes 393220
  1.7 7.6 %collective-permute-start = (bf16[2,2,16,128]{3,2,1,0:T(8,128)(2,1)S(1)}, bf16[2,2,16,128]{3,2,1,0:T(8,128)(2,1)S(1)}, u32[]{:S(2)}, u32[]{:S(2)}) collective-permute-start(bf16[2,2,16,128]{3,2,1,0:T(8,128)(2,1)S(1)} %get-tuple-element.30), channel_id=1, source_target_pairs={{0,2},{1,3},{2,0},{3,1},{4,6},{5,7},{6,4},{7,5},{8,10},{9,11},{10,... | collective-permute-start | bytes 49160 | tf_op jit(solution)/shard_map/ppermute | solution.py:484
  5.8 5.5 %collective-permute-start.1 = (bf16[2,2,16,128]{3,2,1,0:T(8,128)(2,1)S(1)}, bf16[2,2,16,128]{3,2,1,0:T(8,128)(2,1)S(1)}, u32[]{:S(2)}, u32[]{:S(2)}) collective-permute-start(bf16[2,2,16,128]{3,2,1,0:T(8,128)(2,1)S(1)} %get-tuple-element.31), channel_id=1, source_target_pairs={{0,3},{1,2},{2,1},{3,0},{4,7},{5,6},{6,5},{7,4},{8,11},{9,10},{10,... | collective-permute-start | bytes 49160 | tf_op jit(solution)/shard_map/ppermute | solution.py:484
  7.1 4.2 %collective-permute-start.2 = (bf16[2,2,16,128]{3,2,1,0:T(8,128)(2,1)S(1)}, bf16[2,2,16,128]{3,2,1,0:T(8,128)(2,1)S(1)}, u32[]{:S(2)}, u32[]{:S(2)}) collective-permute-start(bf16[2,2,16,128]{3,2,1,0:T(8,128)(2,1)S(1)} %get-tuple-element.32), channel_id=1, source_target_pairs={{0,1},{1,0},{2,3},{3,2},{4,5},{5,4},{6,7},{7,6},{8,9},{9,8},{10,11... | collective-permute-start | bytes 49160 | tf_op jit(solution)/shard_map/ppermute | solution.py:484
  11.3 5.8 %collective-permute-start.5 = (bf16[4,2,2,16,128]{4,3,2,1,0:T(8,128)(2,1)S(1)}, bf16[4,2,2,16,128]{4,3,2,1,0:T(8,128)(2,1)S(1)}, u32[]{:S(2)}, u32[]{:S(2)}) collective-permute-start(bf16[4,2,2,16,128]{4,3,2,1,0:T(8,128)(2,1)S(1)} %pad_maximum_fusion.refs_0_), channel_id=1, source_target_pairs={{0,24},{4,28},{8,16},{12,20},{16,8},{20,12},{24,0},{28,4},{1,25},{... | collective-permute-start | bytes 196616 | tf_op jit(solution)/shard_map/ppermute | solution.py:484
  13.9 4.3 %collective-permute-start.4 = (bf16[4,2,2,16,128]{4,3,2,1,0:T(8,128)(2,1)S(1)}, bf16[4,2,2,16,128]{4,3,2,1,0:T(8,128)(2,1)S(1)}, u32[]{:S(2)}, u32[]{:S(2)}) collective-permute-start(bf16[4,2,2,16,128]{4,3,2,1,0:T(8,128)(2,1)S(1)} %pad_maximum_fusion.refs_0_), channel_id=1, source_target_pairs={{0,16},{4,20},{8,24},{12,28},{16,0},{20,4},{24,8},{28,12},{1,17},{... | collective-permute-start | bytes 196616 | tf_op jit(solution)/shard_map/ppermute | solution.py:484
  14.4 4.3 %collective-permute-start.3 = (bf16[4,2,2,16,128]{4,3,2,1,0:T(8,128)(2,1)S(1)}, bf16[4,2,2,16,128]{4,3,2,1,0:T(8,128)(2,1)S(1)}, u32[]{:S(2)}, u32[]{:S(2)}) collective-permute-start(bf16[4,2,2,16,128]{4,3,2,1,0:T(8,128)(2,1)S(1)} %pad_maximum_fusion.refs_0_), channel_id=1, source_target_pairs={{0,8},{4,12},{8,0},{12,4},{16,24},{20,28},{24,16},{28,20},{1,9},{5... | collective-permute-start | bytes 196616 | tf_op jit(solution)/shard_map/ppermute | solution.py:484
  16.4 4.0 %collective-permute-start.9 = (bf16[4,2,2,16,128]{4,3,2,1,0:T(8,128)(2,1)S(1)}, bf16[4,2,2,16,128]{4,3,2,1,0:T(8,128)(2,1)S(1)}, u32[]{:S(2)}, u32[]{:S(2)}) collective-permute-start(bf16[4,2,2,16,128]{4,3,2,1,0:T(8,128)(2,1)S(1)} %pad_maximum_fusion.refs_0_), channel_id=1, source_target_pairs={{0,4},{4,0},{8,12},{12,8},{16,20},{20,16},{24,28},{28,24},{1,5},{5... | collective-permute-start | bytes 196616 | tf_op jit(solution)/shard_map/ppermute | solution.py:484
  17.2 3.2 %collective-permute-start.6 = (bf16[4,2,2,16,128]{4,3,2,1,0:T(8,128)(2,1)S(1)}, bf16[4,2,2,16,128]{4,3,2,1,0:T(8,128)(2,1)S(1)}, u32[]{:S(2)}, u32[]{:S(2)}) collective-permute-start(bf16[4,2,2,16,128]{4,3,2,1,0:T(8,128)(2,1)S(1)} %collective-permute-done.5.refs_3_), channel_id=1, source_target_pairs={{0,4},{4,0},{8,12},{12,8},{16,20},{20,16},{24,28},{28,24},{1,5},{5... | collective-permute-start | bytes 196616 | tf_op jit(solution)/shard_map/ppermute | solution.py:484
  18.1 2.2 %collective-permute-start.7 = (bf16[4,2,2,16,128]{4,3,2,1,0:T(8,128)(2,1)S(1)}, bf16[4,2,2,16,128]{4,3,2,1,0:T(8,128)(2,1)S(1)}, u32[]{:S(2)}, u32[]{:S(2)}) collective-permute-start(bf16[4,2,2,16,128]{4,3,2,1,0:T(8,128)(2,1)S(1)} %collective-permute-done.4.refs_2_), channel_id=1, source_target_pairs={{0,4},{4,0},{8,12},{12,8},{16,20},{20,16},{24,28},{28,24},{1,5},{5... | collective-permute-start | bytes 196616 | tf_op jit(solution)/shard_map/ppermute | solution.py:484
  18.6 1.7 %collective-permute-start.8 = (bf16[4,2,2,16,128]{4,3,2,1,0:T(8,128)(2,1)S(1)}, bf16[4,2,2,16,128]{4,3,2,1,0:T(8,128)(2,1)S(1)}, u32[]{:S(2)}, u32[]{:S(2)}) collective-permute-start(bf16[4,2,2,16,128]{4,3,2,1,0:T(8,128)(2,1)S(1)} %collective-permute-done.3.refs_1_), channel_id=1, source_target_pairs={{0,4},{4,0},{8,12},{12,8},{16,20},{20,16},{24,28},{28,24},{1,5},{5... | collective-permute-start | bytes 196616 | tf_op jit(solution)/shard_map/ppermute | solution.py:484
  24.1 1.9 %collective-permute-start.10 = (bf16[4,4,2,2,16,128]{5,4,3,2,1,0:T(8,128)(2,1)S(1)}, bf16[4,4,2,2,16,128]{5,4,3,2,1,0:T(8,128)(2,1)S(1)}, u32[]{:S(2)}, u32[]{:S(2)}) collective-permute-start(bf16[4,4,2,2,16,128]{5,4,3,2,1,0:T(8,128)(2,1)S(1)} %get-tuple-element.48), channel_id=1, source_target_pairs={{0,4},{4,0},{8,12},{12,8},{16,20},{20,16},{24,28},{28,24},{1,5},{5... | collective-permute-start | bytes 786440 | tf_op jit(solution)/shard_map/ppermute | solution.py:484
  24.6 14.8 %copy-start.1 = (f32[16,2,8,128]{3,2,1,0:T(8,128)S(1)}, f32[16,2,8,128]{3,2,1,0:T(8,128)}, u32[]{:S(2)}) copy-start(f32[16,2,8,128]{3,2,1,0:T(8,128)} %refs_4_.1) | copy-start | bytes 393220
  24.6 14.8 %copy-start.2 = (f32[16,2,8,128]{3,2,1,0:T(8,128)S(1)}, f32[16,2,8,128]{3,2,1,0:T(8,128)}, u32[]{:S(2)}) copy-start(f32[16,2,8,128]{3,2,1,0:T(8,128)} %refs_5_.1) | copy-start | bytes 393220
  24.6 14.8 %copy-start.3 = (f32[16,2,8,128]{3,2,1,0:T(8,128)S(1)}, f32[16,2,8,128]{3,2,1,0:T(8,128)}, u32[]{:S(2)}) copy-start(f32[16,2,8,128]{3,2,1,0:T(8,128)} %refs_6_.1) | copy-start | bytes 393220
  26.0 5.3 %collective-permute-start.11 = (bf16[4,2,2,16,128]{4,3,2,1,0:T(8,128)(2,1)S(1)}, bf16[4,2,2,16,128]{4,3,2,1,0:T(8,128)(2,1)S(1)}, u32[]{:S(2)}, u32[]{:S(2)}) collective-permute-start(bf16[4,2,2,16,128]{4,3,2,1,0:T(8,128)(2,1)S(1)} %get-tuple-element.50), channel_id=1, source_target_pairs={{0,24},{4,28},{8,16},{12,20},{16,8},{20,12},{24,0},{28,4},{1,25},{... | collective-permute-start | bytes 196616 | tf_op jit(solution)/shard_map/ppermute | solution.py:484
  27.6 5.0 %collective-permute-start.12 = (bf16[4,2,2,16,128]{4,3,2,1,0:T(8,128)(2,1)S(1)}, bf16[4,2,2,16,128]{4,3,2,1,0:T(8,128)(2,1)S(1)}, u32[]{:S(2)}, u32[]{:S(2)}) collective-permute-start(bf16[4,2,2,16,128]{4,3,2,1,0:T(8,128)(2,1)S(1)} %get-tuple-element.51), channel_id=1, source_target_pairs={{0,16},{4,20},{8,24},{12,28},{16,0},{20,4},{24,8},{28,12},{1,17},{... | collective-permute-start | bytes 196616 | tf_op jit(solution)/shard_map/ppermute | solution.py:484
  28.1 4.6 %collective-permute-start.13 = (bf16[4,2,2,16,128]{4,3,2,1,0:T(8,128)(2,1)S(1)}, bf16[4,2,2,16,128]{4,3,2,1,0:T(8,128)(2,1)S(1)}, u32[]{:S(2)}, u32[]{:S(2)}) collective-permute-start(bf16[4,2,2,16,128]{4,3,2,1,0:T(8,128)(2,1)S(1)} %get-tuple-element.52), channel_id=1, source_target_pairs={{0,8},{4,12},{8,0},{12,4},{16,24},{20,28},{24,16},{28,20},{1,9},{5... | collective-permute-start | bytes 196616 | tf_op jit(solution)/shard_map/ppermute | solution.py:484
  32.7 5.6 %collective-permute-start.14 = (bf16[2,2,16,128]{3,2,1,0:T(8,128)(2,1)S(1)}, bf16[2,2,16,128]{3,2,1,0:T(8,128)(2,1)S(1)}, u32[]{:S(2)}, u32[]{:S(2)}) collective-permute-start(bf16[2,2,16,128]{3,2,1,0:T(8,128)(2,1)S(1)} %get-tuple-element.53), channel_id=1, source_target_pairs={{0,3},{1,2},{2,1},{3,0},{4,7},{5,6},{6,5},{7,4},{8,11},{9,10},{10,... | collective-permute-start | bytes 49160 | tf_op jit(solution)/shard_map/ppermute | solution.py:484
  34.8 4.6 %collective-permute-start.15 = (bf16[2,2,16,128]{3,2,1,0:T(8,128)(2,1)S(1)}, bf16[2,2,16,128]{3,2,1,0:T(8,128)(2,1)S(1)}, u32[]{:S(2)}, u32[]{:S(2)}) collective-permute-start(bf16[2,2,16,128]{3,2,1,0:T(8,128)(2,1)S(1)} %get-tuple-element.54), channel_id=1, source_target_pairs={{0,2},{1,3},{2,0},{3,1},{4,6},{5,7},{6,4},{7,5},{8,10},{9,11},{10,... | collective-permute-start | bytes 49160 | tf_op jit(solution)/shard_map/ppermute | solution.py:484
  34.8 4.6 %collective-permute-start.16 = (bf16[2,2,16,128]{3,2,1,0:T(8,128)(2,1)S(1)}, bf16[2,2,16,128]{3,2,1,0:T(8,128)(2,1)S(1)}, u32[]{:S(2)}, u32[]{:S(2)}) collective-permute-start(bf16[2,2,16,128]{3,2,1,0:T(8,128)(2,1)S(1)} %get-tuple-element.55), channel_id=1, source_target_pairs={{0,1},{1,0},{2,3},{3,2},{4,5},{5,4},{6,7},{7,6},{8,9},{9,8},{10,11... | collective-permute-start | bytes 49160 | tf_op jit(solution)/shard_map/ppermute | solution.py:484

commit v13 on v12

--- a/solution.py
+++ b/solution.py
@@ -15,8 +15,8 @@
 beta_second = 0.999
 epsilon = 1e-08
 
-ROW_TILE = 512
-CHUNK = 16
+ROW_TILE = 256
+CHUNK = 32
 DOT_ROWS = 256
 MIB = 1024 * 1024
 
@@ -104,12 +104,17 @@
     return products
 
 
-def gradient_products(key_total, value_total, slot, weights, dscores, queries_ref, grads_ref, tile):
+def gradient_products(
+    key_total, value_total, per_group, weights, dscores, queries_ref, grads_ref, tile
+):
+    slot = tile // per_group
+
     def product(total, left, right_ref):
         def run():
-            total[slot] += lax.dot_general(
+            part = lax.dot_general(
                 left[...], right_ref[tile], ALONG, preferred_element_type=jnp.float32
             )
+            total[slot] = total[slot] + part if tile % per_group else part
 
         return run
 
@@ -234,8 +239,6 @@
     tiles = queries_ref.shape[0]
     factor = score_scale * LOG2E
     load_pairs(pair_refs, keys, values)
-    key_total[...] = jnp.zeros_like(key_total)
-    value_total[...] = jnp.zeros_like(value_total)
 
     def products(tile, buffers):
         slot = tile // per_group
@@ -263,7 +266,7 @@
         return gradient_products(
             key_total,
             value_total,
-            tile // per_group,
+            per_group,
             *buffers[3:],
             queries_ref,
             grads_ref,
@@ -335,8 +338,6 @@
     even, odd = refs[7:9], refs[9:11]
     _, columns, _, own, share, width = out_ref.shape
     tiles = queries_ref.shape[0]
-    key_total[...] = jnp.zeros_like(key_total)
-    value_total[...] = jnp.zeros_like(value_total)
 
     def spread(tile, parity, step, buffers):
         steps = weigh(
@@ -350,7 +351,7 @@
 
     def gather(tile, buffers):
         return gradient_products(
-            key_total, value_total, tile // per_group, *buffers, queries_ref, grads_ref, tile
+            key_total, value_total, per_group, *buffers, queries_ref, grads_ref, tile
         )
 
     interleave(spread(0, 0, 0, even))

time: 40.6 us -> 40.3 us (level)
  no operation moved by 1% of the time
where the time goes in v13:
time: 40.3 us; the launch traced here: 40 us
  starting transfers between devices  17.9 us (44%)
  waiting for transfers between devices  9.57 us (24%)
  Pallas kernels  7.44 us (18%)
  local copies, waits for them, and re-layouts  4.31 us (11%)
  between operations  0.79 us (2%)
    ppermute x17, starting transfers between devices, swap(): lax.ppermute(value, axis, [(place, place ^ flip) for place in range(size)])  17.9 us
    ppermute x17, waiting for transfers between devices, swap(): lax.ppermute(value, axis, [(place, place ^ flip) for place in range(size)])  9.57 us
    pallas_call x1, Pallas kernels, second_half(): pl.pallas_call(functools.partial(second_half_kernel, score_scale, tiles /...  3.46 us
    dynamic_slice x2, local copies, waits for them, and re-layouts, tiles_of(): part = lax.dynamic_slice_in_dim(part, first_group, own, 1)  2.69 us
    pallas_call x1, Pallas kernels, first_half(): pl.pallas_call(functools.partial(first_half_kernel, score_scale, tiles //...  1.62 us
    unnamed x12, local copies, waits for them, and re-layouts  1.3 us
    pallas_call x1, Pallas kernels, finish(): pl.pallas_call(functools.partial(finish_kernel, score_scale, tiles // own...  1.25 us
    pallas_call x1, Pallas kernels, adam(): pl.pallas_call(functools.partial(adam_kernel, len(parts)), out_shape=(sha...  0.89 us
  transfers between devices with their start and end apart: 17, of which 9 were waited for; matrix products, arithmetic and copies ran while one was open for 8% of the time, Pallas kernels for 7%

profile of v13, /device:TPU:0, one launch (start us, length us, event | category | flops | bytes accessed | tf_op | source)
XLA Modules:
  0.0 40.0 jit_solution(14223448871968954469)
XLA Ops:
  0.6 0.0 copy-start
  0.6 0.9 %copy-done = f32[16,2,8,128]{3,2,1,0:T(8,128)S(1)} copy-done((f32[16,2,8,128]{3,2,1,0:T(8,128)S(1)}, f32[16,2,8,128]{3,2,1,0:T(8,128)}, u32[]{:S(2)}) %copy-start) | copy-done | bytes 131096
  1.5 0.1 pack.1
  1.7 4.1 %collective-permute-start = (bf16[2,2,16,128]{3,2,1,0:T(8,128)(2,1)S(1)}, bf16[2,2,16,128]{3,2,1,0:T(8,128)(2,1)S(1)}, u32[]{:S(2)}, u32[]{:S(2)}) collective-permute-start(bf16[2,2,16,128]{3,2,1,0:T(8,128)(2,1)S(1)} %get-tuple-element.30), channel_id=1, source_target_pairs={{0,2},{1,3},{2,0},{3,1},{4,6},{5,7},{6,4},{7,5},{8,10},{9,11},{10,... | collective-permute-start | bytes 49160 | tf_op jit(solution)/shard_map/ppermute | solution.py:485
  5.8 1.3 %collective-permute-start.1 = (bf16[2,2,16,128]{3,2,1,0:T(8,128)(2,1)S(1)}, bf16[2,2,16,128]{3,2,1,0:T(8,128)(2,1)S(1)}, u32[]{:S(2)}, u32[]{:S(2)}) collective-permute-start(bf16[2,2,16,128]{3,2,1,0:T(8,128)(2,1)S(1)} %get-tuple-element.31), channel_id=1, source_target_pairs={{0,3},{1,2},{2,1},{3,0},{4,7},{5,6},{6,5},{7,4},{8,11},{9,10},{10,... | collective-permute-start | bytes 49160 | tf_op jit(solution)/shard_map/ppermute | solution.py:485
  7.1 0.2 collective-permute-start.2
  7.4 2.0 %constant_dynamic-slice_fusion.2 = (bf16[256,2,8,128]{3,2,1,0:T(8,128)(2,1)S(1)}, bf16[256,2,8,128]{3,2,1,0:T(8,128)(2,1)S(1)}) fusion(bf16[256,8,8,128]{3,2,1,0:T(8,128)(2,1)} %bitcast.25, s32[]{:T(128)S(6)} %select_n.9, bf16[256,8,8,128]{3,2,1,0:T(8,128)(2,1)} %bitcast.26), kind=kLoop, calls=%fused_computation.3 | loop fusion | bytes 4194308 | tf_op jit(solution)/shard_map/dynamic_slice | solution.py:516
  9.3 0.0 collective-permute-done
  9.3 2.0 %collective-permute-done.1 = bf16[2,2,16,128]{3,2,1,0:T(8,128)(2,1)S(1)} collective-permute-done((bf16[2,2,16,128]{3,2,1,0:T(8,128)(2,1)S(1)}, bf16[2,2,16,128]{3,2,1,0:T(8,128)(2,1)S(1)}, u32[]{:S(2)}, u32[]{:S(2)}) %collective-permute-start.1) | collective-permute-done | bytes 16416 | tf_op jit(solution)/shard_map/ppermute | solution.py:485
  11.3 0.0 collective-permute-done.2
  11.3 2.5 %collective-permute-start.5 = (bf16[4,2,2,16,128]{4,3,2,1,0:T(8,128)(2,1)S(1)}, bf16[4,2,2,16,128]{4,3,2,1,0:T(8,128)(2,1)S(1)}, u32[]{:S(2)}, u32[]{:S(2)}) collective-permute-start(bf16[4,2,2,16,128]{4,3,2,1,0:T(8,128)(2,1)S(1)} %pad_maximum_fusion.refs_0_), channel_id=1, source_target_pairs={{0,24},{4,28},{8,16},{12,20},{16,8},{20,12},{24,0},{28,4},{1,25},{... | collective-permute-start | bytes 196616 | tf_op jit(solution)/shard_map/ppermute | solution.py:485
  13.9 0.5 %collective-permute-start.4 = (bf16[4,2,2,16,128]{4,3,2,1,0:T(8,128)(2,1)S(1)}, bf16[4,2,2,16,128]{4,3,2,1,0:T(8,128)(2,1)S(1)}, u32[]{:S(2)}, u32[]{:S(2)}) collective-permute-start(bf16[4,2,2,16,128]{4,3,2,1,0:T(8,128)(2,1)S(1)} %pad_maximum_fusion.refs_0_), channel_id=1, source_target_pairs={{0,16},{4,20},{8,24},{12,28},{16,0},{20,4},{24,8},{28,12},{1,17},{... | collective-permute-start | bytes 196616 | tf_op jit(solution)/shard_map/ppermute | solution.py:485
  14.4 0.5 %collective-permute-start.3 = (bf16[4,2,2,16,128]{4,3,2,1,0:T(8,128)(2,1)S(1)}, bf16[4,2,2,16,128]{4,3,2,1,0:T(8,128)(2,1)S(1)}, u32[]{:S(2)}, u32[]{:S(2)}) collective-permute-start(bf16[4,2,2,16,128]{4,3,2,1,0:T(8,128)(2,1)S(1)} %pad_maximum_fusion.refs_0_), channel_id=1, source_target_pairs={{0,8},{4,12},{8,0},{12,4},{16,24},{20,28},{24,16},{28,20},{1,9},{5... | collective-permute-start | bytes 196616 | tf_op jit(solution)/shard_map/ppermute | solution.py:485
  14.9 0.7 %constant_dynamic-slice_fusion = (f32[256,2,8]{0,2,1:T(8,128)S(1)}, f32[256,2,8]{0,2,1:T(8,128)S(1)}) fusion(f32[256,8,8]{0,2,1:T(8,128)} %bitcast.30, s32[]{:T(128)S(6)} %select_n.9, f32[256,8,8]{0,2,1:T(8,128)} %bitcast.31), kind=kLoop, calls=%fused_computation.1 | loop fusion | bytes 65540 | tf_op jit(solution)/shard_map/dynamic_slice | solution.py:516
  15.6 0.1 copy.21
  15.8 0.2 reshape.37.refs_7_
  15.9 0.1 copy.20
  16.1 0.2 reshape.35.refs_6_
  16.2 0.1 copy.19
  16.3 0.1 copy.18
  16.4 0.1 collective-permute-start.9
  16.5 0.7 %collective-permute-done.5.refs_3_ = bf16[4,2,2,16,128]{4,3,2,1,0:T(8,128)(2,1)S(1)} collective-permute-done((bf16[4,2,2,16,128]{4,3,2,1,0:T(8,128)(2,1)S(1)}, bf16[4,2,2,16,128]{4,3,2,1,0:T(8,128)(2,1)S(1)}, u32[]{:S(2)}, u32[]{:S(2)}) %collective-permute-start.5) | collective-permute-done | bytes 65568 | tf_op jit(solution)/shard_map/ppermute | solution.py:485
  17.2 0.0 collective-permute-start.6
  17.2 1.0 %collective-permute-done.4.refs_2_ = bf16[4,2,2,16,128]{4,3,2,1,0:T(8,128)(2,1)S(1)} collective-permute-done((bf16[4,2,2,16,128]{4,3,2,1,0:T(8,128)(2,1)S(1)}, bf16[4,2,2,16,128]{4,3,2,1,0:T(8,128)(2,1)S(1)}, u32[]{:S(2)}, u32[]{:S(2)}) %collective-permute-start.4) | collective-permute-done | bytes 65568 | tf_op jit(solution)/shard_map/ppermute | solution.py:485
  18.1 0.0 collective-permute-start.7
  18.1 0.5 %collective-permute-done.3.refs_1_ = bf16[4,2,2,16,128]{4,3,2,1,0:T(8,128)(2,1)S(1)} collective-permute-done((bf16[4,2,2,16,128]{4,3,2,1,0:T(8,128)(2,1)S(1)}, bf16[4,2,2,16,128]{4,3,2,1,0:T(8,128)(2,1)S(1)}, u32[]{:S(2)}, u32[]{:S(2)}) %collective-permute-start.3) | collective-permute-done | bytes 65568 | tf_op jit(solution)/shard_map/ppermute | solution.py:485
  18.6 0.0 collective-permute-start.8
  18.6 1.6 %first_half.1 = (f32[8,256,256]{2,1,0:T(8,128)S(1)}, f32[8,256,256]{2,1,0:T(8,128)S(1)}, f32[8,256,256]{2,1,0:T(8,128)S(1)}, f32[8,256,256]{2,1,0:T(8,128)S(1)},...) custom-call(bf16[4,2,2,16,128]{4,3,2,1,0:T(8,128)(2,1)S(1)} %pad_maximum_fusion.refs_0_, ...), custom_call_target="tpu_custom_call" | custom-call | flops 536870912 | bytes 8388608 | tf_op jit(solution)/shard_map/first_half/pallas_call | solution.py:213
  20.3 0.0 collective-permute-done.9.refs_3_
  20.3 0.0 collective-permute-done.6.refs_0_
  20.3 0.0 collective-permute-done.7.refs_1_
  20.3 0.0 collective-permute-done.8.refs_2_
  20.3 3.5 %second_half.1 = (bf16[4,4,2,2,16,128]{5,4,3,2,1,0:T(8,128)(2,1)S(1)}, f32[16,1,256]{2,1,0:T(1,128)S(1)}, f32[16,1,256]{2,1,0:T(1,128)S(1)}) custom-call(bf16[4,2,2,16,128]{4,3,2,1,0:T(8,128)(2,1)S(1)} %collective-permute-done.6.refs_0_, bf16[4,2,2,16,128]{4,3,2,1,0:T(8,128)(2,1)S(1)} %collective-permute-done.7.refs_1_, ...), custom_call_target="tpu_custom_call" | custom-call | flops 1073741824 | bytes 2097152 | tf_op jit(solution)/shard_map/second_half/pallas_call | solution.py:309
  23.8 0.6 %collective-permute-start.10 = (bf16[4,4,2,2,16,128]{5,4,3,2,1,0:T(8,128)(2,1)S(1)}, bf16[4,4,2,2,16,128]{5,4,3,2,1,0:T(8,128)(2,1)S(1)}, u32[]{:S(2)}, u32[]{:S(2)}) collective-permute-start(bf16[4,4,2,2,16,128]{5,4,3,2,1,0:T(8,128)(2,1)S(1)} %get-tuple-element.48), channel_id=1, source_target_pairs={{0,4},{4,0},{8,12},{12,8},{16,20},{20,16},{24,28},{28,24},{1,5},{5... | collective-permute-start | bytes 786440 | tf_op jit(solution)/shard_map/ppermute | solution.py:485
  24.3 0.0 copy-start.1
  24.3 0.0 copy-start.2
  24.3 0.0 copy-start.3
  24.3 1.2 %finish.1.mine_ref = f32[4,4,2,2,16,128]{5,4,3,2,1,0:T(8,128)S(1)} custom-call(f32[8,256,256]{2,1,0:T(8,128)S(1)} %get-tuple-element.38.refs_0_, f32[8,256,256]{2,1,0:T(8,128)S(1)} %get-tuple-element.39.refs_1_, f32[8,256,256]{2,1,0:T(8,128)S(1)} %get-tuple-element.40.refs_2_, f32[8,256,256]{2,1,0:T(8,128)S(1)} %get-tuple-element.41.refs_3_, ...), custom_call_target="tpu_custom_call" | custom-call | flops 536870912 | bytes 8388608 | tf_op jit(solution)/shard_map/finish/pallas_call | solution.py:380
  25.6 0.0 collective-permute-done.10.mate_ref
  25.7 1.6 %collective-permute-start.11 = (bf16[4,2,2,16,128]{4,3,2,1,0:T(8,128)(2,1)S(1)}, bf16[4,2,2,16,128]{4,3,2,1,0:T(8,128)(2,1)S(1)}, u32[]{:S(2)}, u32[]{:S(2)}) collective-permute-start(bf16[4,2,2,16,128]{4,3,2,1,0:T(8,128)(2,1)S(1)} %get-tuple-element.50), channel_id=1, source_target_pairs={{0,24},{4,28},{8,16},{12,20},{16,8},{20,12},{24,0},{28,4},{1,25},{... | collective-permute-start | bytes 196616 | tf_op jit(solution)/shard_map/ppermute | solution.py:485
  27.2 0.5 %collective-permute-start.12 = (bf16[4,2,2,16,128]{4,3,2,1,0:T(8,128)(2,1)S(1)}, bf16[4,2,2,16,128]{4,3,2,1,0:T(8,128)(2,1)S(1)}, u32[]{:S(2)}, u32[]{:S(2)}) collective-permute-start(bf16[4,2,2,16,128]{4,3,2,1,0:T(8,128)(2,1)S(1)} %get-tuple-element.51), channel_id=1, source_target_pairs={{0,16},{4,20},{8,24},{12,28},{16,0},{20,4},{24,8},{28,12},{1,17},{... | collective-permute-start | bytes 196616 | tf_op jit(solution)/shard_map/ppermute | solution.py:485
  27.7 1.5 %collective-permute-start.13 = (bf16[4,2,2,16,128]{4,3,2,1,0:T(8,128)(2,1)S(1)}, bf16[4,2,2,16,128]{4,3,2,1,0:T(8,128)(2,1)S(1)}, u32[]{:S(2)}, u32[]{:S(2)}) collective-permute-start(bf16[4,2,2,16,128]{4,3,2,1,0:T(8,128)(2,1)S(1)} %get-tuple-element.52), channel_id=1, source_target_pairs={{0,8},{4,12},{8,0},{12,4},{16,24},{20,28},{24,16},{28,20},{1,9},{5... | collective-permute-start | bytes 196616 | tf_op jit(solution)/shard_map/ppermute | solution.py:485
  29.2 1.8 %collective-permute-done.11.refs_0_ = bf16[4,2,2,16,128]{4,3,2,1,0:T(8,128)(2,1)S(1)} collective-permute-done((bf16[4,2,2,16,128]{4,3,2,1,0:T(8,128)(2,1)S(1)}, bf16[4,2,2,16,128]{4,3,2,1,0:T(8,128)(2,1)S(1)}, u32[]{:S(2)}, u32[]{:S(2)}) %collective-permute-start.11) | collective-permute-done | bytes 65568 | tf_op jit(solution)/shard_map/ppermute | solution.py:485
  31.0 1.3 %collective-permute-done.12.refs_1_ = bf16[4,2,2,16,128]{4,3,2,1,0:T(8,128)(2,1)S(1)} collective-permute-done((bf16[4,2,2,16,128]{4,3,2,1,0:T(8,128)(2,1)S(1)}, bf16[4,2,2,16,128]{4,3,2,1,0:T(8,128)(2,1)S(1)}, u32[]{:S(2)}, u32[]{:S(2)}) %collective-permute-start.12) | collective-permute-done | bytes 65568 | tf_op jit(solution)/shard_map/ppermute | solution.py:485
  32.3 0.1 collective-permute-done.13.refs_2_
  32.4 2.1 %collective-permute-start.14 = (bf16[2,2,16,128]{3,2,1,0:T(8,128)(2,1)S(1)}, bf16[2,2,16,128]{3,2,1,0:T(8,128)(2,1)S(1)}, u32[]{:S(2)}, u32[]{:S(2)}) collective-permute-start(bf16[2,2,16,128]{3,2,1,0:T(8,128)(2,1)S(1)} %get-tuple-element.53), channel_id=1, source_target_pairs={{0,3},{1,2},{2,1},{3,0},{4,7},{5,6},{6,5},{7,4},{8,11},{9,10},{10,... | collective-permute-start | bytes 49160 | tf_op jit(solution)/shard_map/ppermute | solution.py:485
  34.5 0.0 collective-permute-start.15
  34.5 2.4 %collective-permute-start.16 = (bf16[2,2,16,128]{3,2,1,0:T(8,128)(2,1)S(1)}, bf16[2,2,16,128]{3,2,1,0:T(8,128)(2,1)S(1)}, u32[]{:S(2)}, u32[]{:S(2)}) collective-permute-start(bf16[2,2,16,128]{3,2,1,0:T(8,128)(2,1)S(1)} %get-tuple-element.55), channel_id=1, source_target_pairs={{0,1},{1,0},{2,3},{3,2},{4,5},{5,4},{6,7},{7,6},{8,9},{9,8},{10,11... | collective-permute-start | bytes 49160 | tf_op jit(solution)/shard_map/ppermute | solution.py:485
  36.8 1.2 %collective-permute-done.14.refs_0_ = bf16[2,2,16,128]{3,2,1,0:T(8,128)(2,1)S(1)} collective-permute-done((bf16[2,2,16,128]{3,2,1,0:T(8,128)(2,1)S(1)}, bf16[2,2,16,128]{3,2,1,0:T(8,128)(2,1)S(1)}, u32[]{:S(2)}, u32[]{:S(2)}) %collective-permute-start.14) | collective-permute-done | bytes 16416 | tf_op jit(solution)/shard_map/ppermute | solution.py:485
  38.0 1.1 %collective-permute-done.15.refs_1_ = bf16[2,2,16,128]{3,2,1,0:T(8,128)(2,1)S(1)} collective-permute-done((bf16[2,2,16,128]{3,2,1,0:T(8,128)(2,1)S(1)}, bf16[2,2,16,128]{3,2,1,0:T(8,128)(2,1)S(1)}, u32[]{:S(2)}, u32[]{:S(2)}) %collective-permute-start.15) | collective-permute-done | bytes 16416 | tf_op jit(solution)/shard_map/ppermute | solution.py:485
  39.1 0.0 collective-permute-done.16.refs_2_
  39.1 0.0 copy-done.1
  39.1 0.0 copy-done.2
  39.1 0.0 copy-done.3
  39.1 0.9 %adam.1 = (f32[16,2,8,128]{3,2,1,0:T(8,128)}, f32[16,2,8,128]{3,2,1,0:T(8,128)}, f32[16,2,8,128]{3,2,1,0:T(8,128)}) custom-call(bf16[2,2,16,128]{3,2,1,0:T(8,128)(2,1)S(1)} %collective-permute-done.14.refs_0_, bf16[2,2,16,128]{3,2,1,0:T(8,128)(2,1)S(1)} %collective-permute-done.15.refs_1_, bf16[2,2,16,128]{3,2,1,0:T(8,128)(2,1)S(1)} %collective-permute-done.16.refs_2_, ...), custom_call_target="tpu_custom_call" | custom-call | tf_op jit(solution)/shard_map/adam/pallas_call | solution.py:472
  (3 shorter events, 0.1 us)
Async XLA Ops:
  0.6 0.9 %copy-start = (f32[16,2,8,128]{3,2,1,0:T(8,128)S(1)}, f32[16,2,8,128]{3,2,1,0:T(8,128)}, u32[]{:S(2)}) copy-start(f32[16,2,8,128]{3,2,1,0:T(8,128)} %refs_4_.1) | copy-start | bytes 393220
  1.7 7.6 %collective-permute-start = (bf16[2,2,16,128]{3,2,1,0:T(8,128)(2,1)S(1)}, bf16[2,2,16,128]{3,2,1,0:T(8,128)(2,1)S(1)}, u32[]{:S(2)}, u32[]{:S(2)}) collective-permute-start(bf16[2,2,16,128]{3,2,1,0:T(8,128)(2,1)S(1)} %get-tuple-element.30), channel_id=1, source_target_pairs={{0,2},{1,3},{2,0},{3,1},{4,6},{5,7},{6,4},{7,5},{8,10},{9,11},{10,... | collective-permute-start | bytes 49160 | tf_op jit(solution)/shard_map/ppermute | solution.py:485
  5.8 5.5 %collective-permute-start.1 = (bf16[2,2,16,128]{3,2,1,0:T(8,128)(2,1)S(1)}, bf16[2,2,16,128]{3,2,1,0:T(8,128)(2,1)S(1)}, u32[]{:S(2)}, u32[]{:S(2)}) collective-permute-start(bf16[2,2,16,128]{3,2,1,0:T(8,128)(2,1)S(1)} %get-tuple-element.31), channel_id=1, source_target_pairs={{0,3},{1,2},{2,1},{3,0},{4,7},{5,6},{6,5},{7,4},{8,11},{9,10},{10,... | collective-permute-start | bytes 49160 | tf_op jit(solution)/shard_map/ppermute | solution.py:485
  7.1 4.2 %collective-permute-start.2 = (bf16[2,2,16,128]{3,2,1,0:T(8,128)(2,1)S(1)}, bf16[2,2,16,128]{3,2,1,0:T(8,128)(2,1)S(1)}, u32[]{:S(2)}, u32[]{:S(2)}) collective-permute-start(bf16[2,2,16,128]{3,2,1,0:T(8,128)(2,1)S(1)} %get-tuple-element.32), channel_id=1, source_target_pairs={{0,1},{1,0},{2,3},{3,2},{4,5},{5,4},{6,7},{7,6},{8,9},{9,8},{10,11... | collective-permute-start | bytes 49160 | tf_op jit(solution)/shard_map/ppermute | solution.py:485
  11.3 5.8 %collective-permute-start.5 = (bf16[4,2,2,16,128]{4,3,2,1,0:T(8,128)(2,1)S(1)}, bf16[4,2,2,16,128]{4,3,2,1,0:T(8,128)(2,1)S(1)}, u32[]{:S(2)}, u32[]{:S(2)}) collective-permute-start(bf16[4,2,2,16,128]{4,3,2,1,0:T(8,128)(2,1)S(1)} %pad_maximum_fusion.refs_0_), channel_id=1, source_target_pairs={{0,24},{4,28},{8,16},{12,20},{16,8},{20,12},{24,0},{28,4},{1,25},{... | collective-permute-start | bytes 196616 | tf_op jit(solution)/shard_map/ppermute | solution.py:485
  13.9 4.3 %collective-permute-start.4 = (bf16[4,2,2,16,128]{4,3,2,1,0:T(8,128)(2,1)S(1)}, bf16[4,2,2,16,128]{4,3,2,1,0:T(8,128)(2,1)S(1)}, u32[]{:S(2)}, u32[]{:S(2)}) collective-permute-start(bf16[4,2,2,16,128]{4,3,2,1,0:T(8,128)(2,1)S(1)} %pad_maximum_fusion.refs_0_), channel_id=1, source_target_pairs={{0,16},{4,20},{8,24},{12,28},{16,0},{20,4},{24,8},{28,12},{1,17},{... | collective-permute-start | bytes 196616 | tf_op jit(solution)/shard_map/ppermute | solution.py:485
  14.4 4.3 %collective-permute-start.3 = (bf16[4,2,2,16,128]{4,3,2,1,0:T(8,128)(2,1)S(1)}, bf16[4,2,2,16,128]{4,3,2,1,0:T(8,128)(2,1)S(1)}, u32[]{:S(2)}, u32[]{:S(2)}) collective-permute-start(bf16[4,2,2,16,128]{4,3,2,1,0:T(8,128)(2,1)S(1)} %pad_maximum_fusion.refs_0_), channel_id=1, source_target_pairs={{0,8},{4,12},{8,0},{12,4},{16,24},{20,28},{24,16},{28,20},{1,9},{5... | collective-permute-start | bytes 196616 | tf_op jit(solution)/shard_map/ppermute | solution.py:485
  16.4 3.9 %collective-permute-start.9 = (bf16[4,2,2,16,128]{4,3,2,1,0:T(8,128)(2,1)S(1)}, bf16[4,2,2,16,128]{4,3,2,1,0:T(8,128)(2,1)S(1)}, u32[]{:S(2)}, u32[]{:S(2)}) collective-permute-start(bf16[4,2,2,16,128]{4,3,2,1,0:T(8,128)(2,1)S(1)} %pad_maximum_fusion.refs_0_), channel_id=1, source_target_pairs={{0,4},{4,0},{8,12},{12,8},{16,20},{20,16},{24,28},{28,24},{1,5},{5... | collective-permute-start | bytes 196616 | tf_op jit(solution)/shard_map/ppermute | solution.py:485
  17.2 3.1 %collective-permute-start.6 = (bf16[4,2,2,16,128]{4,3,2,1,0:T(8,128)(2,1)S(1)}, bf16[4,2,2,16,128]{4,3,2,1,0:T(8,128)(2,1)S(1)}, u32[]{:S(2)}, u32[]{:S(2)}) collective-permute-start(bf16[4,2,2,16,128]{4,3,2,1,0:T(8,128)(2,1)S(1)} %collective-permute-done.5.refs_3_), channel_id=1, source_target_pairs={{0,4},{4,0},{8,12},{12,8},{16,20},{20,16},{24,28},{28,24},{1,5},{5... | collective-permute-start | bytes 196616 | tf_op jit(solution)/shard_map/ppermute | solution.py:485
  18.1 2.2 %collective-permute-start.7 = (bf16[4,2,2,16,128]{4,3,2,1,0:T(8,128)(2,1)S(1)}, bf16[4,2,2,16,128]{4,3,2,1,0:T(8,128)(2,1)S(1)}, u32[]{:S(2)}, u32[]{:S(2)}) collective-permute-start(bf16[4,2,2,16,128]{4,3,2,1,0:T(8,128)(2,1)S(1)} %collective-permute-done.4.refs_2_), channel_id=1, source_target_pairs={{0,4},{4,0},{8,12},{12,8},{16,20},{20,16},{24,28},{28,24},{1,5},{5... | collective-permute-start | bytes 196616 | tf_op jit(solution)/shard_map/ppermute | solution.py:485
  18.6 1.7 %collective-permute-start.8 = (bf16[4,2,2,16,128]{4,3,2,1,0:T(8,128)(2,1)S(1)}, bf16[4,2,2,16,128]{4,3,2,1,0:T(8,128)(2,1)S(1)}, u32[]{:S(2)}, u32[]{:S(2)}) collective-permute-start(bf16[4,2,2,16,128]{4,3,2,1,0:T(8,128)(2,1)S(1)} %collective-permute-done.3.refs_1_), channel_id=1, source_target_pairs={{0,4},{4,0},{8,12},{12,8},{16,20},{20,16},{24,28},{28,24},{1,5},{5... | collective-permute-start | bytes 196616 | tf_op jit(solution)/shard_map/ppermute | solution.py:485
  23.8 1.8 %collective-permute-start.10 = (bf16[4,4,2,2,16,128]{5,4,3,2,1,0:T(8,128)(2,1)S(1)}, bf16[4,4,2,2,16,128]{5,4,3,2,1,0:T(8,128)(2,1)S(1)}, u32[]{:S(2)}, u32[]{:S(2)}) collective-permute-start(bf16[4,4,2,2,16,128]{5,4,3,2,1,0:T(8,128)(2,1)S(1)} %get-tuple-element.48), channel_id=1, source_target_pairs={{0,4},{4,0},{8,12},{12,8},{16,20},{20,16},{24,28},{28,24},{1,5},{5... | collective-permute-start | bytes 786440 | tf_op jit(solution)/shard_map/ppermute | solution.py:485
  24.3 14.8 %copy-start.1 = (f32[16,2,8,128]{3,2,1,0:T(8,128)S(1)}, f32[16,2,8,128]{3,2,1,0:T(8,128)}, u32[]{:S(2)}) copy-start(f32[16,2,8,128]{3,2,1,0:T(8,128)} %refs_4_.1) | copy-start | bytes 393220
  24.3 14.8 %copy-start.2 = (f32[16,2,8,128]{3,2,1,0:T(8,128)S(1)}, f32[16,2,8,128]{3,2,1,0:T(8,128)}, u32[]{:S(2)}) copy-start(f32[16,2,8,128]{3,2,1,0:T(8,128)} %refs_5_.1) | copy-start | bytes 393220
  24.3 14.8 %copy-start.3 = (f32[16,2,8,128]{3,2,1,0:T(8,128)S(1)}, f32[16,2,8,128]{3,2,1,0:T(8,128)}, u32[]{:S(2)}) copy-start(f32[16,2,8,128]{3,2,1,0:T(8,128)} %refs_6_.1) | copy-start | bytes 393220
  25.7 5.3 %collective-permute-start.11 = (bf16[4,2,2,16,128]{4,3,2,1,0:T(8,128)(2,1)S(1)}, bf16[4,2,2,16,128]{4,3,2,1,0:T(8,128)(2,1)S(1)}, u32[]{:S(2)}, u32[]{:S(2)}) collective-permute-start(bf16[4,2,2,16,128]{4,3,2,1,0:T(8,128)(2,1)S(1)} %get-tuple-element.50), channel_id=1, source_target_pairs={{0,24},{4,28},{8,16},{12,20},{16,8},{20,12},{24,0},{28,4},{1,25},{... | collective-permute-start | bytes 196616 | tf_op jit(solution)/shard_map/ppermute | solution.py:485
  27.2 5.1 %collective-permute-start.12 = (bf16[4,2,2,16,128]{4,3,2,1,0:T(8,128)(2,1)S(1)}, bf16[4,2,2,16,128]{4,3,2,1,0:T(8,128)(2,1)S(1)}, u32[]{:S(2)}, u32[]{:S(2)}) collective-permute-start(bf16[4,2,2,16,128]{4,3,2,1,0:T(8,128)(2,1)S(1)} %get-tuple-element.51), channel_id=1, source_target_pairs={{0,16},{4,20},{8,24},{12,28},{16,0},{20,4},{24,8},{28,12},{1,17},{... | collective-permute-start | bytes 196616 | tf_op jit(solution)/shard_map/ppermute | solution.py:485
  27.7 4.6 %collective-permute-start.13 = (bf16[4,2,2,16,128]{4,3,2,1,0:T(8,128)(2,1)S(1)}, bf16[4,2,2,16,128]{4,3,2,1,0:T(8,128)(2,1)S(1)}, u32[]{:S(2)}, u32[]{:S(2)}) collective-permute-start(bf16[4,2,2,16,128]{4,3,2,1,0:T(8,128)(2,1)S(1)} %get-tuple-element.52), channel_id=1, source_target_pairs={{0,8},{4,12},{8,0},{12,4},{16,24},{20,28},{24,16},{28,20},{1,9},{5... | collective-permute-start | bytes 196616 | tf_op jit(solution)/shard_map/ppermute | solution.py:485
  32.4 5.6 %collective-permute-start.14 = (bf16[2,2,16,128]{3,2,1,0:T(8,128)(2,1)S(1)}, bf16[2,2,16,128]{3,2,1,0:T(8,128)(2,1)S(1)}, u32[]{:S(2)}, u32[]{:S(2)}) collective-permute-start(bf16[2,2,16,128]{3,2,1,0:T(8,128)(2,1)S(1)} %get-tuple-element.53), channel_id=1, source_target_pairs={{0,3},{1,2},{2,1},{3,0},{4,7},{5,6},{6,5},{7,4},{8,11},{9,10},{10,... | collective-permute-start | bytes 49160 | tf_op jit(solution)/shard_map/ppermute | solution.py:485
  34.5 4.6 %collective-permute-start.15 = (bf16[2,2,16,128]{3,2,1,0:T(8,128)(2,1)S(1)}, bf16[2,2,16,128]{3,2,1,0:T(8,128)(2,1)S(1)}, u32[]{:S(2)}, u32[]{:S(2)}) collective-permute-start(bf16[2,2,16,128]{3,2,1,0:T(8,128)(2,1)S(1)} %get-tuple-element.54), channel_id=1, source_target_pairs={{0,2},{1,3},{2,0},{3,1},{4,6},{5,7},{6,4},{7,5},{8,10},{9,11},{10,... | collective-permute-start | bytes 49160 | tf_op jit(solution)/shard_map/ppermute | solution.py:485
  34.5 4.6 %collective-permute-start.16 = (bf16[2,2,16,128]{3,2,1,0:T(8,128)(2,1)S(1)}, bf16[2,2,16,128]{3,2,1,0:T(8,128)(2,1)S(1)}, u32[]{:S(2)}, u32[]{:S(2)}) collective-permute-start(bf16[2,2,16,128]{3,2,1,0:T(8,128)(2,1)S(1)} %get-tuple-element.55), channel_id=1, source_target_pairs={{0,1},{1,0},{2,3},{3,2},{4,5},{5,4},{6,7},{7,6},{8,9},{9,8},{10,11... | collective-permute-start | bytes 49160 | tf_op jit(solution)/shard_map/ppermute | solution.py:485

commit v14 on v13

--- a/solution.py
+++ b/solution.py
@@ -492,6 +492,23 @@
     ]
 
 
+def chip_flips(chips, core):
+    far, *others, own = flips(chips)
+    return [far] + (others[::-1] if core else others) + [own]
+
+
+def chips_swap(values, dp_size):
+    chips = dp_size // 2
+    orders = [chip_flips(chips, core) for core in range(2)]
+    arrived = [
+        lax.ppermute(
+            value, "dp", [(place, place ^ (2 * orders[place % 2][j])) for place in range(dp_size)]
+        )
+        for j, value in enumerate(values[:-1])
+    ]
+    return arrived + [values[-1]]
+
+
 def per_device(
     dp_size, columns, queries, out_grad, self_lse, self_dot, cache, first_moment, second_moment
 ):
@@ -509,7 +526,7 @@
 
     slices = pack(cache, columns, own)
     gathered = jnp.stack(swap_all(slices, "cache", columns, 1, gather_flips))
-    pairs = swap_all([gathered] * chips, "dp", dp_size, 2)
+    pairs = chips_swap([gathered] * chips, dp_size)
     def tiles_of(array):
         parts = array.reshape((tokens, groups, group_size) + array.shape[2:])
         part = lax.dynamic_slice_in_dim(parts, first_token, own_tokens, 0)
@@ -530,7 +547,7 @@
     from_mate = swap(mate, "dp", dp_size, 1)
     mine = finish(kept, query_tiles, grad_tiles, inverse, delta, mate.shape, score_scale)
     by_chip = chip_sum(mine, from_mate)
-    *away, home = swap_all(by_chip, "dp", dp_size, 2)
+    *away, home = chips_swap(by_chip, dp_size)
     by_column = column_sum(home, away)
     parts = swap_all(by_column, "cache", columns, 1)
     return adam(parts, cache, first_moment, second_moment)

time: 40.3 us -> 40.5 us (level)
    ppermute x0 -> x6, starting transfers between devices: none -> 7.11 us  [chips_swap(): lax.ppermute(value, 'dp', [(place, place ^ 2 * orders[place % 2][j]) for...]
    ppermute x17 -> x11, starting transfers between devices: 17.9 us -> 11.2 us  [swap(): lax.ppermute(value, axis, [(place, place ^ flip) for place in range(size)])]
    ppermute x17 -> x11, waiting for transfers between devices: 9.57 us -> 4.28 us  [swap(): lax.ppermute(value, axis, [(place, place ^ flip) for place in range(size)])]
    ppermute x0 -> x6, waiting for transfers between devices: none -> 5.03 us  [chips_swap(): lax.ppermute(value, 'dp', [(place, place ^ 2 * orders[place % 2][j]) for...]
  transfers between devices with their start and end apart: 17 -> 17, of which waited for: 9 -> 8; matrix products, arithmetic and copies ran while one was open for 8% -> 8% of each run, Pallas kernels for 7% -> 7%
where the time goes in v14:
time: 40.5 us; the launch traced here: 40.1 us
  starting transfers between devices  18.3 us (45%)
  waiting for transfers between devices  9.31 us (23%)
  Pallas kernels  7.44 us (18%)
  local copies, waits for them, and re-layouts  4.31 us (11%)
  between operations  0.8 us (2%)
    ppermute x11, starting transfers between devices, swap(): lax.ppermute(value, axis, [(place, place ^ flip) for place in range(size)])  11.2 us
    ppermute x6, starting transfers between devices, chips_swap(): lax.ppermute(value, 'dp', [(place, place ^ 2 * orders[place % 2][j]) for...  7.11 us
    ppermute x6, waiting for transfers between devices, chips_swap(): lax.ppermute(value, 'dp', [(place, place ^ 2 * orders[place % 2][j]) for...  5.03 us
    ppermute x11, waiting for transfers between devices, swap(): lax.ppermute(value, axis, [(place, place ^ flip) for place in range(size)])  4.28 us
    pallas_call x1, Pallas kernels, second_half(): pl.pallas_call(functools.partial(second_half_kernel, score_scale, tiles /...  3.46 us
    dynamic_slice x2, local copies, waits for them, and re-layouts, tiles_of(): part = lax.dynamic_slice_in_dim(part, first_group, own, 1)  2.69 us
    pallas_call x1, Pallas kernels, first_half(): pl.pallas_call(functools.partial(first_half_kernel, score_scale, tiles //...  1.62 us
    unnamed x12, local copies, waits for them, and re-layouts  1.3 us
  transfers between devices with their start and end apart: 17, of which 8 were waited for; matrix products, arithmetic and copies ran while one was open for 8% of the time, Pallas kernels for 7%

profile of v14, /device:TPU:0, one launch (start us, length us, event | category | flops | bytes accessed | tf_op | source)
XLA Modules:
  0.0 40.1 jit_solution(17879375756484579073)
XLA Ops:
  0.6 0.0 copy-start
  0.6 0.9 %copy-done = f32[16,2,8,128]{3,2,1,0:T(8,128)S(1)} copy-done((f32[16,2,8,128]{3,2,1,0:T(8,128)S(1)}, f32[16,2,8,128]{3,2,1,0:T(8,128)}, u32[]{:S(2)}) %copy-start) | copy-done | bytes 131096
  1.5 0.1 pack.1
  1.7 4.1 %collective-permute-start = (bf16[2,2,16,128]{3,2,1,0:T(8,128)(2,1)S(1)}, bf16[2,2,16,128]{3,2,1,0:T(8,128)(2,1)S(1)}, u32[]{:S(2)}, u32[]{:S(2)}) collective-permute-start(bf16[2,2,16,128]{3,2,1,0:T(8,128)(2,1)S(1)} %get-tuple-element.30), channel_id=1, source_target_pairs={{0,2},{1,3},{2,0},{3,1},{4,6},{5,7},{6,4},{7,5},{8,10},{9,11},{10,... | collective-permute-start | bytes 49160 | tf_op jit(solution)/shard_map/ppermute | solution.py:485
  5.8 1.3 %collective-permute-start.1 = (bf16[2,2,16,128]{3,2,1,0:T(8,128)(2,1)S(1)}, bf16[2,2,16,128]{3,2,1,0:T(8,128)(2,1)S(1)}, u32[]{:S(2)}, u32[]{:S(2)}) collective-permute-start(bf16[2,2,16,128]{3,2,1,0:T(8,128)(2,1)S(1)} %get-tuple-element.31), channel_id=1, source_target_pairs={{0,3},{1,2},{2,1},{3,0},{4,7},{5,6},{6,5},{7,4},{8,11},{9,10},{10,... | collective-permute-start | bytes 49160 | tf_op jit(solution)/shard_map/ppermute | solution.py:485
  7.1 0.2 collective-permute-start.2
  7.4 2.0 %constant_dynamic-slice_fusion.2 = (bf16[256,2,8,128]{3,2,1,0:T(8,128)(2,1)S(1)}, bf16[256,2,8,128]{3,2,1,0:T(8,128)(2,1)S(1)}) fusion(bf16[256,8,8,128]{3,2,1,0:T(8,128)(2,1)} %bitcast.25, s32[]{:T(128)S(6)} %select_n.9, bf16[256,8,8,128]{3,2,1,0:T(8,128)(2,1)} %bitcast.26), kind=kLoop, calls=%fused_computation.3 | loop fusion | bytes 4194308 | tf_op jit(solution)/shard_map/dynamic_slice | solution.py:533
  9.3 0.0 collective-permute-done
  9.3 2.0 %collective-permute-done.1 = bf16[2,2,16,128]{3,2,1,0:T(8,128)(2,1)S(1)} collective-permute-done((bf16[2,2,16,128]{3,2,1,0:T(8,128)(2,1)S(1)}, bf16[2,2,16,128]{3,2,1,0:T(8,128)(2,1)S(1)}, u32[]{:S(2)}, u32[]{:S(2)}) %collective-permute-start.1) | collective-permute-done | bytes 16416 | tf_op jit(solution)/shard_map/ppermute | solution.py:485
  11.3 0.0 collective-permute-done.2
  11.3 2.5 %collective-permute-start.5 = (bf16[4,2,2,16,128]{4,3,2,1,0:T(8,128)(2,1)S(1)}, bf16[4,2,2,16,128]{4,3,2,1,0:T(8,128)(2,1)S(1)}, u32[]{:S(2)}, u32[]{:S(2)}) collective-permute-start(bf16[4,2,2,16,128]{4,3,2,1,0:T(8,128)(2,1)S(1)} %pad_maximum_fusion.refs_0_), channel_id=1, source_target_pairs={{0,24},{4,28},{8,16},{12,20},{16,8},{20,12},{24,0},{28,4},{1,25},{... | collective-permute-start | bytes 196616 | tf_op jit(solution)/shard_map/ppermute | solution.py:504
  13.9 0.5 %collective-permute-start.4 = (bf16[4,2,2,16,128]{4,3,2,1,0:T(8,128)(2,1)S(1)}, bf16[4,2,2,16,128]{4,3,2,1,0:T(8,128)(2,1)S(1)}, u32[]{:S(2)}, u32[]{:S(2)}) collective-permute-start(bf16[4,2,2,16,128]{4,3,2,1,0:T(8,128)(2,1)S(1)} %pad_maximum_fusion.refs_0_), channel_id=1, source_target_pairs={{0,16},{4,12},{8,24},{12,4},{16,0},{20,28},{24,8},{28,20},{1,17},{... | collective-permute-start | bytes 196616 | tf_op jit(solution)/shard_map/ppermute | solution.py:504
  14.4 0.5 %collective-permute-start.3 = (bf16[4,2,2,16,128]{4,3,2,1,0:T(8,128)(2,1)S(1)}, bf16[4,2,2,16,128]{4,3,2,1,0:T(8,128)(2,1)S(1)}, u32[]{:S(2)}, u32[]{:S(2)}) collective-permute-start(bf16[4,2,2,16,128]{4,3,2,1,0:T(8,128)(2,1)S(1)} %pad_maximum_fusion.refs_0_), channel_id=1, source_target_pairs={{0,8},{4,20},{8,0},{12,28},{16,24},{20,4},{24,16},{28,12},{1,9},{5... | collective-permute-start | bytes 196616 | tf_op jit(solution)/shard_map/ppermute | solution.py:504
  14.9 0.7 %constant_dynamic-slice_fusion = (f32[256,2,8]{0,2,1:T(8,128)S(1)}, f32[256,2,8]{0,2,1:T(8,128)S(1)}) fusion(f32[256,8,8]{0,2,1:T(8,128)} %bitcast.30, s32[]{:T(128)S(6)} %select_n.9, f32[256,8,8]{0,2,1:T(8,128)} %bitcast.31), kind=kLoop, calls=%fused_computation.1 | loop fusion | bytes 65540 | tf_op jit(solution)/shard_map/dynamic_slice | solution.py:533
  15.6 0.1 copy.21
  15.8 0.2 reshape.37.refs_7_
  15.9 0.1 copy.20
  16.1 0.2 reshape.35.refs_6_
  16.2 0.1 copy.19
  16.3 0.1 copy.18
  16.4 0.1 collective-permute-start.9
  16.5 0.1 collective-permute-done.5.refs_3_
  16.6 0.4 collective-permute-start.6
  17.0 1.2 %collective-permute-done.4.refs_2_ = bf16[4,2,2,16,128]{4,3,2,1,0:T(8,128)(2,1)S(1)} collective-permute-done((bf16[4,2,2,16,128]{4,3,2,1,0:T(8,128)(2,1)S(1)}, bf16[4,2,2,16,128]{4,3,2,1,0:T(8,128)(2,1)S(1)}, u32[]{:S(2)}, u32[]{:S(2)}) %collective-permute-start.4) | collective-permute-done | bytes 65568 | tf_op jit(solution)/shard_map/ppermute | solution.py:504
  18.1 0.0 collective-permute-start.7
  18.1 0.5 %collective-permute-done.3.refs_1_ = bf16[4,2,2,16,128]{4,3,2,1,0:T(8,128)(2,1)S(1)} collective-permute-done((bf16[4,2,2,16,128]{4,3,2,1,0:T(8,128)(2,1)S(1)}, bf16[4,2,2,16,128]{4,3,2,1,0:T(8,128)(2,1)S(1)}, u32[]{:S(2)}, u32[]{:S(2)}) %collective-permute-start.3) | collective-permute-done | bytes 65568 | tf_op jit(solution)/shard_map/ppermute | solution.py:504
  18.6 0.0 collective-permute-start.8
  18.6 1.6 %first_half.1 = (f32[8,256,256]{2,1,0:T(8,128)S(1)}, f32[8,256,256]{2,1,0:T(8,128)S(1)}, f32[8,256,256]{2,1,0:T(8,128)S(1)}, f32[8,256,256]{2,1,0:T(8,128)S(1)},...) custom-call(bf16[4,2,2,16,128]{4,3,2,1,0:T(8,128)(2,1)S(1)} %pad_maximum_fusion.refs_0_, ...), custom_call_target="tpu_custom_call" | custom-call | flops 536870912 | bytes 8388608 | tf_op jit(solution)/shard_map/first_half/pallas_call | solution.py:213
  20.3 0.0 collective-permute-done.9.refs_3_
  20.3 0.0 collective-permute-done.6.refs_0_
  20.3 0.0 collective-permute-done.7.refs_1_
  20.3 0.0 collective-permute-done.8.refs_2_
  20.3 3.5 %second_half.1 = (bf16[4,4,2,2,16,128]{5,4,3,2,1,0:T(8,128)(2,1)S(1)}, f32[16,1,256]{2,1,0:T(1,128)S(1)}, f32[16,1,256]{2,1,0:T(1,128)S(1)}) custom-call(bf16[4,2,2,16,128]{4,3,2,1,0:T(8,128)(2,1)S(1)} %collective-permute-done.6.refs_0_, bf16[4,2,2,16,128]{4,3,2,1,0:T(8,128)(2,1)S(1)} %collective-permute-done.7.refs_1_, ...), custom_call_target="tpu_custom_call" | custom-call | flops 1073741824 | bytes 2097152 | tf_op jit(solution)/shard_map/second_half/pallas_call | solution.py:309
  23.8 0.6 %collective-permute-start.10 = (bf16[4,4,2,2,16,128]{5,4,3,2,1,0:T(8,128)(2,1)S(1)}, bf16[4,4,2,2,16,128]{5,4,3,2,1,0:T(8,128)(2,1)S(1)}, u32[]{:S(2)}, u32[]{:S(2)}) collective-permute-start(bf16[4,4,2,2,16,128]{5,4,3,2,1,0:T(8,128)(2,1)S(1)} %get-tuple-element.48), channel_id=1, source_target_pairs={{0,4},{4,0},{8,12},{12,8},{16,20},{20,16},{24,28},{28,24},{1,5},{5... | collective-permute-start | bytes 786440 | tf_op jit(solution)/shard_map/ppermute | solution.py:485
  24.3 0.0 copy-start.1
  24.3 0.0 copy-start.2
  24.3 0.0 copy-start.3
  24.3 1.2 %finish.1.mine_ref = f32[4,4,2,2,16,128]{5,4,3,2,1,0:T(8,128)S(1)} custom-call(f32[8,256,256]{2,1,0:T(8,128)S(1)} %get-tuple-element.38.refs_0_, f32[8,256,256]{2,1,0:T(8,128)S(1)} %get-tuple-element.39.refs_1_, f32[8,256,256]{2,1,0:T(8,128)S(1)} %get-tuple-element.40.refs_2_, f32[8,256,256]{2,1,0:T(8,128)S(1)} %get-tuple-element.41.refs_3_, ...), custom_call_target="tpu_custom_call" | custom-call | flops 536870912 | bytes 8388608 | tf_op jit(solution)/shard_map/finish/pallas_call | solution.py:380
  25.6 0.0 collective-permute-done.10.mate_ref
  25.7 1.6 %collective-permute-start.11 = (bf16[4,2,2,16,128]{4,3,2,1,0:T(8,128)(2,1)S(1)}, bf16[4,2,2,16,128]{4,3,2,1,0:T(8,128)(2,1)S(1)}, u32[]{:S(2)}, u32[]{:S(2)}) collective-permute-start(bf16[4,2,2,16,128]{4,3,2,1,0:T(8,128)(2,1)S(1)} %get-tuple-element.50), channel_id=1, source_target_pairs={{0,24},{4,28},{8,16},{12,20},{16,8},{20,12},{24,0},{28,4},{1,25},{... | collective-permute-start | bytes 196616 | tf_op jit(solution)/shard_map/ppermute | solution.py:504
  27.2 0.5 %collective-permute-start.12 = (bf16[4,2,2,16,128]{4,3,2,1,0:T(8,128)(2,1)S(1)}, bf16[4,2,2,16,128]{4,3,2,1,0:T(8,128)(2,1)S(1)}, u32[]{:S(2)}, u32[]{:S(2)}) collective-permute-start(bf16[4,2,2,16,128]{4,3,2,1,0:T(8,128)(2,1)S(1)} %get-tuple-element.51), channel_id=1, source_target_pairs={{0,16},{4,12},{8,24},{12,4},{16,0},{20,28},{24,8},{28,20},{1,17},{... | collective-permute-start | bytes 196616 | tf_op jit(solution)/shard_map/ppermute | solution.py:504
  27.7 1.5 %collective-permute-start.13 = (bf16[4,2,2,16,128]{4,3,2,1,0:T(8,128)(2,1)S(1)}, bf16[4,2,2,16,128]{4,3,2,1,0:T(8,128)(2,1)S(1)}, u32[]{:S(2)}, u32[]{:S(2)}) collective-permute-start(bf16[4,2,2,16,128]{4,3,2,1,0:T(8,128)(2,1)S(1)} %get-tuple-element.52), channel_id=1, source_target_pairs={{0,8},{4,20},{8,0},{12,28},{16,24},{20,4},{24,16},{28,12},{1,9},{5... | collective-permute-start | bytes 196616 | tf_op jit(solution)/shard_map/ppermute | solution.py:504
  29.2 2.3 %collective-permute-done.11.refs_0_ = bf16[4,2,2,16,128]{4,3,2,1,0:T(8,128)(2,1)S(1)} collective-permute-done((bf16[4,2,2,16,128]{4,3,2,1,0:T(8,128)(2,1)S(1)}, bf16[4,2,2,16,128]{4,3,2,1,0:T(8,128)(2,1)S(1)}, u32[]{:S(2)}, u32[]{:S(2)}) %collective-permute-start.11) | collective-permute-done | bytes 65568 | tf_op jit(solution)/shard_map/ppermute | solution.py:504
  31.5 0.9 %collective-permute-done.12.refs_1_ = bf16[4,2,2,16,128]{4,3,2,1,0:T(8,128)(2,1)S(1)} collective-permute-done((bf16[4,2,2,16,128]{4,3,2,1,0:T(8,128)(2,1)S(1)}, bf16[4,2,2,16,128]{4,3,2,1,0:T(8,128)(2,1)S(1)}, u32[]{:S(2)}, u32[]{:S(2)}) %collective-permute-start.12) | collective-permute-done | bytes 65568 | tf_op jit(solution)/shard_map/ppermute | solution.py:504
  32.5 0.0 collective-permute-done.13.refs_2_
  32.5 2.1 %collective-permute-start.14 = (bf16[2,2,16,128]{3,2,1,0:T(8,128)(2,1)S(1)}, bf16[2,2,16,128]{3,2,1,0:T(8,128)(2,1)S(1)}, u32[]{:S(2)}, u32[]{:S(2)}) collective-permute-start(bf16[2,2,16,128]{3,2,1,0:T(8,128)(2,1)S(1)} %get-tuple-element.53), channel_id=1, source_target_pairs={{0,3},{1,2},{2,1},{3,0},{4,7},{5,6},{6,5},{7,4},{8,11},{9,10},{10,... | collective-permute-start | bytes 49160 | tf_op jit(solution)/shard_map/ppermute | solution.py:485
  34.6 0.0 collective-permute-start.15
  34.6 2.4 %collective-permute-start.16 = (bf16[2,2,16,128]{3,2,1,0:T(8,128)(2,1)S(1)}, bf16[2,2,16,128]{3,2,1,0:T(8,128)(2,1)S(1)}, u32[]{:S(2)}, u32[]{:S(2)}) collective-permute-start(bf16[2,2,16,128]{3,2,1,0:T(8,128)(2,1)S(1)} %get-tuple-element.55), channel_id=1, source_target_pairs={{0,1},{1,0},{2,3},{3,2},{4,5},{5,4},{6,7},{7,6},{8,9},{9,8},{10,11... | collective-permute-start | bytes 49160 | tf_op jit(solution)/shard_map/ppermute | solution.py:485
  36.9 1.2 %collective-permute-done.14.refs_0_ = bf16[2,2,16,128]{3,2,1,0:T(8,128)(2,1)S(1)} collective-permute-done((bf16[2,2,16,128]{3,2,1,0:T(8,128)(2,1)S(1)}, bf16[2,2,16,128]{3,2,1,0:T(8,128)(2,1)S(1)}, u32[]{:S(2)}, u32[]{:S(2)}) %collective-permute-start.14) | collective-permute-done | bytes 16416 | tf_op jit(solution)/shard_map/ppermute | solution.py:485
  38.2 1.0 %collective-permute-done.15.refs_1_ = bf16[2,2,16,128]{3,2,1,0:T(8,128)(2,1)S(1)} collective-permute-done((bf16[2,2,16,128]{3,2,1,0:T(8,128)(2,1)S(1)}, bf16[2,2,16,128]{3,2,1,0:T(8,128)(2,1)S(1)}, u32[]{:S(2)}, u32[]{:S(2)}) %collective-permute-start.15) | collective-permute-done | bytes 16416 | tf_op jit(solution)/shard_map/ppermute | solution.py:485
  39.2 0.0 collective-permute-done.16.refs_2_
  39.2 0.0 copy-done.1
  39.2 0.0 copy-done.2
  39.2 0.0 copy-done.3
  39.2 0.9 %adam.1 = (f32[16,2,8,128]{3,2,1,0:T(8,128)}, f32[16,2,8,128]{3,2,1,0:T(8,128)}, f32[16,2,8,128]{3,2,1,0:T(8,128)}) custom-call(bf16[2,2,16,128]{3,2,1,0:T(8,128)(2,1)S(1)} %collective-permute-done.14.refs_0_, bf16[2,2,16,128]{3,2,1,0:T(8,128)(2,1)S(1)} %collective-permute-done.15.refs_1_, bf16[2,2,16,128]{3,2,1,0:T(8,128)(2,1)S(1)} %collective-permute-done.16.refs_2_, ...), custom_call_target="tpu_custom_call" | custom-call | tf_op jit(solution)/shard_map/adam/pallas_call | solution.py:472
  (3 shorter events, 0.1 us)
Async XLA Ops:
  0.6 0.9 %copy-start = (f32[16,2,8,128]{3,2,1,0:T(8,128)S(1)}, f32[16,2,8,128]{3,2,1,0:T(8,128)}, u32[]{:S(2)}) copy-start(f32[16,2,8,128]{3,2,1,0:T(8,128)} %refs_4_.1) | copy-start | bytes 393220
  1.7 7.6 %collective-permute-start = (bf16[2,2,16,128]{3,2,1,0:T(8,128)(2,1)S(1)}, bf16[2,2,16,128]{3,2,1,0:T(8,128)(2,1)S(1)}, u32[]{:S(2)}, u32[]{:S(2)}) collective-permute-start(bf16[2,2,16,128]{3,2,1,0:T(8,128)(2,1)S(1)} %get-tuple-element.30), channel_id=1, source_target_pairs={{0,2},{1,3},{2,0},{3,1},{4,6},{5,7},{6,4},{7,5},{8,10},{9,11},{10,... | collective-permute-start | bytes 49160 | tf_op jit(solution)/shard_map/ppermute | solution.py:485
  5.8 5.5 %collective-permute-start.1 = (bf16[2,2,16,128]{3,2,1,0:T(8,128)(2,1)S(1)}, bf16[2,2,16,128]{3,2,1,0:T(8,128)(2,1)S(1)}, u32[]{:S(2)}, u32[]{:S(2)}) collective-permute-start(bf16[2,2,16,128]{3,2,1,0:T(8,128)(2,1)S(1)} %get-tuple-element.31), channel_id=1, source_target_pairs={{0,3},{1,2},{2,1},{3,0},{4,7},{5,6},{6,5},{7,4},{8,11},{9,10},{10,... | collective-permute-start | bytes 49160 | tf_op jit(solution)/shard_map/ppermute | solution.py:485
  7.1 4.2 %collective-permute-start.2 = (bf16[2,2,16,128]{3,2,1,0:T(8,128)(2,1)S(1)}, bf16[2,2,16,128]{3,2,1,0:T(8,128)(2,1)S(1)}, u32[]{:S(2)}, u32[]{:S(2)}) collective-permute-start(bf16[2,2,16,128]{3,2,1,0:T(8,128)(2,1)S(1)} %get-tuple-element.32), channel_id=1, source_target_pairs={{0,1},{1,0},{2,3},{3,2},{4,5},{5,4},{6,7},{7,6},{8,9},{9,8},{10,11... | collective-permute-start | bytes 49160 | tf_op jit(solution)/shard_map/ppermute | solution.py:485
  11.3 5.2 %collective-permute-start.5 = (bf16[4,2,2,16,128]{4,3,2,1,0:T(8,128)(2,1)S(1)}, bf16[4,2,2,16,128]{4,3,2,1,0:T(8,128)(2,1)S(1)}, u32[]{:S(2)}, u32[]{:S(2)}) collective-permute-start(bf16[4,2,2,16,128]{4,3,2,1,0:T(8,128)(2,1)S(1)} %pad_maximum_fusion.refs_0_), channel_id=1, source_target_pairs={{0,24},{4,28},{8,16},{12,20},{16,8},{20,12},{24,0},{28,4},{1,25},{... | collective-permute-start | bytes 196616 | tf_op jit(solution)/shard_map/ppermute | solution.py:504
  13.9 4.3 %collective-permute-start.4 = (bf16[4,2,2,16,128]{4,3,2,1,0:T(8,128)(2,1)S(1)}, bf16[4,2,2,16,128]{4,3,2,1,0:T(8,128)(2,1)S(1)}, u32[]{:S(2)}, u32[]{:S(2)}) collective-permute-start(bf16[4,2,2,16,128]{4,3,2,1,0:T(8,128)(2,1)S(1)} %pad_maximum_fusion.refs_0_), channel_id=1, source_target_pairs={{0,16},{4,12},{8,24},{12,4},{16,0},{20,28},{24,8},{28,20},{1,17},{... | collective-permute-start | bytes 196616 | tf_op jit(solution)/shard_map/ppermute | solution.py:504
  14.4 4.3 %collective-permute-start.3 = (bf16[4,2,2,16,128]{4,3,2,1,0:T(8,128)(2,1)S(1)}, bf16[4,2,2,16,128]{4,3,2,1,0:T(8,128)(2,1)S(1)}, u32[]{:S(2)}, u32[]{:S(2)}) collective-permute-start(bf16[4,2,2,16,128]{4,3,2,1,0:T(8,128)(2,1)S(1)} %pad_maximum_fusion.refs_0_), channel_id=1, source_target_pairs={{0,8},{4,20},{8,0},{12,28},{16,24},{20,4},{24,16},{28,12},{1,9},{5... | collective-permute-start | bytes 196616 | tf_op jit(solution)/shard_map/ppermute | solution.py:504
  16.4 3.9 %collective-permute-start.9 = (bf16[4,2,2,16,128]{4,3,2,1,0:T(8,128)(2,1)S(1)}, bf16[4,2,2,16,128]{4,3,2,1,0:T(8,128)(2,1)S(1)}, u32[]{:S(2)}, u32[]{:S(2)}) collective-permute-start(bf16[4,2,2,16,128]{4,3,2,1,0:T(8,128)(2,1)S(1)} %pad_maximum_fusion.refs_0_), channel_id=1, source_target_pairs={{0,4},{4,0},{8,12},{12,8},{16,20},{20,16},{24,28},{28,24},{1,5},{5... | collective-permute-start | bytes 196616 | tf_op jit(solution)/shard_map/ppermute | solution.py:485
  16.6 3.7 %collective-permute-start.6 = (bf16[4,2,2,16,128]{4,3,2,1,0:T(8,128)(2,1)S(1)}, bf16[4,2,2,16,128]{4,3,2,1,0:T(8,128)(2,1)S(1)}, u32[]{:S(2)}, u32[]{:S(2)}) collective-permute-start(bf16[4,2,2,16,128]{4,3,2,1,0:T(8,128)(2,1)S(1)} %collective-permute-done.5.refs_3_), channel_id=1, source_target_pairs={{0,4},{4,0},{8,12},{12,8},{16,20},{20,16},{24,28},{28,24},{1,5},{5... | collective-permute-start | bytes 196616 | tf_op jit(solution)/shard_map/ppermute | solution.py:485
  18.1 2.2 %collective-permute-start.7 = (bf16[4,2,2,16,128]{4,3,2,1,0:T(8,128)(2,1)S(1)}, bf16[4,2,2,16,128]{4,3,2,1,0:T(8,128)(2,1)S(1)}, u32[]{:S(2)}, u32[]{:S(2)}) collective-permute-start(bf16[4,2,2,16,128]{4,3,2,1,0:T(8,128)(2,1)S(1)} %collective-permute-done.4.refs_2_), channel_id=1, source_target_pairs={{0,4},{4,0},{8,12},{12,8},{16,20},{20,16},{24,28},{28,24},{1,5},{5... | collective-permute-start | bytes 196616 | tf_op jit(solution)/shard_map/ppermute | solution.py:485
  18.6 1.7 %collective-permute-start.8 = (bf16[4,2,2,16,128]{4,3,2,1,0:T(8,128)(2,1)S(1)}, bf16[4,2,2,16,128]{4,3,2,1,0:T(8,128)(2,1)S(1)}, u32[]{:S(2)}, u32[]{:S(2)}) collective-permute-start(bf16[4,2,2,16,128]{4,3,2,1,0:T(8,128)(2,1)S(1)} %collective-permute-done.3.refs_1_), channel_id=1, source_target_pairs={{0,4},{4,0},{8,12},{12,8},{16,20},{20,16},{24,28},{28,24},{1,5},{5... | collective-permute-start | bytes 196616 | tf_op jit(solution)/shard_map/ppermute | solution.py:485
  23.8 1.8 %collective-permute-start.10 = (bf16[4,4,2,2,16,128]{5,4,3,2,1,0:T(8,128)(2,1)S(1)}, bf16[4,4,2,2,16,128]{5,4,3,2,1,0:T(8,128)(2,1)S(1)}, u32[]{:S(2)}, u32[]{:S(2)}) collective-permute-start(bf16[4,4,2,2,16,128]{5,4,3,2,1,0:T(8,128)(2,1)S(1)} %get-tuple-element.48), channel_id=1, source_target_pairs={{0,4},{4,0},{8,12},{12,8},{16,20},{20,16},{24,28},{28,24},{1,5},{5... | collective-permute-start | bytes 786440 | tf_op jit(solution)/shard_map/ppermute | solution.py:485
  24.3 14.9 %copy-start.1 = (f32[16,2,8,128]{3,2,1,0:T(8,128)S(1)}, f32[16,2,8,128]{3,2,1,0:T(8,128)}, u32[]{:S(2)}) copy-start(f32[16,2,8,128]{3,2,1,0:T(8,128)} %refs_4_.1) | copy-start | bytes 393220
  24.3 14.9 %copy-start.2 = (f32[16,2,8,128]{3,2,1,0:T(8,128)S(1)}, f32[16,2,8,128]{3,2,1,0:T(8,128)}, u32[]{:S(2)}) copy-start(f32[16,2,8,128]{3,2,1,0:T(8,128)} %refs_5_.1) | copy-start | bytes 393220
  24.3 14.9 %copy-start.3 = (f32[16,2,8,128]{3,2,1,0:T(8,128)S(1)}, f32[16,2,8,128]{3,2,1,0:T(8,128)}, u32[]{:S(2)}) copy-start(f32[16,2,8,128]{3,2,1,0:T(8,128)} %refs_6_.1) | copy-start | bytes 393220
  25.7 5.9 %collective-permute-start.11 = (bf16[4,2,2,16,128]{4,3,2,1,0:T(8,128)(2,1)S(1)}, bf16[4,2,2,16,128]{4,3,2,1,0:T(8,128)(2,1)S(1)}, u32[]{:S(2)}, u32[]{:S(2)}) collective-permute-start(bf16[4,2,2,16,128]{4,3,2,1,0:T(8,128)(2,1)S(1)} %get-tuple-element.50), channel_id=1, source_target_pairs={{0,24},{4,28},{8,16},{12,20},{16,8},{20,12},{24,0},{28,4},{1,25},{... | collective-permute-start | bytes 196616 | tf_op jit(solution)/shard_map/ppermute | solution.py:504
  27.2 5.2 %collective-permute-start.12 = (bf16[4,2,2,16,128]{4,3,2,1,0:T(8,128)(2,1)S(1)}, bf16[4,2,2,16,128]{4,3,2,1,0:T(8,128)(2,1)S(1)}, u32[]{:S(2)}, u32[]{:S(2)}) collective-permute-start(bf16[4,2,2,16,128]{4,3,2,1,0:T(8,128)(2,1)S(1)} %get-tuple-element.51), channel_id=1, source_target_pairs={{0,16},{4,12},{8,24},{12,4},{16,0},{20,28},{24,8},{28,20},{1,17},{... | collective-permute-start | bytes 196616 | tf_op jit(solution)/shard_map/ppermute | solution.py:504
  27.7 4.7 %collective-permute-start.13 = (bf16[4,2,2,16,128]{4,3,2,1,0:T(8,128)(2,1)S(1)}, bf16[4,2,2,16,128]{4,3,2,1,0:T(8,128)(2,1)S(1)}, u32[]{:S(2)}, u32[]{:S(2)}) collective-permute-start(bf16[4,2,2,16,128]{4,3,2,1,0:T(8,128)(2,1)S(1)} %get-tuple-element.52), channel_id=1, source_target_pairs={{0,8},{4,20},{8,0},{12,28},{16,24},{20,4},{24,16},{28,12},{1,9},{5... | collective-permute-start | bytes 196616 | tf_op jit(solution)/shard_map/ppermute | solution.py:504
  32.5 5.7 %collective-permute-start.14 = (bf16[2,2,16,128]{3,2,1,0:T(8,128)(2,1)S(1)}, bf16[2,2,16,128]{3,2,1,0:T(8,128)(2,1)S(1)}, u32[]{:S(2)}, u32[]{:S(2)}) collective-permute-start(bf16[2,2,16,128]{3,2,1,0:T(8,128)(2,1)S(1)} %get-tuple-element.53), channel_id=1, source_target_pairs={{0,3},{1,2},{2,1},{3,0},{4,7},{5,6},{6,5},{7,4},{8,11},{9,10},{10,... | collective-permute-start | bytes 49160 | tf_op jit(solution)/shard_map/ppermute | solution.py:485
  34.6 4.6 %collective-permute-start.15 = (bf16[2,2,16,128]{3,2,1,0:T(8,128)(2,1)S(1)}, bf16[2,2,16,128]{3,2,1,0:T(8,128)(2,1)S(1)}, u32[]{:S(2)}, u32[]{:S(2)}) collective-permute-start(bf16[2,2,16,128]{3,2,1,0:T(8,128)(2,1)S(1)} %get-tuple-element.54), channel_id=1, source_target_pairs={{0,2},{1,3},{2,0},{3,1},{4,6},{5,7},{6,4},{7,5},{8,10},{9,11},{10,... | collective-permute-start | bytes 49160 | tf_op jit(solution)/shard_map/ppermute | solution.py:485
  34.6 4.6 %collective-permute-start.16 = (bf16[2,2,16,128]{3,2,1,0:T(8,128)(2,1)S(1)}, bf16[2,2,16,128]{3,2,1,0:T(8,128)(2,1)S(1)}, u32[]{:S(2)}, u32[]{:S(2)}) collective-permute-start(bf16[2,2,16,128]{3,2,1,0:T(8,128)(2,1)S(1)} %get-tuple-element.55), channel_id=1, source_target_pairs={{0,1},{1,0},{2,3},{3,2},{4,5},{5,4},{6,7},{7,6},{8,9},{9,8},{10,11... | collective-permute-start | bytes 49160 | tf_op jit(solution)/shard_map/ppermute | solution.py:485

commit v15 on v13

--- a/solution.py
+++ b/solution.py
@@ -16,7 +16,7 @@
 epsilon = 1e-08
 
 ROW_TILE = 256
-CHUNK = 32
+CHUNK = 16
 DOT_ROWS = 256
 MIB = 1024 * 1024
 

time: 40.3 us -> 40.3 us (level)
  no operation moved by 1% of the time
where the time goes in v15:
time: 40.3 us; the launch traced here: 40 us
  starting transfers between devices  17.9 us (44%)
  waiting for transfers between devices  9.56 us (24%)
  Pallas kernels  7.41 us (18%)
  local copies, waits for them, and re-layouts  4.31 us (11%)
  between operations  0.79 us (2%)
    ppermute x17, starting transfers between devices, swap(): lax.ppermute(value, axis, [(place, place ^ flip) for place in range(size)])  17.9 us
    ppermute x17, waiting for transfers between devices, swap(): lax.ppermute(value, axis, [(place, place ^ flip) for place in range(size)])  9.56 us
    pallas_call x1, Pallas kernels, second_half(): pl.pallas_call(functools.partial(second_half_kernel, score_scale, tiles /...  3.44 us
    dynamic_slice x2, local copies, waits for them, and re-layouts, tiles_of(): part = lax.dynamic_slice_in_dim(part, first_group, own, 1)  2.69 us
    pallas_call x1, Pallas kernels, first_half(): pl.pallas_call(functools.partial(first_half_kernel, score_scale, tiles //...  1.61 us
    unnamed x12, local copies, waits for them, and re-layouts  1.3 us
    pallas_call x1, Pallas kernels, finish(): pl.pallas_call(functools.partial(finish_kernel, score_scale, tiles // own...  1.25 us
    pallas_call x1, Pallas kernels, adam(): pl.pallas_call(functools.partial(adam_kernel, len(parts)), out_shape=(sha...  0.89 us
  transfers between devices with their start and end apart: 17, of which 9 were waited for; matrix products, arithmetic and copies ran while one was open for 8% of the time, Pallas kernels for 7%

profile of v15, /device:TPU:0, one launch (start us, length us, event | category | flops | bytes accessed | tf_op | source)
XLA Modules:
  0.0 40.0 jit_solution(15140144501374679683)
XLA Ops:
  0.6 0.0 copy-start
  0.6 0.9 %copy-done = f32[16,2,8,128]{3,2,1,0:T(8,128)S(1)} copy-done((f32[16,2,8,128]{3,2,1,0:T(8,128)S(1)}, f32[16,2,8,128]{3,2,1,0:T(8,128)}, u32[]{:S(2)}) %copy-start) | copy-done | bytes 131096
  1.5 0.1 pack.1
  1.7 4.1 %collective-permute-start = (bf16[2,2,16,128]{3,2,1,0:T(8,128)(2,1)S(1)}, bf16[2,2,16,128]{3,2,1,0:T(8,128)(2,1)S(1)}, u32[]{:S(2)}, u32[]{:S(2)}) collective-permute-start(bf16[2,2,16,128]{3,2,1,0:T(8,128)(2,1)S(1)} %get-tuple-element.30), channel_id=1, source_target_pairs={{0,2},{1,3},{2,0},{3,1},{4,6},{5,7},{6,4},{7,5},{8,10},{9,11},{10,... | collective-permute-start | bytes 49160 | tf_op jit(solution)/shard_map/ppermute | solution.py:485
  5.8 1.3 %collective-permute-start.1 = (bf16[2,2,16,128]{3,2,1,0:T(8,128)(2,1)S(1)}, bf16[2,2,16,128]{3,2,1,0:T(8,128)(2,1)S(1)}, u32[]{:S(2)}, u32[]{:S(2)}) collective-permute-start(bf16[2,2,16,128]{3,2,1,0:T(8,128)(2,1)S(1)} %get-tuple-element.31), channel_id=1, source_target_pairs={{0,3},{1,2},{2,1},{3,0},{4,7},{5,6},{6,5},{7,4},{8,11},{9,10},{10,... | collective-permute-start | bytes 49160 | tf_op jit(solution)/shard_map/ppermute | solution.py:485
  7.1 0.2 collective-permute-start.2
  7.4 2.0 %constant_dynamic-slice_fusion.2 = (bf16[256,2,8,128]{3,2,1,0:T(8,128)(2,1)S(1)}, bf16[256,2,8,128]{3,2,1,0:T(8,128)(2,1)S(1)}) fusion(bf16[256,8,8,128]{3,2,1,0:T(8,128)(2,1)} %bitcast.25, s32[]{:T(128)S(6)} %select_n.9, bf16[256,8,8,128]{3,2,1,0:T(8,128)(2,1)} %bitcast.26), kind=kLoop, calls=%fused_computation.3 | loop fusion | bytes 4194308 | tf_op jit(solution)/shard_map/dynamic_slice | solution.py:516
  9.3 0.0 collective-permute-done
  9.3 2.0 %collective-permute-done.1 = bf16[2,2,16,128]{3,2,1,0:T(8,128)(2,1)S(1)} collective-permute-done((bf16[2,2,16,128]{3,2,1,0:T(8,128)(2,1)S(1)}, bf16[2,2,16,128]{3,2,1,0:T(8,128)(2,1)S(1)}, u32[]{:S(2)}, u32[]{:S(2)}) %collective-permute-start.1) | collective-permute-done | bytes 16416 | tf_op jit(solution)/shard_map/ppermute | solution.py:485
  11.3 0.0 collective-permute-done.2
  11.3 2.5 %collective-permute-start.5 = (bf16[4,2,2,16,128]{4,3,2,1,0:T(8,128)(2,1)S(1)}, bf16[4,2,2,16,128]{4,3,2,1,0:T(8,128)(2,1)S(1)}, u32[]{:S(2)}, u32[]{:S(2)}) collective-permute-start(bf16[4,2,2,16,128]{4,3,2,1,0:T(8,128)(2,1)S(1)} %pad_maximum_fusion.refs_0_), channel_id=1, source_target_pairs={{0,24},{4,28},{8,16},{12,20},{16,8},{20,12},{24,0},{28,4},{1,25},{... | collective-permute-start | bytes 196616 | tf_op jit(solution)/shard_map/ppermute | solution.py:485
  13.9 0.5 %collective-permute-start.4 = (bf16[4,2,2,16,128]{4,3,2,1,0:T(8,128)(2,1)S(1)}, bf16[4,2,2,16,128]{4,3,2,1,0:T(8,128)(2,1)S(1)}, u32[]{:S(2)}, u32[]{:S(2)}) collective-permute-start(bf16[4,2,2,16,128]{4,3,2,1,0:T(8,128)(2,1)S(1)} %pad_maximum_fusion.refs_0_), channel_id=1, source_target_pairs={{0,16},{4,20},{8,24},{12,28},{16,0},{20,4},{24,8},{28,12},{1,17},{... | collective-permute-start | bytes 196616 | tf_op jit(solution)/shard_map/ppermute | solution.py:485
  14.4 0.5 %collective-permute-start.3 = (bf16[4,2,2,16,128]{4,3,2,1,0:T(8,128)(2,1)S(1)}, bf16[4,2,2,16,128]{4,3,2,1,0:T(8,128)(2,1)S(1)}, u32[]{:S(2)}, u32[]{:S(2)}) collective-permute-start(bf16[4,2,2,16,128]{4,3,2,1,0:T(8,128)(2,1)S(1)} %pad_maximum_fusion.refs_0_), channel_id=1, source_target_pairs={{0,8},{4,12},{8,0},{12,4},{16,24},{20,28},{24,16},{28,20},{1,9},{5... | collective-permute-start | bytes 196616 | tf_op jit(solution)/shard_map/ppermute | solution.py:485
  14.9 0.7 %constant_dynamic-slice_fusion = (f32[256,2,8]{0,2,1:T(8,128)S(1)}, f32[256,2,8]{0,2,1:T(8,128)S(1)}) fusion(f32[256,8,8]{0,2,1:T(8,128)} %bitcast.30, s32[]{:T(128)S(6)} %select_n.9, f32[256,8,8]{0,2,1:T(8,128)} %bitcast.31), kind=kLoop, calls=%fused_computation.1 | loop fusion | bytes 65540 | tf_op jit(solution)/shard_map/dynamic_slice | solution.py:516
  15.6 0.1 copy.21
  15.8 0.2 reshape.37.refs_7_
  15.9 0.1 copy.20
  16.1 0.2 reshape.35.refs_6_
  16.2 0.1 copy.19
  16.3 0.1 copy.18
  16.4 0.1 collective-permute-start.9
  16.5 0.7 %collective-permute-done.5.refs_3_ = bf16[4,2,2,16,128]{4,3,2,1,0:T(8,128)(2,1)S(1)} collective-permute-done((bf16[4,2,2,16,128]{4,3,2,1,0:T(8,128)(2,1)S(1)}, bf16[4,2,2,16,128]{4,3,2,1,0:T(8,128)(2,1)S(1)}, u32[]{:S(2)}, u32[]{:S(2)}) %collective-permute-start.5) | collective-permute-done | bytes 65568 | tf_op jit(solution)/shard_map/ppermute | solution.py:485
  17.2 0.0 collective-permute-start.6
  17.2 1.0 %collective-permute-done.4.refs_2_ = bf16[4,2,2,16,128]{4,3,2,1,0:T(8,128)(2,1)S(1)} collective-permute-done((bf16[4,2,2,16,128]{4,3,2,1,0:T(8,128)(2,1)S(1)}, bf16[4,2,2,16,128]{4,3,2,1,0:T(8,128)(2,1)S(1)}, u32[]{:S(2)}, u32[]{:S(2)}) %collective-permute-start.4) | collective-permute-done | bytes 65568 | tf_op jit(solution)/shard_map/ppermute | solution.py:485
  18.1 0.0 collective-permute-start.7
  18.1 0.5 %collective-permute-done.3.refs_1_ = bf16[4,2,2,16,128]{4,3,2,1,0:T(8,128)(2,1)S(1)} collective-permute-done((bf16[4,2,2,16,128]{4,3,2,1,0:T(8,128)(2,1)S(1)}, bf16[4,2,2,16,128]{4,3,2,1,0:T(8,128)(2,1)S(1)}, u32[]{:S(2)}, u32[]{:S(2)}) %collective-permute-start.3) | collective-permute-done | bytes 65568 | tf_op jit(solution)/shard_map/ppermute | solution.py:485
  18.6 0.0 collective-permute-start.8
  18.6 1.6 %first_half.1 = (f32[8,256,256]{2,1,0:T(8,128)S(1)}, f32[8,256,256]{2,1,0:T(8,128)S(1)}, f32[8,256,256]{2,1,0:T(8,128)S(1)}, f32[8,256,256]{2,1,0:T(8,128)S(1)},...) custom-call(bf16[4,2,2,16,128]{4,3,2,1,0:T(8,128)(2,1)S(1)} %pad_maximum_fusion.refs_0_, ...), custom_call_target="tpu_custom_call" | custom-call | flops 536870912 | bytes 8388608 | tf_op jit(solution)/shard_map/first_half/pallas_call | solution.py:213
  20.2 0.0 collective-permute-done.9.refs_3_
  20.3 0.0 collective-permute-done.6.refs_0_
  20.3 0.0 collective-permute-done.7.refs_1_
  20.3 0.0 collective-permute-done.8.refs_2_
  20.3 3.4 %second_half.1 = (bf16[4,4,2,2,16,128]{5,4,3,2,1,0:T(8,128)(2,1)S(1)}, f32[16,1,256]{2,1,0:T(1,128)S(1)}, f32[16,1,256]{2,1,0:T(1,128)S(1)}) custom-call(bf16[4,2,2,16,128]{4,3,2,1,0:T(8,128)(2,1)S(1)} %collective-permute-done.6.refs_0_, bf16[4,2,2,16,128]{4,3,2,1,0:T(8,128)(2,1)S(1)} %collective-permute-done.7.refs_1_, ...), custom_call_target="tpu_custom_call" | custom-call | flops 1073741824 | bytes 2097152 | tf_op jit(solution)/shard_map/second_half/pallas_call | solution.py:309
  23.7 0.6 %collective-permute-start.10 = (bf16[4,4,2,2,16,128]{5,4,3,2,1,0:T(8,128)(2,1)S(1)}, bf16[4,4,2,2,16,128]{5,4,3,2,1,0:T(8,128)(2,1)S(1)}, u32[]{:S(2)}, u32[]{:S(2)}) collective-permute-start(bf16[4,4,2,2,16,128]{5,4,3,2,1,0:T(8,128)(2,1)S(1)} %get-tuple-element.48), channel_id=1, source_target_pairs={{0,4},{4,0},{8,12},{12,8},{16,20},{20,16},{24,28},{28,24},{1,5},{5... | collective-permute-start | bytes 786440 | tf_op jit(solution)/shard_map/ppermute | solution.py:485
  24.3 0.0 copy-start.1
  24.3 0.0 copy-start.2
  24.3 0.0 copy-start.3
  24.3 1.2 %finish.1.mine_ref = f32[4,4,2,2,16,128]{5,4,3,2,1,0:T(8,128)S(1)} custom-call(f32[8,256,256]{2,1,0:T(8,128)S(1)} %get-tuple-element.38.refs_0_, f32[8,256,256]{2,1,0:T(8,128)S(1)} %get-tuple-element.39.refs_1_, f32[8,256,256]{2,1,0:T(8,128)S(1)} %get-tuple-element.40.refs_2_, f32[8,256,256]{2,1,0:T(8,128)S(1)} %get-tuple-element.41.refs_3_, ...), custom_call_target="tpu_custom_call" | custom-call | flops 536870912 | bytes 8388608 | tf_op jit(solution)/shard_map/finish/pallas_call | solution.py:380
  25.6 0.0 collective-permute-done.10.mate_ref
  25.6 1.6 %collective-permute-start.11 = (bf16[4,2,2,16,128]{4,3,2,1,0:T(8,128)(2,1)S(1)}, bf16[4,2,2,16,128]{4,3,2,1,0:T(8,128)(2,1)S(1)}, u32[]{:S(2)}, u32[]{:S(2)}) collective-permute-start(bf16[4,2,2,16,128]{4,3,2,1,0:T(8,128)(2,1)S(1)} %get-tuple-element.50), channel_id=1, source_target_pairs={{0,24},{4,28},{8,16},{12,20},{16,8},{20,12},{24,0},{28,4},{1,25},{... | collective-permute-start | bytes 196616 | tf_op jit(solution)/shard_map/ppermute | solution.py:485
  27.2 0.5 %collective-permute-start.12 = (bf16[4,2,2,16,128]{4,3,2,1,0:T(8,128)(2,1)S(1)}, bf16[4,2,2,16,128]{4,3,2,1,0:T(8,128)(2,1)S(1)}, u32[]{:S(2)}, u32[]{:S(2)}) collective-permute-start(bf16[4,2,2,16,128]{4,3,2,1,0:T(8,128)(2,1)S(1)} %get-tuple-element.51), channel_id=1, source_target_pairs={{0,16},{4,20},{8,24},{12,28},{16,0},{20,4},{24,8},{28,12},{1,17},{... | collective-permute-start | bytes 196616 | tf_op jit(solution)/shard_map/ppermute | solution.py:485
  27.7 1.5 %collective-permute-start.13 = (bf16[4,2,2,16,128]{4,3,2,1,0:T(8,128)(2,1)S(1)}, bf16[4,2,2,16,128]{4,3,2,1,0:T(8,128)(2,1)S(1)}, u32[]{:S(2)}, u32[]{:S(2)}) collective-permute-start(bf16[4,2,2,16,128]{4,3,2,1,0:T(8,128)(2,1)S(1)} %get-tuple-element.52), channel_id=1, source_target_pairs={{0,8},{4,12},{8,0},{12,4},{16,24},{20,28},{24,16},{28,20},{1,9},{5... | collective-permute-start | bytes 196616 | tf_op jit(solution)/shard_map/ppermute | solution.py:485
  29.2 1.8 %collective-permute-done.11.refs_0_ = bf16[4,2,2,16,128]{4,3,2,1,0:T(8,128)(2,1)S(1)} collective-permute-done((bf16[4,2,2,16,128]{4,3,2,1,0:T(8,128)(2,1)S(1)}, bf16[4,2,2,16,128]{4,3,2,1,0:T(8,128)(2,1)S(1)}, u32[]{:S(2)}, u32[]{:S(2)}) %collective-permute-start.11) | collective-permute-done | bytes 65568 | tf_op jit(solution)/shard_map/ppermute | solution.py:485
  30.9 1.3 %collective-permute-done.12.refs_1_ = bf16[4,2,2,16,128]{4,3,2,1,0:T(8,128)(2,1)S(1)} collective-permute-done((bf16[4,2,2,16,128]{4,3,2,1,0:T(8,128)(2,1)S(1)}, bf16[4,2,2,16,128]{4,3,2,1,0:T(8,128)(2,1)S(1)}, u32[]{:S(2)}, u32[]{:S(2)}) %collective-permute-start.12) | collective-permute-done | bytes 65568 | tf_op jit(solution)/shard_map/ppermute | solution.py:485
  32.2 0.1 collective-permute-done.13.refs_2_
  32.3 2.1 %collective-permute-start.14 = (bf16[2,2,16,128]{3,2,1,0:T(8,128)(2,1)S(1)}, bf16[2,2,16,128]{3,2,1,0:T(8,128)(2,1)S(1)}, u32[]{:S(2)}, u32[]{:S(2)}) collective-permute-start(bf16[2,2,16,128]{3,2,1,0:T(8,128)(2,1)S(1)} %get-tuple-element.53), channel_id=1, source_target_pairs={{0,3},{1,2},{2,1},{3,0},{4,7},{5,6},{6,5},{7,4},{8,11},{9,10},{10,... | collective-permute-start | bytes 49160 | tf_op jit(solution)/shard_map/ppermute | solution.py:485
  34.4 0.0 collective-permute-start.15
  34.4 2.4 %collective-permute-start.16 = (bf16[2,2,16,128]{3,2,1,0:T(8,128)(2,1)S(1)}, bf16[2,2,16,128]{3,2,1,0:T(8,128)(2,1)S(1)}, u32[]{:S(2)}, u32[]{:S(2)}) collective-permute-start(bf16[2,2,16,128]{3,2,1,0:T(8,128)(2,1)S(1)} %get-tuple-element.55), channel_id=1, source_target_pairs={{0,1},{1,0},{2,3},{3,2},{4,5},{5,4},{6,7},{7,6},{8,9},{9,8},{10,11... | collective-permute-start | bytes 49160 | tf_op jit(solution)/shard_map/ppermute | solution.py:485
  36.8 1.2 %collective-permute-done.14.refs_0_ = bf16[2,2,16,128]{3,2,1,0:T(8,128)(2,1)S(1)} collective-permute-done((bf16[2,2,16,128]{3,2,1,0:T(8,128)(2,1)S(1)}, bf16[2,2,16,128]{3,2,1,0:T(8,128)(2,1)S(1)}, u32[]{:S(2)}, u32[]{:S(2)}) %collective-permute-start.14) | collective-permute-done | bytes 16416 | tf_op jit(solution)/shard_map/ppermute | solution.py:485
  38.0 1.1 %collective-permute-done.15.refs_1_ = bf16[2,2,16,128]{3,2,1,0:T(8,128)(2,1)S(1)} collective-permute-done((bf16[2,2,16,128]{3,2,1,0:T(8,128)(2,1)S(1)}, bf16[2,2,16,128]{3,2,1,0:T(8,128)(2,1)S(1)}, u32[]{:S(2)}, u32[]{:S(2)}) %collective-permute-start.15) | collective-permute-done | bytes 16416 | tf_op jit(solution)/shard_map/ppermute | solution.py:485
  39.1 0.0 collective-permute-done.16.refs_2_
  39.1 0.0 copy-done.1
  39.1 0.0 copy-done.2
  39.1 0.0 copy-done.3
  39.1 0.9 %adam.1 = (f32[16,2,8,128]{3,2,1,0:T(8,128)}, f32[16,2,8,128]{3,2,1,0:T(8,128)}, f32[16,2,8,128]{3,2,1,0:T(8,128)}) custom-call(bf16[2,2,16,128]{3,2,1,0:T(8,128)(2,1)S(1)} %collective-permute-done.14.refs_0_, bf16[2,2,16,128]{3,2,1,0:T(8,128)(2,1)S(1)} %collective-permute-done.15.refs_1_, bf16[2,2,16,128]{3,2,1,0:T(8,128)(2,1)S(1)} %collective-permute-done.16.refs_2_, ...), custom_call_target="tpu_custom_call" | custom-call | tf_op jit(solution)/shard_map/adam/pallas_call | solution.py:472
  (3 shorter events, 0.1 us)
Async XLA Ops:
  0.6 0.9 %copy-start = (f32[16,2,8,128]{3,2,1,0:T(8,128)S(1)}, f32[16,2,8,128]{3,2,1,0:T(8,128)}, u32[]{:S(2)}) copy-start(f32[16,2,8,128]{3,2,1,0:T(8,128)} %refs_4_.1) | copy-start | bytes 393220
  1.7 7.6 %collective-permute-start = (bf16[2,2,16,128]{3,2,1,0:T(8,128)(2,1)S(1)}, bf16[2,2,16,128]{3,2,1,0:T(8,128)(2,1)S(1)}, u32[]{:S(2)}, u32[]{:S(2)}) collective-permute-start(bf16[2,2,16,128]{3,2,1,0:T(8,128)(2,1)S(1)} %get-tuple-element.30), channel_id=1, source_target_pairs={{0,2},{1,3},{2,0},{3,1},{4,6},{5,7},{6,4},{7,5},{8,10},{9,11},{10,... | collective-permute-start | bytes 49160 | tf_op jit(solution)/shard_map/ppermute | solution.py:485
  5.8 5.5 %collective-permute-start.1 = (bf16[2,2,16,128]{3,2,1,0:T(8,128)(2,1)S(1)}, bf16[2,2,16,128]{3,2,1,0:T(8,128)(2,1)S(1)}, u32[]{:S(2)}, u32[]{:S(2)}) collective-permute-start(bf16[2,2,16,128]{3,2,1,0:T(8,128)(2,1)S(1)} %get-tuple-element.31), channel_id=1, source_target_pairs={{0,3},{1,2},{2,1},{3,0},{4,7},{5,6},{6,5},{7,4},{8,11},{9,10},{10,... | collective-permute-start | bytes 49160 | tf_op jit(solution)/shard_map/ppermute | solution.py:485
  7.1 4.2 %collective-permute-start.2 = (bf16[2,2,16,128]{3,2,1,0:T(8,128)(2,1)S(1)}, bf16[2,2,16,128]{3,2,1,0:T(8,128)(2,1)S(1)}, u32[]{:S(2)}, u32[]{:S(2)}) collective-permute-start(bf16[2,2,16,128]{3,2,1,0:T(8,128)(2,1)S(1)} %get-tuple-element.32), channel_id=1, source_target_pairs={{0,1},{1,0},{2,3},{3,2},{4,5},{5,4},{6,7},{7,6},{8,9},{9,8},{10,11... | collective-permute-start | bytes 49160 | tf_op jit(solution)/shard_map/ppermute | solution.py:485
  11.3 5.8 %collective-permute-start.5 = (bf16[4,2,2,16,128]{4,3,2,1,0:T(8,128)(2,1)S(1)}, bf16[4,2,2,16,128]{4,3,2,1,0:T(8,128)(2,1)S(1)}, u32[]{:S(2)}, u32[]{:S(2)}) collective-permute-start(bf16[4,2,2,16,128]{4,3,2,1,0:T(8,128)(2,1)S(1)} %pad_maximum_fusion.refs_0_), channel_id=1, source_target_pairs={{0,24},{4,28},{8,16},{12,20},{16,8},{20,12},{24,0},{28,4},{1,25},{... | collective-permute-start | bytes 196616 | tf_op jit(solution)/shard_map/ppermute | solution.py:485
  13.9 4.3 %collective-permute-start.4 = (bf16[4,2,2,16,128]{4,3,2,1,0:T(8,128)(2,1)S(1)}, bf16[4,2,2,16,128]{4,3,2,1,0:T(8,128)(2,1)S(1)}, u32[]{:S(2)}, u32[]{:S(2)}) collective-permute-start(bf16[4,2,2,16,128]{4,3,2,1,0:T(8,128)(2,1)S(1)} %pad_maximum_fusion.refs_0_), channel_id=1, source_target_pairs={{0,16},{4,20},{8,24},{12,28},{16,0},{20,4},{24,8},{28,12},{1,17},{... | collective-permute-start | bytes 196616 | tf_op jit(solution)/shard_map/ppermute | solution.py:485
  14.4 4.3 %collective-permute-start.3 = (bf16[4,2,2,16,128]{4,3,2,1,0:T(8,128)(2,1)S(1)}, bf16[4,2,2,16,128]{4,3,2,1,0:T(8,128)(2,1)S(1)}, u32[]{:S(2)}, u32[]{:S(2)}) collective-permute-start(bf16[4,2,2,16,128]{4,3,2,1,0:T(8,128)(2,1)S(1)} %pad_maximum_fusion.refs_0_), channel_id=1, source_target_pairs={{0,8},{4,12},{8,0},{12,4},{16,24},{20,28},{24,16},{28,20},{1,9},{5... | collective-permute-start | bytes 196616 | tf_op jit(solution)/shard_map/ppermute | solution.py:485
  16.4 3.9 %collective-permute-start.9 = (bf16[4,2,2,16,128]{4,3,2,1,0:T(8,128)(2,1)S(1)}, bf16[4,2,2,16,128]{4,3,2,1,0:T(8,128)(2,1)S(1)}, u32[]{:S(2)}, u32[]{:S(2)}) collective-permute-start(bf16[4,2,2,16,128]{4,3,2,1,0:T(8,128)(2,1)S(1)} %pad_maximum_fusion.refs_0_), channel_id=1, source_target_pairs={{0,4},{4,0},{8,12},{12,8},{16,20},{20,16},{24,28},{28,24},{1,5},{5... | collective-permute-start | bytes 196616 | tf_op jit(solution)/shard_map/ppermute | solution.py:485
  17.2 3.1 %collective-permute-start.6 = (bf16[4,2,2,16,128]{4,3,2,1,0:T(8,128)(2,1)S(1)}, bf16[4,2,2,16,128]{4,3,2,1,0:T(8,128)(2,1)S(1)}, u32[]{:S(2)}, u32[]{:S(2)}) collective-permute-start(bf16[4,2,2,16,128]{4,3,2,1,0:T(8,128)(2,1)S(1)} %collective-permute-done.5.refs_3_), channel_id=1, source_target_pairs={{0,4},{4,0},{8,12},{12,8},{16,20},{20,16},{24,28},{28,24},{1,5},{5... | collective-permute-start | bytes 196616 | tf_op jit(solution)/shard_map/ppermute | solution.py:485
  18.1 2.2 %collective-permute-start.7 = (bf16[4,2,2,16,128]{4,3,2,1,0:T(8,128)(2,1)S(1)}, bf16[4,2,2,16,128]{4,3,2,1,0:T(8,128)(2,1)S(1)}, u32[]{:S(2)}, u32[]{:S(2)}) collective-permute-start(bf16[4,2,2,16,128]{4,3,2,1,0:T(8,128)(2,1)S(1)} %collective-permute-done.4.refs_2_), channel_id=1, source_target_pairs={{0,4},{4,0},{8,12},{12,8},{16,20},{20,16},{24,28},{28,24},{1,5},{5... | collective-permute-start | bytes 196616 | tf_op jit(solution)/shard_map/ppermute | solution.py:485
  18.6 1.7 %collective-permute-start.8 = (bf16[4,2,2,16,128]{4,3,2,1,0:T(8,128)(2,1)S(1)}, bf16[4,2,2,16,128]{4,3,2,1,0:T(8,128)(2,1)S(1)}, u32[]{:S(2)}, u32[]{:S(2)}) collective-permute-start(bf16[4,2,2,16,128]{4,3,2,1,0:T(8,128)(2,1)S(1)} %collective-permute-done.3.refs_1_), channel_id=1, source_target_pairs={{0,4},{4,0},{8,12},{12,8},{16,20},{20,16},{24,28},{28,24},{1,5},{5... | collective-permute-start | bytes 196616 | tf_op jit(solution)/shard_map/ppermute | solution.py:485
  23.7 1.8 %collective-permute-start.10 = (bf16[4,4,2,2,16,128]{5,4,3,2,1,0:T(8,128)(2,1)S(1)}, bf16[4,4,2,2,16,128]{5,4,3,2,1,0:T(8,128)(2,1)S(1)}, u32[]{:S(2)}, u32[]{:S(2)}) collective-permute-start(bf16[4,4,2,2,16,128]{5,4,3,2,1,0:T(8,128)(2,1)S(1)} %get-tuple-element.48), channel_id=1, source_target_pairs={{0,4},{4,0},{8,12},{12,8},{16,20},{20,16},{24,28},{28,24},{1,5},{5... | collective-permute-start | bytes 786440 | tf_op jit(solution)/shard_map/ppermute | solution.py:485
  24.3 14.8 %copy-start.1 = (f32[16,2,8,128]{3,2,1,0:T(8,128)S(1)}, f32[16,2,8,128]{3,2,1,0:T(8,128)}, u32[]{:S(2)}) copy-start(f32[16,2,8,128]{3,2,1,0:T(8,128)} %refs_4_.1) | copy-start | bytes 393220
  24.3 14.8 %copy-start.2 = (f32[16,2,8,128]{3,2,1,0:T(8,128)S(1)}, f32[16,2,8,128]{3,2,1,0:T(8,128)}, u32[]{:S(2)}) copy-start(f32[16,2,8,128]{3,2,1,0:T(8,128)} %refs_5_.1) | copy-start | bytes 393220
  24.3 14.8 %copy-start.3 = (f32[16,2,8,128]{3,2,1,0:T(8,128)S(1)}, f32[16,2,8,128]{3,2,1,0:T(8,128)}, u32[]{:S(2)}) copy-start(f32[16,2,8,128]{3,2,1,0:T(8,128)} %refs_6_.1) | copy-start | bytes 393220
  25.6 5.3 %collective-permute-start.11 = (bf16[4,2,2,16,128]{4,3,2,1,0:T(8,128)(2,1)S(1)}, bf16[4,2,2,16,128]{4,3,2,1,0:T(8,128)(2,1)S(1)}, u32[]{:S(2)}, u32[]{:S(2)}) collective-permute-start(bf16[4,2,2,16,128]{4,3,2,1,0:T(8,128)(2,1)S(1)} %get-tuple-element.50), channel_id=1, source_target_pairs={{0,24},{4,28},{8,16},{12,20},{16,8},{20,12},{24,0},{28,4},{1,25},{... | collective-permute-start | bytes 196616 | tf_op jit(solution)/shard_map/ppermute | solution.py:485
  27.2 5.1 %collective-permute-start.12 = (bf16[4,2,2,16,128]{4,3,2,1,0:T(8,128)(2,1)S(1)}, bf16[4,2,2,16,128]{4,3,2,1,0:T(8,128)(2,1)S(1)}, u32[]{:S(2)}, u32[]{:S(2)}) collective-permute-start(bf16[4,2,2,16,128]{4,3,2,1,0:T(8,128)(2,1)S(1)} %get-tuple-element.51), channel_id=1, source_target_pairs={{0,16},{4,20},{8,24},{12,28},{16,0},{20,4},{24,8},{28,12},{1,17},{... | collective-permute-start | bytes 196616 | tf_op jit(solution)/shard_map/ppermute | solution.py:485
  27.7 4.6 %collective-permute-start.13 = (bf16[4,2,2,16,128]{4,3,2,1,0:T(8,128)(2,1)S(1)}, bf16[4,2,2,16,128]{4,3,2,1,0:T(8,128)(2,1)S(1)}, u32[]{:S(2)}, u32[]{:S(2)}) collective-permute-start(bf16[4,2,2,16,128]{4,3,2,1,0:T(8,128)(2,1)S(1)} %get-tuple-element.52), channel_id=1, source_target_pairs={{0,8},{4,12},{8,0},{12,4},{16,24},{20,28},{24,16},{28,20},{1,9},{5... | collective-permute-start | bytes 196616 | tf_op jit(solution)/shard_map/ppermute | solution.py:485
  32.3 5.6 %collective-permute-start.14 = (bf16[2,2,16,128]{3,2,1,0:T(8,128)(2,1)S(1)}, bf16[2,2,16,128]{3,2,1,0:T(8,128)(2,1)S(1)}, u32[]{:S(2)}, u32[]{:S(2)}) collective-permute-start(bf16[2,2,16,128]{3,2,1,0:T(8,128)(2,1)S(1)} %get-tuple-element.53), channel_id=1, source_target_pairs={{0,3},{1,2},{2,1},{3,0},{4,7},{5,6},{6,5},{7,4},{8,11},{9,10},{10,... | collective-permute-start | bytes 49160 | tf_op jit(solution)/shard_map/ppermute | solution.py:485
  34.4 4.6 %collective-permute-start.15 = (bf16[2,2,16,128]{3,2,1,0:T(8,128)(2,1)S(1)}, bf16[2,2,16,128]{3,2,1,0:T(8,128)(2,1)S(1)}, u32[]{:S(2)}, u32[]{:S(2)}) collective-permute-start(bf16[2,2,16,128]{3,2,1,0:T(8,128)(2,1)S(1)} %get-tuple-element.54), channel_id=1, source_target_pairs={{0,2},{1,3},{2,0},{3,1},{4,6},{5,7},{6,4},{7,5},{8,10},{9,11},{10,... | collective-permute-start | bytes 49160 | tf_op jit(solution)/shard_map/ppermute | solution.py:485
  34.4 4.6 %collective-permute-start.16 = (bf16[2,2,16,128]{3,2,1,0:T(8,128)(2,1)S(1)}, bf16[2,2,16,128]{3,2,1,0:T(8,128)(2,1)S(1)}, u32[]{:S(2)}, u32[]{:S(2)}) collective-permute-start(bf16[2,2,16,128]{3,2,1,0:T(8,128)(2,1)S(1)} %get-tuple-element.55), channel_id=1, source_target_pairs={{0,1},{1,0},{2,3},{3,2},{4,5},{5,4},{6,7},{7,6},{8,9},{9,8},{10,11... | collective-permute-start | bytes 49160 | tf_op jit(solution)/shard_map/ppermute | solution.py:485
